TPU v7x, 32 devices: a whole 2x2x4 slice. The times are simulated.
32 devices in a mesh: dp: 16 (over z, y, core), tensor: 2 (over x).
Axes of the slice: x: 2, y: 2, z: 4, core: 2. Of those that a mesh axis runs over, the one named last changes fastest.
Arguments:
- tokens: bfloat16 [8192, 2048], P('dp'), may hold values from -6 to 6
- cotangent: bfloat16 [8192, 2048], P('dp'), may hold values from -6 to 6
- segment_ids: int32 [8192], P('dp'), may hold values from 0 to 47, as said below
- counts: int32 [16], P('dp'), may hold values from 256 to 512, as said below
- mixer_gain: bfloat16 [2048], P(('dp', 'tensor')), may hold values from 0.5 to 1.5
- query_proj: bfloat16 [2048, 1024], P('dp', 'tensor'), may hold values from -0.125 to 0.125
- key_value_matrix: bfloat16 [2048, 2, 256], P('dp', None, 'tensor'), may hold values from -0.125 to 0.125
- attend_proj: bfloat16 [1024, 2048], P('tensor', 'dp'), may hold values from -1 to 1
- inner_proj: bfloat16 [2048, 2, 3072], P('dp', None, 'tensor'), may hold values from -0.125 to 0.125
- state_proj: bfloat16 [2048, 512], P(('dp', 'tensor')), may hold values from -0.125 to 0.125
- step_proj: bfloat16 [2048, 48], P('dp', 'tensor'), may hold values from -0.125 to 0.125
- conv_inner: bfloat16 [5, 3072], P(None, 'tensor'), may hold values from -3 to 3
- conv_state: bfloat16 [5, 512], P(None, ('dp', 'tensor')), may hold values from -3 to 3
- step_bias: bfloat16 [48], P('tensor'), may hold values from -5 to -1
- decay_log: bfloat16 [48], P('tensor'), may hold values from 0 to 2.5
- skip_gain: bfloat16 [48], P('tensor'), may hold values from 0.5 to 1.5
- gated_gain: bfloat16 [3072], P('tensor'), may hold values from 0.5 to 1.5
- mamba_proj: bfloat16 [3072, 2048], P('tensor', 'dp'), may hold values from -0.109375 to 0.109375
- dense_gain: bfloat16 [2048], P(('dp', 'tensor')), may hold values from 0.5 to 1.5
- gateup_proj: bfloat16 [2048, 2, 4096], P('dp', None, 'tensor'), may hold values from -0.125 to 0.125
- down_proj: bfloat16 [4096, 2048], P('tensor', 'dp'), may hold values from -0.1875 to 0.1875
Outputs:
- output: bfloat16 [8192, 2048], P('dp')
- grad_tokens: float32 [8192, 2048], P('dp')
- grad_mixer_gain: float32 [2048], P(('dp', 'tensor'))
- grad_query_proj: float32 [2048, 1024], P('dp', 'tensor')
- grad_keyval_proj: float32 [2048, 2, 256], P('dp', None, 'tensor')
- grad_attend_proj: float32 [1024, 2048], P('tensor', 'dp')
- grad_inner_proj: float32 [2048, 2, 3072], P('dp', None, 'tensor')
- grad_state_proj: float32 [2048, 512], P(('dp', 'tensor'))
- grad_step_proj: float32 [2048, 48], P('dp', 'tensor')
- grad_conv_inner: float32 [5, 3072], P(None, 'tensor')
- grad_conv_state: float32 [5, 512], P(None, ('dp', 'tensor'))
- grad_step_bias: float32 [48], P('tensor')
- grad_decay_log: float32 [48], P('tensor')
- grad_skip_gain: float32 [48], P('tensor')
- grad_gated_gain: float32 [3072], P('tensor')
- grad_mamba_proj: float32 [3072, 2048], P('tensor', 'dp')
- grad_dense_gain: float32 [2048], P(('dp', 'tensor'))
- grad_gateup_proj: float32 [2048, 2, 4096], P('dp', None, 'tensor')
- grad_down_proj: float32 [4096, 2048], P('tensor', 'dp')
Inputs may be any that keep to these rules, and one draw needn't show every extreme that they name: `counts`: row slots at or past a device's count are padding. One index of dp holds exactly 512 live rows and another exactly 256. `segment_ids`: never falling along the rows. A device's rows hold at most three documents of its own, numbered from 3 times its dp index; no document crosses devices; padding rows carry the number of the device's last document.
All inputs are finite; a program needn't handle non-finite values.
Results may differ from a plain program's by a relative error of at most 0.022.
Values may be sent and summed in bfloat16 or wider, within the bound.
A program may use at most 256 MiB of HBM per device.

v0:
```python
import math

import jax
import jax.numpy as jnp
from jax import lax
from jax.sharding import PartitionSpec as P

HP = 64
HEAD_DIMENSION = 128
DSSM = 3072


EPS = 1e-05
THETA = 100000000000.0


def rounded(values):
    return values.astype(jnp.bfloat16)


def matrix_product(left, right):
    return jnp.dot(left, right, preferred_element_type=jnp.float32)


def contract(form, left, right):
    return jnp.einsum(form, left, right, preferred_element_type=jnp.float32)


def rms_scale(values, gain):
    return values * lax.rsqrt(jnp.mean(values * values, axis=-1, keepdims=True) + EPS) * gain


def positions_of(segment):
    row_index = jnp.arange(segment.shape[0], dtype=jnp.int32)
    starts = jnp.concatenate([jnp.ones((1,), jnp.bool_), segment[1:] != segment[:-1]])
    first_row = lax.cummax(jnp.where(starts, row_index, 0), axis=0)
    return row_index - first_row


def rotate(values, position, direction):
    half_width = values.shape[-1] // 2
    frequency = jnp.exp(
        jnp.arange(half_width, dtype=jnp.float32) * (-2.0 * math.log(THETA) / values.shape[-1])
    )
    angles = position.astype(jnp.float32)[:, None] * frequency[None, :]
    cos_table = jnp.cos(angles)[:, None, :]
    sin_table = jnp.sin(angles)[:, None, :] * direction
    first_half = values[..., :half_width]
    second_half = values[..., half_width:]
    return jnp.concatenate(
        [
            first_half * cos_table - second_half * sin_table,
            second_half * cos_table + first_half * sin_table,
        ],
        axis=-1,
    )


def causal_conv(values, kernel, segment):
    tap_count = kernel.shape[0] - 1
    summed = kernel[tap_count] + kernel[tap_count - 1] * values
    for lag_step in range(1, tap_count):
        shifted = jnp.concatenate(
            [jnp.zeros((lag_step, values.shape[1]), values.dtype), values[:-lag_step]], axis=0
        )
        same_doc = jnp.concatenate(
            [jnp.zeros((lag_step,), jnp.bool_), segment[lag_step:] == segment[:-lag_step]]
        )
        summed = summed + kernel[tap_count - 1 - lag_step] * jnp.where(
            same_doc[:, None], shifted, 0.0
        )
    return summed


def decay_matrix(log_decay, causal):
    running = jnp.cumsum(log_decay, axis=0).T
    gaps_ij = running[:, :, None] - running[:, None, :]
    return jnp.where(causal[None], jnp.exp(jnp.where(causal[None], gaps_ij, -60.0)), 0.0)


def conv_silu(values, kernel, segment, valid_rows):
    return jax.nn.silu(causal_conv(values * valid_rows, kernel, segment))


def step_piece(step_raw, bias_in, rate_in, valid_rows):
    step_size = jax.nn.softplus(step_raw + bias_in) * valid_rows
    return (step_size, step_size * -jnp.exp(rate_in))


def local(
    tokens,
    cotangent,
    segment_ids,
    counts,
    mixer_gain,
    query_proj,
    key_value_matrix,
    attend_proj,
    inner_proj,
    state_proj,
    step_proj,
    conv_inner,
    conv_state,
    step_bias,
    decay_log,
    skip_gain,
    gated_gain,
    mamba_proj,
    dense_gain,
    gateup_proj,
    down_proj,
):
    weights_f = (
        lax.all_gather(query_proj, "dp", axis=0, tiled=True),
        lax.all_gather(key_value_matrix, "dp", axis=0, tiled=True),
        lax.all_gather(attend_proj, "dp", axis=1, tiled=True),
        lax.all_gather(inner_proj, "dp", axis=0, tiled=True),
        lax.all_gather(step_proj, "dp", axis=0, tiled=True),
        lax.all_gather(mamba_proj, "dp", axis=1, tiled=True),
        lax.all_gather(gateup_proj, "dp", axis=0, tiled=True),
        lax.all_gather(down_proj, "dp", axis=1, tiled=True),
    )
    shared_f = (
        lax.all_gather(state_proj, ("dp", "tensor"), axis=0, tiled=True),
        lax.all_gather(mixer_gain, ("dp", "tensor"), axis=0, tiled=True),
        lax.all_gather(dense_gain, ("dp", "tensor"), axis=0, tiled=True),
        lax.all_gather(conv_state, ("dp", "tensor"), axis=1, tiled=True),
    )
    wq_full, wkv_full, wo_full, winner_full, wstep_full, wmamba_full, wgu_full, wdown_full = (
        weights_f
    )
    wstate_full = shared_f[0]
    gain_mix = shared_f[1].astype(jnp.float32)
    gain_dense = shared_f[2].astype(jnp.float32)
    kernel_state = shared_f[3].astype(jnp.float32)
    kernel_inner = conv_inner.astype(jnp.float32)
    bias_step = step_bias.astype(jnp.float32)
    log_rates = decay_log.astype(jnp.float32)
    skip_heads = skip_gain.astype(jnp.float32)
    gain_gated = gated_gain.astype(jnp.float32)
    row_count = tokens.shape[0]
    model_width = tokens.shape[1]
    row_index = jnp.arange(row_count, dtype=jnp.int32)
    valid_rows = (row_index < counts[0]).astype(jnp.float32)[:, None]
    position = positions_of(segment_ids)
    causal = (row_index[None, :] <= row_index[:, None]) & (
        segment_ids[None, :] == segment_ids[:, None]
    )
    mask_qk = causal & (row_index[None, :] < counts[0])
    stream = tokens.astype(jnp.float32)
    normed_in = rms_scale(stream, gain_mix)
    hidden_b = rounded(normed_in)
    query_raw = matrix_product(hidden_b, wq_full).reshape(row_count, -1, HEAD_DIMENSION)
    keyval = matrix_product(hidden_b, wkv_full.reshape(model_width, -1)).reshape(
        row_count, 2, -1, HEAD_DIMENSION
    )
    inner = matrix_product(hidden_b, winner_full.reshape(model_width, -1)).reshape(row_count, 2, -1)
    state_in = matrix_product(hidden_b, wstate_full)
    step_raw = matrix_product(hidden_b, wstep_full)
    heads_q = query_raw.shape[1]
    heads_kv = keyval.shape[2]
    group_size = heads_q // heads_kv
    score_scale = HEAD_DIMENSION ** (-0.5)
    query_b = rounded(rotate(query_raw, position, 1.0)).reshape(
        row_count, heads_kv, group_size, HEAD_DIMENSION
    )
    key_b = rounded(rotate(keyval[:, 0], position, 1.0))
    value_b = rounded(keyval[:, 1])

    def masked_scores():
        raw_scores = contract("ikgd,jkd->kgij", query_b, key_b) * score_scale
        return jnp.where(mask_qk[None, None], raw_scores, -1e30)

    scores = masked_scores()
    top_score = jnp.max(scores, axis=-1, keepdims=True)
    weights = jnp.exp(scores - top_score)
    totals = jnp.sum(weights, axis=-1, keepdims=True)
    probs = weights / totals
    log_total = top_score + jnp.log(totals)
    attended_b = rounded(contract("kgij,jkd->ikgd", rounded(probs), value_b).reshape(row_count, -1))
    gate_z = inner[:, 0]
    inner_x = inner[:, 1]
    conv_x, pull_conv_x = jax.vjp(
        lambda values, kernel: conv_silu(values, kernel, segment_ids, valid_rows),
        inner_x,
        kernel_inner,
    )
    conv_bc, pull_conv_bc = jax.vjp(
        lambda values, kernel: conv_silu(values, kernel, segment_ids, valid_rows),
        state_in,
        kernel_state,
    )
    (step_size, log_decay), pull_step = jax.vjp(
        lambda raw_in, bias_in, rate_in: step_piece(raw_in, bias_in, rate_in, valid_rows),
        step_raw,
        bias_step,
        log_rates,
    )
    state_width = conv_bc.shape[1] // 2
    state_b = rounded(conv_bc[:, :state_width])
    state_c = rounded(conv_bc[:, state_width:])
    gram_mat = contract("in,jn->ij", state_c, state_b)
    mixing_f, pull_mixing = jax.vjp(
        lambda gram_in, decay_in: gram_in[None] * decay_matrix(decay_in, causal),
        gram_mat,
        log_decay,
    )
    mixing_b = rounded(mixing_f)
    heads_m = step_size.shape[1]
    x_heads = conv_x.reshape(row_count, heads_m, HP)
    inflow_b = rounded(step_size[:, :, None] * x_heads)
    ssm_out = contract("hij,jhp->ihp", mixing_b, inflow_b)
    mixed_y = (ssm_out + skip_heads[None, :, None] * x_heads).reshape(row_count, -1)
    gated_y, pull_gate = jax.vjp(
        lambda mixed_in, gate_in: mixed_in * jax.nn.silu(gate_in), mixed_y, gate_z
    )
    square_sum = lax.psum(jnp.sum(gated_y * gated_y, axis=-1), "tensor")
    inv_gated = lax.rsqrt(square_sum / DSSM + EPS)
    normed_y, pull_gnorm = jax.vjp(
        lambda gated_in, gain_in, inv_in: gated_in * inv_in[:, None] * gain_in,
        gated_y,
        gain_gated,
        inv_gated,
    )
    normed_b = rounded(normed_y)
    branch = matrix_product(attended_b, wo_full) + matrix_product(normed_b, wmamba_full)
    middle = (
        stream + lax.psum(branch.astype(jnp.bfloat16), "tensor").astype(jnp.float32) * valid_rows
    )
    normed_mid = rms_scale(middle, gain_dense)
    ffn_in_b = rounded(normed_mid)
    gate_up = matrix_product(ffn_in_b, wgu_full.reshape(model_width, -1)).reshape(row_count, 2, -1)
    activated, pull_swiglu = jax.vjp(
        lambda gate_in, up_in: jax.nn.silu(gate_in) * up_in, gate_up[:, 0], gate_up[:, 1]
    )
    activated_b = rounded(activated)
    dense_out = (
        lax.psum(matrix_product(activated_b, wdown_full).astype(jnp.bfloat16), "tensor").astype(
            jnp.float32
        )
        * valid_rows
    )
    output = rounded(middle + dense_out)
    weights_b = (
        lax.all_gather(query_proj, "dp", axis=0, tiled=True),
        lax.all_gather(key_value_matrix, "dp", axis=0, tiled=True),
        lax.all_gather(attend_proj, "dp", axis=1, tiled=True),
        lax.all_gather(inner_proj, "dp", axis=0, tiled=True),
        lax.all_gather(step_proj, "dp", axis=0, tiled=True),
        lax.all_gather(mamba_proj, "dp", axis=1, tiled=True),
        lax.all_gather(gateup_proj, "dp", axis=0, tiled=True),
        lax.all_gather(down_proj, "dp", axis=1, tiled=True),
    )
    shared_b = (
        lax.all_gather(state_proj, ("dp", "tensor"), axis=0, tiled=True),
        lax.all_gather(mixer_gain, ("dp", "tensor"), axis=0, tiled=True),
        lax.all_gather(dense_gain, ("dp", "tensor"), axis=0, tiled=True),
    )
    wstate_back = shared_b[0]
    gain_mix_back = shared_b[1].astype(jnp.float32)
    gain_dense_back = shared_b[2].astype(jnp.float32)
    wq_back, wkv_back, wo_back, winner_back, wstep_back, wmamba_back, wgu_back, wdown_back = (
        weights_b
    )
    upstream = cotangent.astype(jnp.float32)
    dense_grad_b = rounded(upstream * valid_rows)
    grad_down = contract("tf,td->fd", activated_b, dense_grad_b)
    grad_act = contract("td,fd->tf", dense_grad_b, wdown_back)
    grad_gate, grad_up = pull_swiglu(grad_act)
    grad_gu_b = rounded(jnp.stack([grad_gate, grad_up], axis=1))
    grad_gateup = contract("td,tcf->dcf", ffn_in_b, grad_gu_b)
    grad_ffn_in = lax.psum(
        contract("tcf,dcf->td", grad_gu_b, wgu_back).astype(jnp.bfloat16), "tensor"
    ).astype(jnp.float32)
    unused_mid, pull_norm_mid = jax.vjp(rms_scale, middle, gain_dense_back)
    grad_middle_n, grad_dense_gain = pull_norm_mid(grad_ffn_in)
    grad_middle = upstream + grad_middle_n
    dense_reduced = (
        lax.psum_scatter(grad_gateup, "dp", scatter_dimension=0, tiled=True),
        lax.psum_scatter(grad_down, "dp", scatter_dimension=1, tiled=True),
        lax.psum_scatter(grad_dense_gain, "dp", scatter_dimension=0, tiled=True),
    )
    mixer_grad_b = rounded(grad_middle * valid_rows)
    grad_attend = contract("tq,td->qd", attended_b, mixer_grad_b)
    grad_mamba = contract("tm,td->md", normed_b, mixer_grad_b)
    grad_attended_b = rounded(contract("td,qd->tq", mixer_grad_b, wo_back)).reshape(
        row_count, heads_kv, group_size, HEAD_DIMENSION
    )
    grad_normed = contract("td,md->tm", mixer_grad_b, wmamba_back)
    probs_back = jnp.exp(masked_scores() - log_total)
    grad_probs = contract("ikgd,jkd->kgij", grad_attended_b, value_b)
    grad_value = contract("kgij,ikgd->jkd", rounded(probs_back), grad_attended_b)
    grad_scores_b = rounded(
        probs_back * (grad_probs - jnp.sum(grad_probs * probs_back, axis=-1, keepdims=True))
    )
    grad_query = contract("kgij,jkd->ikgd", grad_scores_b, key_b) * score_scale
    grad_key = contract("kgij,ikgd->jkd", grad_scores_b, query_b) * score_scale
    grad_query_b = rounded(
        rotate(grad_query.reshape(row_count, heads_q, HEAD_DIMENSION), position, -1.0)
    ).reshape(row_count, -1)
    grad_keyval_b = jnp.stack(
        [rounded(rotate(grad_key, position, -1.0)), rounded(grad_value)], axis=1
    ).reshape(row_count, 2, -1)
    grad_query_proj = contract("td,tq->dq", hidden_b, grad_query_b)
    grad_keyval = contract("td,tcn->dcn", hidden_b, grad_keyval_b)
    grad_gated_l, grad_gated_gain, grad_inv_part = pull_gnorm(grad_normed)
    grad_inv = lax.psum(grad_inv_part, "tensor")
    grad_gated = grad_gated_l + (grad_inv * -(inv_gated**3) / DSSM)[:, None] * gated_y
    grad_mixed, grad_gate_z = pull_gate(grad_gated)
    grad_heads = grad_mixed.reshape(row_count, heads_m, HP)
    grad_skip = jnp.sum(grad_heads * x_heads, axis=(0, 2))
    grad_ssm_b = rounded(grad_heads)
    grad_mixing = contract("ihp,jhp->hij", grad_ssm_b, inflow_b)
    grad_inflow = contract("hij,ihp->jhp", mixing_b, grad_ssm_b)
    grad_xheads = grad_heads * skip_heads[None, :, None] + grad_inflow * step_size[:, :, None]
    grad_step = jnp.sum(grad_inflow * x_heads, axis=2)
    grad_gram, grad_decay = pull_mixing(grad_mixing)
    grad_gram_b = rounded(grad_gram)
    grad_state_c = contract("ij,jn->in", grad_gram_b, state_b)
    grad_state_b = contract("ij,in->jn", grad_gram_b, state_c)
    grad_bc_in, grad_kernel_state = pull_conv_bc(
        jnp.concatenate([grad_state_b, grad_state_c], axis=1)
    )
    grad_x_in, grad_kernel_inner = pull_conv_x(grad_xheads.reshape(row_count, -1))
    grad_step_raw, grad_step_bias, grad_decay_log = pull_step((grad_step, grad_decay))
    grad_inner_b = rounded(jnp.stack([grad_gate_z, grad_x_in], axis=1))
    grad_step_b = rounded(grad_step_raw)
    grad_inner = contract("td,tcm->dcm", hidden_b, grad_inner_b)
    grad_step_proj = contract("td,th->dh", hidden_b, grad_step_b)
    grad_hidden_part = (
        contract("tq,dq->td", grad_query_b, wq_back)
        + contract("tcn,dcn->td", grad_keyval_b, wkv_back)
        + contract("tcm,dcm->td", grad_inner_b, winner_back)
        + contract("th,dh->td", grad_step_b, wstep_back)
    )
    grad_hidden_sum, grad_bc_full, grad_kernel_full = (
        lax.psum(grad_hidden_part.astype(jnp.bfloat16), "tensor").astype(jnp.float32),
        lax.psum(grad_bc_in.astype(jnp.bfloat16), "tensor").astype(jnp.float32),
        lax.psum(grad_kernel_state.astype(jnp.bfloat16), "tensor").astype(jnp.float32),
    )
    grad_bc_b = rounded(grad_bc_full)
    grad_state_proj = contract("td,tn->dn", hidden_b, grad_bc_b)
    grad_hidden = grad_hidden_sum + contract("tn,dn->td", grad_bc_b, wstate_back)
    unused_in, pull_norm_in = jax.vjp(rms_scale, stream, gain_mix_back)
    grad_stream_n, grad_mixer_gain = pull_norm_in(grad_hidden)
    grad_tokens = grad_middle + grad_stream_n
    reduced = (
        lax.psum_scatter(grad_query_proj, "dp", scatter_dimension=0, tiled=True),
        lax.psum_scatter(grad_keyval, "dp", scatter_dimension=0, tiled=True),
        lax.psum_scatter(grad_attend, "dp", scatter_dimension=1, tiled=True),
        lax.psum_scatter(grad_inner, "dp", scatter_dimension=0, tiled=True),
        lax.psum_scatter(grad_step_proj, "dp", scatter_dimension=0, tiled=True),
        lax.psum_scatter(grad_mamba, "dp", scatter_dimension=1, tiled=True),
        lax.psum_scatter(grad_state_proj, "dp", scatter_dimension=0, tiled=True),
        lax.psum_scatter(grad_mixer_gain, "dp", scatter_dimension=0, tiled=True),
        lax.psum_scatter(grad_kernel_full, "dp", scatter_dimension=1, tiled=True),
    )
    (
        red_query,
        red_keyval,
        red_attend,
        red_inner,
        red_step,
        red_mamba,
        red_state,
        red_mixgain,
        red_kernel,
    ) = reduced
    red_gateup, red_down, red_densegain = dense_reduced
    small_sums = lax.psum(
        (grad_kernel_inner, grad_step_bias, grad_decay_log, grad_skip, grad_gated_gain), "dp"
    )
    tensor_at = lax.axis_index("tensor")
    tensor_count = lax.axis_size("tensor")

    def own_half(values, axis_dim):
        part_width = values.shape[axis_dim] // tensor_count
        return lax.dynamic_slice_in_dim(values, tensor_at * part_width, part_width, axis_dim)

    return (
        output,
        grad_tokens,
        own_half(red_mixgain, 0),
        red_query,
        red_keyval,
        red_attend,
        red_inner,
        own_half(red_state, 0),
        red_step,
        small_sums[0],
        own_half(red_kernel, 1),
        small_sums[1],
        small_sums[2],
        small_sums[3],
        small_sums[4],
        red_mamba,
        own_half(red_densegain, 0),
        red_gateup,
        red_down,
    )


def solution(mesh):
    placed = (
        P("dp", None),
        P("dp", None),
        P("dp"),
        P("dp"),
        P(("dp", "tensor")),
        P("dp", "tensor"),
        P("dp", None, "tensor"),
        P("tensor", "dp"),
        P("dp", None, "tensor"),
        P(("dp", "tensor"), None),
        P("dp", "tensor"),
        P(None, "tensor"),
        P(None, ("dp", "tensor")),
        P("tensor"),
        P("tensor"),
        P("tensor"),
        P("tensor"),
        P("tensor", "dp"),
        P(("dp", "tensor")),
        P("dp", None, "tensor"),
        P("tensor", "dp"),
    )
    return jax.shard_map(
        local,
        mesh=mesh,
        in_specs=placed,
        out_specs=(
            P("dp", None),
            P("dp", None),
            P(("dp", "tensor")),
            P("dp", "tensor"),
            P("dp", None, "tensor"),
            P("tensor", "dp"),
            P("dp", None, "tensor"),
            P(("dp", "tensor"), None),
            P("dp", "tensor"),
            P(None, "tensor"),
            P(None, ("dp", "tensor")),
            P("tensor"),
            P("tensor"),
            P("tensor"),
            P("tensor"),
            P("tensor", "dp"),
            P(("dp", "tensor")),
            P("dp", None, "tensor"),
            P("tensor", "dp"),
        ),
        check_vma=False,
    )
```

profile of v0, /device:TPU:0, one launch (start us, length us, event | category | flops | bytes accessed | tf_op | source)
XLA Modules:
  0.0 2305.3 jit_solution(240375968268078526)
XLA Ops:
  15.2 42.1 %all-reduce.29 = (bf16[2048]{0:T(1024)(128)(2,1)S(1)}, bf16[2048]{0:T(1024)(128)(2,1)}) all-reduce(bf16[2048]{0:T(1024)(128)(2,1)S(1)} %dynamic-update-slice, bf16[2048]{0:T(1024)(128)(2,1)S(1)} %dynamic-update-slice.1), channel_id=1, replica_groups=mesh['dp'=16,'tensor'=2] {'dp','tensor'}, use_global_device_ids=true, to_apply=%add.24 | all-reduce | flops 4096 | bytes 16384
  60.3 21.9 all_gather.51
  86.4 64.3 %all-gather = bf16[32,16,5]{1,2,0:T(8,128)(2,1)S(1)} all-gather(bf16[1,16,5]{1,2,0:T(8,128)(2,1)S(1)} %bitcast.407), channel_id=1, replica_groups=mesh['dp'=16,'tensor'=2] {'dp','tensor'}, dimensions={0}, use_global_device_ids=true | all-gather | bytes 5280 | tf_op jit(solution)/shard_map/all_gather | solution.py:127
  162.1 3.1 fusion.191
  176.9 3.0 convolution_multiply_fusion.1
  185.2 69.7 %all-gather.16.cloned.1.call-done = bf16[2048,2,1536]{2,0,1:T(8,128)(2,1)} async-done(((bf16[128,2,1536]{2,0,1:T(8,128)(2,1)}), bf16[2048,2,1536]{2,0,1:T(8,128)(2,1)}) %all-gather.16.cloned.1.call-update) | async-done | bytes 12582928 | tf_op jit(solution)/shard_map/all_gather | solution.py:117
  255.0 16.8 copy.206
  271.7 9.4 fusion.5
  282.1 5.7 fusion.46
  289.7 3.5 copy.214
  293.2 3.6 copy.207
  296.9 12.8 multiply_reduce_fusion.9
  309.7 3.6 copy.213
  313.3 4.9 psum.91
  318.2 5.6 fusion.101
  323.9 9.2 fusion.180
  333.1 29.2 %all-gather.14.cloned.1.call-done = bf16[512,2048]{1,0:T(8,128)(2,1)} async-done(((bf16[512,128]{1,0:T(8,128)(2,1)}), bf16[512,2048]{1,0:T(8,128)(2,1)}) %all-gather.14.cloned.1.call-update) | async-done | bytes 2097168 | tf_op jit(solution)/shard_map/all_gather | solution.py:116
  362.3 5.4 add_convert_fusion.1
  367.8 2.5 copy.215
  371.1 58.6 %all-reduce.35.cloned.1.call-done = bf16[512,2048]{1,0:T(8,128)(2,1)} async-done(((bf16[512,2048]{1,0:T(8,128)(2,1)}), bf16[512,2048]{1,0:T(8,128)(2,1)}) %all-reduce.35.cloned.1.call-update) | async-done | bytes 2097168 | tf_op jit(solution)/shard_map/psum | solution.py:228
  429.7 2.5 multiply_reduce_fusion.1
  432.3 127.4 %all-gather.22.cloned.1.call-done = bf16[2048,2,2048]{2,0,1:T(8,128)(2,1)} async-done(((bf16[128,2,2048]{2,0,1:T(8,128)(2,1)}), bf16[2048,2,2048]{2,0,1:T(8,128)(2,1)}) %all-gather.22.cloned.1.call-update) | async-done | bytes 16777232 | tf_op jit(solution)/shard_map/all_gather | solution.py:120
  559.7 22.7 copy.216
  582.4 15.2 fusion.1
  597.6 40.7 %all-gather.24.cloned.1.call-done = bf16[2048,2048]{1,0:T(8,128)(2,1)} async-done(((bf16[2048,128]{1,0:T(8,128)(2,1)}), bf16[2048,2048]{1,0:T(8,128)(2,1)}) %all-gather.24.cloned.1.call-update) | async-done | bytes 8388624 | tf_op jit(solution)/shard_map/all_gather | solution.py:121
  638.3 11.8 fusion.64
  652.1 13.4 bitcast_convert_fusion
  667.8 10.5 convolution_convert_fusion
  678.3 48.5 %all-reduce.37.cloned.1.call-done = bf16[512,2048]{1,0:T(8,128)(2,1)} async-done(((bf16[512,2048]{1,0:T(8,128)(2,1)}), bf16[512,2048]{1,0:T(8,128)(2,1)}) %all-reduce.37.cloned.1.call-update) | async-done | bytes 2097168 | tf_op jit(solution)/shard_map/psum | solution.py:272
  726.8 4.8 fusion.17
  743.3 6.1 multiply_reduce_fusion.2
  749.4 5.6 psum.95
  755.7 8.3 multiply_reduce_fusion.3
  764.0 3.7 copy.227
  767.8 12.1 fusion.42
  779.9 17.6 fusion.4
  799.8 3.7 copy.228
  803.6 7.6 multiply_reduce_fusion.7
  831.1 5.0 reduce-window.29
  837.4 5.7 fusion.66
  845.1 3.6 fusion.204
  848.8 9.4 fusion.65
  863.4 5.0 psum.99
  872.1 110.6 %all-reduce.39.cloned.1.call-done = (bf16[512,2048]{1,0:T(8,128)(2,1)}, bf16[512,2048]{1,0:T(8,128)(2,1)}, bf16[512,512]{1,0:T(8,128)(2,1)}) async-done(((bf16[512,2048]{1,0:T(8,128)(2,1)}, bf16[512,2048]{1,0:T(8,128)(2,1)}, bf16[512,512]{1,0:T(8,128)(2,1)}), (bf16[512,2048]{1,0:T(8,128)(2,1)}, bf16[512,2048]{1,0:T(8,128)(2,1)}, bf16[512,512]{1,0:T(8,128)(2,1)})) %all-reduce.39.cloned.1.call-update) | async-done | bytes 4718608 | tf_op jit(solution)/shard_map/psum | solution.py:238
  982.8 4.5 fusion.184
  987.3 13.8 fusion.56
  1001.8 18.3 fusion.47
  1021.6 3.6 fusion.186
  1026.3 4.8 fusion.205
  1031.8 10.6 fusion.179
  1042.5 12.9 fusion.95
  1059.2 47.6 %reduce-scatter.15.cloned.1.call-done = f32[128,2,128]{2,0,1:T(8,128)} async-done(((f32[2048,2,128]{2,0,1:T(8,128)}), f32[128,2,128]{2,0,1:T(8,128)}) %reduce-scatter.15.cloned.1.call-update) | async-done | bytes 131088 | tf_op jit(solution)/shard_map/reduce_scatter | solution.py:349
  1108.4 6.2 fusion.14
  1114.6 60.3 %all-reduce.28 = (f32[2048]{0:T(1024)S(1)}, f32[5,1536]{1,0:T(8,128)}, f32[24]{0:T(128)}, f32[24]{0:T(128)}, f32[24]{0:T(128)}, /*index=5*/f32[1536]{0:T(1024)}, f32[2048]{0:T(1024)S(1)}) all-reduce(f32[2048]{0:T(1024)S(1)} %get-tuple-element.121, f32[5,1536]{1,0:T(8,128)S(1)} %pad_add_fusion, ...), channel_id=2, replica_groups=mesh['dp'=16,'tensor'=2] {'dp'}, use_global_device_ids=true, to_apply=%region_27.28.clone | all-reduce | flops 13384 | bytes 107072
  1176.1 8.2 fusion.21
  1185.9 244.6 %reduce-scatter.19.cloned.1.call-done = f32[128,2,1536]{2,0,1:T(8,128)} async-done(((f32[2048,2,1536]{2,0,1:T(8,128)}), f32[128,2,1536]{2,0,1:T(8,128)}) %reduce-scatter.19.cloned.1.call-update) | async-done | bytes 1572880 | tf_op jit(solution)/shard_map/reduce_scatter | solution.py:351
  1430.5 3.8 copy.239
  1434.3 332.8 %reduce-scatter.27.cloned.1.call-done = f32[128,2,2048]{2,0,1:T(8,128)} async-done(((f32[2048,2,2048]{2,0,1:T(8,128)}), f32[128,2,2048]{2,0,1:T(8,128)}) %reduce-scatter.27.cloned.1.call-update) | async-done | bytes 2097168 | tf_op jit(solution)/shard_map/reduce_scatter | solution.py:279
  1767.1 4.5 copy.240
  1771.6 52.6 %reduce-scatter.23.cloned.1.call-done = f32[128,24]{0,1:T(8,128)} async-done(((f32[2048,24]{0,1:T(8,128)}), f32[128,24]{0,1:T(8,128)}) %reduce-scatter.23.cloned.1.call-update) | async-done | bytes 12304 | tf_op jit(solution)/shard_map/reduce_scatter | solution.py:352
  1824.2 76.3 %reduce-scatter.13.cloned.1.call-done = f32[128,512]{1,0:T(8,128)} async-done(((f32[2048,512]{1,0:T(8,128)}), f32[128,512]{1,0:T(8,128)}) %reduce-scatter.13.cloned.1.call-update) | async-done | bytes 262160 | tf_op jit(solution)/shard_map/reduce_scatter | solution.py:348
  1900.4 75.9 %reduce-scatter.17.cloned.1.call-done = f32[512,128]{1,0:T(8,128)} async-done(((f32[512,2048]{1,0:T(8,128)}), f32[512,128]{1,0:T(8,128)}) %reduce-scatter.17.cloned.1.call-update) | async-done | bytes 262160 | tf_op jit(solution)/shard_map/reduce_scatter | solution.py:350
  1976.3 138.9 %reduce-scatter.25.cloned.1.call-done = f32[1536,128]{1,0:T(8,128)} async-done(((f32[1536,2048]{1,0:T(8,128)}), f32[1536,128]{1,0:T(8,128)}) %reduce-scatter.25.cloned.1.call-update) | async-done | bytes 786448 | tf_op jit(solution)/shard_map/reduce_scatter | solution.py:353
  2115.3 183.0 %reduce-scatter.29.cloned.1.call-done = f32[2048,128]{1,0:T(8,128)} async-done(((f32[2048,2048]{1,0:T(8,128)}), f32[2048,128]{1,0:T(8,128)}) %reduce-scatter.29.cloned.1.call-update) | async-done | bytes 1048592 | tf_op jit(solution)/shard_map/reduce_scatter | solution.py:280
  (473 shorter events, 107.7 us)
Async XLA Ops:
  7.2 7.7 copy-start.138
  7.2 50.7 %copy-start.93 = (bf16[5,1536]{1,0:T(8,128)(2,1)S(1)}, bf16[5,1536]{1,0:T(8,128)(2,1)}, u32[]{:S(2)}) copy-start(bf16[5,1536]{1,0:T(8,128)(2,1)} %param.32) | copy-start | bytes 46084
  7.2 52.6 %copy-start.139 = (bf16[24]{0:T(256)(128)(2,1)S(1)}, bf16[24]{0:T(256)(128)(2,1)}, u32[]{:S(2)}) copy-start(bf16[24]{0:T(256)(128)(2,1)} %param.36) | copy-start | bytes 148
  7.3 53.1 %copy-start.140 = (bf16[24]{0:T(256)(128)(2,1)S(1)}, bf16[24]{0:T(256)(128)(2,1)}, u32[]{:S(2)}) copy-start(bf16[24]{0:T(256)(128)(2,1)} %param.34) | copy-start | bytes 148
  7.3 53.1 %copy-start.122 = (bf16[128,24]{0,1:T(8,128)(2,1)S(1)}, bf16[128,24]{0,1:T(8,128)(2,1)}, u32[]{:S(2)}) copy-start(bf16[128,24]{0,1:T(8,128)(2,1)} %param.31) | copy-start | bytes 18436
  7.3 75.0 %copy-start.141 = (bf16[24]{0:T(256)(128)(2,1)S(1)}, bf16[24]{0:T(256)(128)(2,1)}, u32[]{:S(2)}) copy-start(bf16[24]{0:T(256)(128)(2,1)} %param.35) | copy-start | bytes 148
  7.3 150.3 %all-gather.10.cloned.1.call-start = ((), (), s32[]{:S(2)}) async-start(), calls=%async_computation.10 | async-start | bytes 1114112 | tf_op jit(solution)/shard_map/all_gather | solution.py:115
  9.0 153.2 %all-gather.12.cloned.1.call-start = ((), (), s32[]{:S(2)}) async-start(), calls=%async_computation.11 | async-start | bytes 2228224 | tf_op jit(solution)/shard_map/all_gather | solution.py:114
  9.7 167.1 %all-gather.18.cloned.1.call-start = ((), (), s32[]{:S(2)}) async-start(), calls=%async_computation.14 | async-start | bytes 2162688 | tf_op jit(solution)/shard_map/all_gather | solution.py:124
  10.4 244.5 %all-gather.16.cloned.1.call-start = ((), (), s32[]{:S(2)}) async-start(), calls=%async_computation.13 | async-start | bytes 13369344 | tf_op jit(solution)/shard_map/all_gather | solution.py:117
  12.6 311.2 %all-gather.20.cloned.1.call-start = ((), (), s32[]{:S(2)}) async-start(), calls=%async_computation.15 | async-start | bytes 6684672 | tf_op jit(solution)/shard_map/all_gather | solution.py:119
  13.2 349.0 %all-gather.14.cloned.1.call-start = ((), (), s32[]{:S(2)}) async-start(), calls=%async_computation.12 | async-start | bytes 2228224 | tf_op jit(solution)/shard_map/all_gather | solution.py:116
  13.8 415.9 %all-reduce.35.cloned.1.call-start = ((), (), s32[]{:S(2)}) async-start(), calls=%async_computation.16 | async-start | bytes 4194304 | tf_op jit(solution)/shard_map/psum | solution.py:228
  13.9 46.4 %copy-start.132 = (pred[509]{0:T(512)(128)(4,1)}, pred[509]{0:T(512)(128)(4,1)S(1)}, u32[]{:S(2)}) copy-start(pred[509]{0:T(512)(128)(4,1)S(1)} %slice_compare_fusion) | copy-start | bytes 1531
  14.0 69.7 %copy-start.134 = (pred[510]{0:T(512)(128)(4,1)}, pred[510]{0:T(512)(128)(4,1)S(1)}, u32[]{:S(2)}) copy-start(pred[510]{0:T(512)(128)(4,1)S(1)} %slice_compare_fusion.1) | copy-start | bytes 1534
  14.1 141.4 %copy-start.123 = (f32[64]{0:T(128)}, f32[64]{0:T(128)S(1)}, u32[]{:S(2)}) copy-start(f32[64]{0:T(128)S(1)} %multiply_exponential_fusion) | copy-start | bytes 772
  14.1 72.3 %copy-start.128 = (bf16[5,16]{1,0:T(8,128)(2,1)S(1)}, bf16[5,16]{1,0:T(8,128)(2,1)}, u32[]{:S(2)}) copy-start(bf16[5,16]{1,0:T(8,128)(2,1)} %param.33) | copy-start | bytes 484
  14.6 43.3 %copy-start.98 = (f32[512]{0:T(512)}, f32[512]{0:T(512)S(1)}, u32[]{:S(2)}) copy-start(f32[512]{0:T(512)S(1)} %fusion.22) | copy-start | bytes 6148
  14.6 139.0 %copy-start.125 = (bf16[1536]{0:T(1024)(128)(2,1)S(1)}, bf16[1536]{0:T(1024)(128)(2,1)}, u32[]{:S(2)}) copy-start(bf16[1536]{0:T(1024)(128)(2,1)} %param.37) | copy-start | bytes 9220
  14.6 257.1 %copy-start.82 = (f32[512]{0:T(512)}, f32[512]{0:T(512)S(1)}, u32[]{:S(2)}) copy-start(f32[512]{0:T(512)S(1)} %fusion.162) | copy-start | bytes 6148
  57.2 214.5 %copy-start.59 = (f32[2048]{0:T(1024)}, f32[2048]{0:T(1024)S(1)}, u32[]{:S(2)}) copy-start(f32[2048]{0:T(1024)S(1)} %convert_element_type.191) | copy-start | bytes 24580
  82.2 75.4 %copy-start.127 = (f32[24]{0:T(128)}, f32[24]{0:T(128)S(1)}, u32[]{:S(2)}) copy-start(f32[24]{0:T(128)S(1)} %fusion.164) | copy-start | bytes 292
  157.6 12.4 copy-start.37
  162.1 9.6 copy-start.46
  162.1 9.6 copy-start.48
  176.7 185.5 %copy-start.33 = (bf16[128,4,512]{2,0,1:T(8,128)(2,1)}, bf16[128,4,512]{2,0,1:T(8,128)(2,1)S(1)}, u32[]{:S(2)}) copy-start(bf16[128,4,512]{2,0,1:T(8,128)(2,1)S(1)} %fusion.71) | copy-start | bytes 1572868
  367.7 191.9 %all-gather.22.cloned.1.call-start = ((), (), s32[]{:S(2)}) async-start(), calls=%async_computation.17 | async-start | bytes 17825792 | tf_op jit(solution)/shard_map/all_gather | solution.py:120
  370.3 268.0 %all-gather.24.cloned.1.call-start = ((), (), s32[]{:S(2)}) async-start(), calls=%async_computation.18 | async-start | bytes 8912896 | tf_op jit(solution)/shard_map/all_gather | solution.py:121
  371.1 355.7 %all-reduce.37.cloned.1.call-start = ((), (), s32[]{:S(2)}) async-start(), calls=%async_computation.19 | async-start | bytes 4194304 | tf_op jit(solution)/shard_map/psum | solution.py:272
  371.1 360.5 %copy-start.62 = (f32[2048]{0:T(1024)}, f32[2048]{0:T(1024)S(1)}, u32[]{:S(2)}) copy-start(f32[2048]{0:T(1024)S(1)} %convert_element_type.212) | copy-start | bytes 24580
  432.3 299.4 %copy-start.80 = (f32[512]{0:T(512)}, f32[512]{0:T(512)S(1)}, u32[]{:S(2)}) copy-start(f32[512]{0:T(512)S(1)} %fusion.163) | copy-start | bytes 6148
  652.1 14.5 copy-start.135
  652.1 15.1 copy-start.133
  665.6 317.2 %all-reduce.39.cloned.1.call-start = ((), (), s32[]{:S(2)}) async-start(), calls=%async_computation.30 | async-start | bytes 9437184 | tf_op jit(solution)/shard_map/psum | solution.py:238
  734.0 9.3 copy-start.19
  743.3 12.4 copy-start.12
  767.7 12.2 copy-start.36
  767.7 12.2 copy-start.45
  767.7 12.2 copy-start.58
  767.8 12.1 copy-start.74
  767.8 12.1 copy-start.76
  779.9 17.6 copy-start.22
  803.6 7.6 copy-start.72
  811.2 10.2 copy-start.6
  824.8 12.5 copy-start.7
  824.8 12.5 copy-start.66
  837.4 11.4 slice-start
  837.4 11.4 slice-start.1
  848.8 9.5 copy-start.27
  848.8 9.5 copy-start.55
  848.8 9.5 copy-start.56
  862.7 195.1 %reduce-scatter.31.cloned.1.call-start = ((), (), s32[]{:S(2)}) async-start(), calls=%async_computation.29 | async-start | bytes 278528
  869.2 237.5 %reduce-scatter.15.cloned.1.call-start = ((), (), s32[]{:S(2)}) async-start(), calls=%async_computation.21 | async-start | bytes 2228224 | tf_op jit(solution)/shard_map/reduce_scatter | solution.py:349
  871.7 312.6 %reduce-scatter.21.cloned.1.call-start = ((), (), s32[]{:S(2)}) async-start(), calls=%async_computation.24 | async-start | bytes 4456448 | tf_op jit(solution)/shard_map/reduce_scatter | solution.py:354
  987.2 443.2 %reduce-scatter.19.cloned.1.call-start = ((), (), s32[]{:S(2)}) async-start(), calls=%async_computation.23 | async-start | bytes 26738688 | tf_op jit(solution)/shard_map/reduce_scatter | solution.py:351
  1001.2 765.9 %reduce-scatter.27.cloned.1.call-start = ((), (), s32[]{:S(2)}) async-start(), calls=%async_computation.27 | async-start | bytes 35651584 | tf_op jit(solution)/shard_map/reduce_scatter | solution.py:279
  1020.2 804.0 %reduce-scatter.23.cloned.1.call-start = ((), (), s32[]{:S(2)}) async-start(), calls=%async_computation.25 | async-start | bytes 208896 | tf_op jit(solution)/shard_map/reduce_scatter | solution.py:352
  1021.6 878.8 %reduce-scatter.13.cloned.1.call-start = ((), (), s32[]{:S(2)}) async-start(), calls=%async_computation.20 | async-start | bytes 4456448 | tf_op jit(solution)/shard_map/reduce_scatter | solution.py:348
  1025.3 951.0 %reduce-scatter.17.cloned.1.call-start = ((), (), s32[]{:S(2)}) async-start(), calls=%async_computation.22 | async-start | bytes 4456448 | tf_op jit(solution)/shard_map/reduce_scatter | solution.py:350
  1031.1 1084.1 %reduce-scatter.25.cloned.1.call-start = ((), (), s32[]{:S(2)}) async-start(), calls=%async_computation.26 | async-start | bytes 13369344 | tf_op jit(solution)/shard_map/reduce_scatter | solution.py:353
  1042.5 1255.7 %reduce-scatter.29.cloned.1.call-start = ((), (), s32[]{:S(2)}) async-start(), calls=%async_computation.28 | async-start | bytes 17825792 | tf_op jit(solution)/shard_map/reduce_scatter | solution.py:280
  1055.5 52.9 %copy-start.136 = (bf16[512,512]{1,0:T(8,128)(2,1)S(1)}, bf16[512,512]{1,0:T(8,128)(2,1)}, u32[]{:S(2)}) copy-start(bf16[512,512]{1,0:T(8,128)(2,1)} %get-tuple-element.149) | copy-start | bytes 1572868
  1108.4 67.7 %copy-start.99 = (f32[512]{0:T(512)S(1)}, f32[512]{0:T(512)}, u32[]{:S(2)}) copy-start(f32[512]{0:T(512)} %copy-done.98) | copy-start | bytes 6148
  1108.4 67.7 %copy-start.95 = (f32[512]{0:T(512)S(1)}, f32[512]{0:T(512)}, u32[]{:S(2)}) copy-start(f32[512]{0:T(512)} %copy-done.94) | copy-start | bytes 6148
  (110 other events, 349.8 us)
Sparse Core Ops, SparseCore 0:
  10.9 40.6 all-gather.9
  53.8 40.3 all-gather.11
  97.1 55.3 all-gather.17
  155.3 99.6 all-gather.15
  257.0 63.8 all-gather.19
  322.8 39.3 all-gather.13
  367.8 61.8 all-reduce.34
  432.7 126.9 all-gather.21
  562.0 76.2 all-gather.23
  665.7 61.0 all-reduce.36
  862.8 119.8 all-reduce.38
  986.5 55.2 reduce-scatter.30
  1046.1 60.6 reduce-scatter.14
  1110.4 72.6 reduce-scatter.20
  1187.6 242.8 reduce-scatter.18
  1435.2 331.8 reduce-scatter.26
  1771.4 52.7 reduce-scatter.22
  1829.0 71.4 reduce-scatter.12
  1904.9 71.4 reduce-scatter.16
  1981.3 133.8 reduce-scatter.24
  2120.5 177.6 reduce-scatter.28
where the time goes:
time: 2310 us
  waiting for transfers between devices  1640 us (71%)
  matrix products  238 us (10%)
  blocking collectives  204 us (9%)
  local copies, waits for them, and re-layouts  113 us (5%)
  other arithmetic  90.7 us (4%)
    reduce_scatter x1, waiting for transfers between devices, local(): lax.psum_scatter(grad_gateup, 'dp', scatter_dimension=0, tiled=True)  333 us
    reduce_scatter x1, waiting for transfers between devices, local(): lax.psum_scatter(grad_inner, 'dp', scatter_dimension=0, tiled=True)  245 us
    reduce_scatter x1, waiting for transfers between devices, local(): lax.psum_scatter(grad_down, 'dp', scatter_dimension=1, tiled=True)  183 us
    dot_general x30, matrix products, contract(): return jnp.einsum(form, left, right, preferred_element_type=jnp.float32)  180 us
    reduce_scatter x1, waiting for transfers between devices, local(): lax.psum_scatter(grad_mamba, 'dp', scatter_dimension=1, tiled=True)  139 us
    all_gather x1, waiting for transfers between devices, local(): lax.all_gather(gateup_proj, 'dp', axis=0, tiled=True)  127 us
    psum x1, waiting for transfers between devices, local(): lax.psum(matrix_product(activated_b, wdown_full).astype(jnp.bfloat16), 't...  111 us
    unnamed x2, blocking collectives  102 us
  transfers between devices with their start and end apart: 21, of which 15 were waited for; matrix products, arithmetic and copies ran while one was open for 12% of the time, Pallas kernels for 0%

commit v1 on v0

v1 whole, which is shorter than its diff:
```python
import functools
import math

import jax
import jax.numpy as jnp
from jax import lax
from jax.experimental import pallas as pl
from jax.experimental.pallas import tpu as pltpu
from jax.sharding import PartitionSpec as P

HP = 64
HEAD_DIMENSION = 128
DSSM = 3072
TILE = 256

EPS = 1e-05
THETA = 100000000000.0


def rounded(values):
    return values.astype(jnp.bfloat16)


def contract(form, left, right):
    return jnp.einsum(form, left, right, preferred_element_type=jnp.float32)


def rms_scale(values, gain):
    return values * lax.rsqrt(jnp.mean(values * values, axis=-1, keepdims=True) + EPS) * gain


def cost(flops, traffic, transcendentals=0):
    return pl.CostEstimate(
        flops=flops, bytes_accessed=traffic, transcendentals=transcendentals
    )


def positions_of(segment):
    row_index = jnp.arange(segment.shape[0], dtype=jnp.int32)
    starts = jnp.concatenate([jnp.ones((1,), jnp.bool_), segment[1:] != segment[:-1]])
    first_row = lax.cummax(jnp.where(starts, row_index, 0), axis=0)
    return row_index - first_row


def silu_parts(values):
    gate = jax.nn.sigmoid(values)
    return values * gate, gate * (1.0 + values * (1.0 - gate))


def dot_nn(left, right):
    return lax.dot_general(left, right, (((1,), (0,)), ((), ())), preferred_element_type=jnp.float32)


def dot_nt(left, right):
    return lax.dot_general(left, right, (((1,), (1,)), ((), ())), preferred_element_type=jnp.float32)


def dot_tn(left, right):
    return lax.dot_general(left, right, (((0,), (0,)), ((), ())), preferred_element_type=jnp.float32)


def shifted_rows(values, lag, same_ref):
    columns = values.shape[1]
    mask = same_ref[lag - 1]
    if columns > mask.shape[1]:
        mask = jnp.concatenate([mask] * (columns // mask.shape[1]), axis=1)
    return mask * pltpu.roll(values, lag, 0)


def conv_rows(values, taps, same_ref):
    total = taps[4:5] + taps[3:4] * values
    for lag in range(1, 4):
        total = total + taps[3 - lag : 4 - lag] * shifted_rows(values, lag, same_ref)
    return total


def conv_rows_back(grad, values, taps, same_ref):
    rows = grad.shape[0]
    total = taps[3:4] * grad
    tap_grads = [None] * 5
    tap_grads[4] = jnp.sum(grad, axis=0, keepdims=True)
    tap_grads[3] = jnp.sum(grad * values, axis=0, keepdims=True)
    for lag in range(1, 4):
        mask = same_ref[lag - 1]
        if grad.shape[1] > mask.shape[1]:
            mask = jnp.concatenate([mask] * (grad.shape[1] // mask.shape[1]), axis=1)
        masked = grad * mask
        total = total + taps[3 - lag : 4 - lag] * pltpu.roll(masked, rows - lag, 0)
        tap_grads[3 - lag] = jnp.sum(
            masked * pltpu.roll(values, lag, 0), axis=0, keepdims=True
        )
    return total, tap_grads


def running_sum(values, backward=False):
    rows = values.shape[0]
    index = lax.broadcasted_iota(jnp.int32, values.shape, 0)
    step = 1
    while step < rows:
        if backward:
            moved = pltpu.roll(values, rows - step, 0)
            values = values + jnp.where(index < rows - step, moved, 0.0)
        else:
            moved = pltpu.roll(values, step, 0)
            values = values + jnp.where(index >= step, moved, 0.0)
        step *= 2
    return values


def step_sizes(raw, extra_ref, live):
    shifted = raw + extra_ref[0:1]
    size = (jnp.maximum(shifted, 0.0) + jnp.log1p(jnp.exp(-jnp.abs(shifted)))) * live
    return shifted, size, -size * extra_ref[1:2]


def lane_column(values, lane):
    lanes = lax.broadcasted_iota(jnp.int32, values.shape, 1)
    return jnp.sum(jnp.where(lanes == lane, values, 0.0), axis=1, keepdims=True)


def ssm_forward_kernel(
    u_ref, z_ref, state_b_ref, state_c_ref, step_ref, wide_ref, conv_ref, extra_ref, live_ref, same_ref, mask_ref,
    y_ref, gated_ref, square_ref, gram, sizes, running, running_t,
):
    pair = pl.program_id(0)
    live = live_ref[...]
    rows = live.shape[0]

    @pl.when(pair == 0)
    def _():
        unused, size, decay = step_sizes(step_ref[...], extra_ref, live)
        total = running_sum(decay)
        sizes[...] = size
        running[...] = total
        running_t[...] = total.T
        width = conv_ref.shape[1]
        wide_live = jnp.concatenate([live] * (width // 128), axis=1)
        state = jnp.concatenate([state_b_ref[...], state_c_ref[...]], axis=1) * wide_live
        inner = conv_rows(state, conv_ref[...], same_ref)
        both = (inner * jax.nn.sigmoid(inner)).astype(jnp.bfloat16)
        gram[...] = dot_nt(both[:, width // 2 :], both[:, : width // 2]) * mask_ref[...]
        square_ref[...] = jnp.zeros_like(square_ref)

    taps = wide_ref[...]
    inner = conv_rows(u_ref[...] * live, taps, same_ref)
    x_in = inner * jax.nn.sigmoid(inner)
    left_lanes = lax.broadcasted_iota(jnp.int32, (rows, 128), 1) < HP
    size = sizes[...]
    size_pair = jnp.where(left_lanes, lane_column(size, 2 * pair), lane_column(size, 2 * pair + 1))
    inflow = (size_pair * x_in).astype(jnp.bfloat16)
    total = running[...]
    columns = [lane_column(total, 2 * pair + k) for k in range(2)]
    row_vectors = [running_t[pl.ds(2 * pair + k, 1), :] for k in range(2)]
    skipped = taps[5:6] * x_in
    gate = z_ref[...]
    gate = gate * jax.nn.sigmoid(gate)
    for block in range(rows // TILE):
        top, end = block * TILE, (block + 1) * TILE
        parts = []
        for k in range(2):
            gaps = columns[k][top:end] - row_vectors[k][:, :end]
            mixing = (gram[top:end, :end] * jnp.exp(jnp.minimum(gaps, 0.0))).astype(jnp.bfloat16)
            parts.append(dot_nn(mixing, inflow[:end]))
        mixed = jnp.where(left_lanes[top:end], parts[0], parts[1]) + skipped[top:end]
        y_ref[top:end, :] = mixed
        gated = mixed * gate[top:end]
        gated_ref[top:end, :] = gated
        square_ref[top:end, :] += gated * gated


def ssm_forward(projected, wide, conv_state, extra, live, same, mask, offsets):
    rows = projected.shape[0]
    pairs = wide.shape[1] // 128
    width = conv_state.shape[1]
    const2 = lambda i: (0, 0)
    at = lambda name, size: offsets[name] // size
    block = lambda name: pl.BlockSpec((rows, 128), lambda i, o=at(name, 128): (0, o + i))
    return pl.pallas_call(
        ssm_forward_kernel,
        grid=(pairs,),
        in_specs=[
            block("u"),
            block("z"),
            pl.BlockSpec((rows, width // 2), lambda i: (0, at("state", width // 2))),
            pl.BlockSpec((rows, width // 2), lambda i: (0, at("state", width // 2) + 1)),
            pl.BlockSpec((rows, 128), lambda i: (0, at("step", 128))),
            pl.BlockSpec((8, 128), lambda i: (0, i)),
            pl.BlockSpec((8, width), const2),
            pl.BlockSpec((8, 128), const2),
            pl.BlockSpec((rows, 128), const2),
            pl.BlockSpec((3, rows, 128), lambda i: (0, 0, 0)),
            pl.BlockSpec((rows, rows), const2),
        ],
        out_specs=[
            pl.BlockSpec((rows, 128), lambda i: (0, i)),
            pl.BlockSpec((rows, 128), lambda i: (0, i)),
            pl.BlockSpec((rows, 128), const2),
        ],
        out_shape=[
            jax.ShapeDtypeStruct((rows, pairs * 128), jnp.float32),
            jax.ShapeDtypeStruct((rows, pairs * 128), jnp.float32),
            jax.ShapeDtypeStruct((rows, 128), jnp.float32),
        ],
        scratch_shapes=[
            pltpu.VMEM((rows, rows), jnp.float32),
            pltpu.VMEM((rows, 128), jnp.float32),
            pltpu.VMEM((rows, 128), jnp.float32),
            pltpu.VMEM((128, rows), jnp.float32),
        ],
        compiler_params=pltpu.CompilerParams(vmem_limit_bytes=40 * 2**20),
        name="ssm_forward",
    )(projected, projected, projected, projected, projected, wide, conv_state, extra, live, same, mask)


def ssm_backward_kernel(
    dn_ref, y_ref, u_ref, z_ref, state_b_ref, state_c_ref, step_ref, inverse_ref, own_ref, other_ref,
    wide_ref, conv_ref, extra_ref, live_ref, same_ref, mask_t_ref,
    dz_ref, du_ref, ds_ref, dr_ref, wide_grad_ref, conv_grad_ref, extra_grad_ref,
    gram_t, gram_grad, sizes, decays, running, running_t, size_grad, total_grad, states, state_slopes,
):
    pair = pl.program_id(0)
    live = live_ref[...]
    rows = live.shape[0]
    width = conv_ref.shape[1]
    wide_live = jnp.concatenate([live] * (width // 128), axis=1)

    @pl.when(pair == 0)
    def _():
        unused, size, decay = step_sizes(step_ref[...], extra_ref, live)
        total = running_sum(decay)
        sizes[...] = size
        decays[...] = decay
        running[...] = total
        running_t[...] = total.T
        state = jnp.concatenate([state_b_ref[...], state_c_ref[...]], axis=1) * wide_live
        inner = conv_rows(state, conv_ref[...], same_ref)
        value, slope = silu_parts(inner)
        both = value.astype(jnp.bfloat16)
        states[...] = both
        state_slopes[...] = slope
        gram_t[...] = dot_nt(both[:, : width // 2], both[:, width // 2 :]) * mask_t_ref[...]
        gram_grad[...] = jnp.zeros_like(gram_grad)
        size_grad[...] = jnp.zeros_like(size_grad)
        total_grad[...] = jnp.zeros_like(total_grad)

    taps = wide_ref[...]
    u_live = u_ref[...] * live
    inner = conv_rows(u_live, taps, same_ref)
    x_in, x_slope = silu_parts(inner)
    gate, gate_slope = silu_parts(z_ref[...])
    mixed = y_ref[...]
    gated = mixed * gate
    inverse = inverse_ref[:, 0:1]
    pull = (own_ref[:, 0:1] + other_ref[:, 0:1]) * inverse * inverse * inverse / DSSM
    grad_gated = taps[6:7] * dn_ref[...] * inverse - gated * pull
    grad_mixed = grad_gated * gate
    dz_ref[...] = (grad_gated * mixed * gate_slope).astype(dz_ref.dtype)
    grad_mixed_b = grad_mixed.astype(jnp.bfloat16)
    lanes = lax.broadcasted_iota(jnp.int32, (rows, 128), 1)
    left_lanes = lanes < HP
    size = sizes[...]
    size_pair = jnp.where(left_lanes, lane_column(size, 2 * pair), lane_column(size, 2 * pair + 1))
    inflow = (size_pair * x_in).astype(jnp.bfloat16)
    zero = jnp.zeros_like(inflow)
    inflow_heads = [jnp.where(left_lanes, inflow, zero), jnp.where(left_lanes, zero, inflow)]
    total = running[...]
    columns = [lane_column(total, 2 * pair + k) for k in range(2)]
    row_vectors = [running_t[pl.ds(2 * pair + k, 1), :] for k in range(2)]
    blocks = []
    for block in range(rows // TILE):
        top, end = block * TILE, (block + 1) * TILE
        parts = []
        gram_part = None
        for k in range(2):
            gaps = row_vectors[k][:, top:] - columns[k][top:end]
            decay = jnp.exp(jnp.minimum(gaps, 0.0))
            mixing_t = (gram_t[top:end, top:] * decay).astype(jnp.bfloat16)
            parts.append(dot_nn(mixing_t, grad_mixed_b[top:]))
            term = dot_nt(inflow_heads[k][top:end], grad_mixed_b[top:]) * decay
            gram_part = term if gram_part is None else gram_part + term
        gram_grad[top:end, top:] += gram_part
        blocks.append(jnp.where(left_lanes[top:end], parts[0], parts[1]))
    grad_inflow = jnp.concatenate(blocks, axis=0)
    grad_x = grad_mixed * taps[5:6] + grad_inflow * size_pair
    by_size = grad_inflow * x_in
    mixed_only = mixed - taps[5:6] * x_in
    by_total = grad_mixed_b.astype(jnp.float32) * mixed_only - grad_inflow * inflow.astype(jnp.float32)
    size_sum, total_sum = size_grad[...], total_grad[...]
    for k in range(2):
        mine = left_lanes if k == 0 else jnp.logical_not(left_lanes)
        here = lanes == 2 * pair + k
        size_sum = jnp.where(
            here, jnp.sum(jnp.where(mine, by_size, 0.0), axis=1, keepdims=True), size_sum
        )
        total_sum = jnp.where(
            here, jnp.sum(jnp.where(mine, by_total, 0.0), axis=1, keepdims=True), total_sum
        )
    size_grad[...] = size_sum
    total_grad[...] = total_sum
    grad_u, tap_grads = conv_rows_back(grad_x * x_slope, u_live, taps, same_ref)
    du_ref[...] = (grad_u * live).astype(du_ref.dtype)
    skip_grad = jnp.sum(grad_mixed * x_in, axis=0, keepdims=True)
    wide_grad_ref[...] = jnp.concatenate(
        tap_grads + [skip_grad, jnp.zeros((2, 128), jnp.float32)], axis=0
    )

    @pl.when(pair == pl.num_programs(0) - 1)
    def _():
        half = width // 2
        gram_grad_b = (gram_grad[...] * mask_t_ref[...]).astype(jnp.bfloat16)
        grad_b = dot_nn(gram_grad_b, states[:, half:])
        grad_c = dot_tn(gram_grad_b, states[:, :half])
        grad_bc = jnp.concatenate([grad_b, grad_c], axis=1) * state_slopes[...]
        state = jnp.concatenate([state_b_ref[...], state_c_ref[...]], axis=1) * wide_live
        grad_in, state_taps = conv_rows_back(grad_bc, state, conv_ref[...], same_ref)
        ds_ref[...] = (grad_in * wide_live).astype(ds_ref.dtype)
        conv_grad_ref[...] = jnp.concatenate(
            state_taps + [jnp.zeros((3, width), jnp.float32)], axis=0
        )
        decay_grad = running_sum(total_grad[...], backward=True)
        shifted = step_ref[...] + extra_ref[0:1]
        grad_size = size_grad[...] - decay_grad * extra_ref[1:2]
        grad_raw = grad_size * live * jax.nn.sigmoid(shifted)
        dr_ref[...] = grad_raw.astype(dr_ref.dtype)
        extra_grad_ref[...] = jnp.concatenate(
            [
                jnp.sum(grad_raw, axis=0, keepdims=True),
                jnp.sum(decay_grad * decays[...], axis=0, keepdims=True),
                jnp.zeros((6, 128), jnp.float32),
            ],
            axis=0,
        )


def ssm_backward(
    grad_normed, mixed, projected, inverse, own, other, wide, conv_state, extra, live, same, mask_t, offsets
):
    rows = projected.shape[0]
    pairs = wide.shape[1] // 128
    width = conv_state.shape[1]
    const2 = lambda i: (0, 0)
    at = lambda name, size: offsets[name] // size
    block = lambda name: pl.BlockSpec((rows, 128), lambda i, o=at(name, 128): (0, o + i))
    plain = pl.BlockSpec((rows, 128), lambda i: (0, i))
    f32, b16 = jnp.float32, jnp.bfloat16
    return pl.pallas_call(
        ssm_backward_kernel,
        grid=(pairs,),
        in_specs=[
            plain,
            plain,
            block("u"),
            block("z"),
            pl.BlockSpec((rows, width // 2), lambda i: (0, at("state", width // 2))),
            pl.BlockSpec((rows, width // 2), lambda i: (0, at("state", width // 2) + 1)),
            pl.BlockSpec((rows, 128), lambda i: (0, at("step", 128))),
            pl.BlockSpec((rows, 128), const2),
            pl.BlockSpec((rows, 128), const2),
            pl.BlockSpec((rows, 128), const2),
            pl.BlockSpec((8, 128), lambda i: (0, i)),
            pl.BlockSpec((8, width), const2),
            pl.BlockSpec((8, 128), const2),
            pl.BlockSpec((rows, 128), const2),
            pl.BlockSpec((3, rows, 128), lambda i: (0, 0, 0)),
            pl.BlockSpec((rows, rows), const2),
        ],
        out_specs=[
            plain,
            plain,
            pl.BlockSpec((rows, width), const2),
            pl.BlockSpec((rows, 128), const2),
            pl.BlockSpec((8, 128), lambda i: (0, i)),
            pl.BlockSpec((8, width), const2),
            pl.BlockSpec((8, 128), const2),
        ],
        out_shape=[
            jax.ShapeDtypeStruct((rows, pairs * 128), b16),
            jax.ShapeDtypeStruct((rows, pairs * 128), b16),
            jax.ShapeDtypeStruct((rows, width), b16),
            jax.ShapeDtypeStruct((rows, 128), b16),
            jax.ShapeDtypeStruct((8, pairs * 128), f32),
            jax.ShapeDtypeStruct((8, width), f32),
            jax.ShapeDtypeStruct((8, 128), f32),
        ],
        scratch_shapes=[
            pltpu.VMEM((rows, rows), f32),
            pltpu.VMEM((rows, rows), f32),
            pltpu.VMEM((rows, 128), f32),
            pltpu.VMEM((rows, 128), f32),
            pltpu.VMEM((rows, 128), f32),
            pltpu.VMEM((128, rows), f32),
            pltpu.VMEM((rows, 128), f32),
            pltpu.VMEM((rows, 128), f32),
            pltpu.VMEM((rows, width), b16),
            pltpu.VMEM((rows, width), f32),
        ],
        compiler_params=pltpu.CompilerParams(vmem_limit_bytes=48 * 2**20),
        cost_estimate=cost(1, 1),
        name="ssm_backward",
    )(
        grad_normed, mixed, projected, projected, projected, projected, projected, inverse, own, other,
        wide, conv_state, extra, live, same, mask_t,
    )


def turned(values, cos_ref, sin_ref):
    return values * cos_ref[...] + pltpu.roll(values, HEAD_DIMENSION // 2, 1) * sin_ref[...]


def attention_forward_kernel(
    q_ref, k_ref, v_ref, cos_ref, sin_ref, mask_ref, out_ref, query_ref, key_ref, value_ref, log_ref
):
    head = pl.program_id(0)
    rows = q_ref.shape[0]
    scale = HEAD_DIMENSION**-0.5

    @pl.when(head == 0)
    def _():
        key_ref[...] = turned(k_ref[...], cos_ref, sin_ref).astype(jnp.bfloat16)
        value_ref[...] = v_ref[...].astype(jnp.bfloat16)

    query = turned(q_ref[...], cos_ref, sin_ref).astype(jnp.bfloat16)
    query_ref[...] = query
    for block in range(rows // TILE):
        top, end = block * TILE, (block + 1) * TILE
        scores = dot_nt(query[top:end], key_ref[:end, :]) * scale
        scores = jnp.where(mask_ref[top:end, :end] > 0.0, scores, -1e30)
        largest = jnp.max(scores, axis=1, keepdims=True)
        weights = jnp.exp(scores - largest)
        total = jnp.sum(weights, axis=1, keepdims=True)
        probs = (weights / total).astype(jnp.bfloat16)
        out_ref[top:end, :] = dot_nn(probs, value_ref[:end, :]).astype(out_ref.dtype)
        log_ref[top:end, :] = jnp.broadcast_to(largest + jnp.log(total), (TILE, 128))


def attention_forward(projected, cos, sin, mask, offsets, heads):
    rows = projected.shape[0]
    at = lambda name: offsets[name] // 128
    const2 = lambda i: (0, 0)
    one = pl.BlockSpec((rows, 128), const2)
    each = pl.BlockSpec((rows, 128), lambda i: (0, i))
    b16 = jnp.bfloat16
    return pl.pallas_call(
        attention_forward_kernel,
        grid=(heads,),
        in_specs=[
            pl.BlockSpec((rows, 128), lambda i: (0, at("q") + i)),
            pl.BlockSpec((rows, 128), lambda i: (0, at("kv"))),
            pl.BlockSpec((rows, 128), lambda i: (0, at("kv") + 1)),
            one,
            one,
            pl.BlockSpec((rows, rows), const2),
        ],
        out_specs=[each, each, one, one, each],
        out_shape=[
            jax.ShapeDtypeStruct((rows, heads * 128), b16),
            jax.ShapeDtypeStruct((rows, heads * 128), b16),
            jax.ShapeDtypeStruct((rows, 128), b16),
            jax.ShapeDtypeStruct((rows, 128), b16),
            jax.ShapeDtypeStruct((rows, heads * 128), jnp.float32),
        ],
        compiler_params=pltpu.CompilerParams(vmem_limit_bytes=24 * 2**20),
        name="attention_forward",
    )(projected, projected, projected, cos, sin, mask)


def attention_backward_kernel(
    grad_ref, query_ref, key_ref, value_ref, log_ref, cos_ref, sin_ref, mask_ref,
    dq_ref, dk_ref, dv_ref, key_sum, value_sum,
):
    head = pl.program_id(0)
    rows = query_ref.shape[0]
    scale = HEAD_DIMENSION**-0.5

    @pl.when(head == 0)
    def _():
        key_sum[...] = jnp.zeros_like(key_sum)
        value_sum[...] = jnp.zeros_like(value_sum)

    for block in range(rows // TILE):
        top, end = block * TILE, (block + 1) * TILE
        query = query_ref[top:end, :]
        grad = grad_ref[top:end, :]
        scores = dot_nt(query, key_ref[:end, :]) * scale
        scores = jnp.where(mask_ref[top:end, :end] > 0.0, scores, -1e30)
        probs = jnp.exp(scores - log_ref[top:end, 0:1])
        grad_probs = dot_nt(grad, value_ref[:end, :])
        inner = jnp.sum(grad_probs * probs, axis=1, keepdims=True)
        grad_scores = (probs * (grad_probs - inner)).astype(jnp.bfloat16)
        dq = dot_nn(grad_scores, key_ref[:end, :]) * scale
        dq_ref[top:end, :] = (
            dq * cos_ref[top:end, :]
            - pltpu.roll(dq, HEAD_DIMENSION // 2, 1) * sin_ref[top:end, :]
        ).astype(dq_ref.dtype)
        key_sum[:end, :] += dot_tn(grad_scores, query)
        value_sum[:end, :] += dot_tn(probs.astype(jnp.bfloat16), grad)

    @pl.when(head == pl.num_programs(0) - 1)
    def _():
        dk = key_sum[...] * scale
        dk_ref[...] = (
            dk * cos_ref[...] - pltpu.roll(dk, HEAD_DIMENSION // 2, 1) * sin_ref[...]
        ).astype(dk_ref.dtype)
        dv_ref[...] = value_sum[...].astype(dv_ref.dtype)


def attention_backward(grad, query, key, value, logs, cos, sin, mask):
    rows = query.shape[0]
    heads = query.shape[1] // 128
    const2 = lambda i: (0, 0)
    one = pl.BlockSpec((rows, 128), const2)
    each = pl.BlockSpec((rows, 128), lambda i: (0, i))
    b16 = jnp.bfloat16
    return pl.pallas_call(
        attention_backward_kernel,
        grid=(heads,),
        in_specs=[each, each, one, one, each, one, one, pl.BlockSpec((rows, rows), const2)],
        out_specs=[each, one, one],
        out_shape=[
            jax.ShapeDtypeStruct((rows, heads * 128), b16),
            jax.ShapeDtypeStruct((rows, 128), b16),
            jax.ShapeDtypeStruct((rows, 128), b16),
        ],
        scratch_shapes=[pltpu.VMEM((rows, 128), jnp.float32), pltpu.VMEM((rows, 128), jnp.float32)],
        compiler_params=pltpu.CompilerParams(vmem_limit_bytes=24 * 2**20),
        cost_estimate=cost(1, 1),
        name="attention_backward",
    )(grad, query, key, value, logs, cos, sin, mask)


def feed_forward_kernel(in_ref, gate_w_ref, up_w_ref, act_ref, gate_ref, up_ref):
    gate = dot_nn(in_ref[...], gate_w_ref[...])
    up = dot_nn(in_ref[...], up_w_ref[...])
    gate_ref[...] = gate
    up_ref[...] = up
    act_ref[...] = (gate * jax.nn.sigmoid(gate) * up).astype(act_ref.dtype)


def feed_forward(ffn_in, weights, first, hidden, tile=256):
    rows, model = ffn_in.shape
    steps = hidden // tile
    each = pl.BlockSpec((rows, tile), lambda i: (0, i))
    return pl.pallas_call(
        feed_forward_kernel,
        grid=(steps,),
        in_specs=[
            pl.BlockSpec((rows, model), lambda i: (0, 0)),
            pl.BlockSpec((model, tile), lambda i: (0, first // tile + i)),
            pl.BlockSpec((model, tile), lambda i: (0, first // tile + steps + i)),
        ],
        out_specs=[each, each, each],
        out_shape=[
            jax.ShapeDtypeStruct((rows, hidden), jnp.bfloat16),
            jax.ShapeDtypeStruct((rows, hidden), jnp.float32),
            jax.ShapeDtypeStruct((rows, hidden), jnp.float32),
        ],
        compiler_params=pltpu.CompilerParams(vmem_limit_bytes=32 * 2**20),
        cost_estimate=cost(4 * rows * model * hidden, 4 * model * hidden + 12 * rows * hidden),
        name="feed_forward",
    )(ffn_in, weights, weights)


def feed_forward_back_kernel(
    grad_ref, down_ref, gate_ref, up_ref, gate_w_ref, up_w_ref, dgate_ref, dup_ref, din_ref, total
):
    step = pl.program_id(0)

    @pl.when(step == 0)
    def _():
        total[...] = jnp.zeros_like(total)

    grad_act = dot_nn(grad_ref[...], down_ref[...])
    gate = gate_ref[...]
    value, slope = silu_parts(gate)
    dgate = (grad_act * up_ref[...] * slope).astype(jnp.bfloat16)
    dup = (grad_act * value).astype(jnp.bfloat16)
    dgate_ref[...] = dgate
    dup_ref[...] = dup
    total[...] += dot_nt(dgate, gate_w_ref[...]) + dot_nt(dup, up_w_ref[...])

    @pl.when(step == pl.num_programs(0) - 1)
    def _():
        din_ref[...] = total[...].astype(din_ref.dtype)


def feed_forward_back(grad, down_t, gate, up, weights, first, tile=512):
    rows, model = grad.shape
    hidden = gate.shape[1]
    steps = hidden // tile
    each = pl.BlockSpec((rows, tile), lambda i: (0, i))
    whole = pl.BlockSpec((rows, model), lambda i: (0, 0))
    b16 = jnp.bfloat16
    return pl.pallas_call(
        feed_forward_back_kernel,
        grid=(steps,),
        in_specs=[
            whole,
            pl.BlockSpec((model, tile), lambda i: (0, first // tile + 2 * steps + i)),
            each,
            each,
            pl.BlockSpec((model, tile), lambda i: (0, first // tile + i)),
            pl.BlockSpec((model, tile), lambda i: (0, first // tile + steps + i)),
        ],
        out_specs=[each, each, whole],
        out_shape=[
            jax.ShapeDtypeStruct((rows, hidden), b16),
            jax.ShapeDtypeStruct((rows, hidden), b16),
            jax.ShapeDtypeStruct((rows, model), b16),
        ],
        scratch_shapes=[pltpu.VMEM((rows, model), jnp.float32)],
        compiler_params=pltpu.CompilerParams(vmem_limit_bytes=40 * 2**20),
        cost_estimate=cost(1, 1),
        name="feed_forward_back",
    )(grad, down_t, gate, up, weights, weights)


def norm_back_kernel(
    grad_ref, weight_ref, gated_ref, inverse_ref, gain_ref, dn_ref, row_ref, column_ref
):
    step = pl.program_id(0)

    @pl.when(step == 0)
    def _():
        row_ref[...] = jnp.zeros_like(row_ref)

    grad = dot_nn(grad_ref[...], weight_ref[...])
    dn_ref[...] = grad
    product = grad * gated_ref[...]
    scaled = product * gain_ref[0:1]
    part = scaled[:, :128]
    for k in range(1, scaled.shape[1] // 128):
        part = part + scaled[:, k * 128 : (k + 1) * 128]
    row_ref[...] += part
    total = jnp.sum(product * inverse_ref[:, 0:1], axis=0, keepdims=True)
    column_ref[...] = jnp.broadcast_to(total, column_ref.shape)

    @pl.when(step == pl.num_programs(0) - 1)
    def _():
        row_ref[...] = jnp.broadcast_to(
            jnp.sum(row_ref[...], axis=1, keepdims=True), row_ref.shape
        )


def norm_back(grad, weights, first, gated, inverse, gains, tile=256):
    rows, model = grad.shape
    width = gated.shape[1]
    each = pl.BlockSpec((rows, tile), lambda i: (0, i))
    f32 = jnp.float32
    return pl.pallas_call(
        norm_back_kernel,
        grid=(width // tile,),
        in_specs=[
            pl.BlockSpec((rows, model), lambda i: (0, 0)),
            pl.BlockSpec((model, tile), lambda i: (0, first // tile + i)),
            each,
            pl.BlockSpec((rows, 128), lambda i: (0, 0)),
            pl.BlockSpec((8, tile), lambda i: (0, i)),
        ],
        out_specs=[
            each,
            pl.BlockSpec((rows, 128), lambda i: (0, 0)),
            pl.BlockSpec((8, tile), lambda i: (0, i)),
        ],
        out_shape=[
            jax.ShapeDtypeStruct((rows, width), f32),
            jax.ShapeDtypeStruct((rows, 128), f32),
            jax.ShapeDtypeStruct((8, width), f32),
        ],
        compiler_params=pltpu.CompilerParams(vmem_limit_bytes=24 * 2**20),
        cost_estimate=cost(1, 1),
        name="norm_back",
    )(grad, weights, gated, inverse, gains)


def reorder_kernel(order_ref, in_ref, out_ref):
    width = in_ref.shape[1] // order_ref.shape[0]
    for place in range(order_ref.shape[0]):
        column = pl.multiple_of(order_ref[place] * width, width)
        out_ref[:, place * width : (place + 1) * width] = in_ref[:, pl.ds(column, width)]


def reorder_columns(values, order):
    rows, model = values.shape
    count = order.shape[0]
    width = model // count
    if width % 128:
        return jnp.take(values.reshape(rows, count, width), order, axis=1).reshape(rows, model)
    return pl.pallas_call(
        reorder_kernel,
        in_specs=[
            pl.BlockSpec(memory_space=pltpu.SMEM),
            pl.BlockSpec(memory_space=pltpu.VMEM),
        ],
        out_specs=pl.BlockSpec(memory_space=pltpu.VMEM),
        out_shape=jax.ShapeDtypeStruct(values.shape, values.dtype),
        compiler_params=pltpu.CompilerParams(vmem_limit_bytes=16 * 2**20),
        cost_estimate=cost(1, 1),
        name="reorder_columns",
    )(order, values)


def scatter_part_kernel(left_ref, right_ref, *refs):
    got_refs, out_ref, turned_left = refs[:-2], refs[-2], refs[-1]

    @pl.when(pl.program_id(0) == 0)
    def _():
        turned_left[...] = left_ref[...].T

    total = dot_nn(turned_left[...], right_ref[...])
    for got_ref in got_refs:
        total = total + got_ref[...].astype(jnp.float32)
    out_ref[...] = total.astype(out_ref.dtype)


def scatter_part(left, right, gots, first, size, dtype):
    rows, width = right.shape
    if size % 128 or first % size:
        total = contract("tm,tn->mn", left[:, first : first + size], right)
        for got, start in gots:
            total = total + got[start : start + size].astype(jnp.float32)
        return total.astype(dtype)
    tile = max(t for t in (128, 256, 384, 512) if width % t == 0)
    return pl.pallas_call(
        scatter_part_kernel,
        grid=(width // tile,),
        in_specs=[
            pl.BlockSpec((rows, size), lambda i: (0, first // size)),
            pl.BlockSpec((rows, tile), lambda i: (0, i)),
        ]
        + [
            pl.BlockSpec((size, tile), lambda i, at=start // size: (at, i)) for unused, start in gots
        ],
        out_specs=pl.BlockSpec((size, tile), lambda i: (0, i)),
        out_shape=jax.ShapeDtypeStruct((size, width), dtype),
        scratch_shapes=[pltpu.VMEM((size, rows), jnp.bfloat16)],
        compiler_params=pltpu.CompilerParams(vmem_limit_bytes=32 * 2**20),
        cost_estimate=cost(1, 1),
        name="scatter_part",
    )(left, right, *[got for got, unused in gots])


def product_kernel(left_ref, right_ref, out_ref):
    out_ref[...] = dot_nn(left_ref[...], right_ref[...]).astype(out_ref.dtype)


def product(left, right, first, width, tile=256):
    rows, model = left.shape
    return pl.pallas_call(
        product_kernel,
        grid=(width // tile,),
        in_specs=[
            pl.BlockSpec((rows, model), lambda i: (0, 0)),
            pl.BlockSpec((model, tile), lambda i: (0, first // tile + i)),
        ],
        out_specs=pl.BlockSpec((rows, tile), lambda i: (0, i)),
        out_shape=jax.ShapeDtypeStruct((rows, width), jnp.bfloat16),
        compiler_params=pltpu.CompilerParams(vmem_limit_bytes=24 * 2**20),
        cost_estimate=cost(1, 1),
        name="product",
    )(left, right)


def product_back_kernel(left_ref, right_ref, out_ref):
    out_ref[...] = dot_nt(left_ref[...], right_ref[...]).astype(out_ref.dtype)


def product_back(left, right, first, tile=512):
    rows, width = left.shape
    model = right.shape[0]
    return pl.pallas_call(
        product_back_kernel,
        grid=(model // tile,),
        in_specs=[
            pl.BlockSpec((rows, width), lambda i: (0, 0)),
            pl.BlockSpec((tile, width), lambda i: (i, first // width)),
        ],
        out_specs=pl.BlockSpec((rows, tile), lambda i: (0, i)),
        out_shape=jax.ShapeDtypeStruct((rows, model), jnp.bfloat16),
        compiler_params=pltpu.CompilerParams(vmem_limit_bytes=40 * 2**20),
        cost_estimate=cost(1, 1),
        name="product_back",
    )(left, right)


def join_kernel(ready_ref, got_ref, out_ref):
    out_ref[...] = (ready_ref[...] + got_ref[...].astype(jnp.float32)).astype(out_ref.dtype)


def join_parts(ready, got, start, dtype):
    size, width = ready.shape
    if size % 128 or start % size:
        return (ready + got[start : start + size].astype(jnp.float32)).astype(dtype)
    tile = max(t for t in (128, 256, 384, 512, 768, 1024) if width % t == 0)
    return pl.pallas_call(
        join_kernel,
        grid=(width // tile,),
        in_specs=[
            pl.BlockSpec((size, tile), lambda i: (0, i)),
            pl.BlockSpec((size, tile), lambda i: (start // size, i)),
        ],
        out_specs=pl.BlockSpec((size, tile), lambda i: (0, i)),
        out_shape=jax.ShapeDtypeStruct((size, width), dtype),
        compiler_params=pltpu.CompilerParams(vmem_limit_bytes=24 * 2**20),
        cost_estimate=cost(1, 1),
        name="join_parts",
    )(ready, got)


def rms_back_kernel(value_ref, gain_ref, own_ref, other_ref, base_ref, live_ref, *out_refs):
    values = value_ref[...].astype(jnp.float32)
    gain = gain_ref[0:1]
    grad = own_ref[...].astype(jnp.float32) + other_ref[...].astype(jnp.float32)
    scale = lax.rsqrt(jnp.mean(values * values, axis=1, keepdims=True) + EPS)
    unit = values * scale
    scaled = grad * gain
    pull = jnp.mean(scaled * unit, axis=1, keepdims=True)
    total = base_ref[...].astype(jnp.float32) + (scaled - unit * pull) * scale
    out_refs[0][...] = total
    if len(out_refs) == 3:
        out_refs[2][...] = (total * live_ref[:, 0:1]).astype(jnp.bfloat16)
    gain_grad = jnp.broadcast_to(jnp.sum(grad * unit, axis=0, keepdims=True), out_refs[1].shape)

    @pl.when(pl.program_id(0) == 0)
    def _():
        out_refs[1][...] = gain_grad

    @pl.when(pl.program_id(0) > 0)
    def _():
        out_refs[1][...] += gain_grad


def rms_back(values, gain, own, other, base, live, with_rounded, tile=128):
    rows, model = values.shape
    each = pl.BlockSpec((tile, model), lambda i: (i, 0))
    whole = pl.BlockSpec((8, model), lambda i: (0, 0))
    shapes = [
        jax.ShapeDtypeStruct((rows, model), jnp.float32),
        jax.ShapeDtypeStruct((8, model), jnp.float32),
    ]
    if with_rounded:
        shapes.append(jax.ShapeDtypeStruct((rows, model), jnp.bfloat16))
    return pl.pallas_call(
        rms_back_kernel,
        grid=(rows // tile,),
        in_specs=[each, whole, each, each, each, pl.BlockSpec((tile, 128), lambda i: (i, 0))],
        out_specs=[each, whole, each][: len(shapes)],
        out_shape=shapes,
        compiler_params=pltpu.CompilerParams(vmem_limit_bytes=32 * 2**20),
        cost_estimate=cost(1, 1),
        name="rms_back",
    )(values, gain, own, other, base, live)


def beside_kernel(widths, *refs):
    out_ref, place, refs = refs[-1], 0, list(refs[:-1])
    for width, terms in widths:
        total = refs.pop(0)[...]
        if terms == 2:
            total = total.astype(jnp.float32) + refs.pop(0)[...].astype(jnp.float32)
        out_ref[:, place : place + width] = total.astype(out_ref.dtype)
        place += width
    if place < out_ref.shape[1]:
        out_ref[:, place:] = jnp.zeros((out_ref.shape[0], out_ref.shape[1] - place), out_ref.dtype)


def beside(width, *columns, tile=128):
    groups = [c if isinstance(c, tuple) else (c,) for c in columns]
    widths = tuple((g[0].shape[1], len(g)) for g in groups)
    arrays = [a for g in groups for a in g]
    rows = arrays[0].shape[0]
    return pl.pallas_call(
        functools.partial(beside_kernel, widths),
        grid=(rows // tile,),
        in_specs=[pl.BlockSpec((tile, a.shape[1]), lambda i: (i, 0)) for a in arrays],
        out_specs=pl.BlockSpec((tile, width), lambda i: (i, 0)),
        out_shape=jax.ShapeDtypeStruct((rows, width), jnp.bfloat16),
        compiler_params=pltpu.CompilerParams(vmem_limit_bytes=24 * 2**20),
        cost_estimate=cost(1, 1),
        name="beside",
    )(*arrays)


def hidden_back_kernel(first_ref, second_ref, keep_ref, weight_ref, out_ref, total):
    step = pl.program_id(0)
    half = pl.num_programs(0) // 2

    @pl.when(step == 0)
    def _():
        total[...] = jnp.zeros_like(total)

    left = jnp.where(step < half, first_ref[...], second_ref[...] * keep_ref[0:1])
    total[...] += dot_nt(left, weight_ref[...])

    @pl.when(step == pl.num_programs(0) - 1)
    def _():
        out_ref[...] = total[...].astype(out_ref.dtype)


def hidden_back(first, second, keep, weights, tile=768):
    rows, width = first.shape
    model = weights.shape[0]
    steps = width // tile
    return pl.pallas_call(
        hidden_back_kernel,
        grid=(2 * steps,),
        in_specs=[
            pl.BlockSpec((rows, tile), lambda i: (0, jnp.minimum(i, steps - 1))),
            pl.BlockSpec((rows, tile), lambda i: (0, jnp.maximum(i - steps, 0))),
            pl.BlockSpec((8, tile), lambda i: (0, jnp.maximum(i - steps, 0))),
            pl.BlockSpec((model, tile), lambda i: (0, i)),
        ],
        out_specs=pl.BlockSpec((rows, model), lambda i: (0, 0)),
        out_shape=jax.ShapeDtypeStruct((rows, model), jnp.bfloat16),
        scratch_shapes=[pltpu.VMEM((rows, model), jnp.float32)],
        compiler_params=pltpu.CompilerParams(vmem_limit_bytes=32 * 2**20),
        cost_estimate=cost(1, 1),
        name="hidden_back",
    )(first, second, keep, weights)


def rms_forward_kernel(base_ref, own_ref, other_ref, live_ref, gain_ref, middle_ref, out_ref):
    added = own_ref[...].astype(jnp.float32) + other_ref[...].astype(jnp.float32)
    values = base_ref[...].astype(jnp.float32) + added * live_ref[:, 0:1]
    middle_ref[...] = values
    scale = lax.rsqrt(jnp.mean(values * values, axis=1, keepdims=True) + EPS)
    out_ref[...] = (values * scale * gain_ref[0:1]).astype(out_ref.dtype)


def rms_forward(base, own, other, live, gain, tile=128):
    rows, model = base.shape
    each = pl.BlockSpec((tile, model), lambda i: (i, 0))
    return pl.pallas_call(
        rms_forward_kernel,
        grid=(rows // tile,),
        in_specs=[
            each,
            each,
            each,
            pl.BlockSpec((tile, 128), lambda i: (i, 0)),
            pl.BlockSpec((8, model), lambda i: (0, 0)),
        ],
        out_specs=[each, each],
        out_shape=[
            jax.ShapeDtypeStruct((rows, model), jnp.float32),
            jax.ShapeDtypeStruct((rows, model), jnp.bfloat16),
        ],
        compiler_params=pltpu.CompilerParams(vmem_limit_bytes=32 * 2**20),
        cost_estimate=cost(1, 1),
        name="rms_forward",
    )(base, own, other, live, gain)


def output_kernel(base_ref, own_ref, other_ref, live_ref, out_ref):
    added = own_ref[...].astype(jnp.float32) + other_ref[...].astype(jnp.float32)
    out_ref[...] = (base_ref[...] + added * live_ref[:, 0:1]).astype(out_ref.dtype)


def output_rows(base, own, other, live, tile=128):
    rows, model = base.shape
    each = pl.BlockSpec((tile, model), lambda i: (i, 0))
    return pl.pallas_call(
        output_kernel,
        grid=(rows // tile,),
        in_specs=[each, each, each, pl.BlockSpec((tile, 128), lambda i: (i, 0))],
        out_specs=each,
        out_shape=jax.ShapeDtypeStruct((rows, model), jnp.bfloat16),
        compiler_params=pltpu.CompilerParams(vmem_limit_bytes=24 * 2**20),
        cost_estimate=cost(1, 1),
        name="output_rows",
    )(base, own, other, live)


def stack_kernel(counts, *refs):
    out_ref, place = refs[-1], 0
    out_ref[...] = jnp.zeros_like(out_ref)
    for count, ref in zip(counts, refs):
        out_ref[place : place + count, : ref.shape[1]] = ref[:count, :]
        place += count


def stack_rows(width, *parts):
    counts = tuple(count for unused, count in parts)
    total = -(-sum(counts) // 8) * 8
    vmem = pl.BlockSpec(memory_space=pltpu.VMEM)
    return pl.pallas_call(
        functools.partial(stack_kernel, counts),
        in_specs=[vmem] * len(parts),
        out_specs=vmem,
        out_shape=jax.ShapeDtypeStruct((total, width), jnp.float32),
        compiler_params=pltpu.CompilerParams(vmem_limit_bytes=8 * 2**20),
        cost_estimate=cost(1, 1),
        name="stack_rows",
    )(*[part for part, unused in parts])


def tie(*values):
    return lax.optimization_barrier(values)


def pair_swap(values):
    return lax.ppermute(values, "tensor", [(0, 1), (1, 0)])


def pair_sum(values):
    own = lax.reduce_precision(values.astype(jnp.float32), 8, 7)
    return own + pair_swap(own.astype(jnp.bfloat16)).astype(jnp.float32)


def pair_join(values):
    other = pair_swap(values)
    first = lax.axis_index("tensor") == 0
    return jnp.concatenate(
        [jnp.where(first, values, other), jnp.where(first, other, values)], axis=0
    )


def after(values, *earlier):
    return lax.optimization_barrier((values, *earlier))[0]


def bits_of(count):
    return tuple(1 << place for place in range(count.bit_length() - 1))


def owner_order(bits):
    offsets = [0]
    for bit in reversed(bits):
        offsets = [offset | bit for offset in offsets] + offsets
    return lax.axis_index("dp") ^ jnp.array(offsets, jnp.int32)


def across(values, bit):
    count = lax.axis_size("dp")
    return lax.ppermute(values, "dp", [(i, i ^ bit) for i in range(count)])


class Scatter:
    def __init__(self, left, right, bits):
        self.left, self.right, self.bits = left, right, bits
        self.rows = left.shape[1] // 2 ** len(bits)
        self.got = []
        self.total = None

    def place(self, step):
        count = 2 ** len(self.bits)
        return count - (count >> step), max(count >> (step + 1), 1)

    def meets(self, past, step):
        return (self.place(step)[0] - self.place(past + 1)[0]) * self.rows

    def begin(self, *earlier):
        first, size = self.place(0)
        left = after(self.left, *earlier)
        self.held = scatter_part(left, self.right, [], 0, size * self.rows, jnp.bfloat16)
        return self.held

    def send(self, *earlier):
        self.got.append(across(after(self.held, *earlier), self.bits[len(self.got)]))
        return self.got[-1]

    def prepare(self, *earlier):
        step = len(self.got)
        first, size = self.place(step)
        gots = [(got, self.meets(past, step)) for past, got in enumerate(self.got[:-1])]
        left = after(self.left, *earlier)
        self.ready = scatter_part(
            left, self.right, gots, first * self.rows, size * self.rows, jnp.float32
        )
        return self.ready

    def join(self, *earlier):
        step = len(self.got)
        done = step == len(self.bits)
        self.held = join_parts(
            after(self.ready, *earlier),
            self.got[-1],
            self.meets(step - 1, step),
            jnp.float32 if done else jnp.bfloat16,
        )
        if done:
            self.total = self.held
        return self.held

    def finish(self):
        while self.total is None:
            self.send()
            self.prepare()
            self.join()
        return self.total


def local(
    tokens,
    cotangent,
    segment_ids,
    counts,
    mixer_gain,
    query_proj,
    key_value_matrix,
    attend_proj,
    inner_proj,
    state_proj,
    step_proj,
    conv_inner,
    conv_state,
    step_bias,
    decay_log,
    skip_gain,
    gated_gain,
    mamba_proj,
    dense_gain,
    gateup_proj,
    down_proj,
):
    row_count, model_width = tokens.shape
    shard_rows = query_proj.shape[0]
    dp_count = lax.axis_size("dp")
    bf16, f32 = jnp.bfloat16, jnp.float32
    heads_m = step_proj.shape[1]
    heads_q = query_proj.shape[1] // HEAD_DIMENSION
    q_cols = query_proj.shape[1]
    kv_cols = 2 * key_value_matrix.shape[2]
    x_cols = inner_proj.shape[2]
    state_cols = state_proj.shape[1]
    o_cols = attend_proj.shape[0]
    hidden_cols = gateup_proj.shape[2]
    tap_count = conv_state.shape[0]
    pair_width = conv_state.shape[1]

    small = jnp.concatenate(
        [mixer_gain[:, None], dense_gain[:, None], jnp.zeros((mixer_gain.shape[0], 126), bf16)],
        axis=1,
    )
    small = lax.dynamic_update_slice(small, conv_state.T, (0, 2))
    joined = pair_join(jnp.concatenate([state_proj, small], axis=1))
    step_pad = jnp.zeros((shard_rows, 128 - heads_m), bf16)
    group_mix = jnp.concatenate(
        [
            query_proj,
            key_value_matrix.reshape(shard_rows, -1),
            inner_proj.reshape(shard_rows, -1),
            joined[:, :state_cols],
            step_proj,
            step_pad,
            joined[:, state_cols:],
            attend_proj.T,
            mamba_proj.T,
        ],
        axis=1,
    )
    offsets, place = {}, 0
    for name, width in (
        ("q", q_cols),
        ("kv", kv_cols),
        ("z", x_cols),
        ("u", x_cols),
        ("state", state_cols),
        ("step", 128),
        ("end", 0),
    ):
        offsets[name] = place
        place += width
    out_first = offsets["end"] + 128
    group_ffn = jnp.concatenate([gateup_proj.reshape(shard_rows, -1), down_proj.T], axis=1)
    mix_full = lax.all_gather(group_mix, "dp", axis=0, tiled=True)
    ffn_full = lax.all_gather(after(group_ffn, mix_full), "dp", axis=0, tiled=True)
    out_t = mix_full[:, out_first:]
    down_t = ffn_full[:, 2 * hidden_cols :]

    small_full = mix_full[:, offsets["end"] : out_first]
    w_proj = mix_full[:, : offsets["end"]]
    gain_mix = small_full[:, 0].astype(f32)
    gain_dense = small_full[:, 1].astype(f32)
    conv_full = small_full[:, 2 : 2 + tap_count].reshape(
        dp_count, 2, shard_rows // 2, tap_count
    )[:, :, :pair_width]
    conv_full = conv_full.reshape(dp_count * 2 * pair_width, tap_count).T.astype(f32)
    conv_full = jnp.concatenate([conv_full, jnp.zeros((8 - tap_count, state_cols), f32)], axis=0)
    gain_gated = gated_gain.astype(f32)
    wide = jnp.concatenate(
        [
            conv_inner.astype(f32),
            jnp.repeat(skip_gain.astype(f32), HP)[None],
            gain_gated[None],
            jnp.zeros((1, x_cols), f32),
        ],
        axis=0,
    )
    extra = jnp.zeros((8, 128), f32)
    extra = extra.at[0, :heads_m].set(step_bias.astype(f32))
    extra = extra.at[1, :heads_m].set(jnp.exp(decay_log.astype(f32)))

    row_index = jnp.arange(row_count, dtype=jnp.int32)
    valid_rows = (row_index < counts[0]).astype(f32)[:, None]
    live = jnp.broadcast_to(valid_rows, (row_count, 128))
    position = positions_of(segment_ids)
    causal = (row_index[None, :] <= row_index[:, None]) & (
        segment_ids[None, :] == segment_ids[:, None]
    )
    mask = causal.astype(f32)
    mask_t = (
        (row_index[None, :] >= row_index[:, None]) & (segment_ids[None, :] == segment_ids[:, None])
    ).astype(f32)
    mask_qk = (causal & (row_index[None, :] < counts[0])).astype(f32)
    same = jnp.stack(
        [
            jnp.broadcast_to(((row_index >= lag) & (position >= lag)).astype(f32)[:, None], live.shape)
            for lag in range(1, tap_count - 1)
        ]
    )
    half = HEAD_DIMENSION // 2
    frequency = jnp.exp(
        jnp.arange(half, dtype=f32) * (-2.0 * math.log(THETA) / HEAD_DIMENSION)
    )
    angles = position.astype(f32)[:, None] * frequency[None, :]
    cos = jnp.cos(angles)
    sin = jnp.sin(angles)
    cos = jnp.concatenate([cos, cos], axis=1)
    sin = jnp.concatenate([-sin, sin], axis=1)
    bits = bits_of(dp_count)
    order = owner_order(bits)
    stream = tokens.astype(f32)
    upstream = cotangent.astype(f32)
    dense_grad_b = rounded(upstream * valid_rows)
    dense_split = reorder_columns(dense_grad_b, order)

    gain_dense_rows = jnp.broadcast_to(gain_dense[None], (8, model_width))
    gain_mix_rows = jnp.broadcast_to(gain_mix[None], (8, model_width))

    hidden_b = rounded(rms_scale(stream, gain_mix))
    projected = contract("td,dc->tc", hidden_b, w_proj)
    hidden_split = reorder_columns(hidden_b, order)
    mixed, gated, squares = ssm_forward(
        projected, wide, conv_full, extra, live, same, mask, offsets
    )
    own_squares = jnp.sum(squares, axis=-1)
    other_squares = pair_swap(own_squares)
    attended_b, query_b, key_b, value_b, logs = attention_forward(
        projected, cos, sin, mask_qk, offsets, heads_q
    )
    inverse = lax.rsqrt((own_squares + other_squares) / DSSM + EPS)
    normed_b = rounded(gated * inverse[:, None] * gain_gated)
    branch_in = jnp.concatenate([attended_b, normed_b], axis=1)
    branch_own = rounded(contract("tc,dc->td", branch_in, out_t))
    branch_other = pair_swap(branch_own)
    middle, ffn_in_b = rms_forward(tokens, branch_own, branch_other, live, gain_dense_rows)
    activated_b, gate, up = feed_forward(ffn_in_b, ffn_full, 0, hidden_cols)
    inverse_b = jnp.broadcast_to(inverse[:, None], live.shape)
    gated_rows = jnp.broadcast_to(gain_gated[None], (8, x_cols))
    first = (lax.axis_index("tensor") == 0).astype(bf16)
    early_cols = q_cols + kv_cols + x_cols
    column_at = jnp.arange(early_cols) - x_cols
    keep = jnp.where((column_at >= 0) & (column_at < state_cols), first, jnp.ones((), bf16))
    keep = jnp.broadcast_to(keep[None], (8, early_cols))
    down = Scatter(dense_split, activated_b, bits)
    held = down.begin()

    down.send()
    grad_gate_b, grad_up_b, grad_ffn_part = feed_forward_back(
        after(dense_grad_b, held), ffn_full, gate, up, ffn_full, 0
    )
    ready = down.prepare(grad_ffn_part)

    held = down.join(ready)
    down.send()
    grad_ffn_other = pair_swap(after(grad_ffn_part, held))
    gate_sum = Scatter(reorder_columns(ffn_in_b, order), grad_gate_b, bits)
    up_sum = Scatter(gate_sum.left, grad_up_b, bits)
    held = gate_sum.begin(held)
    gate_sum.send()
    held = up_sum.begin(held)
    up_sum.send()
    ready = down.prepare(held)
    dense_own = product_back(after(activated_b, ready), ffn_full, 2 * hidden_cols)
    ready = gate_sum.prepare(dense_own)

    held = gate_sum.join(ready, down.got[-1], up_sum.got[-1], grad_ffn_other)
    gate_sum.send()
    held = down.join(held)
    down.send()
    dense_other = pair_swap(after(dense_own, held))
    grad_middle, grad_dense_gain, mixer_grad_b = rms_back(
        middle, gain_dense_rows, after(grad_ffn_part, held), grad_ffn_other, cotangent, live, True
    )
    grad_normed, own_rows, column_part = norm_back(
        mixer_grad_b, mix_full, out_first + o_cols, gated, inverse_b, gated_rows
    )
    other_rows = pair_swap(own_rows)
    branch = Scatter(reorder_columns(mixer_grad_b, order), branch_in, bits)
    held = branch.begin(own_rows)
    ready = up_sum.prepare(held)
    held = up_sum.join(ready)
    ready = gate_sum.prepare(held)
    grad_attended_b = product(after(mixer_grad_b, ready), mix_full, out_first, o_cols)
    ready = down.prepare(grad_attended_b)
    grad_query_b, grad_key_b, grad_value_b = attention_backward(
        after(grad_attended_b, ready), query_b, key_b, value_b, logs, cos, sin, mask_qk
    )
    ready = grad_query_b

    round_end = (ready, gate_sum.got[-1], down.got[-1], other_rows, dense_other)
    up_sum.send(*round_end)
    branch.send(*round_end)
    held = gate_sum.join(*round_end)
    gate_sum.send()
    held = down.join(held)
    down.send()
    grad_z_b, grad_u_b, grad_state_part, grad_step_b, wide_grad, conv_grad, extra_grad = (
        ssm_backward(
            after(grad_normed, held),
            mixed,
            projected,
            inverse_b,
            own_rows,
            other_rows,
            wide,
            conv_full,
            extra,
            live,
            same,
            mask_t,
            offsets,
        )
    )
    ready = up_sum.prepare(grad_state_part)
    ready = gate_sum.prepare(ready)
    grad_z_b = after(grad_z_b, ready)
    early_b = beside(early_cols, grad_query_b, grad_key_b, grad_value_b, grad_z_b)
    early = Scatter(hidden_split, early_b, bits)
    held = early.begin()
    ready = branch.prepare(held)
    ready = down.prepare(ready)

    round_end = (ready, up_sum.got[-1], gate_sum.got[-1], down.got[-1], branch.got[-1])
    held = branch.join(*round_end)
    branch.send()
    early.send(*round_end)
    grad_state_other = pair_swap(after(grad_state_part, *round_end))
    held = up_sum.join(held)
    up_sum.send()
    held = gate_sum.join(held)
    gate_sum.send()
    held = down.join(held)
    late_b = beside(
        early_cols, grad_u_b, (grad_state_part, after(grad_state_other, held)), grad_step_b
    )
    late = Scatter(hidden_split, late_b, bits)
    held = late.begin()
    ready = early.prepare(held)
    ready = branch.prepare(ready)
    ready = up_sum.prepare(ready)
    ready = gate_sum.prepare(ready)

    round_end = (ready, branch.got[-1], up_sum.got[-1], gate_sum.got[-1], early.got[-1])
    held = early.join(*round_end)
    early.send()
    late.send(*round_end)
    held = branch.join(held)
    branch.send()
    held = up_sum.join(held)
    up_sum.send()
    held = gate_sum.join(held)
    grad_hidden_own = hidden_back(after(early_b, held), late_b, keep, mix_full)
    ready = late.prepare(grad_hidden_own)
    ready = early.prepare(ready)
    ready = branch.prepare(ready)
    ready = up_sum.prepare(ready)

    round_end = (ready, early.got[-1], branch.got[-1], up_sum.got[-1], late.got[-1])
    held = late.join(*round_end)
    late.send()
    grad_hidden_other = pair_swap(after(grad_hidden_own, *round_end))
    held = early.join(held)
    early.send()
    held = branch.join(held)
    branch.send()
    held = up_sum.join(held)
    output = output_rows(middle, after(dense_own, held), dense_other, live)
    ready = late.prepare(output)
    ready = early.prepare(ready)
    ready = branch.prepare(ready)

    round_end = (ready, late.got[-1], early.got[-1], branch.got[-1], grad_hidden_other)
    held = late.join(*round_end)
    late.send()
    held = early.join(held)
    early.send()
    grad_tokens, grad_mixer_gain = rms_back(
        tokens, gain_mix_rows, after(grad_hidden_own, held), grad_hidden_other, grad_middle, live, False
    )
    own_sums = stack_rows(
        model_width,
        (grad_mixer_gain, 1),
        (grad_dense_gain, 1),
        (wide_grad, tap_count + 1),
        (column_part, 1),
        (conv_grad, tap_count),
        (extra_grad, 2),
    )
    sums = own_sums + across(own_sums, bits[0])
    held = branch.join(sums)
    ready = late.prepare(held)
    ready = early.prepare(ready)
    others = across(after(sums, ready), bits[1])

    held = late.join(ready, early.got[-1], others)
    late.send()
    sums = after(sums, held) + others
    for bit in bits[2:]:
        sums = sums + across(sums, bit)
    held = early.join(sums)
    late.prepare(held)
    late.join()
    at = 2 + tap_count + 2
    conv_sum = sums[at : at + tap_count, :state_cols]
    conv_sum = conv_sum + pair_swap(conv_sum)
    at += tap_count
    skip_sum = jnp.sum(sums[2 + tap_count, :x_cols].reshape(heads_m, HP), axis=1)
    owner = lax.axis_index("dp") * 2 + lax.axis_index("tensor")

    def own_part(values, axis_dim):
        width = values.shape[axis_dim] // (2 * dp_count)
        return lax.dynamic_slice_in_dim(values, owner * width, width, axis_dim)

    red_early, red_late, red_branch = early.finish(), late.finish(), branch.finish()
    state_rows = shard_rows // 2
    red_state = lax.dynamic_slice_in_dim(
        red_late[:, x_cols : x_cols + state_cols],
        lax.axis_index("tensor") * state_rows,
        state_rows,
        0,
    )
    return (
        output,
        grad_tokens,
        own_part(sums[0], 0),
        red_early[:, :q_cols],
        red_early[:, q_cols : q_cols + kv_cols].reshape(shard_rows, 2, -1),
        red_branch[:, :o_cols].T,
        jnp.stack([red_early[:, q_cols + kv_cols :], red_late[:, :x_cols]], axis=1),
        red_state,
        red_late[:, x_cols + state_cols : x_cols + state_cols + heads_m],
        sums[2 : 2 + tap_count, :x_cols],
        own_part(conv_sum, 1),
        sums[at, :heads_m],
        sums[at + 1, :heads_m],
        skip_sum,
        sums[3 + tap_count, :x_cols],
        red_branch[:, o_cols:].T,
        own_part(sums[1], 0),
        jnp.stack([gate_sum.finish(), up_sum.finish()], axis=1),
        down.finish().T,
    )


def solution(mesh):
    placed = (
        P("dp", None),
        P("dp", None),
        P("dp"),
        P("dp"),
        P(("dp", "tensor")),
        P("dp", "tensor"),
        P("dp", None, "tensor"),
        P("tensor", "dp"),
        P("dp", None, "tensor"),
        P(("dp", "tensor"), None),
        P("dp", "tensor"),
        P(None, "tensor"),
        P(None, ("dp", "tensor")),
        P("tensor"),
        P("tensor"),
        P("tensor"),
        P("tensor"),
        P("tensor", "dp"),
        P(("dp", "tensor")),
        P("dp", None, "tensor"),
        P("tensor", "dp"),
    )
    return jax.shard_map(
        local,
        mesh=mesh,
        in_specs=placed,
        out_specs=(
            P("dp", None),
            P("dp", None),
            P(("dp", "tensor")),
            P("dp", "tensor"),
            P("dp", None, "tensor"),
            P("tensor", "dp"),
            P("dp", None, "tensor"),
            P(("dp", "tensor"), None),
            P("dp", "tensor"),
            P(None, "tensor"),
            P(None, ("dp", "tensor")),
            P("tensor"),
            P("tensor"),
            P("tensor"),
            P("tensor"),
            P("tensor", "dp"),
            P(("dp", "tensor")),
            P("dp", None, "tensor"),
            P("tensor", "dp"),
        ),
        check_vma=False,
    )
```

time: 2310 us -> 806 us (0.35)
  waiting for transfers between devices: 1640 us -> 291 us
  Pallas kernels: 0 us -> 301 us
  matrix products: 238 us -> 27.2 us
  blocking collectives: 204 us -> 0 us
  other arithmetic: 90.7 us -> 16.9 us
  starting transfers between devices: 1.84 us -> 36.1 us
    reduce_scatter x9 -> x0, waiting for transfers between devices: 1150 us -> none  [the longest x1 333 us: local(): lax.psum_scatter(grad_gateup, 'dp', scatter_dimension=0, tiled=True)]
    pallas_call x0 -> x75, Pallas kernels: none -> 301 us  [the longest x30 109 us: scatter_part(): pl.pallas_call(scatter_part_kernel, grid=(width // tile,), in_specs=[pl.B...]
    psum x3 -> x0, waiting for transfers between devices: 218 us -> none  [the longest x1 111 us: local(): lax.psum(matrix_product(activated_b, wdown_full).astype(jnp.bfloat16), 't...]
    dot_general x30 -> x2, matrix products: 180 us -> 27.2 us  [contract(): return jnp.einsum(form, left, right, preferred_element_type=jnp.float32)]
    ppermute x0 -> x37, waiting for transfers between devices: none -> 148 us  [the longest x28 88.2 us: across(): return lax.ppermute(values, 'dp', [(i, i ^ bit) for i in range(count)])]
    all_gather x8 -> x2, waiting for transfers between devices: 267 us -> 143 us  [the longest x1 137 us: local(): mix_full = lax.all_gather(group_mix, 'dp', axis=0, tiled=True)]
    unnamed x2 -> x0, blocking collectives: 102 us -> none
    all_gather x2 -> x0, blocking collectives: 86.2 us -> none  [the longest x1 64.3 us: local(): lax.all_gather(conv_state, ('dp', 'tensor'), axis=1, tiled=True)]
  transfers between devices with their start and end apart: 21 -> 39, of which waited for: 15 -> 17; matrix products, arithmetic and copies ran while one was open for 12% -> 8% of each run, Pallas kernels for 0% -> 32%
where the time goes in v1:
time: 806 us; the launch traced here: 800 us
  Pallas kernels  301 us (37%)
  waiting for transfers between devices  291 us (36%)
  local copies, waits for them, and re-layouts  111 us (14%)
  starting transfers between devices  36.1 us (4%)
  matrix products  27.2 us (3%)
  between operations  17.1 us (2%)
  other arithmetic  16.9 us (2%)
    all_gather x1, waiting for transfers between devices, local(): mix_full = lax.all_gather(group_mix, 'dp', axis=0, tiled=True)  137 us
    pallas_call x30, Pallas kernels, scatter_part(): pl.pallas_call(scatter_part_kernel, grid=(width // tile,), in_specs=[pl.B...  109 us
    unnamed x354, local copies, waits for them, and re-layouts  96.6 us
    ppermute x28, waiting for transfers between devices, across(): return lax.ppermute(values, 'dp', [(i, i ^ bit) for i in range(count)])  88.2 us
    ppermute x9, waiting for transfers between devices, pair_swap(): return lax.ppermute(values, 'tensor', [(0, 1), (1, 0)])  59.6 us
    pallas_call x24, Pallas kernels, join_parts(): pl.pallas_call(join_kernel, grid=(width // tile,), in_specs=[pl.BlockSpec...  48.2 us
    pallas_call x1, Pallas kernels, ssm_backward(): pl.pallas_call(ssm_backward_kernel, grid=(pairs,), in_specs=[plain, plain...  28.5 us
    dot_general x2, matrix products, contract(): return jnp.einsum(form, left, right, preferred_element_type=jnp.float32)  27.2 us
  transfers between devices with their start and end apart: 39, of which 17 were waited for; matrix products, arithmetic and copies ran while one was open for 8% of the time, Pallas kernels for 32%

profile of v1, /device:TPU:0, one launch (start us, length us, event | category | flops | bytes accessed | tf_op | source)
XLA Modules:
  0.0 800.2 jit_solution(8662741773993760753)
XLA Ops:
  11.3 2.9 collective-permute-start
  22.5 136.7 %all-gather.3.cloned.1.call-done.weight_ref.right_ref = bf16[2048,6656]{1,0:T(8,128)(2,1)} async-done(((bf16[128,6656]{1,0:T(8,128)(2,1)}), bf16[2048,6656]{1,0:T(8,128)(2,1)}) %all-gather.3.cloned.1.call-update) | async-done | bytes 27262992 | tf_op jit(solution)/shard_map/all_gather | solution.py:1165
  171.7 16.9 %fusion.q_ref.k_ref.v_ref.u_ref.z_ref.state_b_ref.state_c_ref.step_ref = f32[512,4480]{1,0:T(8,128)} fusion(bf16[512,2048]{1,0:T(8,128)(2,1)S(1)} %fusion.6.in_ref, bf16[2048,6656]{1,0:T(8,128)(2,1)} %all-gather.3.cloned.1.call-done.weight_ref.right_ref), kind=kOutput, calls=%fused_computation | convolution fusion | flops 9395240960 | bytes 29622272 | tf_op jit(solution)/shard_map/td,dc->tc/dot_general | solution.py:25
  188.7 14.2 %ssm_forward.1 = (f32[512,1536]{1,0:T(8,128)S(1)}, f32[512,1536]{1,0:T(8,128)S(1)}, f32[512,128]{1,0:T(8,128)S(1)}) custom-call(f32[512,4480]{1,0:T(8,128)} %fusion.q_ref.k_ref.v_ref.u_ref.z_ref.state_b_ref.state_c_ref.step_ref, f32[512,4480]{1,0:T(8,128)} %fusion.q_ref.k_ref.v_ref.u_ref.z_ref.state_b_ref.state_c_ref.step_ref, ...), custom_call_target="tpu_custom_call" | custom-call | tf_op jit(solution)/shard_map/ssm_forward/pallas_call | solution.py:178
  208.2 4.0 copy-done
  212.2 4.7 attention_forward.1
  218.3 10.3 %fusion.7.own_ref = bf16[512,2048]{1,0:T(8,128)(2,1)} fusion(bf16[2048,6656]{1,0:T(8,128)(2,1)} %all-gather.3.cloned.1.call-done.weight_ref.right_ref, bf16[512,1536]{1,0:T(8,128)(2,1)S(1)} %multiply_convert_fusion.1, bf16[512,512]{1,0:T(8,128)(2,1)S(1)} %get-tuple-element.147), kind=kOutput, calls=%fused_computation.11 | convolution fusion | flops 4300210176 | bytes 12582912 | tf_op jit(solution)/shard_map/tc,dc->td/dot_general | solution.py:25
  231.3 45.1 %collective-permute-done.2.other_ref = bf16[512,2048]{1,0:T(8,128)(2,1)} collective-permute-done((bf16[512,2048]{1,0:T(8,128)(2,1)}, bf16[512,2048]{1,0:T(8,128)(2,1)}, u32[]{:S(2)}, u32[]{:S(2)}) %collective-permute-start.2) | collective-permute-done | bytes 2097184 | tf_op jit(solution)/shard_map/ppermute | solution.py:1001
  276.4 3.7 rms_forward.1
  283.5 6.5 all-gather.5.cloned.1.call-done.gate_w_ref.up_w_ref.down_ref.right_ref
  291.6 13.3 %feed_forward.1 = (bf16[512,2048]{1,0:T(8,128)(2,1)S(1)}, f32[512,2048]{1,0:T(8,128)S(1)}, f32[512,2048]{1,0:T(8,128)S(1)}) custom-call(bf16[512,2048]{1,0:T(8,128)(2,1)S(1)} %copy-done.71, bf16[2048,6144]{1,0:T(8,128)(2,1)} %all-gather.5.cloned.1.call-done.gate_w_ref.up_w_ref.down_ref.right_ref, ...), custom_call_target="tpu_custom_call" | custom-call | flops 8589934592 | bytes 29360128 | tf_op jit(solution)/shard_map/feed_forward/pallas_call | solution.py:543
  306.9 4.8 scatter_part.30
  313.4 20.9 %feed_forward_back.1 = (bf16[512,2048]{1,0:T(8,128)(2,1)S(1)}, bf16[512,2048]{1,0:T(8,128)(2,1)S(1)}, bf16[512,2048]{1,0:T(8,128)(2,1)}) custom-call(bf16[512,2048]{1,0:T(8,128)(2,1)S(1)} %copy-done.49, bf16[2048,6144]{1,0:T(8,128)(2,1)} %all-gather.5.cloned.1.call-done.gate_w_ref.up_w_ref.down_ref.right_ref, f32[512,2048]{1,0:T(8,128)S(1)} %get-tuple-element.155.gate_ref, ...), custom_call_target="tpu_custom_call" | custom-call | flops 1 | bytes 1 | tf_op jit(solution)/shard_map/feed_forward_back/pallas_call | solution.py:593
  336.8 2.9 join_parts.24
  339.7 4.7 scatter_part.32
  344.4 5.0 scatter_part.33
  352.5 3.2 scatter_part.34.ready_ref
  357.0 8.3 %product_back.1.own_ref = bf16[512,2048]{1,0:T(8,128)(2,1)} custom-call(bf16[512,2048]{1,0:T(8,128)(2,1)S(1)} %get-tuple-element.164.right_ref.left_ref, bf16[2048,6144]{1,0:T(8,128)(2,1)} %all-gather.5.cloned.1.call-done.gate_w_ref.up_w_ref.down_ref.right_ref), custom_call_target="tpu_custom_call" | custom-call | flops 1 | bytes 1 | tf_op jit(solution)/shard_map/product_back/pallas_call | solution.py:770
  367.8 30.1 %collective-permute-done.4.got_ref.refs_1_ = bf16[512,2048]{1,0:T(8,128)(2,1)} collective-permute-done((bf16[512,2048]{1,0:T(8,128)(2,1)}, bf16[512,2048]{1,0:T(8,128)(2,1)}, u32[]{:S(2)}, u32[]{:S(2)}) %collective-permute-start.4) | collective-permute-done | bytes 2097184 | tf_op jit(solution)/shard_map/ppermute | solution.py:1034
  410.8 4.6 rms_back.2
  416.2 4.0 copy-done.57
  420.2 8.0 norm_back.1
  431.2 4.8 scatter_part.36
  446.5 8.8 %copy-done.1 = bf16[2048,6656]{1,0:T(8,128)(2,1)S(1)} copy-done((bf16[2048,6656]{1,0:T(8,128)(2,1)S(1)}, bf16[2048,6656]{1,0:T(8,128)(2,1)}, u32[]{:S(2)}) %copy-start.1) | copy-done | bytes 27263000
  456.9 3.2 scatter_part.39.ready_ref
  460.2 5.6 attention_backward.1
  470.8 2.6 collective-permute-start.14
  474.5 28.5 %ssm_backward.1 = (bf16[512,1536]{1,0:T(8,128)(2,1)S(1)}, bf16[512,1536]{1,0:T(8,128)(2,1)}, bf16[512,512]{1,0:T(8,128)(2,1)S(1)}, bf16[512,128]{1,0:T(8,128)(2,...) custom-call(f32[512,1536]{1,0:T(8,128)} %copy-done.105, f32[512,1536]{1,0:T(8,128)} %copy-done.104, ...), custom_call_target="tpu_custom_call" | custom-call | flops 1 | bytes 1 | tf_op jit(solution)/shard_map/ssm_backward/pallas_call | solution.py:346
  508.4 3.4 scatter_part.41.ready_ref
  512.8 5.4 scatter_part.42
  524.9 3.2 scatter_part.44.ready_ref
  530.4 2.9 join_parts.30
  543.3 9.8 %collective-permute-done.16.refs_2_ = bf16[512,512]{1,0:T(8,128)(2,1)S(1)} collective-permute-done((bf16[512,512]{1,0:T(8,128)(2,1)S(1)}, bf16[512,512]{1,0:T(8,128)(2,1)S(1)}, u32[]{:S(2)}, u32[]{:S(2)}) %collective-permute-start.16) | collective-permute-done | bytes 524320 | tf_op jit(solution)/shard_map/ppermute | solution.py:1001
  553.5 6.3 scatter_part.45
  559.8 3.4 scatter_part.46.ready_ref
  565.4 3.7 scatter_part.47.ready_ref
  570.4 3.7 scatter_part.48.ready_ref
  574.2 3.0 scatter_part.49.ready_ref
  577.2 4.3 collective-permute-done.17.got_ref.refs_1_
  581.6 3.4 join_parts.34
  596.6 13.8 %hidden_back.1.own_ref = bf16[512,2048]{1,0:T(8,128)(2,1)S(1)} custom-call(bf16[512,2304]{1,0:T(8,128)(2,1)S(1)} %copy-done.9, bf16[512,2304]{1,0:T(8,128)(2,1)S(1)} %copy-done.5, bf16[8,2304]{1,0:T(8,128)(2,1)S(1)} %broadcast_in_dim.50.keep_ref, bf16[2048,6656]{1,0:T(8,128)(2,1)} %all-gather.3.cloned.1.call-done.weight_ref.right_ref), custom_call_target="tpu_custom_call" | custom-call | flops 1 | bytes 1 | tf_op jit(solution)/shard_map/hidden_back/pallas_call | solution.py:903
  610.5 3.4 scatter_part.50.ready_ref
  618.4 2.5 scatter_part.51.ready_ref
  622.4 4.0 scatter_part.52.ready_ref
  626.4 2.9 scatter_part.53.ready_ref
  629.4 9.1 %collective-permute-done.21.got_ref.refs_1_ = bf16[512,2304]{1,0:T(8,128)(2,1)} collective-permute-done((bf16[512,2304]{1,0:T(8,128)(2,1)}, bf16[512,2304]{1,0:T(8,128)(2,1)}, u32[]{:S(2)}, u32[]{:S(2)}) %collective-permute-start.21) | collective-permute-done | bytes 2359328 | tf_op jit(solution)/shard_map/ppermute | solution.py:1034
  640.8 4.3 join_parts.38
  647.0 3.2 join_parts.39
  655.3 5.1 output_rows.1
  660.4 4.5 scatter_part.54.ready_ref
  666.3 4.0 scatter_part.55.ready_ref
  670.4 3.9 scatter_part.56.ready_ref
  675.2 11.6 %collective-permute-done.27.got_ref = bf16[128,2048]{1,0:T(8,128)(2,1)} collective-permute-done((bf16[128,2048]{1,0:T(8,128)(2,1)}, bf16[128,2048]{1,0:T(8,128)(2,1)}, u32[]{:S(2)}, u32[]{:S(2)}) %collective-permute-start.27) | collective-permute-done | bytes 524320 | tf_op jit(solution)/shard_map/ppermute | solution.py:1034
  689.1 3.8 collective-permute-done.28.other_ref
  692.9 4.7 collective-permute-done.25.got_ref.refs_1_
  704.4 6.1 rms_back.3
  718.6 4.1 scatter_part.57.ready_ref
  722.8 4.2 scatter_part.58.ready_ref
  728.5 2.9 copy.67
  733.0 5.7 collective-permute-done.30.got_ref
  743.0 3.4 collective-permute-done.33
  747.0 3.2 collective-permute-start.34
  753.4 15.2 %collective-permute-done.34 = f32[16,2048]{1,0:T(8,128)} collective-permute-done((f32[16,2048]{1,0:T(8,128)}, f32[16,2048]{1,0:T(8,128)}, u32[]{:S(2)}, u32[]{:S(2)}) %collective-permute-start.34) | collective-permute-done | bytes 131104 | tf_op jit(solution)/shard_map/ppermute | solution.py:1034
  777.3 4.0 scatter_part.59.ready_ref
  (538 shorter events, 192.3 us)
Async XLA Ops:
  7.2 151.9 %all-gather.3.cloned.1.call-start = ((), (), s32[]{:S(2)}) async-start(), calls=%async_computation | async-start | bytes 28966912 | tf_op jit(solution)/shard_map/all_gather | solution.py:1165
  11.3 6.2 collective-permute-start
  19.6 270.4 %all-gather.5.cloned.1.call-start = ((), (), s32[]{:S(2)}) async-start(), calls=%async_computation.1 | async-start | bytes 26738688 | tf_op jit(solution)/shard_map/all_gather | solution.py:1166
  21.2 138.0 %copy-start.156 = (bf16[1536]{0:T(1024)(128)(2,1)S(1)}, bf16[1536]{0:T(1024)(128)(2,1)}, u32[]{:S(2)}) copy-start(bf16[1536]{0:T(1024)(128)(2,1)} %param.42) | copy-start | bytes 9220
  21.2 138.0 %copy-start.160 = (bf16[24]{0:T(256)(128)(2,1)S(1)}, bf16[24]{0:T(256)(128)(2,1)}, u32[]{:S(2)}) copy-start(bf16[24]{0:T(256)(128)(2,1)} %param.41) | copy-start | bytes 148
  21.2 138.2 %copy-start.159 = (bf16[5,1536]{1,0:T(8,128)(2,1)S(1)}, bf16[5,1536]{1,0:T(8,128)(2,1)}, u32[]{:S(2)}) copy-start(bf16[5,1536]{1,0:T(8,128)(2,1)} %param.37) | copy-start | bytes 46084
  21.2 138.8 %copy-start.158 = (s32[512]{0:T(512)S(1)}, s32[512]{0:T(512)}, u32[]{:S(2)}) copy-start(s32[512]{0:T(512)} %param.28) | copy-start | bytes 6148
  21.2 139.5 %copy-start.161 = (bf16[24]{0:T(256)(128)(2,1)S(1)}, bf16[24]{0:T(256)(128)(2,1)}, u32[]{:S(2)}) copy-start(bf16[24]{0:T(256)(128)(2,1)} %param.39) | copy-start | bytes 148
  21.2 139.5 %copy-start.162 = (bf16[24]{0:T(256)(128)(2,1)S(1)}, bf16[24]{0:T(256)(128)(2,1)}, u32[]{:S(2)}) copy-start(bf16[24]{0:T(256)(128)(2,1)} %param.40) | copy-start | bytes 148
  22.5 140.3 %copy-start.37 = (bf16[512,2048]{1,0:T(8,128)(2,1)S(1)}, bf16[512,2048]{1,0:T(8,128)(2,1)}, u32[]{:S(2)}) copy-start(bf16[512,2048]{1,0:T(8,128)(2,1)} %value_ref.1) | copy-start | bytes 6291460
  171.7 16.9 %copy-start.72 = (bf16[512,2048]{1,0:T(8,128)(2,1)}, bf16[512,2048]{1,0:T(8,128)(2,1)S(1)}, u32[]{:S(2)}) copy-start(bf16[512,2048]{1,0:T(8,128)(2,1)S(1)} %fusion.6.in_ref) | copy-start | bytes 6291460
  171.7 17.0 %copy-start.78 = (f32[3,512,128]{2,1,0:T(8,128)S(1)}, f32[3,512,128]{2,1,0:T(8,128)}, u32[]{:S(2)}) copy-start(f32[3,512,128]{2,1,0:T(8,128)} %pad_maximum_fusion.4.same_ref) | copy-start | bytes 2359300
  171.7 17.0 %copy-start.94 = (f32[512,512]{1,0:T(8,128)S(1)}, f32[512,512]{1,0:T(8,128)}, u32[]{:S(2)}) copy-start(f32[512,512]{1,0:T(8,128)} %get-tuple-element.306.mask_ref) | copy-start | bytes 3145732
  188.7 19.2 %copy-start.146 = (f32[512,64]{1,0:T(8,128)S(1)}, f32[512,64]{1,0:T(8,128)}, u32[]{:S(2)}) copy-start(f32[512,64]{1,0:T(8,128)} %get-tuple-element.299) | copy-start | bytes 393220
  188.7 19.2 %copy-start.147 = (f32[512,64]{1,0:T(8,128)S(1)}, f32[512,64]{1,0:T(8,128)}, u32[]{:S(2)}) copy-start(f32[512,64]{1,0:T(8,128)} %get-tuple-element.300) | copy-start | bytes 393220
  188.7 19.2 %copy-start.148 = (f32[512,64]{1,0:T(8,128)S(1)}, f32[512,64]{1,0:T(8,128)}, u32[]{:S(2)}) copy-start(f32[512,64]{1,0:T(8,128)} %get-tuple-element.301) | copy-start | bytes 393220
  206.5 10.4 %collective-permute-start.1 = (f32[512]{0:T(512)S(1)}, f32[512]{0:T(512)S(1)}, u32[]{:S(2)}, u32[]{:S(2)}) collective-permute-start(f32[512]{0:T(512)S(1)} %reduce_sum.28), channel_id=1, source_target_pairs={{0,1},{1,0},{2,3},{3,2},{4,5},{5,4},{6,7},{7,6},{8,9},{9,8},{10,11... | collective-permute-start | bytes 6152 | tf_op jit(solution)/shard_map/ppermute | solution.py:1001
  228.7 47.7 %collective-permute-start.2 = (bf16[512,2048]{1,0:T(8,128)(2,1)}, bf16[512,2048]{1,0:T(8,128)(2,1)}, u32[]{:S(2)}, u32[]{:S(2)}) collective-permute-start(bf16[512,2048]{1,0:T(8,128)(2,1)} %fusion.7.own_ref), channel_id=1, source_target_pairs={{0,1},{1,0},{2,3},{3,2},{4,5},{5,4},{6,7},{7,6},{8,9},{9,8},{10,11... | collective-permute-start | bytes 6291464 | tf_op jit(solution)/shard_map/ppermute | solution.py:1001
  229.9 46.5 %copy-start.157 = (f32[2048]{0:T(1024)S(1)}, f32[2048]{0:T(1024)}, u32[]{:S(2)}) copy-start(f32[2048]{0:T(1024)} %get-tuple-element.289) | copy-start | bytes 24580
  229.9 46.5 %copy-start.38 = (bf16[512,2048]{1,0:T(8,128)(2,1)S(1)}, bf16[512,2048]{1,0:T(8,128)(2,1)}, u32[]{:S(2)}) copy-start(bf16[512,2048]{1,0:T(8,128)(2,1)} %value_ref.1) | copy-start | bytes 6291460
  231.3 225.6 %copy-start.20 = (bf16[512,2048]{1,0:T(8,128)(2,1)}, bf16[512,2048]{1,0:T(8,128)(2,1)S(1)}, u32[]{:S(2)}) copy-start(bf16[512,2048]{1,0:T(8,128)(2,1)S(1)} %reorder_columns.4.left_ref) | copy-start | bytes 6291460
  311.8 25.0 %collective-permute-start.3 = (bf16[1024,2048]{1,0:T(8,128)(2,1)}, bf16[1024,2048]{1,0:T(8,128)(2,1)}, u32[]{:S(2)}, u32[]{:S(2)}) collective-permute-start(bf16[1024,2048]{1,0:T(8,128)(2,1)} %scatter_part.30), channel_id=1, source_target_pairs={{0,2},{2,0},{4,6},{6,4},{8,10},{10,8},{12,14},{14,12},{16,18},{18,... | collective-permute-start | bytes 12582920 | tf_op jit(solution)/shard_map/ppermute | solution.py:1034
  313.2 260.9 %copy-start.2 = (bf16[512,2048]{1,0:T(8,128)(2,1)}, bf16[512,2048]{1,0:T(8,128)(2,1)S(1)}, u32[]{:S(2)}) copy-start(bf16[512,2048]{1,0:T(8,128)(2,1)S(1)} %reorder_columns.5.left_ref) | copy-start | bytes 6291460
  334.3 168.8 %copy-start.30 = (bf16[512,2048]{1,0:T(8,128)(2,1)}, bf16[512,2048]{1,0:T(8,128)(2,1)S(1)}, u32[]{:S(2)}) copy-start(bf16[512,2048]{1,0:T(8,128)(2,1)S(1)} %get-tuple-element.162.right_ref) | copy-start | bytes 6291460
  349.4 49.5 %collective-permute-start.5 = (bf16[1024,2048]{1,0:T(8,128)(2,1)}, bf16[1024,2048]{1,0:T(8,128)(2,1)S(1)}, u32[]{:S(2)}, u32[]{:S(2)}) collective-permute-start(bf16[1024,2048]{1,0:T(8,128)(2,1)} %scatter_part.33), channel_id=1, source_target_pairs={{0,2},{2,0},{4,6},{6,4},{8,10},{10,8},{12,14},{14,12},{16,18},{18,... | collective-permute-start | bytes 12582920 | tf_op jit(solution)/shard_map/ppermute | solution.py:1034
  349.6 49.3 %collective-permute-start.7 = (bf16[1024,2048]{1,0:T(8,128)(2,1)}, bf16[1024,2048]{1,0:T(8,128)(2,1)S(1)}, u32[]{:S(2)}, u32[]{:S(2)}) collective-permute-start(bf16[1024,2048]{1,0:T(8,128)(2,1)} %scatter_part.32), channel_id=1, source_target_pairs={{0,2},{2,0},{4,6},{6,4},{8,10},{10,8},{12,14},{14,12},{16,18},{18,... | collective-permute-start | bytes 12582920 | tf_op jit(solution)/shard_map/ppermute | solution.py:1034
  349.9 48.0 %collective-permute-start.4 = (bf16[512,2048]{1,0:T(8,128)(2,1)}, bf16[512,2048]{1,0:T(8,128)(2,1)}, u32[]{:S(2)}, u32[]{:S(2)}) collective-permute-start(bf16[512,2048]{1,0:T(8,128)(2,1)} %join_parts.24), channel_id=1, source_target_pairs={{0,4},{2,6},{4,0},{6,2},{8,12},{10,14},{12,8},{14,10},{16,20},{18,... | collective-permute-start | bytes 6291464 | tf_op jit(solution)/shard_map/ppermute | solution.py:1034
  351.0 47.8 %collective-permute-start.6 = (bf16[512,2048]{1,0:T(8,128)(2,1)}, bf16[512,2048]{1,0:T(8,128)(2,1)}, u32[]{:S(2)}, u32[]{:S(2)}) collective-permute-start(bf16[512,2048]{1,0:T(8,128)(2,1)} %get-tuple-element.169.own_ref), channel_id=1, source_target_pairs={{0,1},{1,0},{2,3},{3,2},{4,5},{5,4},{6,7},{7,6},{8,9},{9,8},{10,11... | collective-permute-start | bytes 6291464 | tf_op jit(solution)/shard_map/ppermute | solution.py:1001
  367.8 35.9 %copy-start.69 = (f32[256,2048]{1,0:T(8,128)S(1)}, f32[256,2048]{1,0:T(8,128)}, u32[]{:S(2)}) copy-start(f32[256,2048]{1,0:T(8,128)} %copy-done.68) | copy-start | bytes 6291460
  398.8 40.9 %copy-start.22 = (bf16[1024,2048]{1,0:T(8,128)(2,1)}, bf16[1024,2048]{1,0:T(8,128)(2,1)S(1)}, u32[]{:S(2)}) copy-start(bf16[1024,2048]{1,0:T(8,128)(2,1)S(1)} %collective-permute-done.5.got_ref.refs_0_) | copy-start | bytes 12582916
  402.9 63.0 %collective-permute-start.8 = (bf16[512,2048]{1,0:T(8,128)(2,1)}, bf16[512,2048]{1,0:T(8,128)(2,1)}, u32[]{:S(2)}, u32[]{:S(2)}) collective-permute-start(bf16[512,2048]{1,0:T(8,128)(2,1)} %join_parts.25), channel_id=1, source_target_pairs={{0,4},{2,6},{4,0},{6,2},{8,12},{10,14},{12,8},{14,10},{16,20},{18,... | collective-permute-start | bytes 6291464 | tf_op jit(solution)/shard_map/ppermute | solution.py:1034
  406.2 59.7 %collective-permute-start.11 = (bf16[512,2048]{1,0:T(8,128)(2,1)}, bf16[512,2048]{1,0:T(8,128)(2,1)}, u32[]{:S(2)}, u32[]{:S(2)}) collective-permute-start(bf16[512,2048]{1,0:T(8,128)(2,1)} %product_back.1.own_ref), channel_id=1, source_target_pairs={{0,1},{1,0},{2,3},{3,2},{4,5},{5,4},{6,7},{7,6},{8,9},{9,8},{10,11... | collective-permute-start | bytes 6291464 | tf_op jit(solution)/shard_map/ppermute | solution.py:1001
  407.7 58.2 %collective-permute-start.9 = (bf16[256,2048]{1,0:T(8,128)(2,1)}, bf16[256,2048]{1,0:T(8,128)(2,1)}, u32[]{:S(2)}, u32[]{:S(2)}) collective-permute-start(bf16[256,2048]{1,0:T(8,128)(2,1)} %join_parts.26), channel_id=1, source_target_pairs={{0,8},{2,10},{4,12},{6,14},{8,0},{10,2},{12,4},{14,6},{16,24},{18,... | collective-permute-start | bytes 3145736 | tf_op jit(solution)/shard_map/ppermute | solution.py:1034
  428.2 37.6 %collective-permute-start.10 = (f32[512,128]{1,0:T(8,128)}, f32[512,128]{1,0:T(8,128)}, u32[]{:S(2)}, u32[]{:S(2)}) collective-permute-start(f32[512,128]{1,0:T(8,128)} %get-tuple-element.171.own_ref), channel_id=1, source_target_pairs={{0,1},{1,0},{2,3},{3,2},{4,5},{5,4},{6,7},{7,6},{8,9},{9,8},{10,11... | collective-permute-start | bytes 786440 | tf_op jit(solution)/shard_map/ppermute | solution.py:1001
  465.9 62.2 %collective-permute-start.15 = (bf16[1024,2048]{1,0:T(8,128)(2,1)}, bf16[1024,2048]{1,0:T(8,128)(2,1)}, u32[]{:S(2)}, u32[]{:S(2)}) collective-permute-start(bf16[1024,2048]{1,0:T(8,128)(2,1)} %scatter_part.36), channel_id=1, source_target_pairs={{0,2},{2,0},{4,6},{6,4},{8,10},{10,8},{12,14},{14,12},{16,18},{18,... | collective-permute-start | bytes 12582920 | tf_op jit(solution)/shard_map/ppermute | solution.py:1034
  466.0 62.1 %collective-permute-start.12 = (bf16[512,2048]{1,0:T(8,128)(2,1)}, bf16[512,2048]{1,0:T(8,128)(2,1)}, u32[]{:S(2)}, u32[]{:S(2)}) collective-permute-start(bf16[512,2048]{1,0:T(8,128)(2,1)} %join_parts.27), channel_id=1, source_target_pairs={{0,4},{2,6},{4,0},{6,2},{8,12},{10,14},{12,8},{14,10},{16,20},{18,... | collective-permute-start | bytes 6291464 | tf_op jit(solution)/shard_map/ppermute | solution.py:1034
  468.4 59.7 %collective-permute-start.13 = (bf16[256,2048]{1,0:T(8,128)(2,1)S(1)}, bf16[256,2048]{1,0:T(8,128)(2,1)S(1)}, u32[]{:S(2)}, u32[]{:S(2)}) collective-permute-start(bf16[256,2048]{1,0:T(8,128)(2,1)S(1)} %join_parts.28), channel_id=1, source_target_pairs={{0,8},{2,10},{4,12},{6,14},{8,0},{10,2},{12,4},{14,6},{16,24},{18,... | collective-permute-start | bytes 3145736 | tf_op jit(solution)/shard_map/ppermute | solution.py:1034
  470.8 57.2 %collective-permute-start.14 = (bf16[128,2048]{1,0:T(8,128)(2,1)}, bf16[128,2048]{1,0:T(8,128)(2,1)}, u32[]{:S(2)}, u32[]{:S(2)}) collective-permute-start(bf16[128,2048]{1,0:T(8,128)(2,1)} %join_parts.29), channel_id=1, source_target_pairs={{0,16},{2,18},{4,20},{6,22},{8,24},{10,26},{12,28},{14,30},{16,0},... | collective-permute-start | bytes 1572872 | tf_op jit(solution)/shard_map/ppermute | solution.py:1034
  512.8 46.9 %copy-start.8 = (bf16[512,2304]{1,0:T(8,128)(2,1)}, bf16[512,2304]{1,0:T(8,128)(2,1)S(1)}, u32[]{:S(2)}) copy-start(bf16[512,2304]{1,0:T(8,128)(2,1)S(1)} %beside.2.right_ref.first_ref) | copy-start | bytes 7077892
  528.1 53.5 %collective-permute-start.20 = (bf16[1024,2304]{1,0:T(8,128)(2,1)}, bf16[1024,2304]{1,0:T(8,128)(2,1)S(1)}, u32[]{:S(2)}, u32[]{:S(2)}) collective-permute-start(bf16[1024,2304]{1,0:T(8,128)(2,1)} %copy-done.80), channel_id=1, source_target_pairs={{0,2},{2,0},{4,6},{6,4},{8,10},{10,8},{12,14},{14,12},{16,18},{18,... | collective-permute-start | bytes 14155784 | tf_op jit(solution)/shard_map/ppermute | solution.py:1034
  533.2 48.3 %collective-permute-start.17 = (bf16[512,2048]{1,0:T(8,128)(2,1)}, bf16[512,2048]{1,0:T(8,128)(2,1)}, u32[]{:S(2)}, u32[]{:S(2)}) collective-permute-start(bf16[512,2048]{1,0:T(8,128)(2,1)} %join_parts.30), channel_id=1, source_target_pairs={{0,4},{2,6},{4,0},{6,2},{8,12},{10,14},{12,8},{14,10},{16,20},{18,... | collective-permute-start | bytes 6291464 | tf_op jit(solution)/shard_map/ppermute | solution.py:1034
  538.2 14.9 %copy-start.112 = (bf16[512,1536]{1,0:T(8,128)(2,1)S(1)}, bf16[512,1536]{1,0:T(8,128)(2,1)}, u32[]{:S(2)}) copy-start(bf16[512,1536]{1,0:T(8,128)(2,1)} %get-tuple-element.196.refs_0_) | copy-start | bytes 4718596
  538.2 14.9 %copy-start.129 = (bf16[512,128]{1,0:T(8,128)(2,1)S(1)}, bf16[512,128]{1,0:T(8,128)(2,1)}, u32[]{:S(2)}) copy-start(bf16[512,128]{1,0:T(8,128)(2,1)} %copy-done.128) | copy-start | bytes 393220
  538.2 39.0 %collective-permute-start.18 = (bf16[256,2048]{1,0:T(8,128)(2,1)}, bf16[256,2048]{1,0:T(8,128)(2,1)S(1)}, u32[]{:S(2)}, u32[]{:S(2)}) collective-permute-start(bf16[256,2048]{1,0:T(8,128)(2,1)} %join_parts.31), channel_id=1, source_target_pairs={{0,8},{2,10},{4,12},{6,14},{8,0},{10,2},{12,4},{14,6},{16,24},{18,... | collective-permute-start | bytes 3145736 | tf_op jit(solution)/shard_map/ppermute | solution.py:1034
  539.4 13.8 %collective-permute-start.16 = (bf16[512,512]{1,0:T(8,128)(2,1)S(1)}, bf16[512,512]{1,0:T(8,128)(2,1)S(1)}, u32[]{:S(2)}, u32[]{:S(2)}) collective-permute-start(bf16[512,512]{1,0:T(8,128)(2,1)S(1)} %copy-done.119), channel_id=1, source_target_pairs={{0,1},{1,0},{2,3},{3,2},{4,5},{5,4},{6,7},{7,6},{8,9},{9,8},{10,11... | collective-permute-start | bytes 1572872 | tf_op jit(solution)/shard_map/ppermute | solution.py:1001
  541.1 36.1 %collective-permute-start.19 = (bf16[128,2048]{1,0:T(8,128)(2,1)}, bf16[128,2048]{1,0:T(8,128)(2,1)}, u32[]{:S(2)}, u32[]{:S(2)}) collective-permute-start(bf16[128,2048]{1,0:T(8,128)(2,1)} %join_parts.32), channel_id=1, source_target_pairs={{0,16},{2,18},{4,20},{6,22},{8,24},{10,26},{12,28},{14,30},{16,0},... | collective-permute-start | bytes 1572872 | tf_op jit(solution)/shard_map/ppermute | solution.py:1034
  581.6 56.9 %collective-permute-start.24 = (bf16[1024,2304]{1,0:T(8,128)(2,1)}, bf16[1024,2304]{1,0:T(8,128)(2,1)}, u32[]{:S(2)}, u32[]{:S(2)}) collective-permute-start(bf16[1024,2304]{1,0:T(8,128)(2,1)} %scatter_part.45), channel_id=1, source_target_pairs={{0,2},{2,0},{4,6},{6,4},{8,10},{10,8},{12,14},{14,12},{16,18},{18,... | collective-permute-start | bytes 14155784 | tf_op jit(solution)/shard_map/ppermute | solution.py:1034
  585.0 53.5 %collective-permute-start.21 = (bf16[512,2304]{1,0:T(8,128)(2,1)}, bf16[512,2304]{1,0:T(8,128)(2,1)}, u32[]{:S(2)}, u32[]{:S(2)}) collective-permute-start(bf16[512,2304]{1,0:T(8,128)(2,1)} %join_parts.34), channel_id=1, source_target_pairs={{0,4},{2,6},{4,0},{6,2},{8,12},{10,14},{12,8},{14,10},{16,20},{18,... | collective-permute-start | bytes 7077896 | tf_op jit(solution)/shard_map/ppermute | solution.py:1034
  588.2 41.1 %collective-permute-start.22 = (bf16[256,2048]{1,0:T(8,128)(2,1)}, bf16[256,2048]{1,0:T(8,128)(2,1)}, u32[]{:S(2)}, u32[]{:S(2)}) collective-permute-start(bf16[256,2048]{1,0:T(8,128)(2,1)} %join_parts.35), channel_id=1, source_target_pairs={{0,8},{2,10},{4,12},{6,14},{8,0},{10,2},{12,4},{14,6},{16,24},{18,... | collective-permute-start | bytes 3145736 | tf_op jit(solution)/shard_map/ppermute | solution.py:1034
  590.3 39.0 %collective-permute-start.23 = (bf16[128,2048]{1,0:T(8,128)(2,1)}, bf16[128,2048]{1,0:T(8,128)(2,1)}, u32[]{:S(2)}, u32[]{:S(2)}) collective-permute-start(bf16[128,2048]{1,0:T(8,128)(2,1)} %join_parts.36), channel_id=1, source_target_pairs={{0,16},{2,18},{4,20},{6,22},{8,24},{10,26},{12,28},{14,30},{16,0},... | collective-permute-start | bytes 1572872 | tf_op jit(solution)/shard_map/ppermute | solution.py:1034
  645.1 52.5 %collective-permute-start.25 = (bf16[512,2304]{1,0:T(8,128)(2,1)}, bf16[512,2304]{1,0:T(8,128)(2,1)S(1)}, u32[]{:S(2)}, u32[]{:S(2)}) collective-permute-start(bf16[512,2304]{1,0:T(8,128)(2,1)} %join_parts.38), channel_id=1, source_target_pairs={{0,4},{2,6},{4,0},{6,2},{8,12},{10,14},{12,8},{14,10},{16,20},{18,... | collective-permute-start | bytes 7077896 | tf_op jit(solution)/shard_map/ppermute | solution.py:1034
  646.2 46.7 %collective-permute-start.28 = (bf16[512,2048]{1,0:T(8,128)(2,1)}, bf16[512,2048]{1,0:T(8,128)(2,1)}, u32[]{:S(2)}, u32[]{:S(2)}) collective-permute-start(bf16[512,2048]{1,0:T(8,128)(2,1)} %copy-done.76), channel_id=1, source_target_pairs={{0,1},{1,0},{2,3},{3,2},{4,5},{5,4},{6,7},{7,6},{8,9},{9,8},{10,11... | collective-permute-start | bytes 6291464 | tf_op jit(solution)/shard_map/ppermute | solution.py:1001
  650.2 37.9 %collective-permute-start.26 = (bf16[256,2304]{1,0:T(8,128)(2,1)}, bf16[256,2304]{1,0:T(8,128)(2,1)S(1)}, u32[]{:S(2)}, u32[]{:S(2)}) collective-permute-start(bf16[256,2304]{1,0:T(8,128)(2,1)} %join_parts.39), channel_id=1, source_target_pairs={{0,8},{2,10},{4,12},{6,14},{8,0},{10,2},{12,4},{14,6},{16,24},{18,... | collective-permute-start | bytes 3538952 | tf_op jit(solution)/shard_map/ppermute | solution.py:1034
  653.2 33.6 %collective-permute-start.27 = (bf16[128,2048]{1,0:T(8,128)(2,1)}, bf16[128,2048]{1,0:T(8,128)(2,1)}, u32[]{:S(2)}, u32[]{:S(2)}) collective-permute-start(bf16[128,2048]{1,0:T(8,128)(2,1)} %join_parts.40), channel_id=1, source_target_pairs={{0,16},{2,18},{4,20},{6,22},{8,24},{10,26},{12,28},{14,30},{16,0},... | collective-permute-start | bytes 1572872 | tf_op jit(solution)/shard_map/ppermute | solution.py:1034
  670.4 27.3 %copy-start.61 = (f32[256,2304]{1,0:T(8,128)S(1)}, f32[256,2304]{1,0:T(8,128)}, u32[]{:S(2)}) copy-start(f32[256,2304]{1,0:T(8,128)} %copy-done.60) | copy-start | bytes 7077892
  670.4 34.0 %copy-start.100 = (f32[512,2048]{1,0:T(8,128)S(1)}, f32[512,2048]{1,0:T(8,128)}, u32[]{:S(2)}) copy-start(f32[512,2048]{1,0:T(8,128)} %copy-done.99) | copy-start | bytes 12582916
  700.9 39.0 %collective-permute-start.32 = (bf16[256,2304]{1,0:T(8,128)(2,1)}, bf16[256,2304]{1,0:T(8,128)(2,1)S(1)}, u32[]{:S(2)}, u32[]{:S(2)}) collective-permute-start(bf16[256,2304]{1,0:T(8,128)(2,1)} %join_parts.42), channel_id=1, source_target_pairs={{0,8},{2,10},{4,12},{6,14},{8,0},{10,2},{12,4},{14,6},{16,24},{18,... | collective-permute-start | bytes 3538952 | tf_op jit(solution)/shard_map/ppermute | solution.py:1034
  703.6 35.1 %collective-permute-start.30 = (bf16[128,2304]{1,0:T(8,128)(2,1)}, bf16[128,2304]{1,0:T(8,128)(2,1)}, u32[]{:S(2)}, u32[]{:S(2)}) collective-permute-start(bf16[128,2304]{1,0:T(8,128)(2,1)} %join_parts.43), channel_id=1, source_target_pairs={{0,16},{2,18},{4,20},{6,22},{8,24},{10,26},{12,28},{14,30},{16,0},... | collective-permute-start | bytes 1769480 | tf_op jit(solution)/shard_map/ppermute | solution.py:1034
  710.6 2.6 collective-permute-start.29
  727.0 6.0 collective-permute-start.31
  741.3 5.0 collective-permute-start.33
  747.0 21.6 %collective-permute-start.34 = (f32[16,2048]{1,0:T(8,128)}, f32[16,2048]{1,0:T(8,128)}, u32[]{:S(2)}, u32[]{:S(2)}) collective-permute-start(f32[16,2048]{1,0:T(8,128)} %add.66), channel_id=1, source_target_pairs={{0,16},{2,18},{4,20},{6,22},{8,24},{10,26},{12,28},{14,30},{16,0},... | collective-permute-start | bytes 393224 | tf_op jit(solution)/shard_map/ppermute | solution.py:1034
  753.3 32.5 %collective-permute-start.35 = (bf16[128,2304]{1,0:T(8,128)(2,1)}, bf16[128,2304]{1,0:T(8,128)(2,1)}, u32[]{:S(2)}, u32[]{:S(2)}) collective-permute-start(bf16[128,2304]{1,0:T(8,128)(2,1)} %copy-done.115), channel_id=1, source_target_pairs={{0,16},{2,18},{4,20},{6,22},{8,24},{10,26},{12,28},{14,30},{16,0},... | collective-permute-start | bytes 1769480 | tf_op jit(solution)/shard_map/ppermute | solution.py:1034
  770.9 14.3 %collective-permute-start.36 = (f32[5,512]{1,0:T(8,128)S(1)}, f32[5,512]{1,0:T(8,128)S(1)}, u32[]{:S(2)}, u32[]{:S(2)}) collective-permute-start(f32[5,512]{1,0:T(8,128)S(1)} %slice.169), channel_id=1, source_target_pairs={{0,1},{1,0},{2,3},{3,2},{4,5},{5,4},{6,7},{7,6},{8,9},{9,8},{10,11... | collective-permute-start | bytes 30728 | tf_op jit(solution)/shard_map/ppermute | solution.py:1001
  (145 other events, 609.7 us)
Sparse Core Ops, SparseCore 0:
  19.7 139.4 all-gather.2
  161.3 128.5 all-gather.4

commit v2 on v1

--- a/solution.py
+++ b/solution.py
@@ -122,11 +122,11 @@
     u_ref, z_ref, state_b_ref, state_c_ref, step_ref, wide_ref, conv_ref, extra_ref, live_ref, same_ref, mask_ref,
     y_ref, gated_ref, square_ref, gram, sizes, running, running_t,
 ):
-    pair = pl.program_id(0)
+    step = pl.program_id(0)
     live = live_ref[...]
     rows = live.shape[0]
 
-    @pl.when(pair == 0)
+    @pl.when(step == 0)
     def _():
         unused, size, decay = step_sizes(step_ref[...], extra_ref, live)
         total = running_sum(decay)
@@ -141,31 +141,34 @@
         gram[...] = dot_nt(both[:, width // 2 :], both[:, : width // 2]) * mask_ref[...]
         square_ref[...] = jnp.zeros_like(square_ref)
 
-    taps = wide_ref[...]
-    inner = conv_rows(u_ref[...] * live, taps, same_ref)
-    x_in = inner * jax.nn.sigmoid(inner)
-    left_lanes = lax.broadcasted_iota(jnp.int32, (rows, 128), 1) < HP
-    size = sizes[...]
-    size_pair = jnp.where(left_lanes, lane_column(size, 2 * pair), lane_column(size, 2 * pair + 1))
-    inflow = (size_pair * x_in).astype(jnp.bfloat16)
-    total = running[...]
-    columns = [lane_column(total, 2 * pair + k) for k in range(2)]
-    row_vectors = [running_t[pl.ds(2 * pair + k, 1), :] for k in range(2)]
-    skipped = taps[5:6] * x_in
-    gate = z_ref[...]
-    gate = gate * jax.nn.sigmoid(gate)
-    for block in range(rows // TILE):
-        top, end = block * TILE, (block + 1) * TILE
-        parts = []
-        for k in range(2):
-            gaps = columns[k][top:end] - row_vectors[k][:, :end]
-            mixing = (gram[top:end, :end] * jnp.exp(jnp.minimum(gaps, 0.0))).astype(jnp.bfloat16)
-            parts.append(dot_nn(mixing, inflow[:end]))
-        mixed = jnp.where(left_lanes[top:end], parts[0], parts[1]) + skipped[top:end]
-        y_ref[top:end, :] = mixed
-        gated = mixed * gate[top:end]
-        gated_ref[top:end, :] = gated
-        square_ref[top:end, :] += gated * gated
+    for part in range(2):
+        pair = 2 * step + part
+        at = slice(part * 128, (part + 1) * 128)
+        taps = wide_ref[:, at]
+        inner = conv_rows(u_ref[:, at] * live, taps, same_ref)
+        x_in = inner * jax.nn.sigmoid(inner)
+        left_lanes = lax.broadcasted_iota(jnp.int32, (rows, 128), 1) < HP
+        size = sizes[...]
+        size_pair = jnp.where(left_lanes, lane_column(size, 2 * pair), lane_column(size, 2 * pair + 1))
+        inflow = (size_pair * x_in).astype(jnp.bfloat16)
+        total = running[...]
+        columns = [lane_column(total, 2 * pair + k) for k in range(2)]
+        row_vectors = [running_t[pl.ds(2 * pair + k, 1), :] for k in range(2)]
+        skipped = taps[5:6] * x_in
+        gate = z_ref[:, at]
+        gate = gate * jax.nn.sigmoid(gate)
+        for block in range(rows // TILE):
+            top, end = block * TILE, (block + 1) * TILE
+            parts = []
+            for k in range(2):
+                gaps = columns[k][top:end] - row_vectors[k][:, :end]
+                mixing = (gram[top:end, :end] * jnp.exp(jnp.minimum(gaps, 0.0))).astype(jnp.bfloat16)
+                parts.append(dot_nn(mixing, inflow[:end]))
+            mixed = jnp.where(left_lanes[top:end], parts[0], parts[1]) + skipped[top:end]
+            y_ref[top:end, at] = mixed
+            gated = mixed * gate[top:end]
+            gated_ref[top:end, at] = gated
+            square_ref[top:end, :] += gated * gated
 
 
 def ssm_forward(projected, wide, conv_state, extra, live, same, mask, offsets):
@@ -174,17 +177,17 @@
     width = conv_state.shape[1]
     const2 = lambda i: (0, 0)
     at = lambda name, size: offsets[name] // size
-    block = lambda name: pl.BlockSpec((rows, 128), lambda i, o=at(name, 128): (0, o + i))
+    block = lambda name: pl.BlockSpec((rows, 128 * 2), lambda i, o=at(name, 128 * 2): (0, o + i))
     return pl.pallas_call(
         ssm_forward_kernel,
-        grid=(pairs,),
+        grid=(pairs // 2,),
         in_specs=[
             block("u"),
             block("z"),
             pl.BlockSpec((rows, width // 2), lambda i: (0, at("state", width // 2))),
             pl.BlockSpec((rows, width // 2), lambda i: (0, at("state", width // 2) + 1)),
             pl.BlockSpec((rows, 128), lambda i: (0, at("step", 128))),
-            pl.BlockSpec((8, 128), lambda i: (0, i)),
+            pl.BlockSpec((8, 128 * 2), lambda i: (0, i)),
             pl.BlockSpec((8, width), const2),
             pl.BlockSpec((8, 128), const2),
             pl.BlockSpec((rows, 128), const2),
@@ -192,8 +195,8 @@
             pl.BlockSpec((rows, rows), const2),
         ],
         out_specs=[
-            pl.BlockSpec((rows, 128), lambda i: (0, i)),
-            pl.BlockSpec((rows, 128), lambda i: (0, i)),
+            pl.BlockSpec((rows, 128 * 2), lambda i: (0, i)),
+            pl.BlockSpec((rows, 128 * 2), lambda i: (0, i)),
             pl.BlockSpec((rows, 128), const2),
         ],
         out_shape=[
@@ -207,7 +210,7 @@
             pltpu.VMEM((rows, 128), jnp.float32),
             pltpu.VMEM((128, rows), jnp.float32),
         ],
-        compiler_params=pltpu.CompilerParams(vmem_limit_bytes=40 * 2**20),
+        compiler_params=pltpu.CompilerParams(vmem_limit_bytes=28 * 2**20),
         name="ssm_forward",
     )(projected, projected, projected, projected, projected, wide, conv_state, extra, live, same, mask)
 
@@ -218,13 +221,13 @@
     dz_ref, du_ref, ds_ref, dr_ref, wide_grad_ref, conv_grad_ref, extra_grad_ref,
     gram_t, gram_grad, sizes, decays, running, running_t, size_grad, total_grad, states, state_slopes,
 ):
-    pair = pl.program_id(0)
+    step = pl.program_id(0)
     live = live_ref[...]
     rows = live.shape[0]
     width = conv_ref.shape[1]
     wide_live = jnp.concatenate([live] * (width // 128), axis=1)
 
-    @pl.when(pair == 0)
+    @pl.when(step == 0)
     def _():
         unused, size, decay = step_sizes(step_ref[...], extra_ref, live)
         total = running_sum(decay)
@@ -243,68 +246,71 @@
         size_grad[...] = jnp.zeros_like(size_grad)
         total_grad[...] = jnp.zeros_like(total_grad)
 
-    taps = wide_ref[...]
-    u_live = u_ref[...] * live
-    inner = conv_rows(u_live, taps, same_ref)
-    x_in, x_slope = silu_parts(inner)
-    gate, gate_slope = silu_parts(z_ref[...])
-    mixed = y_ref[...]
-    gated = mixed * gate
-    inverse = inverse_ref[:, 0:1]
-    pull = (own_ref[:, 0:1] + other_ref[:, 0:1]) * inverse * inverse * inverse / DSSM
-    grad_gated = taps[6:7] * dn_ref[...] * inverse - gated * pull
-    grad_mixed = grad_gated * gate
-    dz_ref[...] = (grad_gated * mixed * gate_slope).astype(dz_ref.dtype)
-    grad_mixed_b = grad_mixed.astype(jnp.bfloat16)
-    lanes = lax.broadcasted_iota(jnp.int32, (rows, 128), 1)
-    left_lanes = lanes < HP
-    size = sizes[...]
-    size_pair = jnp.where(left_lanes, lane_column(size, 2 * pair), lane_column(size, 2 * pair + 1))
-    inflow = (size_pair * x_in).astype(jnp.bfloat16)
-    zero = jnp.zeros_like(inflow)
-    inflow_heads = [jnp.where(left_lanes, inflow, zero), jnp.where(left_lanes, zero, inflow)]
-    total = running[...]
-    columns = [lane_column(total, 2 * pair + k) for k in range(2)]
-    row_vectors = [running_t[pl.ds(2 * pair + k, 1), :] for k in range(2)]
-    blocks = []
-    for block in range(rows // TILE):
-        top, end = block * TILE, (block + 1) * TILE
-        parts = []
-        gram_part = None
+    for part in range(2):
+        pair = 2 * step + part
+        at = slice(part * 128, (part + 1) * 128)
+        taps = wide_ref[:, at]
+        u_live = u_ref[:, at] * live
+        inner = conv_rows(u_live, taps, same_ref)
+        x_in, x_slope = silu_parts(inner)
+        gate, gate_slope = silu_parts(z_ref[:, at])
+        mixed = y_ref[:, at]
+        gated = mixed * gate
+        inverse = inverse_ref[:, 0:1]
+        pull = (own_ref[:, 0:1] + other_ref[:, 0:1]) * inverse * inverse * inverse / DSSM
+        grad_gated = taps[6:7] * dn_ref[:, at] * inverse - gated * pull
+        grad_mixed = grad_gated * gate
+        dz_ref[:, at] = (grad_gated * mixed * gate_slope).astype(dz_ref.dtype)
+        grad_mixed_b = grad_mixed.astype(jnp.bfloat16)
+        lanes = lax.broadcasted_iota(jnp.int32, (rows, 128), 1)
+        left_lanes = lanes < HP
+        size = sizes[...]
+        size_pair = jnp.where(left_lanes, lane_column(size, 2 * pair), lane_column(size, 2 * pair + 1))
+        inflow = (size_pair * x_in).astype(jnp.bfloat16)
+        zero = jnp.zeros_like(inflow)
+        inflow_heads = [jnp.where(left_lanes, inflow, zero), jnp.where(left_lanes, zero, inflow)]
+        total = running[...]
+        columns = [lane_column(total, 2 * pair + k) for k in range(2)]
+        row_vectors = [running_t[pl.ds(2 * pair + k, 1), :] for k in range(2)]
+        blocks = []
+        for block in range(rows // TILE):
+            top, end = block * TILE, (block + 1) * TILE
+            parts = []
+            gram_part = None
+            for k in range(2):
+                gaps = row_vectors[k][:, top:] - columns[k][top:end]
+                decay = jnp.exp(jnp.minimum(gaps, 0.0))
+                mixing_t = (gram_t[top:end, top:] * decay).astype(jnp.bfloat16)
+                parts.append(dot_nn(mixing_t, grad_mixed_b[top:]))
+                term = dot_nt(inflow_heads[k][top:end], grad_mixed_b[top:]) * decay
+                gram_part = term if gram_part is None else gram_part + term
+            gram_grad[top:end, top:] += gram_part
+            blocks.append(jnp.where(left_lanes[top:end], parts[0], parts[1]))
+        grad_inflow = jnp.concatenate(blocks, axis=0)
+        grad_x = grad_mixed * taps[5:6] + grad_inflow * size_pair
+        by_size = grad_inflow * x_in
+        mixed_only = mixed - taps[5:6] * x_in
+        by_total = grad_mixed_b.astype(jnp.float32) * mixed_only - grad_inflow * inflow.astype(jnp.float32)
+        size_sum, total_sum = size_grad[...], total_grad[...]
         for k in range(2):
-            gaps = row_vectors[k][:, top:] - columns[k][top:end]
-            decay = jnp.exp(jnp.minimum(gaps, 0.0))
-            mixing_t = (gram_t[top:end, top:] * decay).astype(jnp.bfloat16)
-            parts.append(dot_nn(mixing_t, grad_mixed_b[top:]))
-            term = dot_nt(inflow_heads[k][top:end], grad_mixed_b[top:]) * decay
-            gram_part = term if gram_part is None else gram_part + term
-        gram_grad[top:end, top:] += gram_part
-        blocks.append(jnp.where(left_lanes[top:end], parts[0], parts[1]))
-    grad_inflow = jnp.concatenate(blocks, axis=0)
-    grad_x = grad_mixed * taps[5:6] + grad_inflow * size_pair
-    by_size = grad_inflow * x_in
-    mixed_only = mixed - taps[5:6] * x_in
-    by_total = grad_mixed_b.astype(jnp.float32) * mixed_only - grad_inflow * inflow.astype(jnp.float32)
-    size_sum, total_sum = size_grad[...], total_grad[...]
-    for k in range(2):
-        mine = left_lanes if k == 0 else jnp.logical_not(left_lanes)
-        here = lanes == 2 * pair + k
-        size_sum = jnp.where(
-            here, jnp.sum(jnp.where(mine, by_size, 0.0), axis=1, keepdims=True), size_sum
+            mine = left_lanes if k == 0 else jnp.logical_not(left_lanes)
+            here = lanes == 2 * pair + k
+            size_sum = jnp.where(
+                here, jnp.sum(jnp.where(mine, by_size, 0.0), axis=1, keepdims=True), size_sum
+            )
+            total_sum = jnp.where(
+                here, jnp.sum(jnp.where(mine, by_total, 0.0), axis=1, keepdims=True), total_sum
+            )
+        size_grad[...] = size_sum
+        total_grad[...] = total_sum
+        grad_u, tap_grads = conv_rows_back(grad_x * x_slope, u_live, taps, same_ref)
+        du_ref[:, at] = (grad_u * live).astype(du_ref.dtype)
+        skip_grad = jnp.sum(grad_mixed * x_in, axis=0, keepdims=True)
+        wide_grad_ref[:, at] = jnp.concatenate(
+            tap_grads + [skip_grad, jnp.zeros((2, 128), jnp.float32)], axis=0
         )
-        total_sum = jnp.where(
-            here, jnp.sum(jnp.where(mine, by_total, 0.0), axis=1, keepdims=True), total_sum
-        )
-    size_grad[...] = size_sum
-    total_grad[...] = total_sum
-    grad_u, tap_grads = conv_rows_back(grad_x * x_slope, u_live, taps, same_ref)
-    du_ref[...] = (grad_u * live).astype(du_ref.dtype)
-    skip_grad = jnp.sum(grad_mixed * x_in, axis=0, keepdims=True)
-    wide_grad_ref[...] = jnp.concatenate(
-        tap_grads + [skip_grad, jnp.zeros((2, 128), jnp.float32)], axis=0
-    )
-
-    @pl.when(pair == pl.num_programs(0) - 1)
+
+    @pl.when(step == pl.num_programs(0) - 1)
     def _():
         half = width // 2
         gram_grad_b = (gram_grad[...] * mask_t_ref[...]).astype(jnp.bfloat16)
@@ -340,12 +346,12 @@
     width = conv_state.shape[1]
     const2 = lambda i: (0, 0)
     at = lambda name, size: offsets[name] // size
-    block = lambda name: pl.BlockSpec((rows, 128), lambda i, o=at(name, 128): (0, o + i))
-    plain = pl.BlockSpec((rows, 128), lambda i: (0, i))
+    block = lambda name: pl.BlockSpec((rows, 128 * 2), lambda i, o=at(name, 128 * 2): (0, o + i))
+    plain = pl.BlockSpec((rows, 128 * 2), lambda i: (0, i))
     f32, b16 = jnp.float32, jnp.bfloat16
     return pl.pallas_call(
         ssm_backward_kernel,
-        grid=(pairs,),
+        grid=(pairs // 2,),
         in_specs=[
             plain,
             plain,
@@ -357,7 +363,7 @@
             pl.BlockSpec((rows, 128), const2),
             pl.BlockSpec((rows, 128), const2),
             pl.BlockSpec((rows, 128), const2),
-            pl.BlockSpec((8, 128), lambda i: (0, i)),
+            pl.BlockSpec((8, 128 * 2), lambda i: (0, i)),
             pl.BlockSpec((8, width), const2),
             pl.BlockSpec((8, 128), const2),
             pl.BlockSpec((rows, 128), const2),
@@ -369,7 +375,7 @@
             plain,
             pl.BlockSpec((rows, width), const2),
             pl.BlockSpec((rows, 128), const2),
-            pl.BlockSpec((8, 128), lambda i: (0, i)),
+            pl.BlockSpec((8, 128 * 2), lambda i: (0, i)),
             pl.BlockSpec((8, width), const2),
             pl.BlockSpec((8, 128), const2),
         ],
@@ -394,7 +400,7 @@
             pltpu.VMEM((rows, width), b16),
             pltpu.VMEM((rows, width), f32),
         ],
-        compiler_params=pltpu.CompilerParams(vmem_limit_bytes=48 * 2**20),
+        compiler_params=pltpu.CompilerParams(vmem_limit_bytes=32 * 2**20),
         cost_estimate=cost(1, 1),
         name="ssm_backward",
     )(
@@ -528,51 +534,21 @@
     )(grad, query, key, value, logs, cos, sin, mask)
 
 
-def feed_forward_kernel(in_ref, gate_w_ref, up_w_ref, act_ref, gate_ref, up_ref):
+def feed_forward_kernel(
+    in_ref, grad_ref, gate_w_ref, up_w_ref, down_ref, act_ref, dgate_ref, dup_ref, din_ref, total
+):
+    step = pl.program_id(0)
+
+    @pl.when(step == 0)
+    def _():
+        total[...] = jnp.zeros_like(total)
+
     gate = dot_nn(in_ref[...], gate_w_ref[...])
     up = dot_nn(in_ref[...], up_w_ref[...])
-    gate_ref[...] = gate
-    up_ref[...] = up
-    act_ref[...] = (gate * jax.nn.sigmoid(gate) * up).astype(act_ref.dtype)
-
-
-def feed_forward(ffn_in, weights, first, hidden, tile=256):
-    rows, model = ffn_in.shape
-    steps = hidden // tile
-    each = pl.BlockSpec((rows, tile), lambda i: (0, i))
-    return pl.pallas_call(
-        feed_forward_kernel,
-        grid=(steps,),
-        in_specs=[
-            pl.BlockSpec((rows, model), lambda i: (0, 0)),
-            pl.BlockSpec((model, tile), lambda i: (0, first // tile + i)),
-            pl.BlockSpec((model, tile), lambda i: (0, first // tile + steps + i)),
-        ],
-        out_specs=[each, each, each],
-        out_shape=[
-            jax.ShapeDtypeStruct((rows, hidden), jnp.bfloat16),
-            jax.ShapeDtypeStruct((rows, hidden), jnp.float32),
-            jax.ShapeDtypeStruct((rows, hidden), jnp.float32),
-        ],
-        compiler_params=pltpu.CompilerParams(vmem_limit_bytes=32 * 2**20),
-        cost_estimate=cost(4 * rows * model * hidden, 4 * model * hidden + 12 * rows * hidden),
-        name="feed_forward",
-    )(ffn_in, weights, weights)
-
-
-def feed_forward_back_kernel(
-    grad_ref, down_ref, gate_ref, up_ref, gate_w_ref, up_w_ref, dgate_ref, dup_ref, din_ref, total
-):
-    step = pl.program_id(0)
-
-    @pl.when(step == 0)
-    def _():
-        total[...] = jnp.zeros_like(total)
-
     grad_act = dot_nn(grad_ref[...], down_ref[...])
-    gate = gate_ref[...]
     value, slope = silu_parts(gate)
-    dgate = (grad_act * up_ref[...] * slope).astype(jnp.bfloat16)
+    act_ref[...] = (value * up).astype(act_ref.dtype)
+    dgate = (grad_act * up * slope).astype(jnp.bfloat16)
     dup = (grad_act * value).astype(jnp.bfloat16)
     dgate_ref[...] = dgate
     dup_ref[...] = dup
@@ -583,39 +559,38 @@
         din_ref[...] = total[...].astype(din_ref.dtype)
 
 
-def feed_forward_back(grad, down_t, gate, up, weights, first, tile=512):
+def feed_forward(ffn_in, grad, weights, hidden, tile=512):
     rows, model = grad.shape
-    hidden = gate.shape[1]
     steps = hidden // tile
     each = pl.BlockSpec((rows, tile), lambda i: (0, i))
     whole = pl.BlockSpec((rows, model), lambda i: (0, 0))
     b16 = jnp.bfloat16
     return pl.pallas_call(
-        feed_forward_back_kernel,
+        feed_forward_kernel,
         grid=(steps,),
         in_specs=[
             whole,
-            pl.BlockSpec((model, tile), lambda i: (0, first // tile + 2 * steps + i)),
-            each,
-            each,
-            pl.BlockSpec((model, tile), lambda i: (0, first // tile + i)),
-            pl.BlockSpec((model, tile), lambda i: (0, first // tile + steps + i)),
-        ],
-        out_specs=[each, each, whole],
+            whole,
+            pl.BlockSpec((model, tile), lambda i: (0, i)),
+            pl.BlockSpec((model, tile), lambda i: (0, steps + i)),
+            pl.BlockSpec((model, tile), lambda i: (0, 2 * steps + i)),
+        ],
+        out_specs=[each, each, each, whole],
         out_shape=[
             jax.ShapeDtypeStruct((rows, hidden), b16),
             jax.ShapeDtypeStruct((rows, hidden), b16),
+            jax.ShapeDtypeStruct((rows, hidden), b16),
             jax.ShapeDtypeStruct((rows, model), b16),
         ],
         scratch_shapes=[pltpu.VMEM((rows, model), jnp.float32)],
-        compiler_params=pltpu.CompilerParams(vmem_limit_bytes=40 * 2**20),
+        compiler_params=pltpu.CompilerParams(vmem_limit_bytes=44 * 2**20),
         cost_estimate=cost(1, 1),
-        name="feed_forward_back",
-    )(grad, down_t, gate, up, weights, weights)
+        name="feed_forward",
+    )(ffn_in, grad, weights, weights, weights)
 
 
 def norm_back_kernel(
-    grad_ref, weight_ref, gated_ref, inverse_ref, gain_ref, dn_ref, row_ref, column_ref
+    grad_ref, weight_ref, gated_ref, inverse_ref, gain_ref, dout_ref, dn_ref, row_ref, column_ref, *, split
 ):
     step = pl.program_id(0)
 
@@ -624,15 +599,22 @@
         row_ref[...] = jnp.zeros_like(row_ref)
 
     grad = dot_nn(grad_ref[...], weight_ref[...])
-    dn_ref[...] = grad
-    product = grad * gated_ref[...]
-    scaled = product * gain_ref[0:1]
-    part = scaled[:, :128]
-    for k in range(1, scaled.shape[1] // 128):
-        part = part + scaled[:, k * 128 : (k + 1) * 128]
-    row_ref[...] += part
-    total = jnp.sum(product * inverse_ref[:, 0:1], axis=0, keepdims=True)
-    column_ref[...] = jnp.broadcast_to(total, column_ref.shape)
+
+    @pl.when(step < split)
+    def _():
+        dout_ref[...] = grad.astype(dout_ref.dtype)
+
+    @pl.when(step >= split)
+    def _():
+        dn_ref[...] = grad
+        product = grad * gated_ref[...]
+        scaled = product * gain_ref[0:1]
+        part = scaled[:, :128]
+        for k in range(1, scaled.shape[1] // 128):
+            part = part + scaled[:, k * 128 : (k + 1) * 128]
+        row_ref[...] += part
+        total = jnp.sum(product * inverse_ref[:, 0:1], axis=0, keepdims=True)
+        column_ref[...] = jnp.broadcast_to(total, column_ref.shape)
 
     @pl.when(step == pl.num_programs(0) - 1)
     def _():
@@ -641,32 +623,35 @@
         )
 
 
-def norm_back(grad, weights, first, gated, inverse, gains, tile=256):
+def norm_back(grad, weights, first, attended, gated, inverse, gains, tile=512):
     rows, model = grad.shape
     width = gated.shape[1]
-    each = pl.BlockSpec((rows, tile), lambda i: (0, i))
+    split = attended // tile
+    later = lambda i: (0, jnp.maximum(i - split, 0))
     f32 = jnp.float32
     return pl.pallas_call(
-        norm_back_kernel,
-        grid=(width // tile,),
+        functools.partial(norm_back_kernel, split=split),
+        grid=((attended + width) // tile,),
         in_specs=[
             pl.BlockSpec((rows, model), lambda i: (0, 0)),
             pl.BlockSpec((model, tile), lambda i: (0, first // tile + i)),
-            each,
+            pl.BlockSpec((rows, tile), later),
             pl.BlockSpec((rows, 128), lambda i: (0, 0)),
-            pl.BlockSpec((8, tile), lambda i: (0, i)),
+            pl.BlockSpec((8, tile), later),
         ],
         out_specs=[
-            each,
+            pl.BlockSpec((rows, tile), lambda i: (0, jnp.minimum(i, split - 1))),
+            pl.BlockSpec((rows, tile), later),
             pl.BlockSpec((rows, 128), lambda i: (0, 0)),
-            pl.BlockSpec((8, tile), lambda i: (0, i)),
+            pl.BlockSpec((8, tile), later),
         ],
         out_shape=[
+            jax.ShapeDtypeStruct((rows, attended), jnp.bfloat16),
             jax.ShapeDtypeStruct((rows, width), f32),
             jax.ShapeDtypeStruct((rows, 128), f32),
             jax.ShapeDtypeStruct((8, width), f32),
         ],
-        compiler_params=pltpu.CompilerParams(vmem_limit_bytes=24 * 2**20),
+        compiler_params=pltpu.CompilerParams(vmem_limit_bytes=40 * 2**20),
         cost_estimate=cost(1, 1),
         name="norm_back",
     )(grad, weights, gated, inverse, gains)
@@ -693,7 +678,7 @@
         ],
         out_specs=pl.BlockSpec(memory_space=pltpu.VMEM),
         out_shape=jax.ShapeDtypeStruct(values.shape, values.dtype),
-        compiler_params=pltpu.CompilerParams(vmem_limit_bytes=16 * 2**20),
+        compiler_params=pltpu.CompilerParams(vmem_limit_bytes=8 * 2**20),
         cost_estimate=cost(1, 1),
         name="reorder_columns",
     )(order, values)
@@ -733,31 +718,10 @@
         out_specs=pl.BlockSpec((size, tile), lambda i: (0, i)),
         out_shape=jax.ShapeDtypeStruct((size, width), dtype),
         scratch_shapes=[pltpu.VMEM((size, rows), jnp.bfloat16)],
-        compiler_params=pltpu.CompilerParams(vmem_limit_bytes=32 * 2**20),
+        compiler_params=pltpu.CompilerParams(vmem_limit_bytes=16 * 2**20),
         cost_estimate=cost(1, 1),
         name="scatter_part",
     )(left, right, *[got for got, unused in gots])
-
-
-def product_kernel(left_ref, right_ref, out_ref):
-    out_ref[...] = dot_nn(left_ref[...], right_ref[...]).astype(out_ref.dtype)
-
-
-def product(left, right, first, width, tile=256):
-    rows, model = left.shape
-    return pl.pallas_call(
-        product_kernel,
-        grid=(width // tile,),
-        in_specs=[
-            pl.BlockSpec((rows, model), lambda i: (0, 0)),
-            pl.BlockSpec((model, tile), lambda i: (0, first // tile + i)),
-        ],
-        out_specs=pl.BlockSpec((rows, tile), lambda i: (0, i)),
-        out_shape=jax.ShapeDtypeStruct((rows, width), jnp.bfloat16),
-        compiler_params=pltpu.CompilerParams(vmem_limit_bytes=24 * 2**20),
-        cost_estimate=cost(1, 1),
-        name="product",
-    )(left, right)
 
 
 def product_back_kernel(left_ref, right_ref, out_ref):
@@ -776,7 +740,7 @@
         ],
         out_specs=pl.BlockSpec((rows, tile), lambda i: (0, i)),
         out_shape=jax.ShapeDtypeStruct((rows, model), jnp.bfloat16),
-        compiler_params=pltpu.CompilerParams(vmem_limit_bytes=40 * 2**20),
+        compiler_params=pltpu.CompilerParams(vmem_limit_bytes=44 * 2**20),
         cost_estimate=cost(1, 1),
         name="product_back",
     )(left, right)
@@ -800,7 +764,7 @@
         ],
         out_specs=pl.BlockSpec((size, tile), lambda i: (0, i)),
         out_shape=jax.ShapeDtypeStruct((size, width), dtype),
-        compiler_params=pltpu.CompilerParams(vmem_limit_bytes=24 * 2**20),
+        compiler_params=pltpu.CompilerParams(vmem_limit_bytes=16 * 2**20),
         cost_estimate=cost(1, 1),
         name="join_parts",
     )(ready, got)
@@ -845,7 +809,7 @@
         in_specs=[each, whole, each, each, each, pl.BlockSpec((tile, 128), lambda i: (i, 0))],
         out_specs=[each, whole, each][: len(shapes)],
         out_shape=shapes,
-        compiler_params=pltpu.CompilerParams(vmem_limit_bytes=32 * 2**20),
+        compiler_params=pltpu.CompilerParams(vmem_limit_bytes=24 * 2**20),
         cost_estimate=cost(1, 1),
         name="rms_back",
     )(values, gain, own, other, base, live)
@@ -874,21 +838,25 @@
         in_specs=[pl.BlockSpec((tile, a.shape[1]), lambda i: (i, 0)) for a in arrays],
         out_specs=pl.BlockSpec((tile, width), lambda i: (i, 0)),
         out_shape=jax.ShapeDtypeStruct((rows, width), jnp.bfloat16),
-        compiler_params=pltpu.CompilerParams(vmem_limit_bytes=24 * 2**20),
+        compiler_params=pltpu.CompilerParams(vmem_limit_bytes=12 * 2**20),
         cost_estimate=cost(1, 1),
         name="beside",
     )(*arrays)
 
 
-def hidden_back_kernel(first_ref, second_ref, keep_ref, weight_ref, out_ref, total):
+def hidden_back_kernel(first_ref, second_ref, third_ref, keep_ref, weight_ref, out_ref, total):
     step = pl.program_id(0)
-    half = pl.num_programs(0) // 2
+    third = pl.num_programs(0) // 3
 
     @pl.when(step == 0)
     def _():
         total[...] = jnp.zeros_like(total)
 
-    left = jnp.where(step < half, first_ref[...], second_ref[...] * keep_ref[0:1])
+    left = jnp.where(
+        step < third,
+        first_ref[...],
+        jnp.where(step < 2 * third, second_ref[...], third_ref[...] * keep_ref[0:1]),
+    )
     total[...] += dot_nt(left, weight_ref[...])
 
     @pl.when(step == pl.num_programs(0) - 1)
@@ -896,26 +864,30 @@
         out_ref[...] = total[...].astype(out_ref.dtype)
 
 
-def hidden_back(first, second, keep, weights, tile=768):
+def hidden_back(first, second, third, keep, weights, tile=768):
     rows, width = first.shape
     model = weights.shape[0]
     steps = width // tile
+    block = lambda part: pl.BlockSpec(
+        (rows, tile), lambda i: (0, jnp.clip(i - part * steps, 0, steps - 1))
+    )
     return pl.pallas_call(
         hidden_back_kernel,
-        grid=(2 * steps,),
+        grid=(3 * steps,),
         in_specs=[
-            pl.BlockSpec((rows, tile), lambda i: (0, jnp.minimum(i, steps - 1))),
-            pl.BlockSpec((rows, tile), lambda i: (0, jnp.maximum(i - steps, 0))),
-            pl.BlockSpec((8, tile), lambda i: (0, jnp.maximum(i - steps, 0))),
+            block(0),
+            block(1),
+            block(2),
+            pl.BlockSpec((8, tile), lambda i: (0, jnp.maximum(i - 2 * steps, 0))),
             pl.BlockSpec((model, tile), lambda i: (0, i)),
         ],
         out_specs=pl.BlockSpec((rows, model), lambda i: (0, 0)),
         out_shape=jax.ShapeDtypeStruct((rows, model), jnp.bfloat16),
         scratch_shapes=[pltpu.VMEM((rows, model), jnp.float32)],
-        compiler_params=pltpu.CompilerParams(vmem_limit_bytes=32 * 2**20),
+        compiler_params=pltpu.CompilerParams(vmem_limit_bytes=40 * 2**20),
         cost_estimate=cost(1, 1),
         name="hidden_back",
-    )(first, second, keep, weights)
+    )(first, second, third, keep, weights)
 
 
 def rms_forward_kernel(base_ref, own_ref, other_ref, live_ref, gain_ref, middle_ref, out_ref):
@@ -944,7 +916,7 @@
             jax.ShapeDtypeStruct((rows, model), jnp.float32),
             jax.ShapeDtypeStruct((rows, model), jnp.bfloat16),
         ],
-        compiler_params=pltpu.CompilerParams(vmem_limit_bytes=32 * 2**20),
+        compiler_params=pltpu.CompilerParams(vmem_limit_bytes=20 * 2**20),
         cost_estimate=cost(1, 1),
         name="rms_forward",
     )(base, own, other, live, gain)
@@ -964,7 +936,7 @@
         in_specs=[each, each, each, pl.BlockSpec((tile, 128), lambda i: (i, 0))],
         out_specs=each,
         out_shape=jax.ShapeDtypeStruct((rows, model), jnp.bfloat16),
-        compiler_params=pltpu.CompilerParams(vmem_limit_bytes=24 * 2**20),
+        compiler_params=pltpu.CompilerParams(vmem_limit_bytes=16 * 2**20),
         cost_estimate=cost(1, 1),
         name="output_rows",
     )(base, own, other, live)
@@ -1068,6 +1040,23 @@
         )
         return self.ready
 
+    def make(self, *earlier):
+        step = len(self.got)
+        first, size = self.place(step)
+        gots = [(got, self.meets(past, step)) for past, got in enumerate(self.got)]
+        done = step == len(self.bits)
+        self.held = scatter_part(
+            after(self.left, *earlier),
+            self.right,
+            gots,
+            first * self.rows,
+            size * self.rows,
+            jnp.float32 if done else jnp.bfloat16,
+        )
+        if done:
+            self.total = self.held
+        return self.held
+
     def join(self, *earlier):
         step = len(self.got)
         done = step == len(self.bits)
@@ -1084,8 +1073,7 @@
     def finish(self):
         while self.total is None:
             self.send()
-            self.prepare()
-            self.join()
+            self.make()
         return self.total
 
 
@@ -1136,9 +1124,9 @@
     step_pad = jnp.zeros((shard_rows, 128 - heads_m), bf16)
     group_mix = jnp.concatenate(
         [
+            inner_proj.reshape(shard_rows, -1),
             query_proj,
             key_value_matrix.reshape(shard_rows, -1),
-            inner_proj.reshape(shard_rows, -1),
             joined[:, :state_cols],
             step_proj,
             step_pad,
@@ -1150,10 +1138,10 @@
     )
     offsets, place = {}, 0
     for name, width in (
+        ("z", x_cols),
+        ("u", x_cols),
         ("q", q_cols),
         ("kv", kv_cols),
-        ("z", x_cols),
-        ("u", x_cols),
         ("state", state_cols),
         ("step", 128),
         ("end", 0),
@@ -1244,67 +1232,64 @@
     branch_own = rounded(contract("tc,dc->td", branch_in, out_t))
     branch_other = pair_swap(branch_own)
     middle, ffn_in_b = rms_forward(tokens, branch_own, branch_other, live, gain_dense_rows)
-    activated_b, gate, up = feed_forward(ffn_in_b, ffn_full, 0, hidden_cols)
     inverse_b = jnp.broadcast_to(inverse[:, None], live.shape)
     gated_rows = jnp.broadcast_to(gain_gated[None], (8, x_cols))
     first = (lax.axis_index("tensor") == 0).astype(bf16)
-    early_cols = q_cols + kv_cols + x_cols
-    column_at = jnp.arange(early_cols) - x_cols
+    column_at = jnp.arange(x_cols) - (q_cols + kv_cols)
     keep = jnp.where((column_at >= 0) & (column_at < state_cols), first, jnp.ones((), bf16))
-    keep = jnp.broadcast_to(keep[None], (8, early_cols))
+    keep = jnp.broadcast_to(keep[None], (8, x_cols))
+    ffn_split = reorder_columns(ffn_in_b, order)
+
+    activated_b, grad_gate_b, grad_up_b, grad_ffn_part = feed_forward(
+        ffn_in_b, after(dense_grad_b, ffn_split, dense_split), ffn_full, hidden_cols
+    )
     down = Scatter(dense_split, activated_b, bits)
+    gate_sum = Scatter(ffn_split, grad_gate_b, bits)
+    up_sum = Scatter(ffn_split, grad_up_b, bits)
     held = down.begin()
-
     down.send()
-    grad_gate_b, grad_up_b, grad_ffn_part = feed_forward_back(
-        after(dense_grad_b, held), ffn_full, gate, up, ffn_full, 0
-    )
-    ready = down.prepare(grad_ffn_part)
+    held = gate_sum.begin(held)
+    ready = down.prepare(held)
 
     held = down.join(ready)
     down.send()
-    grad_ffn_other = pair_swap(after(grad_ffn_part, held))
-    gate_sum = Scatter(reorder_columns(ffn_in_b, order), grad_gate_b, bits)
-    up_sum = Scatter(gate_sum.left, grad_up_b, bits)
-    held = gate_sum.begin(held)
-    gate_sum.send()
+    grad_ffn_other = pair_swap(after(grad_ffn_part, ready))
+    gate_sum.send(ready)
     held = up_sum.begin(held)
-    up_sum.send()
     ready = down.prepare(held)
     dense_own = product_back(after(activated_b, ready), ffn_full, 2 * hidden_cols)
     ready = gate_sum.prepare(dense_own)
 
-    held = gate_sum.join(ready, down.got[-1], up_sum.got[-1], grad_ffn_other)
+    round_end = (ready, down.got[-1], gate_sum.got[-1], grad_ffn_other)
+    held = gate_sum.join(*round_end)
     gate_sum.send()
-    held = down.join(held)
+    up_sum.send(*round_end)
+    held = down.make(held)
     down.send()
-    dense_other = pair_swap(after(dense_own, held))
     grad_middle, grad_dense_gain, mixer_grad_b = rms_back(
         middle, gain_dense_rows, after(grad_ffn_part, held), grad_ffn_other, cotangent, live, True
     )
-    grad_normed, own_rows, column_part = norm_back(
-        mixer_grad_b, mix_full, out_first + o_cols, gated, inverse_b, gated_rows
+    grad_attended_b, grad_normed, own_rows, column_part = norm_back(
+        mixer_grad_b, mix_full, out_first, o_cols, gated, inverse_b, gated_rows
     )
     other_rows = pair_swap(own_rows)
     branch = Scatter(reorder_columns(mixer_grad_b, order), branch_in, bits)
     held = branch.begin(own_rows)
     ready = up_sum.prepare(held)
-    held = up_sum.join(ready)
-    ready = gate_sum.prepare(held)
-    grad_attended_b = product(after(mixer_grad_b, ready), mix_full, out_first, o_cols)
-    ready = down.prepare(grad_attended_b)
     grad_query_b, grad_key_b, grad_value_b = attention_backward(
         after(grad_attended_b, ready), query_b, key_b, value_b, logs, cos, sin, mask_qk
     )
     ready = grad_query_b
 
-    round_end = (ready, gate_sum.got[-1], down.got[-1], other_rows, dense_other)
-    up_sum.send(*round_end)
+    round_end = (ready, gate_sum.got[-1], up_sum.got[-1], down.got[-1], other_rows)
+    held = up_sum.join(*round_end)
+    up_sum.send()
     branch.send(*round_end)
-    held = gate_sum.join(*round_end)
+    held = gate_sum.make(held)
     gate_sum.send()
-    held = down.join(held)
+    held = down.make(held)
     down.send()
+    dense_other = pair_swap(after(dense_own, *round_end))
     grad_z_b, grad_u_b, grad_state_part, grad_step_b, wide_grad, conv_grad, extra_grad = (
         ssm_backward(
             after(grad_normed, held),
@@ -1322,69 +1307,69 @@
             offsets,
         )
     )
-    ready = up_sum.prepare(grad_state_part)
-    ready = gate_sum.prepare(ready)
-    grad_z_b = after(grad_z_b, ready)
-    early_b = beside(early_cols, grad_query_b, grad_key_b, grad_value_b, grad_z_b)
-    early = Scatter(hidden_split, early_b, bits)
-    held = early.begin()
+    z_sum = Scatter(hidden_split, grad_z_b, bits)
+    u_sum = Scatter(hidden_split, grad_u_b, bits)
+    held = z_sum.begin(grad_state_part)
     ready = branch.prepare(held)
-    ready = down.prepare(ready)
-
-    round_end = (ready, up_sum.got[-1], gate_sum.got[-1], down.got[-1], branch.got[-1])
+
+    round_end = (ready, up_sum.got[-1], gate_sum.got[-1], branch.got[-1], down.got[-1], dense_other)
     held = branch.join(*round_end)
     branch.send()
-    early.send(*round_end)
+    z_sum.send(*round_end)
     grad_state_other = pair_swap(after(grad_state_part, *round_end))
-    held = up_sum.join(held)
+    held = up_sum.make(held)
     up_sum.send()
-    held = gate_sum.join(held)
+    held = gate_sum.make(held)
     gate_sum.send()
-    held = down.join(held)
-    late_b = beside(
-        early_cols, grad_u_b, (grad_state_part, after(grad_state_other, held)), grad_step_b
-    )
-    late = Scatter(hidden_split, late_b, bits)
-    held = late.begin()
-    ready = early.prepare(held)
-    ready = branch.prepare(ready)
-    ready = up_sum.prepare(ready)
-    ready = gate_sum.prepare(ready)
-
-    round_end = (ready, branch.got[-1], up_sum.got[-1], gate_sum.got[-1], early.got[-1])
-    held = early.join(*round_end)
-    early.send()
-    late.send(*round_end)
-    held = branch.join(held)
+    held = down.make(held)
+    held = u_sum.begin(held)
+    other_b = beside(
+        x_cols,
+        grad_query_b,
+        grad_key_b,
+        grad_value_b,
+        (grad_state_part, after(grad_state_other, held)),
+        grad_step_b,
+    )
+    other_sum = Scatter(hidden_split, other_b, bits)
+    grad_hidden_own = hidden_back(after(grad_z_b, other_b), grad_u_b, other_b, keep, mix_full)
+    held = other_sum.begin(grad_hidden_own)
+    ready = z_sum.prepare(held)
+
+    round_end = (ready, branch.got[-1], up_sum.got[-1], gate_sum.got[-1], z_sum.got[-1])
+    held = z_sum.join(*round_end)
+    z_sum.send()
+    u_sum.send(*round_end)
+    half_rows = row_count // 2
+    hidden_top = pair_swap(after(grad_hidden_own[:half_rows], *round_end))
+    held = branch.make(held)
     branch.send()
-    held = up_sum.join(held)
+    held = up_sum.make(held)
     up_sum.send()
-    held = gate_sum.join(held)
-    grad_hidden_own = hidden_back(after(early_b, held), late_b, keep, mix_full)
-    ready = late.prepare(grad_hidden_own)
-    ready = early.prepare(ready)
-    ready = branch.prepare(ready)
-    ready = up_sum.prepare(ready)
-
-    round_end = (ready, early.got[-1], branch.got[-1], up_sum.got[-1], late.got[-1])
-    held = late.join(*round_end)
-    late.send()
-    grad_hidden_other = pair_swap(after(grad_hidden_own, *round_end))
-    held = early.join(held)
-    early.send()
-    held = branch.join(held)
+    held = gate_sum.make(held)
+    ready = u_sum.prepare(held)
+
+    round_end = (ready, z_sum.got[-1], u_sum.got[-1], branch.got[-1], up_sum.got[-1], hidden_top)
+    held = u_sum.join(*round_end)
+    u_sum.send()
+    other_sum.send(*round_end)
+    hidden_end = pair_swap(after(grad_hidden_own[half_rows:], *round_end))
+    held = z_sum.make(held)
+    z_sum.send()
+    held = branch.make(held)
     branch.send()
-    held = up_sum.join(held)
+    held = up_sum.make(held)
     output = output_rows(middle, after(dense_own, held), dense_other, live)
-    ready = late.prepare(output)
-    ready = early.prepare(ready)
-    ready = branch.prepare(ready)
-
-    round_end = (ready, late.got[-1], early.got[-1], branch.got[-1], grad_hidden_other)
-    held = late.join(*round_end)
-    late.send()
-    held = early.join(held)
-    early.send()
+    ready = other_sum.prepare(output)
+
+    round_end = (ready, u_sum.got[-1], other_sum.got[-1], z_sum.got[-1], branch.got[-1], hidden_end)
+    held = other_sum.join(*round_end)
+    other_sum.send()
+    held = u_sum.make(held)
+    u_sum.send()
+    held = z_sum.make(held)
+    z_sum.send()
+    grad_hidden_other = jnp.concatenate([hidden_top, hidden_end], axis=0)
     grad_tokens, grad_mixer_gain = rms_back(
         tokens, gain_mix_rows, after(grad_hidden_own, held), grad_hidden_other, grad_middle, live, False
     )
@@ -1398,19 +1383,31 @@
         (extra_grad, 2),
     )
     sums = own_sums + across(own_sums, bits[0])
-    held = branch.join(sums)
-    ready = late.prepare(held)
-    ready = early.prepare(ready)
+    held = branch.make(sums)
+    ready = other_sum.prepare(held)
+    ready = u_sum.prepare(ready)
+    ready = z_sum.prepare(ready)
     others = across(after(sums, ready), bits[1])
 
-    held = late.join(ready, early.got[-1], others)
-    late.send()
+    round_end = (ready, other_sum.got[-1], u_sum.got[-1], z_sum.got[-1], others)
+    held = other_sum.join(*round_end)
+    other_sum.send()
+    held = u_sum.join(held)
+    u_sum.send()
     sums = after(sums, held) + others
-    for bit in bits[2:]:
+    others = across(sums, bits[2])
+    held = z_sum.join(sums)
+    ready = other_sum.prepare(held)
+    ready = u_sum.prepare(ready)
+
+    held = other_sum.join(ready, other_sum.got[-1], u_sum.got[-1], others)
+    other_sum.send()
+    sums = after(sums, held) + others
+    for bit in bits[3:]:
         sums = sums + across(sums, bit)
-    held = early.join(sums)
-    late.prepare(held)
-    late.join()
+    held = u_sum.join(held)
+    other_sum.prepare(held)
+    other_sum.join(sums)
     at = 2 + tap_count + 2
     conv_sum = sums[at : at + tap_count, :state_cols]
     conv_sum = conv_sum + pair_swap(conv_sum)
@@ -1422,10 +1419,11 @@
         width = values.shape[axis_dim] // (2 * dp_count)
         return lax.dynamic_slice_in_dim(values, owner * width, width, axis_dim)
 
-    red_early, red_late, red_branch = early.finish(), late.finish(), branch.finish()
+    red_branch, red_other = branch.finish(), other_sum.finish()
     state_rows = shard_rows // 2
+    state_first = q_cols + kv_cols
     red_state = lax.dynamic_slice_in_dim(
-        red_late[:, x_cols : x_cols + state_cols],
+        red_other[:, state_first : state_first + state_cols],
         lax.axis_index("tensor") * state_rows,
         state_rows,
         0,
@@ -1434,12 +1432,12 @@
         output,
         grad_tokens,
         own_part(sums[0], 0),
-        red_early[:, :q_cols],
-        red_early[:, q_cols : q_cols + kv_cols].reshape(shard_rows, 2, -1),
+        red_other[:, :q_cols],
+        red_other[:, q_cols:state_first].reshape(shard_rows, 2, -1),
         red_branch[:, :o_cols].T,
-        jnp.stack([red_early[:, q_cols + kv_cols :], red_late[:, :x_cols]], axis=1),
+        jnp.stack([z_sum.finish(), u_sum.finish()], axis=1),
         red_state,
-        red_late[:, x_cols + state_cols : x_cols + state_cols + heads_m],
+        red_other[:, state_first + state_cols : state_first + state_cols + heads_m],
         sums[2 : 2 + tap_count, :x_cols],
         own_part(conv_sum, 1),
         sums[at, :heads_m],

time: 806 us -> 739 us (0.917)
  local copies, waits for them, and re-layouts: 111 us -> 71.7 us
  Pallas kernels: 301 us -> 271 us
    unnamed x354 -> x294, local copies, waits for them, and re-layouts: 96.6 us -> 56.7 us
    pallas_call x24 -> x13, Pallas kernels: 48.2 us -> 23.7 us  [join_parts(): pl.pallas_call(join_kernel, grid=(width // tile,), in_specs=[pl.BlockSpec...]
    ppermute x28 -> x32, waiting for transfers between devices: 88.2 us -> 77 us  [across(): return lax.ppermute(values, 'dp', [(i, i ^ bit) for i in range(count)])]
    ppermute x9 -> x10, waiting for transfers between devices: 59.6 us -> 68.3 us  [pair_swap(): return lax.ppermute(values, 'tensor', [(0, 1), (1, 0)])]
    pallas_call x7 -> x5, Pallas kernels: 100 us -> 92.3 us  [the longest x1 30.1 us: feed_forward(): pl.pallas_call(feed_forward_kernel, grid=(steps,), in_specs=[whole, whole...]
    ppermute x28 -> x32, starting transfers between devices: 25.2 us -> 28.6 us  [across(): return lax.ppermute(values, 'dp', [(i, i ^ bit) for i in range(count)])]
    pallas_call x30 -> x35, Pallas kernels: 109 us -> 112 us  [scatter_part(): pl.pallas_call(scatter_part_kernel, grid=(width // tile,), in_specs=[pl.B...]
  transfers between devices with their start and end apart: 39 -> 44, of which waited for: 17 -> 17; matrix products, arithmetic and copies ran while one was open for 8% -> 9% of each run, Pallas kernels for 32% -> 31%
where the time goes in v2:
time: 739 us; the launch traced here: 734 us
  waiting for transfers between devices  287 us (39%)
  Pallas kernels  271 us (37%)
  local copies, waits for them, and re-layouts  71.7 us (10%)
  starting transfers between devices  44 us (6%)
  matrix products  23.7 us (3%)
  other arithmetic  20.3 us (3%)
  between operations  16.9 us (2%)
    all_gather x1, waiting for transfers between devices, local(): mix_full = lax.all_gather(group_mix, 'dp', axis=0, tiled=True)  136 us
    pallas_call x35, Pallas kernels, scatter_part(): pl.pallas_call(scatter_part_kernel, grid=(width // tile,), in_specs=[pl.B...  112 us
    ppermute x32, waiting for transfers between devices, across(): return lax.ppermute(values, 'dp', [(i, i ^ bit) for i in range(count)])  77 us
    ppermute x10, waiting for transfers between devices, pair_swap(): return lax.ppermute(values, 'tensor', [(0, 1), (1, 0)])  68.3 us
    unnamed x294, local copies, waits for them, and re-layouts  56.7 us
    pallas_call x1, Pallas kernels, feed_forward(): pl.pallas_call(feed_forward_kernel, grid=(steps,), in_specs=[whole, whole...  30.1 us
    ppermute x32, starting transfers between devices, across(): return lax.ppermute(values, 'dp', [(i, i ^ bit) for i in range(count)])  28.6 us
    pallas_call x1, Pallas kernels, ssm_backward(): pl.pallas_call(ssm_backward_kernel, grid=(pairs // 2,), in_specs=[plain,...  27.2 us
  transfers between devices with their start and end apart: 44, of which 17 were waited for; matrix products, arithmetic and copies ran while one was open for 9% of the time, Pallas kernels for 31%

profile of v2, /device:TPU:0, one launch (start us, length us, event | category | flops | bytes accessed | tf_op | source)
XLA Modules:
  0.0 734.4 jit_solution(14750166716695633387)
XLA Ops:
  11.2 2.9 collective-permute-start
  24.3 136.1 %all-gather.3.cloned.1.call-done.weight_ref = bf16[2048,6656]{1,0:T(8,128)(2,1)} async-done(((bf16[128,6656]{1,0:T(8,128)(2,1)}), bf16[2048,6656]{1,0:T(8,128)(2,1)}) %all-gather.3.cloned.1.call-update) | async-done | bytes 27262992 | tf_op jit(solution)/shard_map/all_gather | solution.py:1153
  169.7 2.5 convert_reduce_fusion
  172.8 13.9 %fusion.q_ref.k_ref.v_ref.u_ref.z_ref.state_b_ref.state_c_ref.step_ref = f32[512,4480]{1,0:T(8,128)S(1)} fusion(bf16[512,2048]{1,0:T(8,128)(2,1)S(1)} %fusion.6.in_ref, bf16[2048,6656]{1,0:T(8,128)(2,1)} %all-gather.3.cloned.1.call-done.weight_ref), kind=kOutput, calls=%fused_computation | convolution fusion | flops 9395240960 | bytes 29622272 | tf_op jit(solution)/shard_map/td,dc->tc/dot_general | solution.py:25
  190.7 11.2 %ssm_forward.1 = (f32[512,1536]{1,0:T(8,128)S(1)}, f32[512,1536]{1,0:T(8,128)S(1)}, f32[512,128]{1,0:T(8,128)S(1)}) custom-call(f32[512,4480]{1,0:T(8,128)S(1)} %fusion.q_ref.k_ref.v_ref.u_ref.z_ref.state_b_ref.state_c_ref.step_ref, f32[512,4480]{1,0:T(8,128)S(1)} %fusion.q_ref.k_ref.v_ref.u_ref.z_ref.state_b_ref.state_c_ref.step_ref, ...), custom_call_target="tpu_custom_call" | custom-call | tf_op jit(solution)/shard_map/ssm_forward/pallas_call | solution.py:181
  209.8 3.9 copy-done.1
  213.7 4.7 attention_forward.1
  219.8 9.8 %fusion.7.own_ref = bf16[512,2048]{1,0:T(8,128)(2,1)} fusion(bf16[2048,6656]{1,0:T(8,128)(2,1)} %all-gather.3.cloned.1.call-done.weight_ref, bf16[512,1536]{1,0:T(8,128)(2,1)S(1)} %multiply_convert_fusion.1, bf16[512,512]{1,0:T(8,128)(2,1)S(1)} %get-tuple-element.146), kind=kOutput, calls=%fused_computation.11 | convolution fusion | flops 4300210176 | bytes 12582912 | tf_op jit(solution)/shard_map/tc,dc->td/dot_general | solution.py:25
  235.2 42.3 %collective-permute-done.2.other_ref = bf16[512,2048]{1,0:T(8,128)(2,1)} collective-permute-done((bf16[512,2048]{1,0:T(8,128)(2,1)}, bf16[512,2048]{1,0:T(8,128)(2,1)}, u32[]{:S(2)}, u32[]{:S(2)}) %collective-permute-start.2) | collective-permute-done | bytes 2097184 | tf_op jit(solution)/shard_map/ppermute | solution.py:973
  277.5 3.7 rms_forward.1
  285.7 5.5 all-gather.5.cloned.1.call-done.gate_w_ref.up_w_ref.down_ref.right_ref
  291.1 30.1 %feed_forward.1 = (bf16[512,2048]{1,0:T(8,128)(2,1)S(1)}, bf16[512,2048]{1,0:T(8,128)(2,1)S(1)}, bf16[512,2048]{1,0:T(8,128)(2,1)S(1)}, bf16[512,2048]{1,0:T(8,128)(2,1)}) custom-call(bf16[512,2048]{1,0:T(8,128)(2,1)} %copy-done.52, bf16[512,2048]{1,0:T(8,128)(2,1)} %copy-done.43, ...), custom_call_target="tpu_custom_call" | custom-call | flops 1 | bytes 1 | tf_op jit(solution)/shard_map/feed_forward/pallas_call | solution.py:568
  321.2 3.7 scatter_part.37
  325.3 4.7 scatter_part.38
  330.0 2.4 scatter_part.39.ready_ref
  334.2 2.3 join_parts.13
  337.8 8.3 %product_back.1.own_ref = bf16[512,2048]{1,0:T(8,128)(2,1)} custom-call(bf16[512,2048]{1,0:T(8,128)(2,1)S(1)} %get-tuple-element.153.left_ref.right_ref, bf16[2048,6144]{1,0:T(8,128)(2,1)} %all-gather.5.cloned.1.call-done.gate_w_ref.up_w_ref.down_ref.right_ref), custom_call_target="tpu_custom_call" | custom-call | flops 1 | bytes 1 | tf_op jit(solution)/shard_map/product_back/pallas_call | solution.py:734
  347.7 2.4 scatter_part.36.ready_ref
  350.1 4.8 scatter_part.43
  354.9 26.0 %collective-permute-done.6.other_ref = bf16[512,2048]{1,0:T(8,128)(2,1)} collective-permute-done((bf16[512,2048]{1,0:T(8,128)(2,1)}, bf16[512,2048]{1,0:T(8,128)(2,1)}, u32[]{:S(2)}, u32[]{:S(2)}) %collective-permute-start.6) | collective-permute-done | bytes 2097184 | tf_op jit(solution)/shard_map/ppermute | solution.py:973
  380.9 3.5 collective-permute-done.4.refs_1_
  387.6 4.3 scatter_part.40
  393.4 4.8 rms_back.2
  399.0 9.6 %norm_back.1 = (bf16[512,512]{1,0:T(8,128)(2,1)S(1)}, f32[512,1536]{1,0:T(8,128)S(1)}, f32[512,128]{1,0:T(8,128)S(1)}, f32[8,1536]{1,0:T(8,128)S(1)}) custom-call(bf16[512,2048]{1,0:T(8,128)(2,1)S(1)} %get-tuple-element.165.in_ref.grad_ref, bf16[2048,6656]{1,0:T(8,128)(2,1)} %all-gather.3.cloned.1.call-done.weight_ref, f32[512,1536]{1,0:T(8,128)S(1)} %copy-done.51, ...), custom_call_target="tpu_custom_call" | custom-call | flops 1 | bytes 1 | tf_op jit(solution)/shard_map/norm_back/pallas_call | solution.py:632
  411.6 4.8 scatter_part.41
  416.4 2.5 scatter_part.42.ready_ref
  419.0 5.6 attention_backward.1
  426.7 8.1 %collective-permute-done.7.refs_1_ = bf16[512,2048]{1,0:T(8,128)(2,1)} collective-permute-done((bf16[512,2048]{1,0:T(8,128)(2,1)}, bf16[512,2048]{1,0:T(8,128)(2,1)}, u32[]{:S(2)}, u32[]{:S(2)}) %collective-permute-start.7) | collective-permute-done | bytes 2097184 | tf_op jit(solution)/shard_map/ppermute | solution.py:1006
  434.8 3.1 join_parts.15
  439.7 4.9 scatter_part.44
  446.1 4.2 scatter_part.45
  455.3 27.2 %ssm_backward.1 = (bf16[512,1536]{1,0:T(8,128)(2,1)S(1)}, bf16[512,1536]{1,0:T(8,128)(2,1)S(1)}, bf16[512,512]{1,0:T(8,128)(2,1)}, bf16[512,128]{1,0:T(8,128)(2,...) custom-call(f32[512,1536]{1,0:T(8,128)S(1)} %copy-done.79, f32[512,1536]{1,0:T(8,128)S(1)} %copy-done.77, ...), custom_call_target="tpu_custom_call" | custom-call | flops 1 | bytes 1 | tf_op jit(solution)/shard_map/ssm_backward/pallas_call | solution.py:352
  482.5 4.0 scatter_part.46
  486.5 2.5 scatter_part.47.ready_ref
  489.1 3.2 join_parts.16
  493.7 4.5 scatter_part.48
  500.5 3.9 scatter_part.49
  511.4 3.2 scatter_part.50
  514.7 2.9 scatter_part.51
  520.1 14.4 %hidden_back.1.own_ref = bf16[512,2048]{1,0:T(8,128)(2,1)S(1)} custom-call(bf16[512,1536]{1,0:T(8,128)(2,1)S(1)} %copy-done.27, bf16[512,1536]{1,0:T(8,128)(2,1)S(1)} %copy-done.24, bf16[512,1536]{1,0:T(8,128)(2,1)S(1)} %beside.1.third_ref.right_ref, bf16[8,1536]{1,0:T(8,128)(2,1)S(1)} %broadcast_in_dim.50.keep_ref, ...), custom_call_target="tpu_custom_call" | custom-call | flops 1 | bytes 1 | tf_op jit(solution)/shard_map/hidden_back/pallas_call | solution.py:874
  534.4 2.9 scatter_part.52
  545.2 4.5 scatter_part.54
  551.9 3.3 scatter_part.55
  555.9 3.1 scatter_part.56
  561.0 23.9 %collective-permute-done.24.refs_3_ = bf16[128,2048]{1,0:T(8,128)(2,1)S(1)} collective-permute-done((bf16[128,2048]{1,0:T(8,128)(2,1)S(1)}, bf16[128,2048]{1,0:T(8,128)(2,1)S(1)}, u32[]{:S(2)}, u32[]{:S(2)}) %collective-permute-start.24) | collective-permute-done | bytes 524320 | tf_op jit(solution)/shard_map/ppermute | solution.py:1006
  591.3 2.8 scatter_part.58
  594.4 3.0 scatter_part.59
  598.8 3.4 scatter_part.60
  602.2 4.8 output_rows.1
  608.9 13.2 %collective-permute-done.29.refs_3_ = bf16[128,2048]{1,0:T(8,128)(2,1)S(1)} collective-permute-done((bf16[128,2048]{1,0:T(8,128)(2,1)S(1)}, bf16[128,2048]{1,0:T(8,128)(2,1)S(1)}, u32[]{:S(2)}, u32[]{:S(2)}) %collective-permute-start.29) | collective-permute-done | bytes 524320 | tf_op jit(solution)/shard_map/ppermute | solution.py:1006
  628.2 2.4 scatter_part.62
  630.6 3.6 scatter_part.63
  636.6 4.5 rms_back.3
  642.6 3.1 scatter_part.64
  649.5 3.1 scatter_part.67.ready_ref
  656.5 8.6 %collective-permute-done.35 = f32[16,2048]{1,0:T(8,128)S(1)} collective-permute-done((f32[16,2048]{1,0:T(8,128)S(1)}, f32[16,2048]{1,0:T(8,128)S(1)}, u32[]{:S(2)}, u32[]{:S(2)}) %collective-permute-start.35) | collective-permute-done | bytes 131104 | tf_op jit(solution)/shard_map/ppermute | solution.py:1006
  669.5 2.9 copy.67
  685.5 3.2 scatter_part.68.ready_ref
  688.7 2.6 scatter_part.69.ready_ref
  691.3 6.7 collective-permute-done.38
  704.5 2.7 scatter_part.70.ready_ref
  707.2 2.4 copy.64
  709.5 5.4 collective-permute-done.39
  715.5 3.1 collective-permute-start.41
  (476 shorter events, 155.9 us)
Async XLA Ops:
  7.2 153.1 %all-gather.3.cloned.1.call-start = ((), (), s32[]{:S(2)}) async-start(), calls=%async_computation | async-start | bytes 28966912 | tf_op jit(solution)/shard_map/all_gather | solution.py:1153
  11.2 8.0 %collective-permute-start = (bf16[64,640]{1,0:T(8,128)(2,1)S(1)}, bf16[64,640]{1,0:T(8,128)(2,1)S(1)}, u32[]{:S(2)}, u32[]{:S(2)}) collective-permute-start(bf16[64,640]{1,0:T(8,128)(2,1)S(1)} %pad_maximum_fusion.8), channel_id=1, source_target_pairs={{0,1},{1,0},{2,3},{3,2},{4,5},{5,4},{6,7},{7,6},{8,9},{9,8},{10,11... | collective-permute-start | bytes 245768 | tf_op jit(solution)/shard_map/ppermute | solution.py:973
  21.4 269.7 %all-gather.5.cloned.1.call-start = ((), (), s32[]{:S(2)}) async-start(), calls=%async_computation.1 | async-start | bytes 26738688 | tf_op jit(solution)/shard_map/all_gather | solution.py:1154
  22.9 138.1 %copy-start.131 = (s32[512]{0:T(512)S(1)}, s32[512]{0:T(512)}, u32[]{:S(2)}) copy-start(s32[512]{0:T(512)} %param.28) | copy-start | bytes 6148
  23.0 138.6 %copy-start.129 = (bf16[1536]{0:T(1024)(128)(2,1)S(1)}, bf16[1536]{0:T(1024)(128)(2,1)}, u32[]{:S(2)}) copy-start(bf16[1536]{0:T(1024)(128)(2,1)} %param.42) | copy-start | bytes 9220
  23.0 138.6 %copy-start.133 = (bf16[24]{0:T(256)(128)(2,1)S(1)}, bf16[24]{0:T(256)(128)(2,1)}, u32[]{:S(2)}) copy-start(bf16[24]{0:T(256)(128)(2,1)} %param.41) | copy-start | bytes 148
  23.0 138.8 %copy-start.132 = (bf16[5,1536]{1,0:T(8,128)(2,1)S(1)}, bf16[5,1536]{1,0:T(8,128)(2,1)}, u32[]{:S(2)}) copy-start(bf16[5,1536]{1,0:T(8,128)(2,1)} %param.37) | copy-start | bytes 46084
  23.0 138.9 %copy-start.134 = (bf16[24]{0:T(256)(128)(2,1)S(1)}, bf16[24]{0:T(256)(128)(2,1)}, u32[]{:S(2)}) copy-start(bf16[24]{0:T(256)(128)(2,1)} %param.39) | copy-start | bytes 148
  23.0 138.9 %copy-start.135 = (bf16[24]{0:T(256)(128)(2,1)S(1)}, bf16[24]{0:T(256)(128)(2,1)}, u32[]{:S(2)}) copy-start(bf16[24]{0:T(256)(128)(2,1)} %param.40) | copy-start | bytes 148
  24.3 139.7 %copy-start.41 = (bf16[512,2048]{1,0:T(8,128)(2,1)S(1)}, bf16[512,2048]{1,0:T(8,128)(2,1)}, u32[]{:S(2)}) copy-start(bf16[512,2048]{1,0:T(8,128)(2,1)} %value_ref.1) | copy-start | bytes 6291460
  207.0 11.5 %collective-permute-start.1 = (f32[512]{0:T(512)S(1)}, f32[512]{0:T(512)S(1)}, u32[]{:S(2)}, u32[]{:S(2)}) collective-permute-start(f32[512]{0:T(512)S(1)} %reduce_sum.28), channel_id=1, source_target_pairs={{0,1},{1,0},{2,3},{3,2},{4,5},{5,4},{6,7},{7,6},{8,9},{9,8},{10,11... | collective-permute-start | bytes 6152 | tf_op jit(solution)/shard_map/ppermute | solution.py:973
  229.7 47.8 %collective-permute-start.2 = (bf16[512,2048]{1,0:T(8,128)(2,1)}, bf16[512,2048]{1,0:T(8,128)(2,1)}, u32[]{:S(2)}, u32[]{:S(2)}) collective-permute-start(bf16[512,2048]{1,0:T(8,128)(2,1)} %fusion.7.own_ref), channel_id=1, source_target_pairs={{0,1},{1,0},{2,3},{3,2},{4,5},{5,4},{6,7},{7,6},{8,9},{9,8},{10,11... | collective-permute-start | bytes 6291464 | tf_op jit(solution)/shard_map/ppermute | solution.py:973
  232.6 44.9 %copy-start.130 = (f32[2048]{0:T(1024)S(1)}, f32[2048]{0:T(1024)}, u32[]{:S(2)}) copy-start(f32[2048]{0:T(1024)} %get-tuple-element.287) | copy-start | bytes 24580
  285.7 154.0 %copy-start.2 = (bf16[512,2048]{1,0:T(8,128)(2,1)}, bf16[512,2048]{1,0:T(8,128)(2,1)S(1)}, u32[]{:S(2)}) copy-start(bf16[512,2048]{1,0:T(8,128)(2,1)S(1)} %reorder_columns.4.left_ref) | copy-start | bytes 6291460
  291.1 30.1 %copy-start.14 = (bf16[512,2048]{1,0:T(8,128)(2,1)S(1)}, bf16[512,2048]{1,0:T(8,128)(2,1)}, u32[]{:S(2)}) copy-start(bf16[512,2048]{1,0:T(8,128)(2,1)} %copy-done.13) | copy-start | bytes 6291460
  321.2 29.0 %copy-start.28 = (bf16[512,2048]{1,0:T(8,128)(2,1)}, bf16[512,2048]{1,0:T(8,128)(2,1)S(1)}, u32[]{:S(2)}) copy-start(bf16[512,2048]{1,0:T(8,128)(2,1)S(1)} %get-tuple-element.170.right_ref) | copy-start | bytes 6291460
  321.2 124.9 %copy-start.7 = (bf16[512,2048]{1,0:T(8,128)(2,1)}, bf16[512,2048]{1,0:T(8,128)(2,1)S(1)}, u32[]{:S(2)}) copy-start(bf16[512,2048]{1,0:T(8,128)(2,1)S(1)} %get-tuple-element.153.left_ref.right_ref) | copy-start | bytes 6291460
  324.9 9.3 %collective-permute-start.3 = (bf16[1024,2048]{1,0:T(8,128)(2,1)S(1)}, bf16[1024,2048]{1,0:T(8,128)(2,1)S(1)}, u32[]{:S(2)}, u32[]{:S(2)}) collective-permute-start(bf16[1024,2048]{1,0:T(8,128)(2,1)S(1)} %scatter_part.37), channel_id=1, source_target_pairs={{0,2},{2,0},{4,6},{6,4},{8,10},{10,8},{12,14},{14,12},{16,18},{18,... | collective-permute-start | bytes 12582920 | tf_op jit(solution)/shard_map/ppermute | solution.py:1006
  332.4 48.4 %collective-permute-start.5 = (bf16[1024,2048]{1,0:T(8,128)(2,1)}, bf16[1024,2048]{1,0:T(8,128)(2,1)S(1)}, u32[]{:S(2)}, u32[]{:S(2)}) collective-permute-start(bf16[1024,2048]{1,0:T(8,128)(2,1)} %scatter_part.38), channel_id=1, source_target_pairs={{0,2},{2,0},{4,6},{6,4},{8,10},{10,8},{12,14},{14,12},{16,18},{18,... | collective-permute-start | bytes 12582920 | tf_op jit(solution)/shard_map/ppermute | solution.py:1006
  332.8 48.1 %collective-permute-start.6 = (bf16[512,2048]{1,0:T(8,128)(2,1)}, bf16[512,2048]{1,0:T(8,128)(2,1)}, u32[]{:S(2)}, u32[]{:S(2)}) collective-permute-start(bf16[512,2048]{1,0:T(8,128)(2,1)} %get-tuple-element.164.own_ref), channel_id=1, source_target_pairs={{0,1},{1,0},{2,3},{3,2},{4,5},{5,4},{6,7},{7,6},{8,9},{9,8},{10,11... | collective-permute-start | bytes 6291464 | tf_op jit(solution)/shard_map/ppermute | solution.py:973
  334.2 53.3 %copy-start.20 = (bf16[1024,2048]{1,0:T(8,128)(2,1)}, bf16[1024,2048]{1,0:T(8,128)(2,1)S(1)}, u32[]{:S(2)}) copy-start(bf16[1024,2048]{1,0:T(8,128)(2,1)S(1)} %collective-permute-done.3.got_ref.refs_0_) | copy-start | bytes 12582916
  336.6 47.8 %collective-permute-start.4 = (bf16[512,2048]{1,0:T(8,128)(2,1)}, bf16[512,2048]{1,0:T(8,128)(2,1)}, u32[]{:S(2)}, u32[]{:S(2)}) collective-permute-start(bf16[512,2048]{1,0:T(8,128)(2,1)} %join_parts.13), channel_id=1, source_target_pairs={{0,4},{2,6},{4,0},{6,2},{8,12},{10,14},{12,8},{14,10},{16,20},{18,... | collective-permute-start | bytes 6291464 | tf_op jit(solution)/shard_map/ppermute | solution.py:1006
  384.4 50.3 %collective-permute-start.8 = (bf16[1024,2048]{1,0:T(8,128)(2,1)}, bf16[1024,2048]{1,0:T(8,128)(2,1)}, u32[]{:S(2)}, u32[]{:S(2)}) collective-permute-start(bf16[1024,2048]{1,0:T(8,128)(2,1)} %scatter_part.43), channel_id=1, source_target_pairs={{0,2},{2,0},{4,6},{6,4},{8,10},{10,8},{12,14},{14,12},{16,18},{18,... | collective-permute-start | bytes 12582920 | tf_op jit(solution)/shard_map/ppermute | solution.py:1006
  386.4 48.4 %collective-permute-start.7 = (bf16[512,2048]{1,0:T(8,128)(2,1)}, bf16[512,2048]{1,0:T(8,128)(2,1)}, u32[]{:S(2)}, u32[]{:S(2)}) collective-permute-start(bf16[512,2048]{1,0:T(8,128)(2,1)} %join_parts.14), channel_id=1, source_target_pairs={{0,4},{2,6},{4,0},{6,2},{8,12},{10,14},{12,8},{14,10},{16,20},{18,... | collective-permute-start | bytes 6291464 | tf_op jit(solution)/shard_map/ppermute | solution.py:1006
  391.9 34.7 %collective-permute-start.9 = (bf16[256,2048]{1,0:T(8,128)(2,1)}, bf16[256,2048]{1,0:T(8,128)(2,1)}, u32[]{:S(2)}, u32[]{:S(2)}) collective-permute-start(bf16[256,2048]{1,0:T(8,128)(2,1)} %scatter_part.40), channel_id=1, source_target_pairs={{0,8},{2,10},{4,12},{6,14},{8,0},{10,2},{12,4},{14,6},{16,24},{18,... | collective-permute-start | bytes 3145736 | tf_op jit(solution)/shard_map/ppermute | solution.py:1006
  408.6 18.0 %collective-permute-start.10 = (f32[512,128]{1,0:T(8,128)S(1)}, f32[512,128]{1,0:T(8,128)S(1)}, u32[]{:S(2)}, u32[]{:S(2)}) collective-permute-start(f32[512,128]{1,0:T(8,128)S(1)} %get-tuple-element.167.own_ref), channel_id=1, source_target_pairs={{0,1},{1,0},{2,3},{3,2},{4,5},{5,4},{6,7},{7,6},{8,9},{9,8},{10,11... | collective-permute-start | bytes 786440 | tf_op jit(solution)/shard_map/ppermute | solution.py:973
  410.3 76.1 %copy-start.11 = (bf16[512,2048]{1,0:T(8,128)(2,1)}, bf16[512,2048]{1,0:T(8,128)(2,1)S(1)}, u32[]{:S(2)}) copy-start(bf16[512,2048]{1,0:T(8,128)(2,1)S(1)} %pad_maximum_fusion.right_ref) | copy-start | bytes 6291460
  411.6 74.9 %copy-start.9 = (bf16[512,2048]{1,0:T(8,128)(2,1)}, bf16[512,2048]{1,0:T(8,128)(2,1)S(1)}, u32[]{:S(2)}) copy-start(bf16[512,2048]{1,0:T(8,128)(2,1)S(1)} %reorder_columns.6.left_ref) | copy-start | bytes 6291460
  434.8 54.3 %collective-permute-start.13 = (bf16[1024,2048]{1,0:T(8,128)(2,1)}, bf16[1024,2048]{1,0:T(8,128)(2,1)}, u32[]{:S(2)}, u32[]{:S(2)}) collective-permute-start(bf16[1024,2048]{1,0:T(8,128)(2,1)} %scatter_part.41), channel_id=1, source_target_pairs={{0,2},{2,0},{4,6},{6,4},{8,10},{10,8},{12,14},{14,12},{16,18},{18,... | collective-permute-start | bytes 12582920 | tf_op jit(solution)/shard_map/ppermute | solution.py:1006
  437.9 51.1 %collective-permute-start.11 = (bf16[512,2048]{1,0:T(8,128)(2,1)}, bf16[512,2048]{1,0:T(8,128)(2,1)}, u32[]{:S(2)}, u32[]{:S(2)}) collective-permute-start(bf16[512,2048]{1,0:T(8,128)(2,1)} %join_parts.15), channel_id=1, source_target_pairs={{0,4},{2,6},{4,0},{6,2},{8,12},{10,14},{12,8},{14,10},{16,20},{18,... | collective-permute-start | bytes 6291464 | tf_op jit(solution)/shard_map/ppermute | solution.py:1006
  439.1 49.9 %collective-permute-start.15 = (bf16[512,2048]{1,0:T(8,128)(2,1)}, bf16[512,2048]{1,0:T(8,128)(2,1)}, u32[]{:S(2)}, u32[]{:S(2)}) collective-permute-start(bf16[512,2048]{1,0:T(8,128)(2,1)} %product_back.1.own_ref), channel_id=1, source_target_pairs={{0,1},{1,0},{2,3},{3,2},{4,5},{5,4},{6,7},{7,6},{8,9},{9,8},{10,11... | collective-permute-start | bytes 6291464 | tf_op jit(solution)/shard_map/ppermute | solution.py:973
  444.6 44.4 %collective-permute-start.12 = (bf16[256,2048]{1,0:T(8,128)(2,1)}, bf16[256,2048]{1,0:T(8,128)(2,1)S(1)}, u32[]{:S(2)}, u32[]{:S(2)}) collective-permute-start(bf16[256,2048]{1,0:T(8,128)(2,1)} %scatter_part.44), channel_id=1, source_target_pairs={{0,8},{2,10},{4,12},{6,14},{8,0},{10,2},{12,4},{14,6},{16,24},{18,... | collective-permute-start | bytes 3145736 | tf_op jit(solution)/shard_map/ppermute | solution.py:1006
  450.3 38.7 %collective-permute-start.14 = (bf16[128,2048]{1,0:T(8,128)(2,1)}, bf16[128,2048]{1,0:T(8,128)(2,1)S(1)}, u32[]{:S(2)}, u32[]{:S(2)}) collective-permute-start(bf16[128,2048]{1,0:T(8,128)(2,1)} %scatter_part.45), channel_id=1, source_target_pairs={{0,16},{2,18},{4,20},{6,22},{8,24},{10,26},{12,28},{14,30},{16,0},... | collective-permute-start | bytes 1572872 | tf_op jit(solution)/shard_map/ppermute | solution.py:1006
  489.1 51.5 %collective-permute-start.20 = (bf16[1024,1536]{1,0:T(8,128)(2,1)}, bf16[1024,1536]{1,0:T(8,128)(2,1)}, u32[]{:S(2)}, u32[]{:S(2)}) collective-permute-start(bf16[1024,1536]{1,0:T(8,128)(2,1)} %scatter_part.46), channel_id=1, source_target_pairs={{0,2},{2,0},{4,6},{6,4},{8,10},{10,8},{12,14},{14,12},{16,18},{18,... | collective-permute-start | bytes 9437192 | tf_op jit(solution)/shard_map/ppermute | solution.py:1006
  492.4 48.2 %collective-permute-start.17 = (bf16[512,2048]{1,0:T(8,128)(2,1)}, bf16[512,2048]{1,0:T(8,128)(2,1)}, u32[]{:S(2)}, u32[]{:S(2)}) collective-permute-start(bf16[512,2048]{1,0:T(8,128)(2,1)} %join_parts.16), channel_id=1, source_target_pairs={{0,4},{2,6},{4,0},{6,2},{8,12},{10,14},{12,8},{14,10},{16,20},{18,... | collective-permute-start | bytes 6291464 | tf_op jit(solution)/shard_map/ppermute | solution.py:1006
  498.2 41.0 %collective-permute-start.18 = (bf16[256,2048]{1,0:T(8,128)(2,1)}, bf16[256,2048]{1,0:T(8,128)(2,1)}, u32[]{:S(2)}, u32[]{:S(2)}) collective-permute-start(bf16[256,2048]{1,0:T(8,128)(2,1)} %scatter_part.48), channel_id=1, source_target_pairs={{0,8},{2,10},{4,12},{6,14},{8,0},{10,2},{12,4},{14,6},{16,24},{18,... | collective-permute-start | bytes 3145736 | tf_op jit(solution)/shard_map/ppermute | solution.py:1006
  499.0 18.7 %collective-permute-start.16 = (bf16[512,512]{1,0:T(8,128)(2,1)}, bf16[512,512]{1,0:T(8,128)(2,1)}, u32[]{:S(2)}, u32[]{:S(2)}) collective-permute-start(bf16[512,512]{1,0:T(8,128)(2,1)} %get-tuple-element.193.refs_3_), channel_id=1, source_target_pairs={{0,1},{1,0},{2,3},{3,2},{4,5},{5,4},{6,7},{7,6},{8,9},{9,8},{10,11... | collective-permute-start | bytes 1572872 | tf_op jit(solution)/shard_map/ppermute | solution.py:973
  504.4 34.9 %collective-permute-start.19 = (bf16[128,2048]{1,0:T(8,128)(2,1)}, bf16[128,2048]{1,0:T(8,128)(2,1)}, u32[]{:S(2)}, u32[]{:S(2)}) collective-permute-start(bf16[128,2048]{1,0:T(8,128)(2,1)} %scatter_part.49), channel_id=1, source_target_pairs={{0,16},{2,18},{4,20},{6,22},{8,24},{10,26},{12,28},{14,30},{16,0},... | collective-permute-start | bytes 1572872 | tf_op jit(solution)/shard_map/ppermute | solution.py:1006
  520.0 125.7 %copy-start.5 = (bf16[512,1536]{1,0:T(8,128)(2,1)}, bf16[512,1536]{1,0:T(8,128)(2,1)S(1)}, u32[]{:S(2)}) copy-start(bf16[512,1536]{1,0:T(8,128)(2,1)S(1)} %beside.1.third_ref.right_ref) | copy-start | bytes 4718596
  540.6 45.9 %collective-permute-start.22 = (bf16[1024,1536]{1,0:T(8,128)(2,1)S(1)}, bf16[1024,1536]{1,0:T(8,128)(2,1)S(1)}, u32[]{:S(2)}, u32[]{:S(2)}) collective-permute-start(bf16[1024,1536]{1,0:T(8,128)(2,1)S(1)} %scatter_part.51), channel_id=1, source_target_pairs={{0,2},{2,0},{4,6},{6,4},{8,10},{10,8},{12,14},{14,12},{16,18},{18,... | collective-permute-start | bytes 9437192 | tf_op jit(solution)/shard_map/ppermute | solution.py:1006
  542.3 44.1 %collective-permute-start.21 = (bf16[512,1536]{1,0:T(8,128)(2,1)S(1)}, bf16[512,1536]{1,0:T(8,128)(2,1)S(1)}, u32[]{:S(2)}, u32[]{:S(2)}) collective-permute-start(bf16[512,1536]{1,0:T(8,128)(2,1)S(1)} %join_parts.17), channel_id=1, source_target_pairs={{0,4},{2,6},{4,0},{6,2},{8,12},{10,14},{12,8},{14,10},{16,20},{18,... | collective-permute-start | bytes 4718600 | tf_op jit(solution)/shard_map/ppermute | solution.py:1006
  549.7 36.7 %collective-permute-start.23 = (bf16[256,2048]{1,0:T(8,128)(2,1)}, bf16[256,2048]{1,0:T(8,128)(2,1)S(1)}, u32[]{:S(2)}, u32[]{:S(2)}) collective-permute-start(bf16[256,2048]{1,0:T(8,128)(2,1)} %scatter_part.54), channel_id=1, source_target_pairs={{0,8},{2,10},{4,12},{6,14},{8,0},{10,2},{12,4},{14,6},{16,24},{18,... | collective-permute-start | bytes 3145736 | tf_op jit(solution)/shard_map/ppermute | solution.py:1006
  550.4 36.0 %collective-permute-start.25 = (bf16[256,2048]{1,0:T(8,128)(2,1)}, bf16[256,2048]{1,0:T(8,128)(2,1)S(1)}, u32[]{:S(2)}, u32[]{:S(2)}) collective-permute-start(bf16[256,2048]{1,0:T(8,128)(2,1)} %get-tuple-element.212), channel_id=1, source_target_pairs={{0,1},{1,0},{2,3},{3,2},{4,5},{5,4},{6,7},{7,6},{8,9},{9,8},{10,11... | collective-permute-start | bytes 3145736 | tf_op jit(solution)/shard_map/ppermute | solution.py:973
  555.3 29.6 %collective-permute-start.24 = (bf16[128,2048]{1,0:T(8,128)(2,1)S(1)}, bf16[128,2048]{1,0:T(8,128)(2,1)S(1)}, u32[]{:S(2)}, u32[]{:S(2)}) collective-permute-start(bf16[128,2048]{1,0:T(8,128)(2,1)S(1)} %scatter_part.55), channel_id=1, source_target_pairs={{0,16},{2,18},{4,20},{6,22},{8,24},{10,26},{12,28},{14,30},{16,0},... | collective-permute-start | bytes 1572872 | tf_op jit(solution)/shard_map/ppermute | solution.py:1006
  561.0 28.8 %copy-start.122 = (bf16[256,2048]{1,0:T(8,128)(2,1)S(1)}, bf16[256,2048]{1,0:T(8,128)(2,1)}, u32[]{:S(2)}) copy-start(bf16[256,2048]{1,0:T(8,128)(2,1)} %get-tuple-element.220) | copy-start | bytes 3145732
  586.4 60.8 %copy-start.37 = (bf16[1024,1536]{1,0:T(8,128)(2,1)}, bf16[1024,1536]{1,0:T(8,128)(2,1)S(1)}, u32[]{:S(2)}) copy-start(bf16[1024,1536]{1,0:T(8,128)(2,1)S(1)} %collective-permute-done.22.got_ref.refs_0_) | copy-start | bytes 9437188
  586.4 38.0 %collective-permute-start.27 = (bf16[1024,1536]{1,0:T(8,128)(2,1)S(1)}, bf16[1024,1536]{1,0:T(8,128)(2,1)S(1)}, u32[]{:S(2)}, u32[]{:S(2)}) collective-permute-start(bf16[1024,1536]{1,0:T(8,128)(2,1)S(1)} %scatter_part.52), channel_id=1, source_target_pairs={{0,2},{2,0},{4,6},{6,4},{8,10},{10,8},{12,14},{14,12},{16,18},{18,... | collective-permute-start | bytes 9437192 | tf_op jit(solution)/shard_map/ppermute | solution.py:1006
  588.2 36.3 %collective-permute-start.26 = (bf16[512,1536]{1,0:T(8,128)(2,1)S(1)}, bf16[512,1536]{1,0:T(8,128)(2,1)S(1)}, u32[]{:S(2)}, u32[]{:S(2)}) collective-permute-start(bf16[512,1536]{1,0:T(8,128)(2,1)S(1)} %join_parts.18), channel_id=1, source_target_pairs={{0,4},{2,6},{4,0},{6,2},{8,12},{10,14},{12,8},{14,10},{16,20},{18,... | collective-permute-start | bytes 4718600 | tf_op jit(solution)/shard_map/ppermute | solution.py:1006
  589.8 34.6 %collective-permute-start.30 = (bf16[256,2048]{1,0:T(8,128)(2,1)S(1)}, bf16[256,2048]{1,0:T(8,128)(2,1)}, u32[]{:S(2)}, u32[]{:S(2)}) collective-permute-start(bf16[256,2048]{1,0:T(8,128)(2,1)S(1)} %copy-done.122), channel_id=1, source_target_pairs={{0,1},{1,0},{2,3},{3,2},{4,5},{5,4},{6,7},{7,6},{8,9},{9,8},{10,11... | collective-permute-start | bytes 3145736 | tf_op jit(solution)/shard_map/ppermute | solution.py:973
  594.1 30.3 %collective-permute-start.28 = (bf16[256,1536]{1,0:T(8,128)(2,1)S(1)}, bf16[256,1536]{1,0:T(8,128)(2,1)S(1)}, u32[]{:S(2)}, u32[]{:S(2)}) collective-permute-start(bf16[256,1536]{1,0:T(8,128)(2,1)S(1)} %scatter_part.58), channel_id=1, source_target_pairs={{0,8},{2,10},{4,12},{6,14},{8,0},{10,2},{12,4},{14,6},{16,24},{18,... | collective-permute-start | bytes 2359304 | tf_op jit(solution)/shard_map/ppermute | solution.py:1006
  597.5 24.7 %collective-permute-start.29 = (bf16[128,2048]{1,0:T(8,128)(2,1)S(1)}, bf16[128,2048]{1,0:T(8,128)(2,1)S(1)}, u32[]{:S(2)}, u32[]{:S(2)}) collective-permute-start(bf16[128,2048]{1,0:T(8,128)(2,1)S(1)} %scatter_part.59), channel_id=1, source_target_pairs={{0,16},{2,18},{4,20},{6,22},{8,24},{10,26},{12,28},{14,30},{16,0},... | collective-permute-start | bytes 1572872 | tf_op jit(solution)/shard_map/ppermute | solution.py:1006
  624.5 22.7 %copy-start.47 = (bf16[512,1536]{1,0:T(8,128)(2,1)}, bf16[512,1536]{1,0:T(8,128)(2,1)S(1)}, u32[]{:S(2)}) copy-start(bf16[512,1536]{1,0:T(8,128)(2,1)S(1)} %collective-permute-done.26.refs_1_) | copy-start | bytes 4718596
  624.5 21.3 %copy-start.39 = (bf16[1024,1536]{1,0:T(8,128)(2,1)}, bf16[1024,1536]{1,0:T(8,128)(2,1)S(1)}, u32[]{:S(2)}) copy-start(bf16[1024,1536]{1,0:T(8,128)(2,1)S(1)} %collective-permute-done.27.got_ref.refs_0_) | copy-start | bytes 9437188
  626.5 38.6 %collective-permute-start.32 = (bf16[512,1536]{1,0:T(8,128)(2,1)}, bf16[512,1536]{1,0:T(8,128)(2,1)}, u32[]{:S(2)}, u32[]{:S(2)}) collective-permute-start(bf16[512,1536]{1,0:T(8,128)(2,1)} %join_parts.19), channel_id=1, source_target_pairs={{0,4},{2,6},{4,0},{6,2},{8,12},{10,14},{12,8},{14,10},{16,20},{18,... | collective-permute-start | bytes 4718600 | tf_op jit(solution)/shard_map/ppermute | solution.py:1006
  630.6 34.5 %collective-permute-start.33 = (bf16[256,1536]{1,0:T(8,128)(2,1)}, bf16[256,1536]{1,0:T(8,128)(2,1)}, u32[]{:S(2)}, u32[]{:S(2)}) collective-permute-start(bf16[256,1536]{1,0:T(8,128)(2,1)} %scatter_part.62), channel_id=1, source_target_pairs={{0,8},{2,10},{4,12},{6,14},{8,0},{10,2},{12,4},{14,6},{16,24},{18,... | collective-permute-start | bytes 2359304 | tf_op jit(solution)/shard_map/ppermute | solution.py:1006
  634.1 30.9 %collective-permute-start.34 = (bf16[128,1536]{1,0:T(8,128)(2,1)}, bf16[128,1536]{1,0:T(8,128)(2,1)}, u32[]{:S(2)}, u32[]{:S(2)}) collective-permute-start(bf16[128,1536]{1,0:T(8,128)(2,1)} %scatter_part.63), channel_id=1, source_target_pairs={{0,16},{2,18},{4,20},{6,22},{8,24},{10,26},{12,28},{14,30},{16,0},... | collective-permute-start | bytes 1179656 | tf_op jit(solution)/shard_map/ppermute | solution.py:1006
  641.2 1.4 collective-permute-start.31
  653.6 11.5 %collective-permute-start.35 = (f32[16,2048]{1,0:T(8,128)S(1)}, f32[16,2048]{1,0:T(8,128)S(1)}, u32[]{:S(2)}, u32[]{:S(2)}) collective-permute-start(f32[16,2048]{1,0:T(8,128)S(1)} %add.64), channel_id=1, source_target_pairs={{0,4},{2,6},{4,0},{6,2},{8,12},{10,14},{12,8},{14,10},{16,20},{18,... | collective-permute-start | bytes 393224 | tf_op jit(solution)/shard_map/ppermute | solution.py:1006
  668.6 29.5 %collective-permute-start.36 = (bf16[256,1536]{1,0:T(8,128)(2,1)}, bf16[256,1536]{1,0:T(8,128)(2,1)}, u32[]{:S(2)}, u32[]{:S(2)}) collective-permute-start(bf16[256,1536]{1,0:T(8,128)(2,1)} %join_parts.20), channel_id=1, source_target_pairs={{0,8},{2,10},{4,12},{6,14},{8,0},{10,2},{12,4},{14,6},{16,24},{18,... | collective-permute-start | bytes 2359304 | tf_op jit(solution)/shard_map/ppermute | solution.py:1006
  674.3 23.8 %collective-permute-start.37 = (bf16[128,1536]{1,0:T(8,128)(2,1)}, bf16[128,1536]{1,0:T(8,128)(2,1)}, u32[]{:S(2)}, u32[]{:S(2)}) collective-permute-start(bf16[128,1536]{1,0:T(8,128)(2,1)} %join_parts.21), channel_id=1, source_target_pairs={{0,16},{2,18},{4,20},{6,22},{8,24},{10,26},{12,28},{14,30},{16,0},... | collective-permute-start | bytes 1179656 | tf_op jit(solution)/shard_map/ppermute | solution.py:1006
  679.0 19.0 %collective-permute-start.38 = (f32[16,2048]{1,0:T(8,128)S(1)}, f32[16,2048]{1,0:T(8,128)}, u32[]{:S(2)}, u32[]{:S(2)}) collective-permute-start(f32[16,2048]{1,0:T(8,128)S(1)} %add.65), channel_id=1, source_target_pairs={{0,8},{2,10},{4,12},{6,14},{8,0},{10,2},{12,4},{14,6},{16,24},{18,... | collective-permute-start | bytes 393224 | tf_op jit(solution)/shard_map/ppermute | solution.py:1006
  700.2 14.7 %collective-permute-start.39 = (f32[16,2048]{1,0:T(8,128)S(1)}, f32[16,2048]{1,0:T(8,128)S(1)}, u32[]{:S(2)}, u32[]{:S(2)}) collective-permute-start(f32[16,2048]{1,0:T(8,128)S(1)} %add.66), channel_id=1, source_target_pairs={{0,16},{2,18},{4,20},{6,22},{8,24},{10,26},{12,28},{14,30},{16,0},... | collective-permute-start | bytes 393224 | tf_op jit(solution)/shard_map/ppermute | solution.py:1006
  700.9 22.5 %collective-permute-start.40 = (bf16[128,1536]{1,0:T(8,128)(2,1)S(1)}, bf16[128,1536]{1,0:T(8,128)(2,1)}, u32[]{:S(2)}, u32[]{:S(2)}) collective-permute-start(bf16[128,1536]{1,0:T(8,128)(2,1)S(1)} %join_parts.23), channel_id=1, source_target_pairs={{0,16},{2,18},{4,20},{6,22},{8,24},{10,26},{12,28},{14,30},{16,0},... | collective-permute-start | bytes 1179656 | tf_op jit(solution)/shard_map/ppermute | solution.py:1006
  715.5 6.2 collective-permute-start.41
  (120 other events, 508.2 us)
Sparse Core Ops, SparseCore 0:
  21.5 138.7 all-gather.2
  162.5 128.5 all-gather.4

commit v3 on v2

--- a/solution.py
+++ b/solution.py
@@ -6,6 +6,7 @@
 from jax import lax
 from jax.experimental import pallas as pl
 from jax.experimental.pallas import tpu as pltpu
+from jax.experimental.layout import Layout, with_layout_constraint
 from jax.sharding import PartitionSpec as P
 
 HP = 64
@@ -116,6 +117,15 @@
 def lane_column(values, lane):
     lanes = lax.broadcasted_iota(jnp.int32, values.shape, 1)
     return jnp.sum(jnp.where(lanes == lane, values, 0.0), axis=1, keepdims=True)
+
+
+def head_sums(values, pair):
+    lanes = lax.broadcasted_iota(jnp.int32, (128, 128), 0)
+    heads = lax.broadcasted_iota(jnp.int32, (128, 128), 1)
+    chosen = (heads == 2 * pair + lanes // HP).astype(jnp.bfloat16)
+    high = values.astype(jnp.bfloat16)
+    low = (values - high.astype(jnp.float32)).astype(jnp.bfloat16)
+    return dot_nn(jnp.concatenate([high, low], axis=1), jnp.concatenate([chosen, chosen], axis=0))
 
 
 def ssm_forward_kernel(
@@ -218,7 +228,7 @@
 def ssm_backward_kernel(
     dn_ref, y_ref, u_ref, z_ref, state_b_ref, state_c_ref, step_ref, inverse_ref, own_ref, other_ref,
     wide_ref, conv_ref, extra_ref, live_ref, same_ref, mask_t_ref,
-    dz_ref, du_ref, ds_ref, dr_ref, wide_grad_ref, conv_grad_ref, extra_grad_ref,
+    dz_ref, du_ref, ds_ref, dr_ref, wide_grad_ref, extra_grad_ref,
     gram_t, gram_grad, sizes, decays, running, running_t, size_grad, total_grad, states, state_slopes,
 ):
     step = pl.program_id(0)
@@ -291,18 +301,8 @@
         by_size = grad_inflow * x_in
         mixed_only = mixed - taps[5:6] * x_in
         by_total = grad_mixed_b.astype(jnp.float32) * mixed_only - grad_inflow * inflow.astype(jnp.float32)
-        size_sum, total_sum = size_grad[...], total_grad[...]
-        for k in range(2):
-            mine = left_lanes if k == 0 else jnp.logical_not(left_lanes)
-            here = lanes == 2 * pair + k
-            size_sum = jnp.where(
-                here, jnp.sum(jnp.where(mine, by_size, 0.0), axis=1, keepdims=True), size_sum
-            )
-            total_sum = jnp.where(
-                here, jnp.sum(jnp.where(mine, by_total, 0.0), axis=1, keepdims=True), total_sum
-            )
-        size_grad[...] = size_sum
-        total_grad[...] = total_sum
+        size_grad[...] += head_sums(by_size, pair)
+        total_grad[...] += head_sums(by_total, pair)
         grad_u, tap_grads = conv_rows_back(grad_x * x_slope, u_live, taps, same_ref)
         du_ref[:, at] = (grad_u * live).astype(du_ref.dtype)
         skip_grad = jnp.sum(grad_mixed * x_in, axis=0, keepdims=True)
@@ -319,10 +319,10 @@
         grad_bc = jnp.concatenate([grad_b, grad_c], axis=1) * state_slopes[...]
         state = jnp.concatenate([state_b_ref[...], state_c_ref[...]], axis=1) * wide_live
         grad_in, state_taps = conv_rows_back(grad_bc, state, conv_ref[...], same_ref)
-        ds_ref[...] = (grad_in * wide_live).astype(ds_ref.dtype)
-        conv_grad_ref[...] = jnp.concatenate(
-            state_taps + [jnp.zeros((3, width), jnp.float32)], axis=0
-        )
+        ds_ref[:rows, :] = (grad_in * wide_live).astype(ds_ref.dtype)
+        ds_ref[rows:, :] = jnp.concatenate(
+            state_taps + [jnp.zeros((11, width), jnp.float32)], axis=0
+        ).astype(ds_ref.dtype)
         decay_grad = running_sum(total_grad[...], backward=True)
         shifted = step_ref[...] + extra_ref[0:1]
         grad_size = size_grad[...] - decay_grad * extra_ref[1:2]
@@ -373,19 +373,17 @@
         out_specs=[
             plain,
             plain,
-            pl.BlockSpec((rows, width), const2),
+            pl.BlockSpec((rows + 16, width), const2),
             pl.BlockSpec((rows, 128), const2),
             pl.BlockSpec((8, 128 * 2), lambda i: (0, i)),
-            pl.BlockSpec((8, width), const2),
             pl.BlockSpec((8, 128), const2),
         ],
         out_shape=[
             jax.ShapeDtypeStruct((rows, pairs * 128), b16),
             jax.ShapeDtypeStruct((rows, pairs * 128), b16),
-            jax.ShapeDtypeStruct((rows, width), b16),
+            jax.ShapeDtypeStruct((rows + 16, width), b16),
             jax.ShapeDtypeStruct((rows, 128), b16),
             jax.ShapeDtypeStruct((8, pairs * 128), f32),
-            jax.ShapeDtypeStruct((8, width), f32),
             jax.ShapeDtypeStruct((8, 128), f32),
         ],
         scratch_shapes=[
@@ -684,6 +682,10 @@
     )(order, values)
 
 
+def widest(width, most):
+    return max(t for t in range(128, most + 1, 128) if width % t == 0)
+
+
 def scatter_part_kernel(left_ref, right_ref, *refs):
     got_refs, out_ref, turned_left = refs[:-2], refs[-2], refs[-1]
 
@@ -704,7 +706,7 @@
         for got, start in gots:
             total = total + got[start : start + size].astype(jnp.float32)
         return total.astype(dtype)
-    tile = max(t for t in (128, 256, 384, 512) if width % t == 0)
+    tile = widest(width, 2304 if size <= 256 else 1152)
     return pl.pallas_call(
         scatter_part_kernel,
         grid=(width // tile,),
@@ -718,7 +720,7 @@
         out_specs=pl.BlockSpec((size, tile), lambda i: (0, i)),
         out_shape=jax.ShapeDtypeStruct((size, width), dtype),
         scratch_shapes=[pltpu.VMEM((size, rows), jnp.bfloat16)],
-        compiler_params=pltpu.CompilerParams(vmem_limit_bytes=16 * 2**20),
+        compiler_params=pltpu.CompilerParams(vmem_limit_bytes=24 * 2**20),
         cost_estimate=cost(1, 1),
         name="scatter_part",
     )(left, right, *[got for got, unused in gots])
@@ -746,23 +748,36 @@
     )(left, right)
 
 
-def join_kernel(ready_ref, got_ref, out_ref):
-    out_ref[...] = (ready_ref[...] + got_ref[...].astype(jnp.float32)).astype(out_ref.dtype)
+def join_kernel(start, ready_ref, got_ref, out_ref):
+    size = ready_ref.shape[0]
+    got = got_ref[start : start + size, :].astype(jnp.float32)
+    out_ref[...] = (ready_ref[...] + got).astype(out_ref.dtype)
 
 
 def join_parts(ready, got, start, dtype):
     size, width = ready.shape
     if size % 128 or start % size:
         return (ready + got[start : start + size].astype(jnp.float32)).astype(dtype)
-    tile = max(t for t in (128, 256, 384, 512, 768, 1024) if width % t == 0)
-    return pl.pallas_call(
-        join_kernel,
-        grid=(width // tile,),
-        in_specs=[
-            pl.BlockSpec((size, tile), lambda i: (0, i)),
-            pl.BlockSpec((size, tile), lambda i: (start // size, i)),
-        ],
-        out_specs=pl.BlockSpec((size, tile), lambda i: (0, i)),
+    if size > 256:
+        tile = widest(width, 1152)
+        return pl.pallas_call(
+            functools.partial(join_kernel, 0),
+            grid=(width // tile,),
+            in_specs=[
+                pl.BlockSpec((size, tile), lambda i: (0, i)),
+                pl.BlockSpec((size, tile), lambda i: (start // size, i)),
+            ],
+            out_specs=pl.BlockSpec((size, tile), lambda i: (0, i)),
+            out_shape=jax.ShapeDtypeStruct((size, width), dtype),
+            compiler_params=pltpu.CompilerParams(vmem_limit_bytes=24 * 2**20),
+            cost_estimate=cost(1, 1),
+            name="join_parts",
+        )(ready, got)
+    vmem = pl.BlockSpec(memory_space=pltpu.VMEM)
+    return pl.pallas_call(
+        functools.partial(join_kernel, start),
+        in_specs=[vmem, vmem],
+        out_specs=vmem,
         out_shape=jax.ShapeDtypeStruct((size, width), dtype),
         compiler_params=pltpu.CompilerParams(vmem_limit_bytes=16 * 2**20),
         cost_estimate=cost(1, 1),
@@ -793,7 +808,7 @@
         out_refs[1][...] += gain_grad
 
 
-def rms_back(values, gain, own, other, base, live, with_rounded, tile=128):
+def rms_back(values, gain, own, other, base, live, with_rounded, tile=256):
     rows, model = values.shape
     each = pl.BlockSpec((tile, model), lambda i: (i, 0))
     whole = pl.BlockSpec((8, model), lambda i: (0, 0))
@@ -809,7 +824,7 @@
         in_specs=[each, whole, each, each, each, pl.BlockSpec((tile, 128), lambda i: (i, 0))],
         out_specs=[each, whole, each][: len(shapes)],
         out_shape=shapes,
-        compiler_params=pltpu.CompilerParams(vmem_limit_bytes=24 * 2**20),
+        compiler_params=pltpu.CompilerParams(vmem_limit_bytes=40 * 2**20),
         cost_estimate=cost(1, 1),
         name="rms_back",
     )(values, gain, own, other, base, live)
@@ -827,35 +842,36 @@
         out_ref[:, place:] = jnp.zeros((out_ref.shape[0], out_ref.shape[1] - place), out_ref.dtype)
 
 
-def beside(width, *columns, tile=128):
+def beside(width, *columns, tile=256):
     groups = [c if isinstance(c, tuple) else (c,) for c in columns]
     widths = tuple((g[0].shape[1], len(g)) for g in groups)
     arrays = [a for g in groups for a in g]
-    rows = arrays[0].shape[0]
+    rows = min(a.shape[0] for a in arrays)
     return pl.pallas_call(
         functools.partial(beside_kernel, widths),
         grid=(rows // tile,),
         in_specs=[pl.BlockSpec((tile, a.shape[1]), lambda i: (i, 0)) for a in arrays],
         out_specs=pl.BlockSpec((tile, width), lambda i: (i, 0)),
         out_shape=jax.ShapeDtypeStruct((rows, width), jnp.bfloat16),
-        compiler_params=pltpu.CompilerParams(vmem_limit_bytes=12 * 2**20),
+        compiler_params=pltpu.CompilerParams(vmem_limit_bytes=16 * 2**20),
         cost_estimate=cost(1, 1),
         name="beside",
     )(*arrays)
 
 
-def hidden_back_kernel(first_ref, second_ref, third_ref, keep_ref, weight_ref, out_ref, total):
+def hidden_back_kernel(
+    first_ref, second_ref, third_ref, keep_ref, weight_ref, out_ref, total, *, ends
+):
     step = pl.program_id(0)
-    third = pl.num_programs(0) // 3
 
     @pl.when(step == 0)
     def _():
         total[...] = jnp.zeros_like(total)
 
     left = jnp.where(
-        step < third,
+        step < ends[0],
         first_ref[...],
-        jnp.where(step < 2 * third, second_ref[...], third_ref[...] * keep_ref[0:1]),
+        jnp.where(step < ends[1], second_ref[...], third_ref[...] * keep_ref[0:1]),
     )
     total[...] += dot_nt(left, weight_ref[...])
 
@@ -865,20 +881,21 @@
 
 
 def hidden_back(first, second, third, keep, weights, tile=768):
-    rows, width = first.shape
+    rows = first.shape[0]
     model = weights.shape[0]
-    steps = width // tile
-    block = lambda part: pl.BlockSpec(
-        (rows, tile), lambda i: (0, jnp.clip(i - part * steps, 0, steps - 1))
-    )
-    return pl.pallas_call(
-        hidden_back_kernel,
-        grid=(3 * steps,),
+    counts = [part.shape[1] // tile for part in (first, second, third)]
+    ends = (counts[0], counts[0] + counts[1])
+    block = lambda start, count: pl.BlockSpec(
+        (rows, tile), lambda i: (0, jnp.clip(i - start, 0, count - 1))
+    )
+    return pl.pallas_call(
+        functools.partial(hidden_back_kernel, ends=ends),
+        grid=(sum(counts),),
         in_specs=[
-            block(0),
-            block(1),
-            block(2),
-            pl.BlockSpec((8, tile), lambda i: (0, jnp.maximum(i - 2 * steps, 0))),
+            block(0, counts[0]),
+            block(ends[0], counts[1]),
+            block(ends[1], counts[2]),
+            pl.BlockSpec((8, tile), lambda i: (0, jnp.clip(i - ends[1], 0, counts[2] - 1))),
             pl.BlockSpec((model, tile), lambda i: (0, i)),
         ],
         out_specs=pl.BlockSpec((rows, model), lambda i: (0, 0)),
@@ -898,7 +915,7 @@
     out_ref[...] = (values * scale * gain_ref[0:1]).astype(out_ref.dtype)
 
 
-def rms_forward(base, own, other, live, gain, tile=128):
+def rms_forward(base, own, other, live, gain, tile=256):
     rows, model = base.shape
     each = pl.BlockSpec((tile, model), lambda i: (i, 0))
     return pl.pallas_call(
@@ -916,7 +933,7 @@
             jax.ShapeDtypeStruct((rows, model), jnp.float32),
             jax.ShapeDtypeStruct((rows, model), jnp.bfloat16),
         ],
-        compiler_params=pltpu.CompilerParams(vmem_limit_bytes=20 * 2**20),
+        compiler_params=pltpu.CompilerParams(vmem_limit_bytes=28 * 2**20),
         cost_estimate=cost(1, 1),
         name="rms_forward",
     )(base, own, other, live, gain)
@@ -927,7 +944,7 @@
     out_ref[...] = (base_ref[...] + added * live_ref[:, 0:1]).astype(out_ref.dtype)
 
 
-def output_rows(base, own, other, live, tile=128):
+def output_rows(base, own, other, live, tile=256):
     rows, model = base.shape
     each = pl.BlockSpec((tile, model), lambda i: (i, 0))
     return pl.pallas_call(
@@ -936,33 +953,72 @@
         in_specs=[each, each, each, pl.BlockSpec((tile, 128), lambda i: (i, 0))],
         out_specs=each,
         out_shape=jax.ShapeDtypeStruct((rows, model), jnp.bfloat16),
-        compiler_params=pltpu.CompilerParams(vmem_limit_bytes=16 * 2**20),
+        compiler_params=pltpu.CompilerParams(vmem_limit_bytes=24 * 2**20),
         cost_estimate=cost(1, 1),
         name="output_rows",
     )(base, own, other, live)
 
 
-def stack_kernel(counts, *refs):
-    out_ref, place = refs[-1], 0
+def stack_kernel(layout, *refs):
+    out_ref, place, refs = refs[-1], 0, list(refs[:-1])
     out_ref[...] = jnp.zeros_like(out_ref)
-    for count, ref in zip(counts, refs):
-        out_ref[place : place + count, : ref.shape[1]] = ref[:count, :]
+    for start, count, terms in layout:
+        total = refs.pop(0)[start : start + count, :].astype(jnp.float32)
+        if terms == 2:
+            total = total + refs.pop(0)[start : start + count, :].astype(jnp.float32)
+        out_ref[place : place + count, : total.shape[1]] = total
         place += count
 
 
 def stack_rows(width, *parts):
-    counts = tuple(count for unused, count in parts)
-    total = -(-sum(counts) // 8) * 8
+    layout = tuple((start, count, len(arrays)) for arrays, start, count in parts)
+    total = -(-sum(count for unused, count, terms in layout) // 8) * 8
     vmem = pl.BlockSpec(memory_space=pltpu.VMEM)
-    return pl.pallas_call(
-        functools.partial(stack_kernel, counts),
-        in_specs=[vmem] * len(parts),
+    arrays = [array for arrays, start, count in parts for array in arrays]
+    return pl.pallas_call(
+        functools.partial(stack_kernel, layout),
+        in_specs=[vmem] * len(arrays),
         out_specs=vmem,
         out_shape=jax.ShapeDtypeStruct((total, width), jnp.float32),
         compiler_params=pltpu.CompilerParams(vmem_limit_bytes=8 * 2**20),
         cost_estimate=cost(1, 1),
         name="stack_rows",
-    )(*[part for part, unused in parts])
+    )(*arrays)
+
+
+def add_kernel(left_ref, right_ref, out_ref):
+    out_ref[...] = left_ref[...] + right_ref[...]
+
+
+def add_rows(left, right):
+    vmem = pl.BlockSpec(memory_space=pltpu.VMEM)
+    return pl.pallas_call(
+        add_kernel,
+        in_specs=[vmem, vmem],
+        out_specs=vmem,
+        out_shape=jax.ShapeDtypeStruct(left.shape, left.dtype),
+        compiler_params=pltpu.CompilerParams(vmem_limit_bytes=8 * 2**20),
+        cost_estimate=cost(1, 1),
+        name="add_rows",
+    )(left, right)
+
+
+def turn_kernel(in_ref, out_ref):
+    out_ref[...] = in_ref[...].T
+
+
+def turned_copy(values, tile=512):
+    rows, width = values.shape
+    return pl.pallas_call(
+        turn_kernel,
+        grid=(width // tile,),
+        in_specs=[pl.BlockSpec((rows, tile), lambda i: (0, i))],
+        out_specs=pl.BlockSpec((tile, rows), lambda i: (i, 0)),
+        out_shape=jax.ShapeDtypeStruct((width, rows), values.dtype),
+        compiler_params=pltpu.CompilerParams(vmem_limit_bytes=8 * 2**20),
+        cost_estimate=cost(1, 1),
+        name="turned_copy",
+    )(values)
 
 
 def tie(*values):
@@ -1075,6 +1131,12 @@
             self.send()
             self.make()
         return self.total
+
+
+def side_by_side(first, second):
+    return with_layout_constraint(
+        jnp.stack([first, second], axis=1), Layout(major_to_minor=(0, 1, 2))
+    )
 
 
 def local(
@@ -1116,21 +1178,40 @@
     pair_width = conv_state.shape[1]
 
     small = jnp.concatenate(
-        [mixer_gain[:, None], dense_gain[:, None], jnp.zeros((mixer_gain.shape[0], 126), bf16)],
-        axis=1,
-    )
-    small = lax.dynamic_update_slice(small, conv_state.T, (0, 2))
-    joined = pair_join(jnp.concatenate([state_proj, small], axis=1))
+        [
+            jnp.concatenate([mixer_gain, dense_gain])[None],
+            jnp.pad(conv_state, ((0, 0), (0, 2 * mixer_gain.shape[0] - pair_width))),
+        ],
+        axis=0,
+    )
+    state_rows_full = pair_join(state_proj)
+    small_pair = pair_join(small[None])
+    gain_half = mixer_gain.shape[0]
+    small_rows = jnp.concatenate(
+        [
+            small_pair[:, 0, :gain_half].reshape(1, -1),
+            small_pair[:, 0, gain_half:].reshape(1, -1),
+            jnp.pad(
+                jnp.concatenate([small_pair[0, 1:, :pair_width], small_pair[1, 1:, :pair_width]], axis=1),
+                ((0, 0), (0, shard_rows - 2 * pair_width)),
+            ),
+        ],
+        axis=0,
+    )
+    small_block = jnp.pad(
+        small_rows, ((0, shard_rows - small_rows.shape[0]), (0, 128 - shard_rows))
+    )
     step_pad = jnp.zeros((shard_rows, 128 - heads_m), bf16)
     group_mix = jnp.concatenate(
         [
-            inner_proj.reshape(shard_rows, -1),
+            inner_proj[:, 0],
             query_proj,
             key_value_matrix.reshape(shard_rows, -1),
-            joined[:, :state_cols],
+            inner_proj[:, 1],
+            state_rows_full,
             step_proj,
             step_pad,
-            joined[:, state_cols:],
+            small_block,
             attend_proj.T,
             mamba_proj.T,
         ],
@@ -1139,9 +1220,9 @@
     offsets, place = {}, 0
     for name, width in (
         ("z", x_cols),
-        ("u", x_cols),
         ("q", q_cols),
         ("kv", kv_cols),
+        ("u", x_cols),
         ("state", state_cols),
         ("step", 128),
         ("end", 0),
@@ -1157,12 +1238,11 @@
 
     small_full = mix_full[:, offsets["end"] : out_first]
     w_proj = mix_full[:, : offsets["end"]]
-    gain_mix = small_full[:, 0].astype(f32)
-    gain_dense = small_full[:, 1].astype(f32)
-    conv_full = small_full[:, 2 : 2 + tap_count].reshape(
-        dp_count, 2, shard_rows // 2, tap_count
-    )[:, :, :pair_width]
-    conv_full = conv_full.reshape(dp_count * 2 * pair_width, tap_count).T.astype(f32)
+    small_full = small_full.reshape(dp_count, shard_rows, 128)
+    gain_mix = small_full[:, 0, :shard_rows].reshape(-1).astype(f32)
+    gain_dense = small_full[:, 1, :shard_rows].reshape(-1).astype(f32)
+    conv_full = small_full[:, 2 : 2 + tap_count, : 2 * pair_width].astype(f32)
+    conv_full = jnp.swapaxes(conv_full, 0, 1).reshape(tap_count, -1)
     conv_full = jnp.concatenate([conv_full, jnp.zeros((8 - tap_count, state_cols), f32)], axis=0)
     gain_gated = gated_gain.astype(f32)
     wide = jnp.concatenate(
@@ -1235,9 +1315,9 @@
     inverse_b = jnp.broadcast_to(inverse[:, None], live.shape)
     gated_rows = jnp.broadcast_to(gain_gated[None], (8, x_cols))
     first = (lax.axis_index("tensor") == 0).astype(bf16)
-    column_at = jnp.arange(x_cols) - (q_cols + kv_cols)
-    keep = jnp.where((column_at >= 0) & (column_at < state_cols), first, jnp.ones((), bf16))
-    keep = jnp.broadcast_to(keep[None], (8, x_cols))
+    last_cols = offsets["end"] + 128 - offsets["state"]
+    keep = jnp.where(jnp.arange(last_cols) < state_cols, first, jnp.ones((), bf16))
+    keep = jnp.broadcast_to(keep[None], (8, last_cols))
     ffn_split = reorder_columns(ffn_in_b, order)
 
     activated_b, grad_gate_b, grad_up_b, grad_ffn_part = feed_forward(
@@ -1290,7 +1370,7 @@
     held = down.make(held)
     down.send()
     dense_other = pair_swap(after(dense_own, *round_end))
-    grad_z_b, grad_u_b, grad_state_part, grad_step_b, wide_grad, conv_grad, extra_grad = (
+    grad_z_b, grad_u_b, grad_state_part, grad_step_b, wide_grad, extra_grad = (
         ssm_backward(
             after(grad_normed, held),
             mixed,
@@ -1307,7 +1387,9 @@
             offsets,
         )
     )
-    z_sum = Scatter(hidden_split, grad_z_b, bits)
+    head_cols = x_cols + q_cols + kv_cols
+    head_b = beside(head_cols, grad_z_b, grad_query_b, grad_key_b, grad_value_b)
+    z_sum = Scatter(hidden_split, head_b, bits)
     u_sum = Scatter(hidden_split, grad_u_b, bits)
     held = z_sum.begin(grad_state_part)
     ready = branch.prepare(held)
@@ -1321,18 +1403,10 @@
     up_sum.send()
     held = gate_sum.make(held)
     gate_sum.send()
-    held = down.make(held)
     held = u_sum.begin(held)
-    other_b = beside(
-        x_cols,
-        grad_query_b,
-        grad_key_b,
-        grad_value_b,
-        (grad_state_part, after(grad_state_other, held)),
-        grad_step_b,
-    )
+    other_b = beside(last_cols, (grad_state_part, after(grad_state_other, held)), grad_step_b)
     other_sum = Scatter(hidden_split, other_b, bits)
-    grad_hidden_own = hidden_back(after(grad_z_b, other_b), grad_u_b, other_b, keep, mix_full)
+    grad_hidden_own = hidden_back(after(head_b, other_b), grad_u_b, other_b, keep, mix_full)
     held = other_sum.begin(grad_hidden_own)
     ready = z_sum.prepare(held)
 
@@ -1340,77 +1414,89 @@
     held = z_sum.join(*round_end)
     z_sum.send()
     u_sum.send(*round_end)
-    half_rows = row_count // 2
-    hidden_top = pair_swap(after(grad_hidden_own[:half_rows], *round_end))
+    grad_hidden_other = pair_swap(after(grad_hidden_own, *round_end))
     held = branch.make(held)
     branch.send()
     held = up_sum.make(held)
     up_sum.send()
     held = gate_sum.make(held)
-    ready = u_sum.prepare(held)
-
-    round_end = (ready, z_sum.got[-1], u_sum.got[-1], branch.got[-1], up_sum.got[-1], hidden_top)
+    held = down.make(held)
+    red_down = turned_copy(after(down.finish(), held))
+    output = output_rows(middle, after(dense_own, red_down), dense_other, live)
+    ready = u_sum.prepare(output)
+    ready = z_sum.prepare(ready)
+    ready = branch.prepare(ready)
+    ready = up_sum.prepare(ready)
+
+    round_end = (ready, z_sum.got[-1], u_sum.got[-1], branch.got[-1], up_sum.got[-1], grad_hidden_other)
     held = u_sum.join(*round_end)
     u_sum.send()
     other_sum.send(*round_end)
-    hidden_end = pair_swap(after(grad_hidden_own[half_rows:], *round_end))
-    held = z_sum.make(held)
+    held = z_sum.join(held)
     z_sum.send()
-    held = branch.make(held)
+    held = branch.join(held)
     branch.send()
-    held = up_sum.make(held)
-    output = output_rows(middle, after(dense_own, held), dense_other, live)
-    ready = other_sum.prepare(output)
-
-    round_end = (ready, u_sum.got[-1], other_sum.got[-1], z_sum.got[-1], branch.got[-1], hidden_end)
-    held = other_sum.join(*round_end)
-    other_sum.send()
-    held = u_sum.make(held)
-    u_sum.send()
-    held = z_sum.make(held)
-    z_sum.send()
-    grad_hidden_other = jnp.concatenate([hidden_top, hidden_end], axis=0)
+    held = up_sum.join(held)
+    red_gateup = side_by_side(after(gate_sum.finish(), held), up_sum.finish())
     grad_tokens, grad_mixer_gain = rms_back(
-        tokens, gain_mix_rows, after(grad_hidden_own, held), grad_hidden_other, grad_middle, live, False
+        tokens, gain_mix_rows, after(grad_hidden_own, red_gateup), grad_hidden_other, grad_middle, live, False
     )
     own_sums = stack_rows(
         model_width,
-        (grad_mixer_gain, 1),
-        (grad_dense_gain, 1),
-        (wide_grad, tap_count + 1),
-        (column_part, 1),
-        (conv_grad, tap_count),
-        (extra_grad, 2),
-    )
-    sums = own_sums + across(own_sums, bits[0])
-    held = branch.make(sums)
-    ready = other_sum.prepare(held)
+        ((grad_mixer_gain,), 0, 1),
+        ((grad_dense_gain,), 0, 1),
+        ((wide_grad,), 0, tap_count + 1),
+        ((column_part,), 0, 1),
+        ((grad_state_part, grad_state_other), row_count, tap_count),
+        ((extra_grad,), 0, 2),
+    )
+    sums = add_rows(own_sums, across(own_sums, bits[0]))
+    ready = other_sum.prepare(sums)
     ready = u_sum.prepare(ready)
     ready = z_sum.prepare(ready)
-    others = across(after(sums, ready), bits[1])
-
-    round_end = (ready, other_sum.got[-1], u_sum.got[-1], z_sum.got[-1], others)
+    ready = branch.prepare(ready)
+
+    round_end = (ready, u_sum.got[-1], other_sum.got[-1], z_sum.got[-1], branch.got[-1])
     held = other_sum.join(*round_end)
     other_sum.send()
     held = u_sum.join(held)
     u_sum.send()
-    sums = after(sums, held) + others
+    others = across(after(sums, *round_end), bits[1])
+    held = z_sum.join(held)
+    z_sum.send()
+    held = branch.join(held)
+    red_branch = branch.finish()
+    red_attend = turned_copy(after(red_branch[:, :o_cols], held))
+    red_mamba = turned_copy(after(red_branch[:, o_cols:], red_attend))
+    ready = other_sum.prepare(red_mamba)
+    ready = u_sum.prepare(ready)
+    ready = z_sum.prepare(ready)
+
+    round_end = (ready, other_sum.got[-1], u_sum.got[-1], z_sum.got[-1], others)
+    held = other_sum.join(*round_end)
+    other_sum.send()
+    sums = add_rows(after(sums, held), others)
     others = across(sums, bits[2])
-    held = z_sum.join(sums)
+    held = u_sum.join(sums)
+    u_sum.send()
+    held = z_sum.join(held)
     ready = other_sum.prepare(held)
     ready = u_sum.prepare(ready)
 
     held = other_sum.join(ready, other_sum.got[-1], u_sum.got[-1], others)
     other_sum.send()
-    sums = after(sums, held) + others
-    for bit in bits[3:]:
-        sums = sums + across(sums, bit)
-    held = u_sum.join(held)
-    other_sum.prepare(held)
-    other_sum.join(sums)
+    sums = add_rows(after(sums, held), others)
+    others = across(sums, bits[3])
+    held = u_sum.join(sums)
+    ready = other_sum.prepare(held)
+    held = other_sum.join(ready)
+    red_head = after(z_sum.finish(), held)
+    red_inner = side_by_side(red_head[:, :x_cols], u_sum.finish())
+    sums = add_rows(after(sums, held), others)
+    for bit in bits[4:]:
+        sums = add_rows(sums, across(sums, bit))
     at = 2 + tap_count + 2
     conv_sum = sums[at : at + tap_count, :state_cols]
-    conv_sum = conv_sum + pair_swap(conv_sum)
     at += tap_count
     skip_sum = jnp.sum(sums[2 + tap_count, :x_cols].reshape(heads_m, HP), axis=1)
     owner = lax.axis_index("dp") * 2 + lax.axis_index("tensor")
@@ -1419,35 +1505,32 @@
         width = values.shape[axis_dim] // (2 * dp_count)
         return lax.dynamic_slice_in_dim(values, owner * width, width, axis_dim)
 
-    red_branch, red_other = branch.finish(), other_sum.finish()
+    red_other = other_sum.finish()
     state_rows = shard_rows // 2
-    state_first = q_cols + kv_cols
     red_state = lax.dynamic_slice_in_dim(
-        red_other[:, state_first : state_first + state_cols],
-        lax.axis_index("tensor") * state_rows,
-        state_rows,
-        0,
-    )
+        red_other[:, :state_cols], lax.axis_index("tensor") * state_rows, state_rows, 0
+    )
+    kv_first = x_cols + q_cols
     return (
         output,
         grad_tokens,
         own_part(sums[0], 0),
-        red_other[:, :q_cols],
-        red_other[:, q_cols:state_first].reshape(shard_rows, 2, -1),
-        red_branch[:, :o_cols].T,
-        jnp.stack([z_sum.finish(), u_sum.finish()], axis=1),
+        red_head[:, x_cols:kv_first],
+        red_head[:, kv_first:].reshape(shard_rows, 2, -1),
+        red_attend,
+        red_inner,
         red_state,
-        red_other[:, state_first + state_cols : state_first + state_cols + heads_m],
+        red_other[:, state_cols : state_cols + heads_m],
         sums[2 : 2 + tap_count, :x_cols],
         own_part(conv_sum, 1),
         sums[at, :heads_m],
         sums[at + 1, :heads_m],
         skip_sum,
         sums[3 + tap_count, :x_cols],
-        red_branch[:, o_cols:].T,
+        red_mamba,
         own_part(sums[1], 0),
-        jnp.stack([gate_sum.finish(), up_sum.finish()], axis=1),
-        down.finish().T,
+        red_gateup,
+        red_down,
     )
 
 

time: 739 us -> 736 us (level)
  waiting for transfers between devices: 287 us -> 319 us
  Pallas kernels: 271 us -> 248 us
  local copies, waits for them, and re-layouts: 71.7 us -> 56.9 us
    pallas_call x35, Pallas kernels: 112 us -> 79.6 us  [scatter_part(): pl.pallas_call(scatter_part_kernel, grid=(width // tile,), in_specs=[pl.B...]
    ppermute x10 -> x9, waiting for transfers between devices: 68.3 us -> 84.2 us  [pair_swap(): return lax.ppermute(values, 'tensor', [(0, 1), (1, 0)])]
    unnamed x294 -> x277, local copies, waits for them, and re-layouts: 56.7 us -> 41.1 us
    pallas_call x15 -> x28, Pallas kernels: 38.1 us -> 51.1 us  [the longest x7 17.3 us: join_parts(): pl.pallas_call(functools.partial(join_kernel, 0), grid=(width // tile,),...]
    ppermute x32, waiting for transfers between devices: 77 us -> 88.2 us  [across(): return lax.ppermute(values, 'dp', [(i, i ^ bit) for i in range(count)])]
    ppermute x32, starting transfers between devices: 28.6 us -> 37.3 us  [across(): return lax.ppermute(values, 'dp', [(i, i ^ bit) for i in range(count)])]
    ppermute x10 -> x9, starting transfers between devices: 15.2 us -> 8.92 us  [pair_swap(): return lax.ppermute(values, 'tensor', [(0, 1), (1, 0)])]
  transfers between devices with their start and end apart: 44 -> 43, of which waited for: 17 -> 23; matrix products, arithmetic and copies ran while one was open for 9% -> 7% of each run, Pallas kernels for 31% -> 28%
where the time goes in v3:
time: 736 us; the launch traced here: 732 us
  waiting for transfers between devices  319 us (43%)
  Pallas kernels  248 us (34%)
  local copies, waits for them, and re-layouts  56.9 us (8%)
  starting transfers between devices  46.4 us (6%)
  matrix products  23.6 us (3%)
  other arithmetic  20.9 us (3%)
  between operations  16.8 us (2%)
    all_gather x1, waiting for transfers between devices, local(): mix_full = lax.all_gather(group_mix, 'dp', axis=0, tiled=True)  137 us
    ppermute x32, waiting for transfers between devices, across(): return lax.ppermute(values, 'dp', [(i, i ^ bit) for i in range(count)])  88.2 us
    ppermute x9, waiting for transfers between devices, pair_swap(): return lax.ppermute(values, 'tensor', [(0, 1), (1, 0)])  84.2 us
    pallas_call x35, Pallas kernels, scatter_part(): pl.pallas_call(scatter_part_kernel, grid=(width // tile,), in_specs=[pl.B...  79.6 us
    unnamed x277, local copies, waits for them, and re-layouts  41.1 us
    ppermute x32, starting transfers between devices, across(): return lax.ppermute(values, 'dp', [(i, i ^ bit) for i in range(count)])  37.3 us
    pallas_call x1, Pallas kernels, feed_forward(): pl.pallas_call(feed_forward_kernel, grid=(steps,), in_specs=[whole, whole...  30.1 us
    pallas_call x1, Pallas kernels, ssm_backward(): pl.pallas_call(ssm_backward_kernel, grid=(pairs // 2,), in_specs=[plain,...  25.4 us
  transfers between devices with their start and end apart: 43, of which 23 were waited for; matrix products, arithmetic and copies ran while one was open for 7% of the time, Pallas kernels for 28%

profile of v3, /device:TPU:0, one launch (start us, length us, event | category | flops | bytes accessed | tf_op | source)
XLA Modules:
  0.0 732.3 jit_solution(157866048152728979)
XLA Ops:
  8.7 3.0 collective-permute-start.1
  11.8 2.8 fusion.36
  21.1 137.4 %all-gather.3.cloned.1.call-done.weight_ref = bf16[2048,6656]{1,0:T(8,128)(2,1)} async-done(((bf16[128,6656]{1,0:T(8,128)(2,1)}), bf16[2048,6656]{1,0:T(8,128)(2,1)}) %all-gather.3.cloned.1.call-update) | async-done | bytes 27262992 | tf_op jit(solution)/shard_map/all_gather | solution.py:1234
  163.5 2.1 fusion.10
  169.8 13.9 %fusion.q_ref.k_ref.v_ref.u_ref.z_ref.state_b_ref.state_c_ref.step_ref = f32[512,4480]{1,0:T(8,128)S(1)} fusion(bf16[512,2048]{1,0:T(8,128)(2,1)S(1)} %fusion.6.in_ref, bf16[2048,6656]{1,0:T(8,128)(2,1)} %all-gather.3.cloned.1.call-done.weight_ref), kind=kOutput, calls=%fused_computation | convolution fusion | flops 9395240960 | bytes 29622272 | tf_op jit(solution)/shard_map/td,dc->tc/dot_general | solution.py:26
  185.9 11.1 %ssm_forward.1 = (f32[512,1536]{1,0:T(8,128)S(1)}, f32[512,1536]{1,0:T(8,128)S(1)}, f32[512,128]{1,0:T(8,128)S(1)}) custom-call(f32[512,4480]{1,0:T(8,128)S(1)} %fusion.q_ref.k_ref.v_ref.u_ref.z_ref.state_b_ref.state_c_ref.step_ref, f32[512,4480]{1,0:T(8,128)S(1)} %fusion.q_ref.k_ref.v_ref.u_ref.z_ref.state_b_ref.state_c_ref.step_ref, ...), custom_call_target="tpu_custom_call" | custom-call | tf_op jit(solution)/shard_map/ssm_forward/pallas_call | solution.py:191
  203.5 4.0 copy-done.1
  208.6 4.7 attention_forward.1
  214.8 9.7 %fusion.7.own_ref = bf16[512,2048]{1,0:T(8,128)(2,1)} fusion(bf16[2048,6656]{1,0:T(8,128)(2,1)} %all-gather.3.cloned.1.call-done.weight_ref, bf16[512,1536]{1,0:T(8,128)(2,1)S(1)} %multiply_convert_fusion.1, bf16[512,512]{1,0:T(8,128)(2,1)S(1)} %get-tuple-element.154), kind=kOutput, calls=%fused_computation.11 | convolution fusion | flops 4300210176 | bytes 12582912 | tf_op jit(solution)/shard_map/tc,dc->td/dot_general | solution.py:26
  229.7 42.6 %collective-permute-done.3.other_ref = bf16[512,2048]{1,0:T(8,128)(2,1)} collective-permute-done((bf16[512,2048]{1,0:T(8,128)(2,1)}, bf16[512,2048]{1,0:T(8,128)(2,1)}, u32[]{:S(2)}, u32[]{:S(2)}) %collective-permute-start.3) | collective-permute-done | bytes 2097184 | tf_op jit(solution)/shard_map/ppermute | solution.py:1029
  272.3 3.2 rms_forward.1
  279.9 9.4 %all-gather.5.cloned.1.call-done.gate_w_ref.up_w_ref.down_ref.right_ref = bf16[2048,6144]{1,0:T(8,128)(2,1)} async-done(((bf16[128,6144]{1,0:T(8,128)(2,1)}), bf16[2048,6144]{1,0:T(8,128)(2,1)}) %all-gather.5.cloned.1.call-update) | async-done | bytes 25165840 | tf_op jit(solution)/shard_map/all_gather | solution.py:1235
  289.3 30.1 %feed_forward.1 = (bf16[512,2048]{1,0:T(8,128)(2,1)S(1)}, bf16[512,2048]{1,0:T(8,128)(2,1)S(1)}, bf16[512,2048]{1,0:T(8,128)(2,1)S(1)}, bf16[512,2048]{1,0:T(8,128)(2,1)}) custom-call(bf16[512,2048]{1,0:T(8,128)(2,1)} %copy-done.57, bf16[512,2048]{1,0:T(8,128)(2,1)} %copy-done.45, ...), custom_call_target="tpu_custom_call" | custom-call | flops 1 | bytes 1 | tf_op jit(solution)/shard_map/feed_forward/pallas_call | solution.py:566
  319.5 3.4 scatter_part.37
  323.2 4.5 scatter_part.38
  327.7 2.5 scatter_part.39.ready_ref
  332.0 2.3 join_parts.19
  335.5 8.2 %product_back.1.own_ref = bf16[512,2048]{1,0:T(8,128)(2,1)} custom-call(bf16[512,2048]{1,0:T(8,128)(2,1)S(1)} %get-tuple-element.161.left_ref.right_ref, bf16[2048,6144]{1,0:T(8,128)(2,1)} %all-gather.5.cloned.1.call-done.gate_w_ref.up_w_ref.down_ref.right_ref), custom_call_target="tpu_custom_call" | custom-call | flops 1 | bytes 1 | tf_op jit(solution)/shard_map/product_back/pallas_call | solution.py:736
  343.7 2.1 scatter_part.36.ready_ref
  345.8 4.5 scatter_part.43
  350.3 28.3 %collective-permute-done.7.other_ref = bf16[512,2048]{1,0:T(8,128)(2,1)} collective-permute-done((bf16[512,2048]{1,0:T(8,128)(2,1)}, bf16[512,2048]{1,0:T(8,128)(2,1)}, u32[]{:S(2)}, u32[]{:S(2)}) %collective-permute-start.7) | collective-permute-done | bytes 2097184 | tf_op jit(solution)/shard_map/ppermute | solution.py:1029
  378.6 3.5 collective-permute-done.5.refs_1_
  388.9 5.1 rms_back.2
  396.7 8.2 %norm_back.1 = (bf16[512,512]{1,0:T(8,128)(2,1)S(1)}, f32[512,1536]{1,0:T(8,128)S(1)}, f32[512,128]{1,0:T(8,128)S(1)}, f32[8,1536]{1,0:T(8,128)S(1)}) custom-call(bf16[512,2048]{1,0:T(8,128)(2,1)S(1)} %get-tuple-element.173.in_ref.grad_ref, bf16[2048,6656]{1,0:T(8,128)(2,1)} %all-gather.3.cloned.1.call-done.weight_ref, f32[512,1536]{1,0:T(8,128)S(1)} %copy-done.54, ...), custom_call_target="tpu_custom_call" | custom-call | flops 1 | bytes 1 | tf_op jit(solution)/shard_map/norm_back/pallas_call | solution.py:630
  407.9 4.5 scatter_part.41
  413.7 2.1 scatter_part.42.ready_ref
  415.9 5.8 attention_backward.1
  423.2 9.1 %collective-permute-done.8.refs_1_ = bf16[512,2048]{1,0:T(8,128)(2,1)S(1)} collective-permute-done((bf16[512,2048]{1,0:T(8,128)(2,1)}, bf16[512,2048]{1,0:T(8,128)(2,1)S(1)}, u32[]{:S(2)}, u32[]{:S(2)}) %collective-permute-start.8) | collective-permute-done | bytes 2097184 | tf_op jit(solution)/shard_map/ppermute | solution.py:1062
  432.4 3.7 join_parts.21
  438.0 2.3 copy-done.47
  442.7 2.4 scatter_part.45
  448.4 25.4 %ssm_backward.1 = (bf16[512,1536]{1,0:T(8,128)(2,1)S(1)}, bf16[512,1536]{1,0:T(8,128)(2,1)S(1)}, bf16[528,512]{1,0:T(8,128)(2,1)}, bf16[512,128]{1,0:T(8,128)(2,...) custom-call(f32[512,1536]{1,0:T(8,128)S(1)} %copy-done.80, f32[512,1536]{1,0:T(8,128)S(1)} %copy-done.78, ...), custom_call_target="tpu_custom_call" | custom-call | flops 1 | bytes 1 | tf_op jit(solution)/shard_map/ssm_backward/pallas_call | solution.py:352
  474.9 5.3 scatter_part.46
  485.2 3.2 join_parts.22
  489.4 3.6 scatter_part.48
  496.2 2.2 collective-permute-start.20
  499.8 3.7 scatter_part.50
  503.6 4.9 collective-permute-done.17.refs_1_.refs_5_
  511.5 15.1 %hidden_back.1.own_ref = bf16[512,2048]{1,0:T(8,128)(2,1)} custom-call(bf16[512,2304]{1,0:T(8,128)(2,1)S(1)} %copy-done.8, bf16[512,1536]{1,0:T(8,128)(2,1)S(1)} %copy-done.30, bf16[512,768]{1,0:T(8,128)(2,1)S(1)} %beside.3.third_ref.right_ref, bf16[8,768]{1,0:T(8,128)(2,1)S(1)} %broadcast_in_dim.47.keep_ref, ...), custom_call_target="tpu_custom_call" | custom-call | flops 1 | bytes 1 | tf_op jit(solution)/shard_map/hidden_back/pallas_call | solution.py:891
  526.6 2.2 scatter_part.51
  528.9 2.4 scatter_part.52.ready_ref
  531.4 5.2 collective-permute-done.18.refs_1_
  536.6 3.5 join_parts.23
  541.5 3.3 scatter_part.53
  546.4 2.9 scatter_part.54
  549.3 2.5 collective-permute-start.25
  557.9 3.5 output_rows.1
  563.2 2.1 scatter_part.58.ready_ref
  569.1 11.6 %collective-permute-done.25.got_ref = bf16[128,2048]{1,0:T(8,128)(2,1)} collective-permute-done((bf16[128,2048]{1,0:T(8,128)(2,1)}, bf16[128,2048]{1,0:T(8,128)(2,1)}, u32[]{:S(2)}, u32[]{:S(2)}) %collective-permute-start.25) | collective-permute-done | bytes 524320 | tf_op jit(solution)/shard_map/ppermute | solution.py:1062
  581.6 7.4 %collective-permute-done.26.other_ref = bf16[512,2048]{1,0:T(8,128)(2,1)} collective-permute-done((bf16[512,2048]{1,0:T(8,128)(2,1)}, bf16[512,2048]{1,0:T(8,128)(2,1)}, u32[]{:S(2)}, u32[]{:S(2)}) %collective-permute-start.26) | collective-permute-done | bytes 2097184 | tf_op jit(solution)/shard_map/ppermute | solution.py:1029
  589.0 5.1 collective-permute-done.22.got_ref.refs_1_
  594.1 2.5 join_parts.24
  597.5 2.9 join_parts.25
  602.8 2.4 collective-permute-start.31
  607.8 3.2 pad_maximum_fusion.1
  611.1 6.4 rms_back.3
  626.1 13.2 %collective-permute-done.31.got_ref = bf16[128,2048]{1,0:T(8,128)(2,1)} collective-permute-done((bf16[128,2048]{1,0:T(8,128)(2,1)}, bf16[128,2048]{1,0:T(8,128)(2,1)}, u32[]{:S(2)}, u32[]{:S(2)}) %collective-permute-start.31) | collective-permute-done | bytes 524320 | tf_op jit(solution)/shard_map/ppermute | solution.py:1062
  642.4 2.5 collective-permute-start.33
  657.6 9.0 %collective-permute-done.35.right_ref = f32[16,2048]{1,0:T(8,128)S(1)} collective-permute-done((f32[16,2048]{1,0:T(8,128)S(1)}, f32[16,2048]{1,0:T(8,128)S(1)}, u32[]{:S(2)}, u32[]{:S(2)}) %collective-permute-start.35) | collective-permute-done | bytes 131104 | tf_op jit(solution)/shard_map/ppermute | solution.py:1062
  666.6 7.6 %collective-permute-done.34.got_ref = bf16[128,2304]{1,0:T(8,128)(2,1)S(1)} collective-permute-done((bf16[128,2304]{1,0:T(8,128)(2,1)S(1)}, bf16[128,2304]{1,0:T(8,128)(2,1)S(1)}, u32[]{:S(2)}, u32[]{:S(2)}) %collective-permute-start.34) | collective-permute-done | bytes 589856 | tf_op jit(solution)/shard_map/ppermute | solution.py:1062
  675.1 2.7 collective-permute-start.37
  683.5 14.2 %collective-permute-done.38.right_ref = f32[16,2048]{1,0:T(8,128)S(1)} collective-permute-done((f32[16,2048]{1,0:T(8,128)S(1)}, f32[16,2048]{1,0:T(8,128)S(1)}, u32[]{:S(2)}, u32[]{:S(2)}) %collective-permute-start.38) | collective-permute-done | bytes 131104 | tf_op jit(solution)/shard_map/ppermute | solution.py:1062
  707.7 4.7 collective-permute-done.39.got_ref
  722.7 2.6 pad_maximum_fusion.3
  (477 shorter events, 149.8 us)
Async XLA Ops:
  7.2 151.4 %all-gather.3.cloned.1.call-start = ((), (), s32[]{:S(2)}) async-start(), calls=%async_computation | async-start | bytes 28966912 | tf_op jit(solution)/shard_map/all_gather | solution.py:1234
  8.7 7.1 collective-permute-start.1
  11.7 4.5 collective-permute-start
  18.2 271.1 %all-gather.5.cloned.1.call-start = ((), (), s32[]{:S(2)}) async-start(), calls=%async_computation.1 | async-start | bytes 26738688 | tf_op jit(solution)/shard_map/all_gather | solution.py:1235
  19.8 139.4 %copy-start.123 = (s32[512]{0:T(512)S(1)}, s32[512]{0:T(512)}, u32[]{:S(2)}) copy-start(s32[512]{0:T(512)} %param.28) | copy-start | bytes 6148
  19.8 140.0 %copy-start.122 = (bf16[1536]{0:T(1024)(128)(2,1)S(1)}, bf16[1536]{0:T(1024)(128)(2,1)}, u32[]{:S(2)}) copy-start(bf16[1536]{0:T(1024)(128)(2,1)} %param.42) | copy-start | bytes 9220
  19.8 140.0 %copy-start.128 = (bf16[24]{0:T(256)(128)(2,1)S(1)}, bf16[24]{0:T(256)(128)(2,1)}, u32[]{:S(2)}) copy-start(bf16[24]{0:T(256)(128)(2,1)} %param.41) | copy-start | bytes 148
  19.8 140.2 %copy-start.125 = (bf16[5,1536]{1,0:T(8,128)(2,1)S(1)}, bf16[5,1536]{1,0:T(8,128)(2,1)}, u32[]{:S(2)}) copy-start(bf16[5,1536]{1,0:T(8,128)(2,1)} %param.37) | copy-start | bytes 46084
  19.9 140.2 %copy-start.129 = (bf16[24]{0:T(256)(128)(2,1)S(1)}, bf16[24]{0:T(256)(128)(2,1)}, u32[]{:S(2)}) copy-start(bf16[24]{0:T(256)(128)(2,1)} %param.39) | copy-start | bytes 148
  19.9 140.2 %copy-start.130 = (bf16[24]{0:T(256)(128)(2,1)S(1)}, bf16[24]{0:T(256)(128)(2,1)}, u32[]{:S(2)}) copy-start(bf16[24]{0:T(256)(128)(2,1)} %param.40) | copy-start | bytes 148
  21.1 139.9 %copy-start.41 = (bf16[512,2048]{1,0:T(8,128)(2,1)S(1)}, bf16[512,2048]{1,0:T(8,128)(2,1)}, u32[]{:S(2)}) copy-start(bf16[512,2048]{1,0:T(8,128)(2,1)} %value_ref.1) | copy-start | bytes 6291460
  169.8 13.9 %copy-start.58 = (bf16[512,2048]{1,0:T(8,128)(2,1)}, bf16[512,2048]{1,0:T(8,128)(2,1)S(1)}, u32[]{:S(2)}) copy-start(bf16[512,2048]{1,0:T(8,128)(2,1)S(1)} %fusion.6.in_ref) | copy-start | bytes 6291460
  200.5 13.0 %collective-permute-start.2 = (f32[512]{0:T(512)S(1)}, f32[512]{0:T(512)S(1)}, u32[]{:S(2)}, u32[]{:S(2)}) collective-permute-start(f32[512]{0:T(512)S(1)} %reduce_sum.28), channel_id=1, source_target_pairs={{0,1},{1,0},{2,3},{3,2},{4,5},{5,4},{6,7},{7,6},{8,9},{9,8},{10,11... | collective-permute-start | bytes 6152 | tf_op jit(solution)/shard_map/ppermute | solution.py:1029
  224.5 47.8 %collective-permute-start.3 = (bf16[512,2048]{1,0:T(8,128)(2,1)}, bf16[512,2048]{1,0:T(8,128)(2,1)}, u32[]{:S(2)}, u32[]{:S(2)}) collective-permute-start(bf16[512,2048]{1,0:T(8,128)(2,1)} %fusion.7.own_ref), channel_id=1, source_target_pairs={{0,1},{1,0},{2,3},{3,2},{4,5},{5,4},{6,7},{7,6},{8,9},{9,8},{10,11... | collective-permute-start | bytes 6291464 | tf_op jit(solution)/shard_map/ppermute | solution.py:1029
  227.1 45.2 %copy-start.124 = (f32[16,1,128]{2,1,0:T(1,128)S(1)}, f32[16,1,128]{2,1,0:T(1,128)}, u32[]{:S(2)}) copy-start(f32[16,1,128]{2,1,0:T(1,128)} %get-tuple-element.309) | copy-start | bytes 24580
  279.9 158.1 %copy-start.4 = (bf16[512,2048]{1,0:T(8,128)(2,1)}, bf16[512,2048]{1,0:T(8,128)(2,1)S(1)}, u32[]{:S(2)}) copy-start(bf16[512,2048]{1,0:T(8,128)(2,1)S(1)} %reorder_columns.4.left_ref) | copy-start | bytes 6291460
  289.3 30.1 %copy-start.18 = (bf16[512,2048]{1,0:T(8,128)(2,1)S(1)}, bf16[512,2048]{1,0:T(8,128)(2,1)}, u32[]{:S(2)}) copy-start(bf16[512,2048]{1,0:T(8,128)(2,1)} %copy-done.17) | copy-start | bytes 6291460
  319.5 24.2 %copy-start.31 = (bf16[512,2048]{1,0:T(8,128)(2,1)}, bf16[512,2048]{1,0:T(8,128)(2,1)S(1)}, u32[]{:S(2)}) copy-start(bf16[512,2048]{1,0:T(8,128)(2,1)S(1)} %get-tuple-element.164.right_ref) | copy-start | bytes 6291460
  319.5 65.8 %copy-start.9 = (bf16[512,2048]{1,0:T(8,128)(2,1)}, bf16[512,2048]{1,0:T(8,128)(2,1)S(1)}, u32[]{:S(2)}) copy-start(bf16[512,2048]{1,0:T(8,128)(2,1)S(1)} %get-tuple-element.161.left_ref.right_ref) | copy-start | bytes 6291460
  322.9 9.1 %collective-permute-start.4 = (bf16[1024,2048]{1,0:T(8,128)(2,1)S(1)}, bf16[1024,2048]{1,0:T(8,128)(2,1)S(1)}, u32[]{:S(2)}, u32[]{:S(2)}) collective-permute-start(bf16[1024,2048]{1,0:T(8,128)(2,1)S(1)} %scatter_part.37), channel_id=1, source_target_pairs={{0,2},{2,0},{4,6},{6,4},{8,10},{10,8},{12,14},{14,12},{16,18},{18,... | collective-permute-start | bytes 12582920 | tf_op jit(solution)/shard_map/ppermute | solution.py:1062
  330.2 48.4 %collective-permute-start.6 = (bf16[1024,2048]{1,0:T(8,128)(2,1)}, bf16[1024,2048]{1,0:T(8,128)(2,1)S(1)}, u32[]{:S(2)}, u32[]{:S(2)}) collective-permute-start(bf16[1024,2048]{1,0:T(8,128)(2,1)} %scatter_part.38), channel_id=1, source_target_pairs={{0,2},{2,0},{4,6},{6,4},{8,10},{10,8},{12,14},{14,12},{16,18},{18,... | collective-permute-start | bytes 12582920 | tf_op jit(solution)/shard_map/ppermute | solution.py:1062
  330.5 48.1 %collective-permute-start.7 = (bf16[512,2048]{1,0:T(8,128)(2,1)}, bf16[512,2048]{1,0:T(8,128)(2,1)}, u32[]{:S(2)}, u32[]{:S(2)}) collective-permute-start(bf16[512,2048]{1,0:T(8,128)(2,1)} %get-tuple-element.172.own_ref), channel_id=1, source_target_pairs={{0,1},{1,0},{2,3},{3,2},{4,5},{5,4},{6,7},{7,6},{8,9},{9,8},{10,11... | collective-permute-start | bytes 6291464 | tf_op jit(solution)/shard_map/ppermute | solution.py:1029
  332.0 53.3 %copy-start.21 = (bf16[1024,2048]{1,0:T(8,128)(2,1)}, bf16[1024,2048]{1,0:T(8,128)(2,1)S(1)}, u32[]{:S(2)}) copy-start(bf16[1024,2048]{1,0:T(8,128)(2,1)S(1)} %collective-permute-done.4.got_ref.refs_0_) | copy-start | bytes 12582916
  334.3 47.8 %collective-permute-start.5 = (bf16[512,2048]{1,0:T(8,128)(2,1)}, bf16[512,2048]{1,0:T(8,128)(2,1)}, u32[]{:S(2)}, u32[]{:S(2)}) collective-permute-start(bf16[512,2048]{1,0:T(8,128)(2,1)} %join_parts.19), channel_id=1, source_target_pairs={{0,4},{2,6},{4,0},{6,2},{8,12},{10,14},{12,8},{14,10},{16,20},{18,... | collective-permute-start | bytes 6291464 | tf_op jit(solution)/shard_map/ppermute | solution.py:1062
  382.1 50.2 %collective-permute-start.9 = (bf16[1024,2048]{1,0:T(8,128)(2,1)}, bf16[1024,2048]{1,0:T(8,128)(2,1)}, u32[]{:S(2)}, u32[]{:S(2)}) collective-permute-start(bf16[1024,2048]{1,0:T(8,128)(2,1)} %scatter_part.43), channel_id=1, source_target_pairs={{0,2},{2,0},{4,6},{6,4},{8,10},{10,8},{12,14},{14,12},{16,18},{18,... | collective-permute-start | bytes 12582920 | tf_op jit(solution)/shard_map/ppermute | solution.py:1062
  384.0 48.3 %collective-permute-start.8 = (bf16[512,2048]{1,0:T(8,128)(2,1)}, bf16[512,2048]{1,0:T(8,128)(2,1)S(1)}, u32[]{:S(2)}, u32[]{:S(2)}) collective-permute-start(bf16[512,2048]{1,0:T(8,128)(2,1)} %join_parts.20), channel_id=1, source_target_pairs={{0,4},{2,6},{4,0},{6,2},{8,12},{10,14},{12,8},{14,10},{16,20},{18,... | collective-permute-start | bytes 6291464 | tf_op jit(solution)/shard_map/ppermute | solution.py:1062
  387.3 35.9 %collective-permute-start.10 = (bf16[256,2048]{1,0:T(8,128)(2,1)S(1)}, bf16[256,2048]{1,0:T(8,128)(2,1)S(1)}, u32[]{:S(2)}, u32[]{:S(2)}) collective-permute-start(bf16[256,2048]{1,0:T(8,128)(2,1)S(1)} %scatter_part.40), channel_id=1, source_target_pairs={{0,8},{2,10},{4,12},{6,14},{8,0},{10,2},{12,4},{14,6},{16,24},{18,... | collective-permute-start | bytes 3145736 | tf_op jit(solution)/shard_map/ppermute | solution.py:1062
  405.0 18.2 %collective-permute-start.11 = (f32[512,128]{1,0:T(8,128)S(1)}, f32[512,128]{1,0:T(8,128)S(1)}, u32[]{:S(2)}, u32[]{:S(2)}) collective-permute-start(f32[512,128]{1,0:T(8,128)S(1)} %get-tuple-element.175.own_ref), channel_id=1, source_target_pairs={{0,1},{1,0},{2,3},{3,2},{4,5},{5,4},{6,7},{7,6},{8,9},{9,8},{10,11... | collective-permute-start | bytes 786440 | tf_op jit(solution)/shard_map/ppermute | solution.py:1029
  406.7 73.6 %copy-start.12 = (bf16[512,2048]{1,0:T(8,128)(2,1)}, bf16[512,2048]{1,0:T(8,128)(2,1)S(1)}, u32[]{:S(2)}) copy-start(bf16[512,2048]{1,0:T(8,128)(2,1)S(1)} %pad_maximum_fusion.right_ref) | copy-start | bytes 6291460
  423.2 19.5 %copy-start.65 = (bf16[256,2048]{1,0:T(8,128)(2,1)}, bf16[256,2048]{1,0:T(8,128)(2,1)S(1)}, u32[]{:S(2)}) copy-start(bf16[256,2048]{1,0:T(8,128)(2,1)S(1)} %collective-permute-done.10.refs_2_) | copy-start | bytes 3145732
  432.3 52.9 %collective-permute-start.14 = (bf16[1024,2048]{1,0:T(8,128)(2,1)}, bf16[1024,2048]{1,0:T(8,128)(2,1)}, u32[]{:S(2)}, u32[]{:S(2)}) collective-permute-start(bf16[1024,2048]{1,0:T(8,128)(2,1)} %scatter_part.41), channel_id=1, source_target_pairs={{0,2},{2,0},{4,6},{6,4},{8,10},{10,8},{12,14},{14,12},{16,18},{18,... | collective-permute-start | bytes 12582920 | tf_op jit(solution)/shard_map/ppermute | solution.py:1062
  436.1 48.1 %collective-permute-start.12 = (bf16[512,2048]{1,0:T(8,128)(2,1)}, bf16[512,2048]{1,0:T(8,128)(2,1)}, u32[]{:S(2)}, u32[]{:S(2)}) collective-permute-start(bf16[512,2048]{1,0:T(8,128)(2,1)} %join_parts.21), channel_id=1, source_target_pairs={{0,4},{2,6},{4,0},{6,2},{8,12},{10,14},{12,8},{14,10},{16,20},{18,... | collective-permute-start | bytes 6291464 | tf_op jit(solution)/shard_map/ppermute | solution.py:1062
  437.4 47.8 %collective-permute-start.16 = (bf16[512,2048]{1,0:T(8,128)(2,1)}, bf16[512,2048]{1,0:T(8,128)(2,1)}, u32[]{:S(2)}, u32[]{:S(2)}) collective-permute-start(bf16[512,2048]{1,0:T(8,128)(2,1)} %product_back.1.own_ref), channel_id=1, source_target_pairs={{0,1},{1,0},{2,3},{3,2},{4,5},{5,4},{6,7},{7,6},{8,9},{9,8},{10,11... | collective-permute-start | bytes 6291464 | tf_op jit(solution)/shard_map/ppermute | solution.py:1029
  441.1 42.7 %collective-permute-start.13 = (bf16[256,2048]{1,0:T(8,128)(2,1)S(1)}, bf16[256,2048]{1,0:T(8,128)(2,1)S(1)}, u32[]{:S(2)}, u32[]{:S(2)}) collective-permute-start(bf16[256,2048]{1,0:T(8,128)(2,1)S(1)} %scatter_part.44), channel_id=1, source_target_pairs={{0,8},{2,10},{4,12},{6,14},{8,0},{10,2},{12,4},{14,6},{16,24},{18,... | collective-permute-start | bytes 3145736 | tf_op jit(solution)/shard_map/ppermute | solution.py:1062
  445.1 38.6 %collective-permute-start.15 = (bf16[128,2048]{1,0:T(8,128)(2,1)S(1)}, bf16[128,2048]{1,0:T(8,128)(2,1)S(1)}, u32[]{:S(2)}, u32[]{:S(2)}) collective-permute-start(bf16[128,2048]{1,0:T(8,128)(2,1)S(1)} %scatter_part.45), channel_id=1, source_target_pairs={{0,16},{2,18},{4,20},{6,22},{8,24},{10,26},{12,28},{14,30},{16,0},... | collective-permute-start | bytes 1572872 | tf_op jit(solution)/shard_map/ppermute | solution.py:1062
  448.3 26.7 %copy-start.2 = (bf16[512,2048]{1,0:T(8,128)(2,1)}, bf16[512,2048]{1,0:T(8,128)(2,1)S(1)}, u32[]{:S(2)}) copy-start(bf16[512,2048]{1,0:T(8,128)(2,1)S(1)} %reorder_columns.7.left_ref) | copy-start | bytes 6291460
  448.3 25.4 %copy-start.93 = (bf16[512,512]{1,0:T(8,128)(2,1)S(1)}, bf16[512,512]{1,0:T(8,128)(2,1)}, u32[]{:S(2)}) copy-start(bf16[512,512]{1,0:T(8,128)(2,1)} %copy-done.92) | copy-start | bytes 1572868
  448.4 25.4 %copy-start.105 = (bf16[512,128]{1,0:T(8,128)(2,1)S(1)}, bf16[512,128]{1,0:T(8,128)(2,1)}, u32[]{:S(2)}) copy-start(bf16[512,128]{1,0:T(8,128)(2,1)} %copy-done.104) | copy-start | bytes 393220
  485.2 51.4 %collective-permute-start.21 = (bf16[1024,2304]{1,0:T(8,128)(2,1)}, bf16[1024,2304]{1,0:T(8,128)(2,1)}, u32[]{:S(2)}, u32[]{:S(2)}) collective-permute-start(bf16[1024,2304]{1,0:T(8,128)(2,1)} %scatter_part.46), channel_id=1, source_target_pairs={{0,2},{2,0},{4,6},{6,4},{8,10},{10,8},{12,14},{14,12},{16,18},{18,... | collective-permute-start | bytes 14155784 | tf_op jit(solution)/shard_map/ppermute | solution.py:1062
  488.4 48.2 %collective-permute-start.18 = (bf16[512,2048]{1,0:T(8,128)(2,1)}, bf16[512,2048]{1,0:T(8,128)(2,1)}, u32[]{:S(2)}, u32[]{:S(2)}) collective-permute-start(bf16[512,2048]{1,0:T(8,128)(2,1)} %join_parts.22), channel_id=1, source_target_pairs={{0,4},{2,6},{4,0},{6,2},{8,12},{10,14},{12,8},{14,10},{16,20},{18,... | collective-permute-start | bytes 6291464 | tf_op jit(solution)/shard_map/ppermute | solution.py:1062
  493.0 38.4 %collective-permute-start.19 = (bf16[256,2048]{1,0:T(8,128)(2,1)}, bf16[256,2048]{1,0:T(8,128)(2,1)}, u32[]{:S(2)}, u32[]{:S(2)}) collective-permute-start(bf16[256,2048]{1,0:T(8,128)(2,1)} %scatter_part.48), channel_id=1, source_target_pairs={{0,8},{2,10},{4,12},{6,14},{8,0},{10,2},{12,4},{14,6},{16,24},{18,... | collective-permute-start | bytes 3145736 | tf_op jit(solution)/shard_map/ppermute | solution.py:1062
  494.2 14.3 %collective-permute-start.17 = (bf16[528,512]{1,0:T(8,128)(2,1)}, bf16[528,512]{1,0:T(8,128)(2,1)S(1)}, u32[]{:S(2)}, u32[]{:S(2)}) collective-permute-start(bf16[528,512]{1,0:T(8,128)(2,1)} %get-tuple-element.201.refs_0_.refs_4_), channel_id=1, source_target_pairs={{0,1},{1,0},{2,3},{3,2},{4,5},{5,4},{6,7},{7,6},{8,9},{9,8},{10,11... | collective-permute-start | bytes 1622024 | tf_op jit(solution)/shard_map/ppermute | solution.py:1029
  496.2 35.1 %collective-permute-start.20 = (bf16[128,2048]{1,0:T(8,128)(2,1)}, bf16[128,2048]{1,0:T(8,128)(2,1)}, u32[]{:S(2)}, u32[]{:S(2)}) collective-permute-start(bf16[128,2048]{1,0:T(8,128)(2,1)} %scatter_part.49), channel_id=1, source_target_pairs={{0,16},{2,18},{4,20},{6,22},{8,24},{10,26},{12,28},{14,30},{16,0},... | collective-permute-start | bytes 1572872 | tf_op jit(solution)/shard_map/ppermute | solution.py:1062
  536.6 57.6 %collective-permute-start.23 = (bf16[1024,1536]{1,0:T(8,128)(2,1)}, bf16[1024,1536]{1,0:T(8,128)(2,1)}, u32[]{:S(2)}, u32[]{:S(2)}) collective-permute-start(bf16[1024,1536]{1,0:T(8,128)(2,1)} %scatter_part.50), channel_id=1, source_target_pairs={{0,2},{2,0},{4,6},{6,4},{8,10},{10,8},{12,14},{14,12},{16,18},{18,... | collective-permute-start | bytes 9437192 | tf_op jit(solution)/shard_map/ppermute | solution.py:1062
  540.1 54.0 %collective-permute-start.22 = (bf16[512,2304]{1,0:T(8,128)(2,1)}, bf16[512,2304]{1,0:T(8,128)(2,1)}, u32[]{:S(2)}, u32[]{:S(2)}) collective-permute-start(bf16[512,2304]{1,0:T(8,128)(2,1)} %join_parts.23), channel_id=1, source_target_pairs={{0,4},{2,6},{4,0},{6,2},{8,12},{10,14},{12,8},{14,10},{16,20},{18,... | collective-permute-start | bytes 7077896 | tf_op jit(solution)/shard_map/ppermute | solution.py:1062
  541.0 48.1 %collective-permute-start.26 = (bf16[512,2048]{1,0:T(8,128)(2,1)}, bf16[512,2048]{1,0:T(8,128)(2,1)}, u32[]{:S(2)}, u32[]{:S(2)}) collective-permute-start(bf16[512,2048]{1,0:T(8,128)(2,1)} %hidden_back.1.own_ref), channel_id=1, source_target_pairs={{0,1},{1,0},{2,3},{3,2},{4,5},{5,4},{6,7},{7,6},{8,9},{9,8},{10,11... | collective-permute-start | bytes 6291464 | tf_op jit(solution)/shard_map/ppermute | solution.py:1029
  544.9 36.8 %collective-permute-start.24 = (bf16[256,2048]{1,0:T(8,128)(2,1)}, bf16[256,2048]{1,0:T(8,128)(2,1)S(1)}, u32[]{:S(2)}, u32[]{:S(2)}) collective-permute-start(bf16[256,2048]{1,0:T(8,128)(2,1)} %scatter_part.53), channel_id=1, source_target_pairs={{0,8},{2,10},{4,12},{6,14},{8,0},{10,2},{12,4},{14,6},{16,24},{18,... | collective-permute-start | bytes 3145736 | tf_op jit(solution)/shard_map/ppermute | solution.py:1062
  549.3 31.5 %collective-permute-start.25 = (bf16[128,2048]{1,0:T(8,128)(2,1)}, bf16[128,2048]{1,0:T(8,128)(2,1)}, u32[]{:S(2)}, u32[]{:S(2)}) collective-permute-start(bf16[128,2048]{1,0:T(8,128)(2,1)} %scatter_part.54), channel_id=1, source_target_pairs={{0,16},{2,18},{4,20},{6,22},{8,24},{10,26},{12,28},{14,30},{16,0},... | collective-permute-start | bytes 1572872 | tf_op jit(solution)/shard_map/ppermute | solution.py:1062
  581.6 20.2 %copy-start.69 = (bf16[256,2048]{1,0:T(8,128)(2,1)}, bf16[256,2048]{1,0:T(8,128)(2,1)S(1)}, u32[]{:S(2)}) copy-start(bf16[256,2048]{1,0:T(8,128)(2,1)S(1)} %collective-permute-done.24.got_ref.refs_2_) | copy-start | bytes 3145732
  596.6 43.6 %collective-permute-start.28 = (bf16[512,1536]{1,0:T(8,128)(2,1)}, bf16[512,1536]{1,0:T(8,128)(2,1)}, u32[]{:S(2)}, u32[]{:S(2)}) collective-permute-start(bf16[512,1536]{1,0:T(8,128)(2,1)} %join_parts.24), channel_id=1, source_target_pairs={{0,4},{2,6},{4,0},{6,2},{8,12},{10,14},{12,8},{14,10},{16,20},{18,... | collective-permute-start | bytes 4718600 | tf_op jit(solution)/shard_map/ppermute | solution.py:1062
  597.5 42.8 %collective-permute-start.29 = (bf16[1024,768]{1,0:T(8,128)(2,1)}, bf16[1024,768]{1,0:T(8,128)(2,1)S(1)}, u32[]{:S(2)}, u32[]{:S(2)}) collective-permute-start(bf16[1024,768]{1,0:T(8,128)(2,1)} %scatter_part.51), channel_id=1, source_target_pairs={{0,2},{2,0},{4,6},{6,4},{8,10},{10,8},{12,14},{14,12},{16,18},{18,... | collective-permute-start | bytes 4718600 | tf_op jit(solution)/shard_map/ppermute | solution.py:1062
  600.3 39.9 %collective-permute-start.30 = (bf16[256,2304]{1,0:T(8,128)(2,1)}, bf16[256,2304]{1,0:T(8,128)(2,1)}, u32[]{:S(2)}, u32[]{:S(2)}) collective-permute-start(bf16[256,2304]{1,0:T(8,128)(2,1)} %join_parts.25), channel_id=1, source_target_pairs={{0,8},{2,10},{4,12},{6,14},{8,0},{10,2},{12,4},{14,6},{16,24},{18,... | collective-permute-start | bytes 3538952 | tf_op jit(solution)/shard_map/ppermute | solution.py:1062
  602.8 36.5 %collective-permute-start.31 = (bf16[128,2048]{1,0:T(8,128)(2,1)}, bf16[128,2048]{1,0:T(8,128)(2,1)}, u32[]{:S(2)}, u32[]{:S(2)}) collective-permute-start(bf16[128,2048]{1,0:T(8,128)(2,1)} %join_parts.26), channel_id=1, source_target_pairs={{0,16},{2,18},{4,20},{6,22},{8,24},{10,26},{12,28},{14,30},{16,0},... | collective-permute-start | bytes 1572872 | tf_op jit(solution)/shard_map/ppermute | solution.py:1062
  618.6 1.4 collective-permute-start.27
  640.3 39.7 %copy-start.43 = (bf16[1024,768]{1,0:T(8,128)(2,1)}, bf16[1024,768]{1,0:T(8,128)(2,1)S(1)}, u32[]{:S(2)}) copy-start(bf16[1024,768]{1,0:T(8,128)(2,1)S(1)} %collective-permute-done.29.got_ref.refs_0_) | copy-start | bytes 4718596
  642.4 32.5 %collective-permute-start.33 = (bf16[256,1536]{1,0:T(8,128)(2,1)S(1)}, bf16[256,1536]{1,0:T(8,128)(2,1)S(1)}, u32[]{:S(2)}, u32[]{:S(2)}) collective-permute-start(bf16[256,1536]{1,0:T(8,128)(2,1)S(1)} %join_parts.29), channel_id=1, source_target_pairs={{0,8},{2,10},{4,12},{6,14},{8,0},{10,2},{12,4},{14,6},{16,24},{18,... | collective-permute-start | bytes 2359304 | tf_op jit(solution)/shard_map/ppermute | solution.py:1062
  644.9 30.1 %collective-permute-start.32 = (bf16[512,768]{1,0:T(8,128)(2,1)S(1)}, bf16[512,768]{1,0:T(8,128)(2,1)S(1)}, u32[]{:S(2)}, u32[]{:S(2)}) collective-permute-start(bf16[512,768]{1,0:T(8,128)(2,1)S(1)} %join_parts.28), channel_id=1, source_target_pairs={{0,4},{2,6},{4,0},{6,2},{8,12},{10,14},{12,8},{14,10},{16,20},{18,... | collective-permute-start | bytes 2359304 | tf_op jit(solution)/shard_map/ppermute | solution.py:1062
  647.5 26.7 %collective-permute-start.34 = (bf16[128,2304]{1,0:T(8,128)(2,1)S(1)}, bf16[128,2304]{1,0:T(8,128)(2,1)S(1)}, u32[]{:S(2)}, u32[]{:S(2)}) collective-permute-start(bf16[128,2304]{1,0:T(8,128)(2,1)S(1)} %join_parts.30), channel_id=1, source_target_pairs={{0,16},{2,18},{4,20},{6,22},{8,24},{10,26},{12,28},{14,30},{16,0},... | collective-permute-start | bytes 1769480 | tf_op jit(solution)/shard_map/ppermute | solution.py:1062
  648.3 18.3 %collective-permute-start.35 = (f32[16,2048]{1,0:T(8,128)S(1)}, f32[16,2048]{1,0:T(8,128)S(1)}, u32[]{:S(2)}, u32[]{:S(2)}) collective-permute-start(f32[16,2048]{1,0:T(8,128)S(1)} %add_rows.4.left_ref), channel_id=1, source_target_pairs={{0,4},{2,6},{4,0},{6,2},{8,12},{10,14},{12,8},{14,10},{16,20},{18,... | collective-permute-start | bytes 393224 | tf_op jit(solution)/shard_map/ppermute | solution.py:1062
  675.1 22.6 %collective-permute-start.37 = (bf16[128,1536]{1,0:T(8,128)(2,1)S(1)}, bf16[128,1536]{1,0:T(8,128)(2,1)S(1)}, u32[]{:S(2)}, u32[]{:S(2)}) collective-permute-start(bf16[128,1536]{1,0:T(8,128)(2,1)S(1)} %join_parts.33), channel_id=1, source_target_pairs={{0,16},{2,18},{4,20},{6,22},{8,24},{10,26},{12,28},{14,30},{16,0},... | collective-permute-start | bytes 1179656 | tf_op jit(solution)/shard_map/ppermute | solution.py:1062
  677.8 19.9 %collective-permute-start.36 = (bf16[256,768]{1,0:T(8,128)(2,1)S(1)}, bf16[256,768]{1,0:T(8,128)(2,1)S(1)}, u32[]{:S(2)}, u32[]{:S(2)}) collective-permute-start(bf16[256,768]{1,0:T(8,128)(2,1)S(1)} %join_parts.32), channel_id=1, source_target_pairs={{0,8},{2,10},{4,12},{6,14},{8,0},{10,2},{12,4},{14,6},{16,24},{18,... | collective-permute-start | bytes 1179656 | tf_op jit(solution)/shard_map/ppermute | solution.py:1062
  678.4 19.3 %collective-permute-start.38 = (f32[16,2048]{1,0:T(8,128)S(1)}, f32[16,2048]{1,0:T(8,128)S(1)}, u32[]{:S(2)}, u32[]{:S(2)}) collective-permute-start(f32[16,2048]{1,0:T(8,128)S(1)} %add_rows.5.left_ref), channel_id=1, source_target_pairs={{0,8},{2,10},{4,12},{6,14},{8,0},{10,2},{12,4},{14,6},{16,24},{18,... | collective-permute-start | bytes 393224 | tf_op jit(solution)/shard_map/ppermute | solution.py:1062
  698.5 13.9 %collective-permute-start.39 = (bf16[128,768]{1,0:T(8,128)(2,1)}, bf16[128,768]{1,0:T(8,128)(2,1)}, u32[]{:S(2)}, u32[]{:S(2)}) collective-permute-start(bf16[128,768]{1,0:T(8,128)(2,1)} %join_parts.35), channel_id=1, source_target_pairs={{0,16},{2,18},{4,20},{6,22},{8,24},{10,26},{12,28},{14,30},{16,0},... | collective-permute-start | bytes 589832 | tf_op jit(solution)/shard_map/ppermute | solution.py:1062
  700.4 13.6 %collective-permute-start.40 = (f32[16,2048]{1,0:T(8,128)}, f32[16,2048]{1,0:T(8,128)}, u32[]{:S(2)}, u32[]{:S(2)}) collective-permute-start(f32[16,2048]{1,0:T(8,128)} %add_rows.6.left_ref), channel_id=1, source_target_pairs={{0,16},{2,18},{4,20},{6,22},{8,24},{10,26},{12,28},{14,30},{16,0},... | collective-permute-start | bytes 393224 | tf_op jit(solution)/shard_map/ppermute | solution.py:1062
  (116 other events, 489.3 us)
Sparse Core Ops, SparseCore 0:
  18.4 140.1 all-gather.2
  160.7 128.5 all-gather.4

commit v4 on v3

--- a/solution.py
+++ b/solution.py
@@ -859,43 +859,31 @@
     )(*arrays)
 
 
-def hidden_back_kernel(
-    first_ref, second_ref, third_ref, keep_ref, weight_ref, out_ref, total, *, ends
-):
+def hidden_back_kernel(left_ref, keep_ref, weight_ref, out_ref, total):
     step = pl.program_id(0)
+    last = pl.num_programs(0) - 1
 
     @pl.when(step == 0)
     def _():
         total[...] = jnp.zeros_like(total)
 
-    left = jnp.where(
-        step < ends[0],
-        first_ref[...],
-        jnp.where(step < ends[1], second_ref[...], third_ref[...] * keep_ref[0:1]),
-    )
+    left = jnp.where(step == last, left_ref[...] * keep_ref[0:1], left_ref[...])
     total[...] += dot_nt(left, weight_ref[...])
 
-    @pl.when(step == pl.num_programs(0) - 1)
+    @pl.when(step == last)
     def _():
         out_ref[...] = total[...].astype(out_ref.dtype)
 
 
-def hidden_back(first, second, third, keep, weights, tile=768):
-    rows = first.shape[0]
-    model = weights.shape[0]
-    counts = [part.shape[1] // tile for part in (first, second, third)]
-    ends = (counts[0], counts[0] + counts[1])
-    block = lambda start, count: pl.BlockSpec(
-        (rows, tile), lambda i: (0, jnp.clip(i - start, 0, count - 1))
-    )
-    return pl.pallas_call(
-        functools.partial(hidden_back_kernel, ends=ends),
-        grid=(sum(counts),),
+def hidden_back(left, keep, weights):
+    rows, width = left.shape
+    model, tile = weights.shape[0], keep.shape[1]
+    return pl.pallas_call(
+        hidden_back_kernel,
+        grid=(width // tile,),
         in_specs=[
-            block(0, counts[0]),
-            block(ends[0], counts[1]),
-            block(ends[1], counts[2]),
-            pl.BlockSpec((8, tile), lambda i: (0, jnp.clip(i - ends[1], 0, counts[2] - 1))),
+            pl.BlockSpec((rows, tile), lambda i: (0, i)),
+            pl.BlockSpec((8, tile), lambda i: (0, 0)),
             pl.BlockSpec((model, tile), lambda i: (0, i)),
         ],
         out_specs=pl.BlockSpec((rows, model), lambda i: (0, 0)),
@@ -904,7 +892,7 @@
         compiler_params=pltpu.CompilerParams(vmem_limit_bytes=40 * 2**20),
         cost_estimate=cost(1, 1),
         name="hidden_back",
-    )(first, second, third, keep, weights)
+    )(left, keep, weights)
 
 
 def rms_forward_kernel(base_ref, own_ref, other_ref, live_ref, gain_ref, middle_ref, out_ref):
@@ -1387,10 +1375,10 @@
             offsets,
         )
     )
-    head_cols = x_cols + q_cols + kv_cols
-    head_b = beside(head_cols, grad_z_b, grad_query_b, grad_key_b, grad_value_b)
+    head_b = beside(x_cols + q_cols, grad_z_b, grad_query_b)
     z_sum = Scatter(hidden_split, head_b, bits)
-    u_sum = Scatter(hidden_split, grad_u_b, bits)
+    inner_b = beside(kv_cols + x_cols, grad_key_b, grad_value_b, after(grad_u_b, head_b))
+    u_sum = Scatter(hidden_split, inner_b, bits)
     held = z_sum.begin(grad_state_part)
     ready = branch.prepare(held)
 
@@ -1406,7 +1394,8 @@
     held = u_sum.begin(held)
     other_b = beside(last_cols, (grad_state_part, after(grad_state_other, held)), grad_step_b)
     other_sum = Scatter(hidden_split, other_b, bits)
-    grad_hidden_own = hidden_back(after(head_b, other_b), grad_u_b, other_b, keep, mix_full)
+    columns_b = beside(offsets["end"] + 128, head_b, inner_b, other_b)
+    grad_hidden_own = hidden_back(columns_b, keep, mix_full)
     held = other_sum.begin(grad_hidden_own)
     ready = z_sum.prepare(held)
 
@@ -1491,7 +1480,8 @@
     ready = other_sum.prepare(held)
     held = other_sum.join(ready)
     red_head = after(z_sum.finish(), held)
-    red_inner = side_by_side(red_head[:, :x_cols], u_sum.finish())
+    red_next = u_sum.finish()
+    red_inner = side_by_side(red_head[:, :x_cols], red_next[:, kv_cols:])
     sums = add_rows(after(sums, held), others)
     for bit in bits[4:]:
         sums = add_rows(sums, across(sums, bit))
@@ -1510,13 +1500,12 @@
     red_state = lax.dynamic_slice_in_dim(
         red_other[:, :state_cols], lax.axis_index("tensor") * state_rows, state_rows, 0
     )
-    kv_first = x_cols + q_cols
     return (
         output,
         grad_tokens,
         own_part(sums[0], 0),
-        red_head[:, x_cols:kv_first],
-        red_head[:, kv_first:].reshape(shard_rows, 2, -1),
+        red_head[:, x_cols:],
+        red_next[:, :kv_cols].reshape(shard_rows, 2, -1),
         red_attend,
         red_inner,
         red_state,

time: 736 us -> 731 us (level)
  waiting for transfers between devices: 319 us -> 304 us
  local copies, waits for them, and re-layouts: 56.9 us -> 69.9 us
    unnamed x277 -> x279, local copies, waits for them, and re-layouts: 41.1 us -> 53.9 us
    ppermute x9, waiting for transfers between devices: 84.2 us -> 76.1 us  [pair_swap(): return lax.ppermute(values, 'tensor', [(0, 1), (1, 0)])]
    ppermute x32, waiting for transfers between devices: 88.2 us -> 80.5 us  [across(): return lax.ppermute(values, 'dp', [(i, i ^ bit) for i in range(count)])]
  transfers between devices with their start and end apart: 43 -> 43, of which waited for: 23 -> 21; matrix products, arithmetic and copies ran while one was open for 7% -> 7% of each run, Pallas kernels for 28% -> 29%
where the time goes in v4:
time: 731 us; the launch traced here: 726 us
  waiting for transfers between devices  304 us (42%)
  Pallas kernels  248 us (34%)
  local copies, waits for them, and re-layouts  69.9 us (10%)
  starting transfers between devices  43.3 us (6%)
  matrix products  23.6 us (3%)
  other arithmetic  20.9 us (3%)
  between operations  16.8 us (2%)
    all_gather x1, waiting for transfers between devices, local(): mix_full = lax.all_gather(group_mix, 'dp', axis=0, tiled=True)  137 us
    ppermute x32, waiting for transfers between devices, across(): return lax.ppermute(values, 'dp', [(i, i ^ bit) for i in range(count)])  80.5 us
    pallas_call x35, Pallas kernels, scatter_part(): pl.pallas_call(scatter_part_kernel, grid=(width // tile,), in_specs=[pl.B...  77.9 us
    ppermute x9, waiting for transfers between devices, pair_swap(): return lax.ppermute(values, 'tensor', [(0, 1), (1, 0)])  76.1 us
    unnamed x279, local copies, waits for them, and re-layouts  53.9 us
    ppermute x32, starting transfers between devices, across(): return lax.ppermute(values, 'dp', [(i, i ^ bit) for i in range(count)])  33.3 us
    pallas_call x1, Pallas kernels, feed_forward(): pl.pallas_call(feed_forward_kernel, grid=(steps,), in_specs=[whole, whole...  30.1 us
    pallas_call x1, Pallas kernels, ssm_backward(): pl.pallas_call(ssm_backward_kernel, grid=(pairs // 2,), in_specs=[plain,...  25.4 us
  transfers between devices with their start and end apart: 43, of which 21 were waited for; matrix products, arithmetic and copies ran while one was open for 7% of the time, Pallas kernels for 29%

profile of v4, /device:TPU:0, one launch (start us, length us, event | category | flops | bytes accessed | tf_op | source)
XLA Modules:
  0.0 725.9 jit_solution(3442120407570364224)
XLA Ops:
  8.7 3.0 collective-permute-start.1
  11.8 2.8 fusion.36
  21.1 137.4 %all-gather.3.cloned.1.call-done.weight_ref = bf16[2048,6656]{1,0:T(8,128)(2,1)} async-done(((bf16[128,6656]{1,0:T(8,128)(2,1)}), bf16[2048,6656]{1,0:T(8,128)(2,1)}) %all-gather.3.cloned.1.call-update) | async-done | bytes 27262992 | tf_op jit(solution)/shard_map/all_gather | solution.py:1222
  163.5 2.1 fusion.10
  169.8 13.9 %fusion.q_ref.k_ref.v_ref.u_ref.z_ref.state_b_ref.state_c_ref.step_ref = f32[512,4480]{1,0:T(8,128)S(1)} fusion(bf16[512,2048]{1,0:T(8,128)(2,1)S(1)} %fusion.6.in_ref, bf16[2048,6656]{1,0:T(8,128)(2,1)} %all-gather.3.cloned.1.call-done.weight_ref), kind=kOutput, calls=%fused_computation | convolution fusion | flops 9395240960 | bytes 29622272 | tf_op jit(solution)/shard_map/td,dc->tc/dot_general | solution.py:26
  185.9 11.1 %ssm_forward.1 = (f32[512,1536]{1,0:T(8,128)S(1)}, f32[512,1536]{1,0:T(8,128)S(1)}, f32[512,128]{1,0:T(8,128)S(1)}) custom-call(f32[512,4480]{1,0:T(8,128)S(1)} %fusion.q_ref.k_ref.v_ref.u_ref.z_ref.state_b_ref.state_c_ref.step_ref, f32[512,4480]{1,0:T(8,128)S(1)} %fusion.q_ref.k_ref.v_ref.u_ref.z_ref.state_b_ref.state_c_ref.step_ref, ...), custom_call_target="tpu_custom_call" | custom-call | tf_op jit(solution)/shard_map/ssm_forward/pallas_call | solution.py:191
  203.4 4.0 copy-done.1
  208.6 4.7 attention_forward.1
  214.8 9.7 %fusion.7.own_ref = bf16[512,2048]{1,0:T(8,128)(2,1)} fusion(bf16[2048,6656]{1,0:T(8,128)(2,1)} %all-gather.3.cloned.1.call-done.weight_ref, bf16[512,1536]{1,0:T(8,128)(2,1)S(1)} %multiply_convert_fusion.1, bf16[512,512]{1,0:T(8,128)(2,1)S(1)} %get-tuple-element.154), kind=kOutput, calls=%fused_computation.11 | convolution fusion | flops 4300210176 | bytes 12582912 | tf_op jit(solution)/shard_map/tc,dc->td/dot_general | solution.py:26
  225.0 2.1 multiply_convert_fusion.in_ref.grad_ref
  229.7 42.5 %collective-permute-done.3.other_ref = bf16[512,2048]{1,0:T(8,128)(2,1)} collective-permute-done((bf16[512,2048]{1,0:T(8,128)(2,1)}, bf16[512,2048]{1,0:T(8,128)(2,1)}, u32[]{:S(2)}, u32[]{:S(2)}) %collective-permute-start.3) | collective-permute-done | bytes 2097184 | tf_op jit(solution)/shard_map/ppermute | solution.py:1017
  272.3 3.2 rms_forward.1
  279.9 9.5 %all-gather.5.cloned.1.call-done.gate_w_ref.up_w_ref.down_ref.right_ref = bf16[2048,6144]{1,0:T(8,128)(2,1)} async-done(((bf16[128,6144]{1,0:T(8,128)(2,1)}), bf16[2048,6144]{1,0:T(8,128)(2,1)}) %all-gather.5.cloned.1.call-update) | async-done | bytes 25165840 | tf_op jit(solution)/shard_map/all_gather | solution.py:1223
  289.3 30.1 %feed_forward.1 = (bf16[512,2048]{1,0:T(8,128)(2,1)S(1)}, bf16[512,2048]{1,0:T(8,128)(2,1)S(1)}, bf16[512,2048]{1,0:T(8,128)(2,1)S(1)}, bf16[512,2048]{1,0:T(8,128)(2,1)}) custom-call(bf16[512,2048]{1,0:T(8,128)(2,1)} %copy-done.56, bf16[512,2048]{1,0:T(8,128)(2,1)} %copy-done.44, ...), custom_call_target="tpu_custom_call" | custom-call | flops 1 | bytes 1 | tf_op jit(solution)/shard_map/feed_forward/pallas_call | solution.py:566
  319.4 3.4 scatter_part.37
  323.1 4.5 scatter_part.38
  327.6 2.3 scatter_part.39.ready_ref
  331.7 2.3 join_parts.19
  335.2 8.2 %product_back.1.own_ref = bf16[512,2048]{1,0:T(8,128)(2,1)} custom-call(bf16[512,2048]{1,0:T(8,128)(2,1)S(1)} %get-tuple-element.161.left_ref.right_ref, bf16[2048,6144]{1,0:T(8,128)(2,1)} %all-gather.5.cloned.1.call-done.gate_w_ref.up_w_ref.down_ref.right_ref), custom_call_target="tpu_custom_call" | custom-call | flops 1 | bytes 1 | tf_op jit(solution)/shard_map/product_back/pallas_call | solution.py:736
  343.4 2.1 scatter_part.36.ready_ref
  345.5 4.5 scatter_part.43
  350.0 28.3 %collective-permute-done.7.other_ref = bf16[512,2048]{1,0:T(8,128)(2,1)} collective-permute-done((bf16[512,2048]{1,0:T(8,128)(2,1)}, bf16[512,2048]{1,0:T(8,128)(2,1)}, u32[]{:S(2)}, u32[]{:S(2)}) %collective-permute-start.7) | collective-permute-done | bytes 2097184 | tf_op jit(solution)/shard_map/ppermute | solution.py:1017
  378.3 3.5 collective-permute-done.5.refs_1_
  388.6 5.1 rms_back.2
  396.4 8.2 %norm_back.1 = (bf16[512,512]{1,0:T(8,128)(2,1)S(1)}, f32[512,1536]{1,0:T(8,128)S(1)}, f32[512,128]{1,0:T(8,128)S(1)}, f32[8,1536]{1,0:T(8,128)S(1)}) custom-call(bf16[512,2048]{1,0:T(8,128)(2,1)S(1)} %get-tuple-element.173.in_ref.grad_ref, bf16[2048,6656]{1,0:T(8,128)(2,1)} %all-gather.3.cloned.1.call-done.weight_ref, f32[512,1536]{1,0:T(8,128)S(1)} %copy-done.53, ...), custom_call_target="tpu_custom_call" | custom-call | flops 1 | bytes 1 | tf_op jit(solution)/shard_map/norm_back/pallas_call | solution.py:630
  407.6 4.5 scatter_part.41
  413.4 2.1 scatter_part.42.ready_ref
  415.6 6.0 attention_backward.1
  423.0 9.1 %collective-permute-done.8.refs_1_ = bf16[512,2048]{1,0:T(8,128)(2,1)S(1)} collective-permute-done((bf16[512,2048]{1,0:T(8,128)(2,1)}, bf16[512,2048]{1,0:T(8,128)(2,1)S(1)}, u32[]{:S(2)}, u32[]{:S(2)}) %collective-permute-start.8) | collective-permute-done | bytes 2097184 | tf_op jit(solution)/shard_map/ppermute | solution.py:1050
  432.1 3.7 join_parts.21
  437.7 2.3 copy-done.46
  442.4 2.4 scatter_part.45
  448.0 2.6 copy-done.79
  450.6 25.4 %ssm_backward.1 = (bf16[512,1536]{1,0:T(8,128)(2,1)S(1)}, bf16[512,1536]{1,0:T(8,128)(2,1)S(1)}, bf16[528,512]{1,0:T(8,128)(2,1)}, bf16[512,128]{1,0:T(8,128)(2,...) custom-call(f32[512,1536]{1,0:T(8,128)S(1)} %copy-done.79, f32[512,1536]{1,0:T(8,128)S(1)} %copy-done.77, ...), custom_call_target="tpu_custom_call" | custom-call | flops 1 | bytes 1 | tf_op jit(solution)/shard_map/ssm_backward/pallas_call | solution.py:352
  477.2 4.7 scatter_part.46
  483.1 2.1 scatter_part.47.ready_ref
  485.4 3.7 join_parts.22
  490.1 3.6 scatter_part.48
  499.7 4.4 scatter_part.50
  504.1 4.4 collective-permute-done.17.refs_1_.refs_5_
  511.9 15.1 %hidden_back.1.own_ref = bf16[512,2048]{1,0:T(8,128)(2,1)} custom-call(bf16[512,4608]{1,0:T(8,128)(2,1)S(1)} %beside.7.left_ref, bf16[8,768]{1,0:T(8,128)(2,1)S(1)} %broadcast_in_dim.47.keep_ref, bf16[2048,6656]{1,0:T(8,128)(2,1)} %all-gather.3.cloned.1.call-done.weight_ref), custom_call_target="tpu_custom_call" | custom-call | flops 1 | bytes 1 | tf_op jit(solution)/shard_map/hidden_back/pallas_call | solution.py:881
  527.0 2.2 scatter_part.51
  529.2 2.1 scatter_part.52.ready_ref
  531.3 5.4 collective-permute-done.18.refs_1_
  536.8 3.1 join_parts.23
  542.1 3.3 scatter_part.53
  546.0 2.9 scatter_part.54
  548.9 2.1 collective-permute-start.25
  562.1 3.5 output_rows.1
  573.5 6.7 collective-permute-done.25.got_ref
  582.0 6.3 collective-permute-done.22.got_ref.refs_1_
  589.2 2.1 join_parts.24
  592.5 2.8 join_parts.25
  596.4 2.1 join_parts.26
  602.7 3.2 pad_maximum_fusion.1
  605.9 2.2 copy-done.73
  608.1 6.5 rms_back.3
  623.5 7.5 %collective-permute-done.31.got_ref = bf16[128,2048]{1,0:T(8,128)(2,1)} collective-permute-done((bf16[128,2048]{1,0:T(8,128)(2,1)}, bf16[128,2048]{1,0:T(8,128)(2,1)}, u32[]{:S(2)}, u32[]{:S(2)}) %collective-permute-start.31) | collective-permute-done | bytes 524320 | tf_op jit(solution)/shard_map/ppermute | solution.py:1050
  649.2 9.0 %collective-permute-done.35.right_ref = f32[16,2048]{1,0:T(8,128)S(1)} collective-permute-done((f32[16,2048]{1,0:T(8,128)S(1)}, f32[16,2048]{1,0:T(8,128)S(1)}, u32[]{:S(2)}, u32[]{:S(2)}) %collective-permute-start.35) | collective-permute-done | bytes 131104 | tf_op jit(solution)/shard_map/ppermute | solution.py:1050
  658.3 9.0 %collective-permute-done.34.got_ref = bf16[128,2048]{1,0:T(8,128)(2,1)S(1)} collective-permute-done((bf16[128,2048]{1,0:T(8,128)(2,1)S(1)}, bf16[128,2048]{1,0:T(8,128)(2,1)S(1)}, u32[]{:S(2)}, u32[]{:S(2)}) %collective-permute-start.34) | collective-permute-done | bytes 524320 | tf_op jit(solution)/shard_map/ppermute | solution.py:1050
  668.2 2.7 collective-permute-start.37
  676.9 14.8 %collective-permute-done.38.right_ref = f32[16,2048]{1,0:T(8,128)S(1)} collective-permute-done((f32[16,2048]{1,0:T(8,128)S(1)}, f32[16,2048]{1,0:T(8,128)S(1)}, u32[]{:S(2)}, u32[]{:S(2)}) %collective-permute-start.38) | collective-permute-done | bytes 131104 | tf_op jit(solution)/shard_map/ppermute | solution.py:1050
  703.2 3.0 collective-permute-done.39.got_ref
  716.2 2.6 pad_maximum_fusion.3
  (481 shorter events, 159.3 us)
Async XLA Ops:
  7.2 151.4 %all-gather.3.cloned.1.call-start = ((), (), s32[]{:S(2)}) async-start(), calls=%async_computation | async-start | bytes 28966912 | tf_op jit(solution)/shard_map/all_gather | solution.py:1222
  8.7 7.1 collective-permute-start.1
  11.7 4.5 collective-permute-start
  18.2 271.1 %all-gather.5.cloned.1.call-start = ((), (), s32[]{:S(2)}) async-start(), calls=%async_computation.1 | async-start | bytes 26738688 | tf_op jit(solution)/shard_map/all_gather | solution.py:1223
  19.8 139.4 %copy-start.124 = (s32[512]{0:T(512)S(1)}, s32[512]{0:T(512)}, u32[]{:S(2)}) copy-start(s32[512]{0:T(512)} %param.28) | copy-start | bytes 6148
  19.8 140.0 %copy-start.123 = (bf16[1536]{0:T(1024)(128)(2,1)S(1)}, bf16[1536]{0:T(1024)(128)(2,1)}, u32[]{:S(2)}) copy-start(bf16[1536]{0:T(1024)(128)(2,1)} %param.42) | copy-start | bytes 9220
  19.8 140.0 %copy-start.129 = (bf16[24]{0:T(256)(128)(2,1)S(1)}, bf16[24]{0:T(256)(128)(2,1)}, u32[]{:S(2)}) copy-start(bf16[24]{0:T(256)(128)(2,1)} %param.41) | copy-start | bytes 148
  19.8 140.2 %copy-start.126 = (bf16[5,1536]{1,0:T(8,128)(2,1)S(1)}, bf16[5,1536]{1,0:T(8,128)(2,1)}, u32[]{:S(2)}) copy-start(bf16[5,1536]{1,0:T(8,128)(2,1)} %param.37) | copy-start | bytes 46084
  19.9 140.2 %copy-start.130 = (bf16[24]{0:T(256)(128)(2,1)S(1)}, bf16[24]{0:T(256)(128)(2,1)}, u32[]{:S(2)}) copy-start(bf16[24]{0:T(256)(128)(2,1)} %param.39) | copy-start | bytes 148
  19.9 140.2 %copy-start.131 = (bf16[24]{0:T(256)(128)(2,1)S(1)}, bf16[24]{0:T(256)(128)(2,1)}, u32[]{:S(2)}) copy-start(bf16[24]{0:T(256)(128)(2,1)} %param.40) | copy-start | bytes 148
  21.1 139.9 %copy-start.40 = (bf16[512,2048]{1,0:T(8,128)(2,1)S(1)}, bf16[512,2048]{1,0:T(8,128)(2,1)}, u32[]{:S(2)}) copy-start(bf16[512,2048]{1,0:T(8,128)(2,1)} %value_ref.1) | copy-start | bytes 6291460
  169.7 13.9 %copy-start.57 = (bf16[512,2048]{1,0:T(8,128)(2,1)}, bf16[512,2048]{1,0:T(8,128)(2,1)S(1)}, u32[]{:S(2)}) copy-start(bf16[512,2048]{1,0:T(8,128)(2,1)S(1)} %fusion.6.in_ref) | copy-start | bytes 6291460
  183.7 13.3 %copy-start = (f32[512,4480]{1,0:T(8,128)}, f32[512,4480]{1,0:T(8,128)S(1)}, u32[]{:S(2)}) copy-start(f32[512,4480]{1,0:T(8,128)S(1)} %fusion.q_ref.k_ref.v_ref.u_ref.z_ref.state_b_ref.state_c_ref.step_ref) | copy-start | bytes 27525124
  200.5 13.0 %collective-permute-start.2 = (f32[512]{0:T(512)S(1)}, f32[512]{0:T(512)S(1)}, u32[]{:S(2)}, u32[]{:S(2)}) collective-permute-start(f32[512]{0:T(512)S(1)} %reduce_sum.28), channel_id=1, source_target_pairs={{0,1},{1,0},{2,3},{3,2},{4,5},{5,4},{6,7},{7,6},{8,9},{9,8},{10,11... | collective-permute-start | bytes 6152 | tf_op jit(solution)/shard_map/ppermute | solution.py:1017
  224.5 47.8 %collective-permute-start.3 = (bf16[512,2048]{1,0:T(8,128)(2,1)}, bf16[512,2048]{1,0:T(8,128)(2,1)}, u32[]{:S(2)}, u32[]{:S(2)}) collective-permute-start(bf16[512,2048]{1,0:T(8,128)(2,1)} %fusion.7.own_ref), channel_id=1, source_target_pairs={{0,1},{1,0},{2,3},{3,2},{4,5},{5,4},{6,7},{7,6},{8,9},{9,8},{10,11... | collective-permute-start | bytes 6291464 | tf_op jit(solution)/shard_map/ppermute | solution.py:1017
  227.1 45.1 %copy-start.125 = (f32[16,1,128]{2,1,0:T(1,128)S(1)}, f32[16,1,128]{2,1,0:T(1,128)}, u32[]{:S(2)}) copy-start(f32[16,1,128]{2,1,0:T(1,128)} %get-tuple-element.309) | copy-start | bytes 24580
  279.9 157.8 %copy-start.4 = (bf16[512,2048]{1,0:T(8,128)(2,1)}, bf16[512,2048]{1,0:T(8,128)(2,1)S(1)}, u32[]{:S(2)}) copy-start(bf16[512,2048]{1,0:T(8,128)(2,1)S(1)} %reorder_columns.4.left_ref) | copy-start | bytes 6291460
  289.3 30.1 %copy-start.18 = (bf16[512,2048]{1,0:T(8,128)(2,1)S(1)}, bf16[512,2048]{1,0:T(8,128)(2,1)}, u32[]{:S(2)}) copy-start(bf16[512,2048]{1,0:T(8,128)(2,1)} %copy-done.17) | copy-start | bytes 6291460
  319.4 24.0 %copy-start.30 = (bf16[512,2048]{1,0:T(8,128)(2,1)}, bf16[512,2048]{1,0:T(8,128)(2,1)S(1)}, u32[]{:S(2)}) copy-start(bf16[512,2048]{1,0:T(8,128)(2,1)S(1)} %get-tuple-element.164.right_ref) | copy-start | bytes 6291460
  319.4 65.6 %copy-start.9 = (bf16[512,2048]{1,0:T(8,128)(2,1)}, bf16[512,2048]{1,0:T(8,128)(2,1)S(1)}, u32[]{:S(2)}) copy-start(bf16[512,2048]{1,0:T(8,128)(2,1)S(1)} %get-tuple-element.161.left_ref.right_ref) | copy-start | bytes 6291460
  322.8 8.9 %collective-permute-start.4 = (bf16[1024,2048]{1,0:T(8,128)(2,1)S(1)}, bf16[1024,2048]{1,0:T(8,128)(2,1)S(1)}, u32[]{:S(2)}, u32[]{:S(2)}) collective-permute-start(bf16[1024,2048]{1,0:T(8,128)(2,1)S(1)} %scatter_part.37), channel_id=1, source_target_pairs={{0,2},{2,0},{4,6},{6,4},{8,10},{10,8},{12,14},{14,12},{16,18},{18,... | collective-permute-start | bytes 12582920 | tf_op jit(solution)/shard_map/ppermute | solution.py:1050
  329.9 48.4 %collective-permute-start.6 = (bf16[1024,2048]{1,0:T(8,128)(2,1)}, bf16[1024,2048]{1,0:T(8,128)(2,1)S(1)}, u32[]{:S(2)}, u32[]{:S(2)}) collective-permute-start(bf16[1024,2048]{1,0:T(8,128)(2,1)} %scatter_part.38), channel_id=1, source_target_pairs={{0,2},{2,0},{4,6},{6,4},{8,10},{10,8},{12,14},{14,12},{16,18},{18,... | collective-permute-start | bytes 12582920 | tf_op jit(solution)/shard_map/ppermute | solution.py:1050
  330.2 48.1 %collective-permute-start.7 = (bf16[512,2048]{1,0:T(8,128)(2,1)}, bf16[512,2048]{1,0:T(8,128)(2,1)}, u32[]{:S(2)}, u32[]{:S(2)}) collective-permute-start(bf16[512,2048]{1,0:T(8,128)(2,1)} %get-tuple-element.172.own_ref), channel_id=1, source_target_pairs={{0,1},{1,0},{2,3},{3,2},{4,5},{5,4},{6,7},{7,6},{8,9},{9,8},{10,11... | collective-permute-start | bytes 6291464 | tf_op jit(solution)/shard_map/ppermute | solution.py:1017
  331.7 53.3 %copy-start.21 = (bf16[1024,2048]{1,0:T(8,128)(2,1)}, bf16[1024,2048]{1,0:T(8,128)(2,1)S(1)}, u32[]{:S(2)}) copy-start(bf16[1024,2048]{1,0:T(8,128)(2,1)S(1)} %collective-permute-done.4.got_ref.refs_0_) | copy-start | bytes 12582916
  334.0 47.8 %collective-permute-start.5 = (bf16[512,2048]{1,0:T(8,128)(2,1)}, bf16[512,2048]{1,0:T(8,128)(2,1)}, u32[]{:S(2)}, u32[]{:S(2)}) collective-permute-start(bf16[512,2048]{1,0:T(8,128)(2,1)} %join_parts.19), channel_id=1, source_target_pairs={{0,4},{2,6},{4,0},{6,2},{8,12},{10,14},{12,8},{14,10},{16,20},{18,... | collective-permute-start | bytes 6291464 | tf_op jit(solution)/shard_map/ppermute | solution.py:1050
  381.8 50.2 %collective-permute-start.9 = (bf16[1024,2048]{1,0:T(8,128)(2,1)}, bf16[1024,2048]{1,0:T(8,128)(2,1)}, u32[]{:S(2)}, u32[]{:S(2)}) collective-permute-start(bf16[1024,2048]{1,0:T(8,128)(2,1)} %scatter_part.43), channel_id=1, source_target_pairs={{0,2},{2,0},{4,6},{6,4},{8,10},{10,8},{12,14},{14,12},{16,18},{18,... | collective-permute-start | bytes 12582920 | tf_op jit(solution)/shard_map/ppermute | solution.py:1050
  383.8 48.3 %collective-permute-start.8 = (bf16[512,2048]{1,0:T(8,128)(2,1)}, bf16[512,2048]{1,0:T(8,128)(2,1)S(1)}, u32[]{:S(2)}, u32[]{:S(2)}) collective-permute-start(bf16[512,2048]{1,0:T(8,128)(2,1)} %join_parts.20), channel_id=1, source_target_pairs={{0,4},{2,6},{4,0},{6,2},{8,12},{10,14},{12,8},{14,10},{16,20},{18,... | collective-permute-start | bytes 6291464 | tf_op jit(solution)/shard_map/ppermute | solution.py:1050
  387.0 35.9 %collective-permute-start.10 = (bf16[256,2048]{1,0:T(8,128)(2,1)S(1)}, bf16[256,2048]{1,0:T(8,128)(2,1)S(1)}, u32[]{:S(2)}, u32[]{:S(2)}) collective-permute-start(bf16[256,2048]{1,0:T(8,128)(2,1)S(1)} %scatter_part.40), channel_id=1, source_target_pairs={{0,8},{2,10},{4,12},{6,14},{8,0},{10,2},{12,4},{14,6},{16,24},{18,... | collective-permute-start | bytes 3145736 | tf_op jit(solution)/shard_map/ppermute | solution.py:1050
  404.7 18.3 %collective-permute-start.11 = (f32[512,128]{1,0:T(8,128)S(1)}, f32[512,128]{1,0:T(8,128)S(1)}, u32[]{:S(2)}, u32[]{:S(2)}) collective-permute-start(f32[512,128]{1,0:T(8,128)S(1)} %get-tuple-element.175.own_ref), channel_id=1, source_target_pairs={{0,1},{1,0},{2,3},{3,2},{4,5},{5,4},{6,7},{7,6},{8,9},{9,8},{10,11... | collective-permute-start | bytes 786440 | tf_op jit(solution)/shard_map/ppermute | solution.py:1017
  406.3 75.5 %copy-start.12 = (bf16[512,2048]{1,0:T(8,128)(2,1)}, bf16[512,2048]{1,0:T(8,128)(2,1)S(1)}, u32[]{:S(2)}) copy-start(bf16[512,2048]{1,0:T(8,128)(2,1)S(1)} %pad_maximum_fusion.right_ref) | copy-start | bytes 6291460
  423.0 19.4 %copy-start.62 = (bf16[256,2048]{1,0:T(8,128)(2,1)}, bf16[256,2048]{1,0:T(8,128)(2,1)S(1)}, u32[]{:S(2)}) copy-start(bf16[256,2048]{1,0:T(8,128)(2,1)S(1)} %collective-permute-done.10.refs_2_) | copy-start | bytes 3145732
  432.0 53.3 %collective-permute-start.14 = (bf16[1024,2048]{1,0:T(8,128)(2,1)}, bf16[1024,2048]{1,0:T(8,128)(2,1)}, u32[]{:S(2)}, u32[]{:S(2)}) collective-permute-start(bf16[1024,2048]{1,0:T(8,128)(2,1)} %scatter_part.41), channel_id=1, source_target_pairs={{0,2},{2,0},{4,6},{6,4},{8,10},{10,8},{12,14},{14,12},{16,18},{18,... | collective-permute-start | bytes 12582920 | tf_op jit(solution)/shard_map/ppermute | solution.py:1050
  435.9 49.4 %collective-permute-start.12 = (bf16[512,2048]{1,0:T(8,128)(2,1)}, bf16[512,2048]{1,0:T(8,128)(2,1)}, u32[]{:S(2)}, u32[]{:S(2)}) collective-permute-start(bf16[512,2048]{1,0:T(8,128)(2,1)} %join_parts.21), channel_id=1, source_target_pairs={{0,4},{2,6},{4,0},{6,2},{8,12},{10,14},{12,8},{14,10},{16,20},{18,... | collective-permute-start | bytes 6291464 | tf_op jit(solution)/shard_map/ppermute | solution.py:1050
  437.1 48.2 %collective-permute-start.16 = (bf16[512,2048]{1,0:T(8,128)(2,1)}, bf16[512,2048]{1,0:T(8,128)(2,1)}, u32[]{:S(2)}, u32[]{:S(2)}) collective-permute-start(bf16[512,2048]{1,0:T(8,128)(2,1)} %product_back.1.own_ref), channel_id=1, source_target_pairs={{0,1},{1,0},{2,3},{3,2},{4,5},{5,4},{6,7},{7,6},{8,9},{9,8},{10,11... | collective-permute-start | bytes 6291464 | tf_op jit(solution)/shard_map/ppermute | solution.py:1017
  440.8 44.5 %collective-permute-start.13 = (bf16[256,2048]{1,0:T(8,128)(2,1)S(1)}, bf16[256,2048]{1,0:T(8,128)(2,1)S(1)}, u32[]{:S(2)}, u32[]{:S(2)}) collective-permute-start(bf16[256,2048]{1,0:T(8,128)(2,1)S(1)} %scatter_part.44), channel_id=1, source_target_pairs={{0,8},{2,10},{4,12},{6,14},{8,0},{10,2},{12,4},{14,6},{16,24},{18,... | collective-permute-start | bytes 3145736 | tf_op jit(solution)/shard_map/ppermute | solution.py:1050
  444.8 40.4 %collective-permute-start.15 = (bf16[128,2048]{1,0:T(8,128)(2,1)S(1)}, bf16[128,2048]{1,0:T(8,128)(2,1)S(1)}, u32[]{:S(2)}, u32[]{:S(2)}) collective-permute-start(bf16[128,2048]{1,0:T(8,128)(2,1)S(1)} %scatter_part.45), channel_id=1, source_target_pairs={{0,16},{2,18},{4,20},{6,22},{8,24},{10,26},{12,28},{14,30},{16,0},... | collective-permute-start | bytes 1572872 | tf_op jit(solution)/shard_map/ppermute | solution.py:1050
  448.0 29.2 %copy-start.2 = (bf16[512,2048]{1,0:T(8,128)(2,1)}, bf16[512,2048]{1,0:T(8,128)(2,1)S(1)}, u32[]{:S(2)}) copy-start(bf16[512,2048]{1,0:T(8,128)(2,1)S(1)} %reorder_columns.7.left_ref) | copy-start | bytes 6291460
  485.3 51.4 %collective-permute-start.21 = (bf16[1024,2048]{1,0:T(8,128)(2,1)}, bf16[1024,2048]{1,0:T(8,128)(2,1)}, u32[]{:S(2)}, u32[]{:S(2)}) collective-permute-start(bf16[1024,2048]{1,0:T(8,128)(2,1)} %scatter_part.46), channel_id=1, source_target_pairs={{0,2},{2,0},{4,6},{6,4},{8,10},{10,8},{12,14},{14,12},{16,18},{18,... | collective-permute-start | bytes 12582920 | tf_op jit(solution)/shard_map/ppermute | solution.py:1050
  489.1 47.7 %collective-permute-start.18 = (bf16[512,2048]{1,0:T(8,128)(2,1)}, bf16[512,2048]{1,0:T(8,128)(2,1)}, u32[]{:S(2)}, u32[]{:S(2)}) collective-permute-start(bf16[512,2048]{1,0:T(8,128)(2,1)} %join_parts.22), channel_id=1, source_target_pairs={{0,4},{2,6},{4,0},{6,2},{8,12},{10,14},{12,8},{14,10},{16,20},{18,... | collective-permute-start | bytes 6291464 | tf_op jit(solution)/shard_map/ppermute | solution.py:1050
  493.7 37.6 %collective-permute-start.19 = (bf16[256,2048]{1,0:T(8,128)(2,1)}, bf16[256,2048]{1,0:T(8,128)(2,1)}, u32[]{:S(2)}, u32[]{:S(2)}) collective-permute-start(bf16[256,2048]{1,0:T(8,128)(2,1)} %scatter_part.48), channel_id=1, source_target_pairs={{0,8},{2,10},{4,12},{6,14},{8,0},{10,2},{12,4},{14,6},{16,24},{18,... | collective-permute-start | bytes 3145736 | tf_op jit(solution)/shard_map/ppermute | solution.py:1050
  494.7 13.8 %collective-permute-start.17 = (bf16[528,512]{1,0:T(8,128)(2,1)}, bf16[528,512]{1,0:T(8,128)(2,1)S(1)}, u32[]{:S(2)}, u32[]{:S(2)}) collective-permute-start(bf16[528,512]{1,0:T(8,128)(2,1)} %get-tuple-element.203.refs_0_.refs_4_), channel_id=1, source_target_pairs={{0,1},{1,0},{2,3},{3,2},{4,5},{5,4},{6,7},{7,6},{8,9},{9,8},{10,11... | collective-permute-start | bytes 1622024 | tf_op jit(solution)/shard_map/ppermute | solution.py:1017
  496.8 34.5 %collective-permute-start.20 = (bf16[128,2048]{1,0:T(8,128)(2,1)}, bf16[128,2048]{1,0:T(8,128)(2,1)}, u32[]{:S(2)}, u32[]{:S(2)}) collective-permute-start(bf16[128,2048]{1,0:T(8,128)(2,1)} %scatter_part.49), channel_id=1, source_target_pairs={{0,16},{2,18},{4,20},{6,22},{8,24},{10,26},{12,28},{14,30},{16,0},... | collective-permute-start | bytes 1572872 | tf_op jit(solution)/shard_map/ppermute | solution.py:1050
  499.7 11.8 %copy-start.8 = (bf16[512,2048]{1,0:T(8,128)(2,1)S(1)}, bf16[512,2048]{1,0:T(8,128)(2,1)}, u32[]{:S(2)}) copy-start(bf16[512,2048]{1,0:T(8,128)(2,1)} %copy-done.7) | copy-start | bytes 6291460
  536.8 52.4 %collective-permute-start.23 = (bf16[1024,1792]{1,0:T(8,128)(2,1)}, bf16[1024,1792]{1,0:T(8,128)(2,1)S(1)}, u32[]{:S(2)}, u32[]{:S(2)}) collective-permute-start(bf16[1024,1792]{1,0:T(8,128)(2,1)} %scatter_part.50), channel_id=1, source_target_pairs={{0,2},{2,0},{4,6},{6,4},{8,10},{10,8},{12,14},{14,12},{16,18},{18,... | collective-permute-start | bytes 11010056 | tf_op jit(solution)/shard_map/ppermute | solution.py:1050
  539.9 48.4 %collective-permute-start.22 = (bf16[512,2048]{1,0:T(8,128)(2,1)}, bf16[512,2048]{1,0:T(8,128)(2,1)}, u32[]{:S(2)}, u32[]{:S(2)}) collective-permute-start(bf16[512,2048]{1,0:T(8,128)(2,1)} %join_parts.23), channel_id=1, source_target_pairs={{0,4},{2,6},{4,0},{6,2},{8,12},{10,14},{12,8},{14,10},{16,20},{18,... | collective-permute-start | bytes 6291464 | tf_op jit(solution)/shard_map/ppermute | solution.py:1050
  541.1 48.1 %collective-permute-start.26 = (bf16[512,2048]{1,0:T(8,128)(2,1)}, bf16[512,2048]{1,0:T(8,128)(2,1)}, u32[]{:S(2)}, u32[]{:S(2)}) collective-permute-start(bf16[512,2048]{1,0:T(8,128)(2,1)} %hidden_back.1.own_ref), channel_id=1, source_target_pairs={{0,1},{1,0},{2,3},{3,2},{4,5},{5,4},{6,7},{7,6},{8,9},{9,8},{10,11... | collective-permute-start | bytes 6291464 | tf_op jit(solution)/shard_map/ppermute | solution.py:1017
  545.4 36.6 %collective-permute-start.24 = (bf16[256,2048]{1,0:T(8,128)(2,1)}, bf16[256,2048]{1,0:T(8,128)(2,1)}, u32[]{:S(2)}, u32[]{:S(2)}) collective-permute-start(bf16[256,2048]{1,0:T(8,128)(2,1)} %scatter_part.53), channel_id=1, source_target_pairs={{0,8},{2,10},{4,12},{6,14},{8,0},{10,2},{12,4},{14,6},{16,24},{18,... | collective-permute-start | bytes 3145736 | tf_op jit(solution)/shard_map/ppermute | solution.py:1050
  548.9 31.4 %collective-permute-start.25 = (bf16[128,2048]{1,0:T(8,128)(2,1)}, bf16[128,2048]{1,0:T(8,128)(2,1)}, u32[]{:S(2)}, u32[]{:S(2)}) collective-permute-start(bf16[128,2048]{1,0:T(8,128)(2,1)} %scatter_part.54), channel_id=1, source_target_pairs={{0,16},{2,18},{4,20},{6,22},{8,24},{10,26},{12,28},{14,30},{16,0},... | collective-permute-start | bytes 1572872 | tf_op jit(solution)/shard_map/ppermute | solution.py:1050
  591.6 41.6 %collective-permute-start.28 = (bf16[512,1792]{1,0:T(8,128)(2,1)}, bf16[512,1792]{1,0:T(8,128)(2,1)}, u32[]{:S(2)}, u32[]{:S(2)}) collective-permute-start(bf16[512,1792]{1,0:T(8,128)(2,1)} %join_parts.24), channel_id=1, source_target_pairs={{0,4},{2,6},{4,0},{6,2},{8,12},{10,14},{12,8},{14,10},{16,20},{18,... | collective-permute-start | bytes 5505032 | tf_op jit(solution)/shard_map/ppermute | solution.py:1050
  592.5 39.9 %collective-permute-start.29 = (bf16[1024,768]{1,0:T(8,128)(2,1)}, bf16[1024,768]{1,0:T(8,128)(2,1)S(1)}, u32[]{:S(2)}, u32[]{:S(2)}) collective-permute-start(bf16[1024,768]{1,0:T(8,128)(2,1)} %scatter_part.51), channel_id=1, source_target_pairs={{0,2},{2,0},{4,6},{6,4},{8,10},{10,8},{12,14},{14,12},{16,18},{18,... | collective-permute-start | bytes 4718600 | tf_op jit(solution)/shard_map/ppermute | solution.py:1050
  595.2 37.1 %collective-permute-start.30 = (bf16[256,2048]{1,0:T(8,128)(2,1)}, bf16[256,2048]{1,0:T(8,128)(2,1)}, u32[]{:S(2)}, u32[]{:S(2)}) collective-permute-start(bf16[256,2048]{1,0:T(8,128)(2,1)} %join_parts.25), channel_id=1, source_target_pairs={{0,8},{2,10},{4,12},{6,14},{8,0},{10,2},{12,4},{14,6},{16,24},{18,... | collective-permute-start | bytes 3145736 | tf_op jit(solution)/shard_map/ppermute | solution.py:1050
  598.5 32.5 %collective-permute-start.31 = (bf16[128,2048]{1,0:T(8,128)(2,1)}, bf16[128,2048]{1,0:T(8,128)(2,1)}, u32[]{:S(2)}, u32[]{:S(2)}) collective-permute-start(bf16[128,2048]{1,0:T(8,128)(2,1)} %join_parts.26), channel_id=1, source_target_pairs={{0,16},{2,18},{4,20},{6,22},{8,24},{10,26},{12,28},{14,30},{16,0},... | collective-permute-start | bytes 1572872 | tf_op jit(solution)/shard_map/ppermute | solution.py:1050
  615.7 1.4 collective-permute-start.27
  632.3 40.7 %copy-start.42 = (bf16[1024,768]{1,0:T(8,128)(2,1)}, bf16[1024,768]{1,0:T(8,128)(2,1)S(1)}, u32[]{:S(2)}) copy-start(bf16[1024,768]{1,0:T(8,128)(2,1)S(1)} %collective-permute-done.29.got_ref.refs_0_) | copy-start | bytes 4718596
  635.0 33.1 %collective-permute-start.33 = (bf16[256,1792]{1,0:T(8,128)(2,1)S(1)}, bf16[256,1792]{1,0:T(8,128)(2,1)S(1)}, u32[]{:S(2)}, u32[]{:S(2)}) collective-permute-start(bf16[256,1792]{1,0:T(8,128)(2,1)S(1)} %join_parts.29), channel_id=1, source_target_pairs={{0,8},{2,10},{4,12},{6,14},{8,0},{10,2},{12,4},{14,6},{16,24},{18,... | collective-permute-start | bytes 2752520 | tf_op jit(solution)/shard_map/ppermute | solution.py:1050
  636.6 30.7 %collective-permute-start.32 = (bf16[512,768]{1,0:T(8,128)(2,1)S(1)}, bf16[512,768]{1,0:T(8,128)(2,1)S(1)}, u32[]{:S(2)}, u32[]{:S(2)}) collective-permute-start(bf16[512,768]{1,0:T(8,128)(2,1)S(1)} %join_parts.28), channel_id=1, source_target_pairs={{0,4},{2,6},{4,0},{6,2},{8,12},{10,14},{12,8},{14,10},{16,20},{18,... | collective-permute-start | bytes 2359304 | tf_op jit(solution)/shard_map/ppermute | solution.py:1050
  638.7 28.6 %collective-permute-start.34 = (bf16[128,2048]{1,0:T(8,128)(2,1)S(1)}, bf16[128,2048]{1,0:T(8,128)(2,1)S(1)}, u32[]{:S(2)}, u32[]{:S(2)}) collective-permute-start(bf16[128,2048]{1,0:T(8,128)(2,1)S(1)} %join_parts.30), channel_id=1, source_target_pairs={{0,16},{2,18},{4,20},{6,22},{8,24},{10,26},{12,28},{14,30},{16,0},... | collective-permute-start | bytes 1572872 | tf_op jit(solution)/shard_map/ppermute | solution.py:1050
  640.2 18.0 %collective-permute-start.35 = (f32[16,2048]{1,0:T(8,128)S(1)}, f32[16,2048]{1,0:T(8,128)S(1)}, u32[]{:S(2)}, u32[]{:S(2)}) collective-permute-start(f32[16,2048]{1,0:T(8,128)S(1)} %add_rows.4.left_ref), channel_id=1, source_target_pairs={{0,4},{2,6},{4,0},{6,2},{8,12},{10,14},{12,8},{14,10},{16,20},{18,... | collective-permute-start | bytes 393224 | tf_op jit(solution)/shard_map/ppermute | solution.py:1050
  668.2 23.5 %collective-permute-start.37 = (bf16[128,1792]{1,0:T(8,128)(2,1)S(1)}, bf16[128,1792]{1,0:T(8,128)(2,1)S(1)}, u32[]{:S(2)}, u32[]{:S(2)}) collective-permute-start(bf16[128,1792]{1,0:T(8,128)(2,1)S(1)} %join_parts.33), channel_id=1, source_target_pairs={{0,16},{2,18},{4,20},{6,22},{8,24},{10,26},{12,28},{14,30},{16,0},... | collective-permute-start | bytes 1376264 | tf_op jit(solution)/shard_map/ppermute | solution.py:1050
  671.0 20.8 %collective-permute-start.36 = (bf16[256,768]{1,0:T(8,128)(2,1)S(1)}, bf16[256,768]{1,0:T(8,128)(2,1)S(1)}, u32[]{:S(2)}, u32[]{:S(2)}) collective-permute-start(bf16[256,768]{1,0:T(8,128)(2,1)S(1)} %join_parts.32), channel_id=1, source_target_pairs={{0,8},{2,10},{4,12},{6,14},{8,0},{10,2},{12,4},{14,6},{16,24},{18,... | collective-permute-start | bytes 1179656 | tf_op jit(solution)/shard_map/ppermute | solution.py:1050
  671.0 20.8 %collective-permute-start.38 = (f32[16,2048]{1,0:T(8,128)S(1)}, f32[16,2048]{1,0:T(8,128)S(1)}, u32[]{:S(2)}, u32[]{:S(2)}) collective-permute-start(f32[16,2048]{1,0:T(8,128)S(1)} %add_rows.5.left_ref), channel_id=1, source_target_pairs={{0,8},{2,10},{4,12},{6,14},{8,0},{10,2},{12,4},{14,6},{16,24},{18,... | collective-permute-start | bytes 393224 | tf_op jit(solution)/shard_map/ppermute | solution.py:1050
  692.5 13.7 %collective-permute-start.39 = (bf16[128,768]{1,0:T(8,128)(2,1)}, bf16[128,768]{1,0:T(8,128)(2,1)}, u32[]{:S(2)}, u32[]{:S(2)}) collective-permute-start(bf16[128,768]{1,0:T(8,128)(2,1)} %join_parts.35), channel_id=1, source_target_pairs={{0,16},{2,18},{4,20},{6,22},{8,24},{10,26},{12,28},{14,30},{16,0},... | collective-permute-start | bytes 589832 | tf_op jit(solution)/shard_map/ppermute | solution.py:1050
  695.1 13.1 %collective-permute-start.40 = (f32[16,2048]{1,0:T(8,128)}, f32[16,2048]{1,0:T(8,128)}, u32[]{:S(2)}, u32[]{:S(2)}) collective-permute-start(f32[16,2048]{1,0:T(8,128)} %add_rows.6.left_ref), channel_id=1, source_target_pairs={{0,16},{2,18},{4,20},{6,22},{8,24},{10,26},{12,28},{14,30},{16,0},... | collective-permute-start | bytes 393224 | tf_op jit(solution)/shard_map/ppermute | solution.py:1050
  703.2 11.1 %slice-start.3 = ((f32[128,2048]{1,0:T(8,128)}), f32[128,1536]{1,0:T(8,128)S(1)}, s32[]{:S(2)}) async-start(f32[128,2048]{1,0:T(8,128)} %copy-done.69), calls=%async_computation.5 | async-start | bytes 1572864 | tf_op jit(solution)/shard_map/slice | solution.py:1484
  (116 other events, 431.1 us)
Sparse Core Ops, SparseCore 0:
  18.4 140.1 all-gather.2
  160.7 128.5 all-gather.4

commit v5 on v4

--- a/solution.py
+++ b/solution.py
@@ -751,13 +751,14 @@
 def join_kernel(start, ready_ref, got_ref, out_ref):
     size = ready_ref.shape[0]
     got = got_ref[start : start + size, :].astype(jnp.float32)
-    out_ref[...] = (ready_ref[...] + got).astype(out_ref.dtype)
+    out_ref[...] = (ready_ref[...].astype(jnp.float32) + got).astype(out_ref.dtype)
 
 
 def join_parts(ready, got, start, dtype):
     size, width = ready.shape
     if size % 128 or start % size:
-        return (ready + got[start : start + size].astype(jnp.float32)).astype(dtype)
+        got = got[start : start + size].astype(jnp.float32)
+        return (ready.astype(jnp.float32) + got).astype(dtype)
     if size > 256:
         tile = widest(width, 1152)
         return pl.pallas_call(
@@ -954,20 +955,20 @@
         total = refs.pop(0)[start : start + count, :].astype(jnp.float32)
         if terms == 2:
             total = total + refs.pop(0)[start : start + count, :].astype(jnp.float32)
-        out_ref[place : place + count, : total.shape[1]] = total
+        out_ref[place : place + count, : total.shape[1]] = total.astype(out_ref.dtype)
         place += count
 
 
 def stack_rows(width, *parts):
     layout = tuple((start, count, len(arrays)) for arrays, start, count in parts)
-    total = -(-sum(count for unused, count, terms in layout) // 8) * 8
+    total = -(-sum(count for unused, count, terms in layout) // 16) * 16
     vmem = pl.BlockSpec(memory_space=pltpu.VMEM)
     arrays = [array for arrays, start, count in parts for array in arrays]
     return pl.pallas_call(
         functools.partial(stack_kernel, layout),
         in_specs=[vmem] * len(arrays),
         out_specs=vmem,
-        out_shape=jax.ShapeDtypeStruct((total, width), jnp.float32),
+        out_shape=jax.ShapeDtypeStruct((total, width), jnp.bfloat16),
         compiler_params=pltpu.CompilerParams(vmem_limit_bytes=8 * 2**20),
         cost_estimate=cost(1, 1),
         name="stack_rows",
@@ -975,7 +976,8 @@
 
 
 def add_kernel(left_ref, right_ref, out_ref):
-    out_ref[...] = left_ref[...] + right_ref[...]
+    total = left_ref[...].astype(jnp.float32) + right_ref[...].astype(jnp.float32)
+    out_ref[...] = total.astype(out_ref.dtype)
 
 
 def add_rows(left, right):
@@ -1079,8 +1081,9 @@
         first, size = self.place(step)
         gots = [(got, self.meets(past, step)) for past, got in enumerate(self.got[:-1])]
         left = after(self.left, *earlier)
+        dtype = jnp.bfloat16 if step == 1 else jnp.float32
         self.ready = scatter_part(
-            left, self.right, gots, first * self.rows, size * self.rows, jnp.float32
+            left, self.right, gots, first * self.rows, size * self.rows, dtype
         )
         return self.ready
 
@@ -1485,6 +1488,7 @@
     sums = add_rows(after(sums, held), others)
     for bit in bits[4:]:
         sums = add_rows(sums, across(sums, bit))
+    sums = sums.astype(f32)
     at = 2 + tap_count + 2
     conv_sum = sums[at : at + tap_count, :state_cols]
     at += tap_count

time: 731 us -> 727 us (level)
    unnamed x279 -> x295, local copies, waits for them, and re-layouts: 53.9 us -> 50.6 us
  transfers between devices with their start and end apart: 43 -> 43, of which waited for: 21 -> 23; matrix products, arithmetic and copies ran while one was open for 7% -> 7% of each run, Pallas kernels for 29% -> 29%
where the time goes in v5:
time: 727 us; the launch traced here: 723 us
  waiting for transfers between devices  301 us (41%)
  Pallas kernels  248 us (34%)
  local copies, waits for them, and re-layouts  66.5 us (9%)
  starting transfers between devices  46 us (6%)
  matrix products  23.6 us (3%)
  other arithmetic  20.9 us (3%)
  between operations  16.9 us (2%)
    all_gather x1, waiting for transfers between devices, local(): mix_full = lax.all_gather(group_mix, 'dp', axis=0, tiled=True)  137 us
    ppermute x32, waiting for transfers between devices, across(): return lax.ppermute(values, 'dp', [(i, i ^ bit) for i in range(count)])  78.1 us
    pallas_call x35, Pallas kernels, scatter_part(): pl.pallas_call(scatter_part_kernel, grid=(width // tile,), in_specs=[pl.B...  78.1 us
    ppermute x9, waiting for transfers between devices, pair_swap(): return lax.ppermute(values, 'tensor', [(0, 1), (1, 0)])  75.9 us
    unnamed x295, local copies, waits for them, and re-layouts  50.6 us
    ppermute x32, starting transfers between devices, across(): return lax.ppermute(values, 'dp', [(i, i ^ bit) for i in range(count)])  36.1 us
    pallas_call x1, Pallas kernels, feed_forward(): pl.pallas_call(feed_forward_kernel, grid=(steps,), in_specs=[whole, whole...  30.1 us
    pallas_call x1, Pallas kernels, ssm_backward(): pl.pallas_call(ssm_backward_kernel, grid=(pairs // 2,), in_specs=[plain,...  25.4 us
  transfers between devices with their start and end apart: 43, of which 23 were waited for; matrix products, arithmetic and copies ran while one was open for 7% of the time, Pallas kernels for 29%

profile of v5, /device:TPU:0, one launch (start us, length us, event | category | flops | bytes accessed | tf_op | source)
XLA Modules:
  0.0 722.7 jit_solution(8891349043014452400)
XLA Ops:
  8.7 3.0 collective-permute-start.1
  11.8 2.8 fusion.36
  21.1 137.4 %all-gather.3.cloned.1.call-done.weight_ref = bf16[2048,6656]{1,0:T(8,128)(2,1)} async-done(((bf16[128,6656]{1,0:T(8,128)(2,1)}), bf16[2048,6656]{1,0:T(8,128)(2,1)}) %all-gather.3.cloned.1.call-update) | async-done | bytes 27262992 | tf_op jit(solution)/shard_map/all_gather | solution.py:1225
  163.5 2.1 fusion.10
  169.7 13.9 %fusion.q_ref.k_ref.v_ref.u_ref.z_ref.state_b_ref.state_c_ref.step_ref = f32[512,4480]{1,0:T(8,128)S(1)} fusion(bf16[512,2048]{1,0:T(8,128)(2,1)S(1)} %fusion.6.in_ref, bf16[2048,6656]{1,0:T(8,128)(2,1)} %all-gather.3.cloned.1.call-done.weight_ref), kind=kOutput, calls=%fused_computation | convolution fusion | flops 9395240960 | bytes 29622272 | tf_op jit(solution)/shard_map/td,dc->tc/dot_general | solution.py:26
  183.8 2.0 copy-done.71
  185.9 11.1 %ssm_forward.1 = (f32[512,1536]{1,0:T(8,128)S(1)}, f32[512,1536]{1,0:T(8,128)S(1)}, f32[512,128]{1,0:T(8,128)S(1)}) custom-call(f32[512,4480]{1,0:T(8,128)S(1)} %fusion.q_ref.k_ref.v_ref.u_ref.z_ref.state_b_ref.state_c_ref.step_ref, f32[512,4480]{1,0:T(8,128)S(1)} %fusion.q_ref.k_ref.v_ref.u_ref.z_ref.state_b_ref.state_c_ref.step_ref, ...), custom_call_target="tpu_custom_call" | custom-call | tf_op jit(solution)/shard_map/ssm_forward/pallas_call | solution.py:191
  203.4 4.0 copy-done.1
  208.6 4.7 attention_forward.1
  214.7 9.7 %fusion.7.own_ref = bf16[512,2048]{1,0:T(8,128)(2,1)} fusion(bf16[2048,6656]{1,0:T(8,128)(2,1)} %all-gather.3.cloned.1.call-done.weight_ref, bf16[512,1536]{1,0:T(8,128)(2,1)S(1)} %multiply_convert_fusion.1, bf16[512,512]{1,0:T(8,128)(2,1)S(1)} %get-tuple-element.154), kind=kOutput, calls=%fused_computation.11 | convolution fusion | flops 4300210176 | bytes 12582912 | tf_op jit(solution)/shard_map/tc,dc->td/dot_general | solution.py:26
  225.0 2.1 multiply_convert_fusion.in_ref.grad_ref
  229.7 42.5 %collective-permute-done.3.other_ref = bf16[512,2048]{1,0:T(8,128)(2,1)} collective-permute-done((bf16[512,2048]{1,0:T(8,128)(2,1)}, bf16[512,2048]{1,0:T(8,128)(2,1)}, u32[]{:S(2)}, u32[]{:S(2)}) %collective-permute-start.3) | collective-permute-done | bytes 2097184 | tf_op jit(solution)/shard_map/ppermute | solution.py:1019
  272.3 3.2 rms_forward.1
  275.4 2.0 copy-done.49
  279.9 9.5 %all-gather.5.cloned.1.call-done.gate_w_ref.up_w_ref.down_ref.right_ref = bf16[2048,6144]{1,0:T(8,128)(2,1)} async-done(((bf16[128,6144]{1,0:T(8,128)(2,1)}), bf16[2048,6144]{1,0:T(8,128)(2,1)}) %all-gather.5.cloned.1.call-update) | async-done | bytes 25165840 | tf_op jit(solution)/shard_map/all_gather | solution.py:1226
  289.3 30.1 %feed_forward.1 = (bf16[512,2048]{1,0:T(8,128)(2,1)S(1)}, bf16[512,2048]{1,0:T(8,128)(2,1)S(1)}, bf16[512,2048]{1,0:T(8,128)(2,1)S(1)}, bf16[512,2048]{1,0:T(8,128)(2,1)}) custom-call(bf16[512,2048]{1,0:T(8,128)(2,1)} %copy-done.56, bf16[512,2048]{1,0:T(8,128)(2,1)} %copy-done.44, ...), custom_call_target="tpu_custom_call" | custom-call | flops 1 | bytes 1 | tf_op jit(solution)/shard_map/feed_forward/pallas_call | solution.py:566
  319.4 3.4 scatter_part.37
  323.1 4.5 scatter_part.38
  327.6 2.2 scatter_part.39.ready_ref
  331.6 2.2 join_parts.19
  335.0 8.2 %product_back.1.own_ref = bf16[512,2048]{1,0:T(8,128)(2,1)} custom-call(bf16[512,2048]{1,0:T(8,128)(2,1)S(1)} %get-tuple-element.161.left_ref.right_ref, bf16[2048,6144]{1,0:T(8,128)(2,1)} %all-gather.5.cloned.1.call-done.gate_w_ref.up_w_ref.down_ref.right_ref), custom_call_target="tpu_custom_call" | custom-call | flops 1 | bytes 1 | tf_op jit(solution)/shard_map/product_back/pallas_call | solution.py:736
  345.1 4.5 scatter_part.43
  349.6 28.6 %collective-permute-done.7.other_ref = bf16[512,2048]{1,0:T(8,128)(2,1)} collective-permute-done((bf16[512,2048]{1,0:T(8,128)(2,1)}, bf16[512,2048]{1,0:T(8,128)(2,1)}, u32[]{:S(2)}, u32[]{:S(2)}) %collective-permute-start.7) | collective-permute-done | bytes 2097184 | tf_op jit(solution)/shard_map/ppermute | solution.py:1019
  378.2 3.4 collective-permute-done.5.refs_1_
  384.7 2.0 scatter_part.40
  388.3 5.1 rms_back.2
  396.1 8.2 %norm_back.1 = (bf16[512,512]{1,0:T(8,128)(2,1)S(1)}, f32[512,1536]{1,0:T(8,128)S(1)}, f32[512,128]{1,0:T(8,128)S(1)}, f32[8,1536]{1,0:T(8,128)S(1)}) custom-call(bf16[512,2048]{1,0:T(8,128)(2,1)S(1)} %get-tuple-element.173.in_ref.grad_ref, bf16[2048,6656]{1,0:T(8,128)(2,1)} %all-gather.3.cloned.1.call-done.weight_ref, f32[512,1536]{1,0:T(8,128)S(1)} %copy-done.53, ...), custom_call_target="tpu_custom_call" | custom-call | flops 1 | bytes 1 | tf_op jit(solution)/shard_map/norm_back/pallas_call | solution.py:630
  407.3 4.5 scatter_part.41
  415.3 6.0 attention_backward.1
  423.4 8.3 %collective-permute-done.8.refs_1_ = bf16[512,2048]{1,0:T(8,128)(2,1)S(1)} collective-permute-done((bf16[512,2048]{1,0:T(8,128)(2,1)}, bf16[512,2048]{1,0:T(8,128)(2,1)S(1)}, u32[]{:S(2)}, u32[]{:S(2)}) %collective-permute-start.8) | collective-permute-done | bytes 2097184 | tf_op jit(solution)/shard_map/ppermute | solution.py:1052
  431.8 3.7 join_parts.21
  441.6 3.2 scatter_part.45
  444.8 2.3 collective-permute-start.15
  448.4 25.4 %ssm_backward.1 = (bf16[512,1536]{1,0:T(8,128)(2,1)S(1)}, bf16[512,1536]{1,0:T(8,128)(2,1)S(1)}, bf16[528,512]{1,0:T(8,128)(2,1)}, bf16[512,128]{1,0:T(8,128)(2,...) custom-call(f32[512,1536]{1,0:T(8,128)S(1)} %copy-done.79, f32[512,1536]{1,0:T(8,128)S(1)} %copy-done.77, ...), custom_call_target="tpu_custom_call" | custom-call | flops 1 | bytes 1 | tf_op jit(solution)/shard_map/ssm_backward/pallas_call | solution.py:352
  474.9 4.7 scatter_part.46
  484.0 4.3 join_parts.22
  489.0 3.7 scatter_part.48
  499.5 4.4 scatter_part.50
  503.9 3.4 collective-permute-done.17.refs_1_.refs_5_
  510.7 15.1 %hidden_back.1.own_ref = bf16[512,2048]{1,0:T(8,128)(2,1)} custom-call(bf16[512,4608]{1,0:T(8,128)(2,1)S(1)} %beside.7.left_ref, bf16[8,768]{1,0:T(8,128)(2,1)S(1)} %broadcast_in_dim.47.keep_ref, bf16[2048,6656]{1,0:T(8,128)(2,1)} %all-gather.3.cloned.1.call-done.weight_ref), custom_call_target="tpu_custom_call" | custom-call | flops 1 | bytes 1 | tf_op jit(solution)/shard_map/hidden_back/pallas_call | solution.py:882
  525.8 2.2 scatter_part.51
  530.0 5.4 collective-permute-done.18.refs_1_
  535.4 3.1 join_parts.23
  540.2 3.4 scatter_part.53
  544.8 2.9 scatter_part.54
  547.7 2.4 collective-permute-start.25
  561.2 3.0 output_rows.1
  572.0 7.2 collective-permute-done.25.got_ref
  580.2 6.7 collective-permute-done.22.got_ref.refs_1_
  587.5 2.2 join_parts.24
  591.1 2.8 join_parts.25
  595.3 2.1 join_parts.26
  601.8 3.2 pad_maximum_fusion.1
  605.0 2.2 copy-done.73
  607.2 6.5 rms_back.3
  621.2 8.7 %collective-permute-done.31.got_ref = bf16[128,2048]{1,0:T(8,128)(2,1)} collective-permute-done((bf16[128,2048]{1,0:T(8,128)(2,1)}, bf16[128,2048]{1,0:T(8,128)(2,1)}, u32[]{:S(2)}, u32[]{:S(2)}) %collective-permute-start.31) | collective-permute-done | bytes 524320 | tf_op jit(solution)/shard_map/ppermute | solution.py:1052
  633.3 2.3 collective-permute-start.33
  648.4 7.6 %collective-permute-done.35.right_ref = bf16[16,2048]{1,0:T(8,128)(2,1)S(1)} collective-permute-done((bf16[16,2048]{1,0:T(8,128)(2,1)S(1)}, bf16[16,2048]{1,0:T(8,128)(2,1)S(1)}, u32[]{:S(2)}, u32[]{:S(2)}) %collective-permute-start.35) | collective-permute-done | bytes 65568 | tf_op jit(solution)/shard_map/ppermute | solution.py:1052
  656.0 10.4 %collective-permute-done.34.got_ref = bf16[128,2048]{1,0:T(8,128)(2,1)S(1)} collective-permute-done((bf16[128,2048]{1,0:T(8,128)(2,1)S(1)}, bf16[128,2048]{1,0:T(8,128)(2,1)S(1)}, u32[]{:S(2)}, u32[]{:S(2)}) %collective-permute-start.34) | collective-permute-done | bytes 524320 | tf_op jit(solution)/shard_map/ppermute | solution.py:1052
  667.3 2.7 collective-permute-start.37
  670.0 2.0 collective-permute-start.38
  676.0 14.1 %collective-permute-done.38.right_ref = bf16[16,2048]{1,0:T(8,128)(2,1)S(1)} collective-permute-done((bf16[16,2048]{1,0:T(8,128)(2,1)S(1)}, bf16[16,2048]{1,0:T(8,128)(2,1)S(1)}, u32[]{:S(2)}, u32[]{:S(2)}) %collective-permute-start.38) | collective-permute-done | bytes 65568 | tf_op jit(solution)/shard_map/ppermute | solution.py:1052
  692.4 2.1 collective-permute-start.40
  713.0 2.6 pad_maximum_fusion.3
  (498 shorter events, 156.8 us)
Async XLA Ops:
  7.2 151.4 %all-gather.3.cloned.1.call-start = ((), (), s32[]{:S(2)}) async-start(), calls=%async_computation | async-start | bytes 28966912 | tf_op jit(solution)/shard_map/all_gather | solution.py:1225
  8.7 7.1 collective-permute-start.1
  11.7 4.5 collective-permute-start
  18.2 271.1 %all-gather.5.cloned.1.call-start = ((), (), s32[]{:S(2)}) async-start(), calls=%async_computation.1 | async-start | bytes 26738688 | tf_op jit(solution)/shard_map/all_gather | solution.py:1226
  19.8 139.4 %copy-start.132 = (s32[512]{0:T(512)S(1)}, s32[512]{0:T(512)}, u32[]{:S(2)}) copy-start(s32[512]{0:T(512)} %param.28) | copy-start | bytes 6148
  19.8 140.0 %copy-start.131 = (bf16[1536]{0:T(1024)(128)(2,1)S(1)}, bf16[1536]{0:T(1024)(128)(2,1)}, u32[]{:S(2)}) copy-start(bf16[1536]{0:T(1024)(128)(2,1)} %param.42) | copy-start | bytes 9220
  19.8 140.0 %copy-start.137 = (bf16[24]{0:T(256)(128)(2,1)S(1)}, bf16[24]{0:T(256)(128)(2,1)}, u32[]{:S(2)}) copy-start(bf16[24]{0:T(256)(128)(2,1)} %param.41) | copy-start | bytes 148
  19.8 140.2 %copy-start.134 = (bf16[5,1536]{1,0:T(8,128)(2,1)S(1)}, bf16[5,1536]{1,0:T(8,128)(2,1)}, u32[]{:S(2)}) copy-start(bf16[5,1536]{1,0:T(8,128)(2,1)} %param.37) | copy-start | bytes 46084
  19.9 140.2 %copy-start.138 = (bf16[24]{0:T(256)(128)(2,1)S(1)}, bf16[24]{0:T(256)(128)(2,1)}, u32[]{:S(2)}) copy-start(bf16[24]{0:T(256)(128)(2,1)} %param.39) | copy-start | bytes 148
  19.9 140.2 %copy-start.139 = (bf16[24]{0:T(256)(128)(2,1)S(1)}, bf16[24]{0:T(256)(128)(2,1)}, u32[]{:S(2)}) copy-start(bf16[24]{0:T(256)(128)(2,1)} %param.40) | copy-start | bytes 148
  21.1 139.9 %copy-start.40 = (bf16[512,2048]{1,0:T(8,128)(2,1)S(1)}, bf16[512,2048]{1,0:T(8,128)(2,1)}, u32[]{:S(2)}) copy-start(bf16[512,2048]{1,0:T(8,128)(2,1)} %value_ref.1) | copy-start | bytes 6291460
  169.7 13.9 %copy-start.57 = (bf16[512,2048]{1,0:T(8,128)(2,1)}, bf16[512,2048]{1,0:T(8,128)(2,1)S(1)}, u32[]{:S(2)}) copy-start(bf16[512,2048]{1,0:T(8,128)(2,1)S(1)} %fusion.6.in_ref) | copy-start | bytes 6291460
  183.7 13.3 %copy-start = (f32[512,4480]{1,0:T(8,128)}, f32[512,4480]{1,0:T(8,128)S(1)}, u32[]{:S(2)}) copy-start(f32[512,4480]{1,0:T(8,128)S(1)} %fusion.q_ref.k_ref.v_ref.u_ref.z_ref.state_b_ref.state_c_ref.step_ref) | copy-start | bytes 27525124
  200.5 13.0 %collective-permute-start.2 = (f32[512]{0:T(512)S(1)}, f32[512]{0:T(512)S(1)}, u32[]{:S(2)}, u32[]{:S(2)}) collective-permute-start(f32[512]{0:T(512)S(1)} %reduce_sum.28), channel_id=1, source_target_pairs={{0,1},{1,0},{2,3},{3,2},{4,5},{5,4},{6,7},{7,6},{8,9},{9,8},{10,11... | collective-permute-start | bytes 6152 | tf_op jit(solution)/shard_map/ppermute | solution.py:1019
  224.5 47.8 %collective-permute-start.3 = (bf16[512,2048]{1,0:T(8,128)(2,1)}, bf16[512,2048]{1,0:T(8,128)(2,1)}, u32[]{:S(2)}, u32[]{:S(2)}) collective-permute-start(bf16[512,2048]{1,0:T(8,128)(2,1)} %fusion.7.own_ref), channel_id=1, source_target_pairs={{0,1},{1,0},{2,3},{3,2},{4,5},{5,4},{6,7},{7,6},{8,9},{9,8},{10,11... | collective-permute-start | bytes 6291464 | tf_op jit(solution)/shard_map/ppermute | solution.py:1019
  227.1 45.1 %copy-start.133 = (f32[16,1,128]{2,1,0:T(1,128)S(1)}, f32[16,1,128]{2,1,0:T(1,128)}, u32[]{:S(2)}) copy-start(f32[16,1,128]{2,1,0:T(1,128)} %get-tuple-element.309) | copy-start | bytes 24580
  279.9 157.4 %copy-start.4 = (bf16[512,2048]{1,0:T(8,128)(2,1)}, bf16[512,2048]{1,0:T(8,128)(2,1)S(1)}, u32[]{:S(2)}) copy-start(bf16[512,2048]{1,0:T(8,128)(2,1)S(1)} %reorder_columns.4.left_ref) | copy-start | bytes 6291460
  289.3 30.1 %copy-start.13 = (bf16[512,2048]{1,0:T(8,128)(2,1)S(1)}, bf16[512,2048]{1,0:T(8,128)(2,1)}, u32[]{:S(2)}) copy-start(bf16[512,2048]{1,0:T(8,128)(2,1)} %copy-done.12) | copy-start | bytes 6291460
  319.4 23.8 %copy-start.30 = (bf16[512,2048]{1,0:T(8,128)(2,1)}, bf16[512,2048]{1,0:T(8,128)(2,1)S(1)}, u32[]{:S(2)}) copy-start(bf16[512,2048]{1,0:T(8,128)(2,1)S(1)} %get-tuple-element.164.right_ref) | copy-start | bytes 6291460
  319.4 65.3 %copy-start.9 = (bf16[512,2048]{1,0:T(8,128)(2,1)}, bf16[512,2048]{1,0:T(8,128)(2,1)S(1)}, u32[]{:S(2)}) copy-start(bf16[512,2048]{1,0:T(8,128)(2,1)S(1)} %get-tuple-element.161.left_ref.right_ref) | copy-start | bytes 6291460
  322.8 8.8 %collective-permute-start.4 = (bf16[1024,2048]{1,0:T(8,128)(2,1)S(1)}, bf16[1024,2048]{1,0:T(8,128)(2,1)S(1)}, u32[]{:S(2)}, u32[]{:S(2)}) collective-permute-start(bf16[1024,2048]{1,0:T(8,128)(2,1)S(1)} %scatter_part.37), channel_id=1, source_target_pairs={{0,2},{2,0},{4,6},{6,4},{8,10},{10,8},{12,14},{14,12},{16,18},{18,... | collective-permute-start | bytes 12582920 | tf_op jit(solution)/shard_map/ppermute | solution.py:1052
  329.8 48.4 %collective-permute-start.6 = (bf16[1024,2048]{1,0:T(8,128)(2,1)}, bf16[1024,2048]{1,0:T(8,128)(2,1)S(1)}, u32[]{:S(2)}, u32[]{:S(2)}) collective-permute-start(bf16[1024,2048]{1,0:T(8,128)(2,1)} %scatter_part.38), channel_id=1, source_target_pairs={{0,2},{2,0},{4,6},{6,4},{8,10},{10,8},{12,14},{14,12},{16,18},{18,... | collective-permute-start | bytes 12582920 | tf_op jit(solution)/shard_map/ppermute | solution.py:1052
  330.1 48.1 %collective-permute-start.7 = (bf16[512,2048]{1,0:T(8,128)(2,1)}, bf16[512,2048]{1,0:T(8,128)(2,1)}, u32[]{:S(2)}, u32[]{:S(2)}) collective-permute-start(bf16[512,2048]{1,0:T(8,128)(2,1)} %get-tuple-element.172.own_ref), channel_id=1, source_target_pairs={{0,1},{1,0},{2,3},{3,2},{4,5},{5,4},{6,7},{7,6},{8,9},{9,8},{10,11... | collective-permute-start | bytes 6291464 | tf_op jit(solution)/shard_map/ppermute | solution.py:1019
  331.6 53.1 %copy-start.21 = (bf16[1024,2048]{1,0:T(8,128)(2,1)}, bf16[1024,2048]{1,0:T(8,128)(2,1)S(1)}, u32[]{:S(2)}) copy-start(bf16[1024,2048]{1,0:T(8,128)(2,1)S(1)} %collective-permute-done.4.got_ref.refs_0_) | copy-start | bytes 12582916
  333.8 47.8 %collective-permute-start.5 = (bf16[512,2048]{1,0:T(8,128)(2,1)}, bf16[512,2048]{1,0:T(8,128)(2,1)}, u32[]{:S(2)}, u32[]{:S(2)}) collective-permute-start(bf16[512,2048]{1,0:T(8,128)(2,1)} %join_parts.19), channel_id=1, source_target_pairs={{0,4},{2,6},{4,0},{6,2},{8,12},{10,14},{12,8},{14,10},{16,20},{18,... | collective-permute-start | bytes 6291464 | tf_op jit(solution)/shard_map/ppermute | solution.py:1052
  381.6 50.1 %collective-permute-start.9 = (bf16[1024,2048]{1,0:T(8,128)(2,1)}, bf16[1024,2048]{1,0:T(8,128)(2,1)}, u32[]{:S(2)}, u32[]{:S(2)}) collective-permute-start(bf16[1024,2048]{1,0:T(8,128)(2,1)} %scatter_part.43), channel_id=1, source_target_pairs={{0,2},{2,0},{4,6},{6,4},{8,10},{10,8},{12,14},{14,12},{16,18},{18,... | collective-permute-start | bytes 12582920 | tf_op jit(solution)/shard_map/ppermute | solution.py:1052
  383.5 48.3 %collective-permute-start.8 = (bf16[512,2048]{1,0:T(8,128)(2,1)}, bf16[512,2048]{1,0:T(8,128)(2,1)S(1)}, u32[]{:S(2)}, u32[]{:S(2)}) collective-permute-start(bf16[512,2048]{1,0:T(8,128)(2,1)} %join_parts.20), channel_id=1, source_target_pairs={{0,4},{2,6},{4,0},{6,2},{8,12},{10,14},{12,8},{14,10},{16,20},{18,... | collective-permute-start | bytes 6291464 | tf_op jit(solution)/shard_map/ppermute | solution.py:1052
  386.7 36.7 %collective-permute-start.10 = (bf16[256,2048]{1,0:T(8,128)(2,1)S(1)}, bf16[256,2048]{1,0:T(8,128)(2,1)S(1)}, u32[]{:S(2)}, u32[]{:S(2)}) collective-permute-start(bf16[256,2048]{1,0:T(8,128)(2,1)S(1)} %scatter_part.40), channel_id=1, source_target_pairs={{0,8},{2,10},{4,12},{6,14},{8,0},{10,2},{12,4},{14,6},{16,24},{18,... | collective-permute-start | bytes 3145736 | tf_op jit(solution)/shard_map/ppermute | solution.py:1052
  404.4 19.1 %collective-permute-start.11 = (f32[512,128]{1,0:T(8,128)S(1)}, f32[512,128]{1,0:T(8,128)S(1)}, u32[]{:S(2)}, u32[]{:S(2)}) collective-permute-start(f32[512,128]{1,0:T(8,128)S(1)} %get-tuple-element.175.own_ref), channel_id=1, source_target_pairs={{0,1},{1,0},{2,3},{3,2},{4,5},{5,4},{6,7},{7,6},{8,9},{9,8},{10,11... | collective-permute-start | bytes 786440 | tf_op jit(solution)/shard_map/ppermute | solution.py:1019
  406.1 73.5 %copy-start.16 = (bf16[512,2048]{1,0:T(8,128)(2,1)}, bf16[512,2048]{1,0:T(8,128)(2,1)S(1)}, u32[]{:S(2)}) copy-start(bf16[512,2048]{1,0:T(8,128)(2,1)S(1)} %pad_maximum_fusion.right_ref) | copy-start | bytes 6291460
  415.3 22.0 %copy-start.31 = (bf16[512,2048]{1,0:T(8,128)(2,1)S(1)}, bf16[512,2048]{1,0:T(8,128)(2,1)}, u32[]{:S(2)}) copy-start(bf16[512,2048]{1,0:T(8,128)(2,1)} %copy-done.30) | copy-start | bytes 6291460
  423.4 18.1 %copy-start.62 = (bf16[256,2048]{1,0:T(8,128)(2,1)}, bf16[256,2048]{1,0:T(8,128)(2,1)S(1)}, u32[]{:S(2)}) copy-start(bf16[256,2048]{1,0:T(8,128)(2,1)S(1)} %collective-permute-done.10.refs_2_) | copy-start | bytes 3145732
  431.7 52.3 %collective-permute-start.14 = (bf16[1024,2048]{1,0:T(8,128)(2,1)}, bf16[1024,2048]{1,0:T(8,128)(2,1)}, u32[]{:S(2)}, u32[]{:S(2)}) collective-permute-start(bf16[1024,2048]{1,0:T(8,128)(2,1)} %scatter_part.41), channel_id=1, source_target_pairs={{0,2},{2,0},{4,6},{6,4},{8,10},{10,8},{12,14},{14,12},{16,18},{18,... | collective-permute-start | bytes 12582920 | tf_op jit(solution)/shard_map/ppermute | solution.py:1052
  435.5 47.7 %collective-permute-start.12 = (bf16[512,2048]{1,0:T(8,128)(2,1)}, bf16[512,2048]{1,0:T(8,128)(2,1)}, u32[]{:S(2)}, u32[]{:S(2)}) collective-permute-start(bf16[512,2048]{1,0:T(8,128)(2,1)} %join_parts.21), channel_id=1, source_target_pairs={{0,4},{2,6},{4,0},{6,2},{8,12},{10,14},{12,8},{14,10},{16,20},{18,... | collective-permute-start | bytes 6291464 | tf_op jit(solution)/shard_map/ppermute | solution.py:1052
  436.7 47.3 %collective-permute-start.16 = (bf16[512,2048]{1,0:T(8,128)(2,1)}, bf16[512,2048]{1,0:T(8,128)(2,1)S(1)}, u32[]{:S(2)}, u32[]{:S(2)}) collective-permute-start(bf16[512,2048]{1,0:T(8,128)(2,1)} %product_back.1.own_ref), channel_id=1, source_target_pairs={{0,1},{1,0},{2,3},{3,2},{4,5},{5,4},{6,7},{7,6},{8,9},{9,8},{10,11... | collective-permute-start | bytes 6291464 | tf_op jit(solution)/shard_map/ppermute | solution.py:1019
  440.0 43.0 %collective-permute-start.13 = (bf16[256,2048]{1,0:T(8,128)(2,1)S(1)}, bf16[256,2048]{1,0:T(8,128)(2,1)S(1)}, u32[]{:S(2)}, u32[]{:S(2)}) collective-permute-start(bf16[256,2048]{1,0:T(8,128)(2,1)S(1)} %scatter_part.44), channel_id=1, source_target_pairs={{0,8},{2,10},{4,12},{6,14},{8,0},{10,2},{12,4},{14,6},{16,24},{18,... | collective-permute-start | bytes 3145736 | tf_op jit(solution)/shard_map/ppermute | solution.py:1052
  444.8 38.2 %collective-permute-start.15 = (bf16[128,2048]{1,0:T(8,128)(2,1)}, bf16[128,2048]{1,0:T(8,128)(2,1)S(1)}, u32[]{:S(2)}, u32[]{:S(2)}) collective-permute-start(bf16[128,2048]{1,0:T(8,128)(2,1)} %scatter_part.45), channel_id=1, source_target_pairs={{0,16},{2,18},{4,20},{6,22},{8,24},{10,26},{12,28},{14,30},{16,0},... | collective-permute-start | bytes 1572872 | tf_op jit(solution)/shard_map/ppermute | solution.py:1052
  448.3 26.7 %copy-start.2 = (bf16[512,2048]{1,0:T(8,128)(2,1)}, bf16[512,2048]{1,0:T(8,128)(2,1)S(1)}, u32[]{:S(2)}) copy-start(bf16[512,2048]{1,0:T(8,128)(2,1)S(1)} %reorder_columns.7.left_ref) | copy-start | bytes 6291460
  448.4 25.4 %copy-start.100 = (bf16[512,512]{1,0:T(8,128)(2,1)S(1)}, bf16[512,512]{1,0:T(8,128)(2,1)}, u32[]{:S(2)}) copy-start(bf16[512,512]{1,0:T(8,128)(2,1)} %copy-done.99) | copy-start | bytes 1572868
  484.0 51.4 %collective-permute-start.21 = (bf16[1024,2048]{1,0:T(8,128)(2,1)}, bf16[1024,2048]{1,0:T(8,128)(2,1)}, u32[]{:S(2)}, u32[]{:S(2)}) collective-permute-start(bf16[1024,2048]{1,0:T(8,128)(2,1)} %scatter_part.46), channel_id=1, source_target_pairs={{0,2},{2,0},{4,6},{6,4},{8,10},{10,8},{12,14},{14,12},{16,18},{18,... | collective-permute-start | bytes 12582920 | tf_op jit(solution)/shard_map/ppermute | solution.py:1052
  488.3 47.0 %collective-permute-start.18 = (bf16[512,2048]{1,0:T(8,128)(2,1)}, bf16[512,2048]{1,0:T(8,128)(2,1)}, u32[]{:S(2)}, u32[]{:S(2)}) collective-permute-start(bf16[512,2048]{1,0:T(8,128)(2,1)} %join_parts.22), channel_id=1, source_target_pairs={{0,4},{2,6},{4,0},{6,2},{8,12},{10,14},{12,8},{14,10},{16,20},{18,... | collective-permute-start | bytes 6291464 | tf_op jit(solution)/shard_map/ppermute | solution.py:1052
  492.7 37.3 %collective-permute-start.19 = (bf16[256,2048]{1,0:T(8,128)(2,1)}, bf16[256,2048]{1,0:T(8,128)(2,1)}, u32[]{:S(2)}, u32[]{:S(2)}) collective-permute-start(bf16[256,2048]{1,0:T(8,128)(2,1)} %scatter_part.48), channel_id=1, source_target_pairs={{0,8},{2,10},{4,12},{6,14},{8,0},{10,2},{12,4},{14,6},{16,24},{18,... | collective-permute-start | bytes 3145736 | tf_op jit(solution)/shard_map/ppermute | solution.py:1052
  493.8 13.5 %collective-permute-start.17 = (bf16[528,512]{1,0:T(8,128)(2,1)}, bf16[528,512]{1,0:T(8,128)(2,1)S(1)}, u32[]{:S(2)}, u32[]{:S(2)}) collective-permute-start(bf16[528,512]{1,0:T(8,128)(2,1)} %get-tuple-element.203.refs_0_.refs_4_), channel_id=1, source_target_pairs={{0,1},{1,0},{2,3},{3,2},{4,5},{5,4},{6,7},{7,6},{8,9},{9,8},{10,11... | collective-permute-start | bytes 1622024 | tf_op jit(solution)/shard_map/ppermute | solution.py:1019
  495.9 34.0 %collective-permute-start.20 = (bf16[128,2048]{1,0:T(8,128)(2,1)}, bf16[128,2048]{1,0:T(8,128)(2,1)}, u32[]{:S(2)}, u32[]{:S(2)}) collective-permute-start(bf16[128,2048]{1,0:T(8,128)(2,1)} %scatter_part.49), channel_id=1, source_target_pairs={{0,16},{2,18},{4,20},{6,22},{8,24},{10,26},{12,28},{14,30},{16,0},... | collective-permute-start | bytes 1572872 | tf_op jit(solution)/shard_map/ppermute | solution.py:1052
  535.4 52.1 %collective-permute-start.23 = (bf16[1024,1792]{1,0:T(8,128)(2,1)}, bf16[1024,1792]{1,0:T(8,128)(2,1)S(1)}, u32[]{:S(2)}, u32[]{:S(2)}) collective-permute-start(bf16[1024,1792]{1,0:T(8,128)(2,1)} %scatter_part.50), channel_id=1, source_target_pairs={{0,2},{2,0},{4,6},{6,4},{8,10},{10,8},{12,14},{14,12},{16,18},{18,... | collective-permute-start | bytes 11010056 | tf_op jit(solution)/shard_map/ppermute | solution.py:1052
  538.5 48.4 %collective-permute-start.22 = (bf16[512,2048]{1,0:T(8,128)(2,1)}, bf16[512,2048]{1,0:T(8,128)(2,1)}, u32[]{:S(2)}, u32[]{:S(2)}) collective-permute-start(bf16[512,2048]{1,0:T(8,128)(2,1)} %join_parts.23), channel_id=1, source_target_pairs={{0,4},{2,6},{4,0},{6,2},{8,12},{10,14},{12,8},{14,10},{16,20},{18,... | collective-permute-start | bytes 6291464 | tf_op jit(solution)/shard_map/ppermute | solution.py:1052
  539.4 48.1 %collective-permute-start.26 = (bf16[512,2048]{1,0:T(8,128)(2,1)}, bf16[512,2048]{1,0:T(8,128)(2,1)}, u32[]{:S(2)}, u32[]{:S(2)}) collective-permute-start(bf16[512,2048]{1,0:T(8,128)(2,1)} %hidden_back.1.own_ref), channel_id=1, source_target_pairs={{0,1},{1,0},{2,3},{3,2},{4,5},{5,4},{6,7},{7,6},{8,9},{9,8},{10,11... | collective-permute-start | bytes 6291464 | tf_op jit(solution)/shard_map/ppermute | solution.py:1019
  543.6 36.6 %collective-permute-start.24 = (bf16[256,2048]{1,0:T(8,128)(2,1)}, bf16[256,2048]{1,0:T(8,128)(2,1)}, u32[]{:S(2)}, u32[]{:S(2)}) collective-permute-start(bf16[256,2048]{1,0:T(8,128)(2,1)} %scatter_part.53), channel_id=1, source_target_pairs={{0,8},{2,10},{4,12},{6,14},{8,0},{10,2},{12,4},{14,6},{16,24},{18,... | collective-permute-start | bytes 3145736 | tf_op jit(solution)/shard_map/ppermute | solution.py:1052
  547.7 31.5 %collective-permute-start.25 = (bf16[128,2048]{1,0:T(8,128)(2,1)}, bf16[128,2048]{1,0:T(8,128)(2,1)}, u32[]{:S(2)}, u32[]{:S(2)}) collective-permute-start(bf16[128,2048]{1,0:T(8,128)(2,1)} %scatter_part.54), channel_id=1, source_target_pairs={{0,16},{2,18},{4,20},{6,22},{8,24},{10,26},{12,28},{14,30},{16,0},... | collective-permute-start | bytes 1572872 | tf_op jit(solution)/shard_map/ppermute | solution.py:1052
  589.9 41.6 %collective-permute-start.28 = (bf16[512,1792]{1,0:T(8,128)(2,1)}, bf16[512,1792]{1,0:T(8,128)(2,1)}, u32[]{:S(2)}, u32[]{:S(2)}) collective-permute-start(bf16[512,1792]{1,0:T(8,128)(2,1)} %join_parts.24), channel_id=1, source_target_pairs={{0,4},{2,6},{4,0},{6,2},{8,12},{10,14},{12,8},{14,10},{16,20},{18,... | collective-permute-start | bytes 5505032 | tf_op jit(solution)/shard_map/ppermute | solution.py:1052
  591.1 39.9 %collective-permute-start.29 = (bf16[1024,768]{1,0:T(8,128)(2,1)}, bf16[1024,768]{1,0:T(8,128)(2,1)S(1)}, u32[]{:S(2)}, u32[]{:S(2)}) collective-permute-start(bf16[1024,768]{1,0:T(8,128)(2,1)} %scatter_part.51), channel_id=1, source_target_pairs={{0,2},{2,0},{4,6},{6,4},{8,10},{10,8},{12,14},{14,12},{16,18},{18,... | collective-permute-start | bytes 4718600 | tf_op jit(solution)/shard_map/ppermute | solution.py:1052
  593.8 37.1 %collective-permute-start.30 = (bf16[256,2048]{1,0:T(8,128)(2,1)}, bf16[256,2048]{1,0:T(8,128)(2,1)}, u32[]{:S(2)}, u32[]{:S(2)}) collective-permute-start(bf16[256,2048]{1,0:T(8,128)(2,1)} %join_parts.25), channel_id=1, source_target_pairs={{0,8},{2,10},{4,12},{6,14},{8,0},{10,2},{12,4},{14,6},{16,24},{18,... | collective-permute-start | bytes 3145736 | tf_op jit(solution)/shard_map/ppermute | solution.py:1052
  597.4 32.5 %collective-permute-start.31 = (bf16[128,2048]{1,0:T(8,128)(2,1)}, bf16[128,2048]{1,0:T(8,128)(2,1)}, u32[]{:S(2)}, u32[]{:S(2)}) collective-permute-start(bf16[128,2048]{1,0:T(8,128)(2,1)} %join_parts.26), channel_id=1, source_target_pairs={{0,16},{2,18},{4,20},{6,22},{8,24},{10,26},{12,28},{14,30},{16,0},... | collective-permute-start | bytes 1572872 | tf_op jit(solution)/shard_map/ppermute | solution.py:1052
  614.8 1.3 collective-permute-start.27
  631.0 41.2 %copy-start.42 = (bf16[1024,768]{1,0:T(8,128)(2,1)}, bf16[1024,768]{1,0:T(8,128)(2,1)S(1)}, u32[]{:S(2)}) copy-start(bf16[1024,768]{1,0:T(8,128)(2,1)S(1)} %collective-permute-done.29.got_ref.refs_0_) | copy-start | bytes 4718596
  633.3 33.8 %collective-permute-start.33 = (bf16[256,1792]{1,0:T(8,128)(2,1)S(1)}, bf16[256,1792]{1,0:T(8,128)(2,1)S(1)}, u32[]{:S(2)}, u32[]{:S(2)}) collective-permute-start(bf16[256,1792]{1,0:T(8,128)(2,1)S(1)} %join_parts.29), channel_id=1, source_target_pairs={{0,8},{2,10},{4,12},{6,14},{8,0},{10,2},{12,4},{14,6},{16,24},{18,... | collective-permute-start | bytes 2752520 | tf_op jit(solution)/shard_map/ppermute | solution.py:1052
  635.7 30.7 %collective-permute-start.32 = (bf16[512,768]{1,0:T(8,128)(2,1)S(1)}, bf16[512,768]{1,0:T(8,128)(2,1)S(1)}, u32[]{:S(2)}, u32[]{:S(2)}) collective-permute-start(bf16[512,768]{1,0:T(8,128)(2,1)S(1)} %join_parts.28), channel_id=1, source_target_pairs={{0,4},{2,6},{4,0},{6,2},{8,12},{10,14},{12,8},{14,10},{16,20},{18,... | collective-permute-start | bytes 2359304 | tf_op jit(solution)/shard_map/ppermute | solution.py:1052
  637.8 28.6 %collective-permute-start.34 = (bf16[128,2048]{1,0:T(8,128)(2,1)S(1)}, bf16[128,2048]{1,0:T(8,128)(2,1)S(1)}, u32[]{:S(2)}, u32[]{:S(2)}) collective-permute-start(bf16[128,2048]{1,0:T(8,128)(2,1)S(1)} %join_parts.30), channel_id=1, source_target_pairs={{0,16},{2,18},{4,20},{6,22},{8,24},{10,26},{12,28},{14,30},{16,0},... | collective-permute-start | bytes 1572872 | tf_op jit(solution)/shard_map/ppermute | solution.py:1052
  639.3 16.7 %collective-permute-start.35 = (bf16[16,2048]{1,0:T(8,128)(2,1)S(1)}, bf16[16,2048]{1,0:T(8,128)(2,1)S(1)}, u32[]{:S(2)}, u32[]{:S(2)}) collective-permute-start(bf16[16,2048]{1,0:T(8,128)(2,1)S(1)} %add_rows.4.left_ref), channel_id=1, source_target_pairs={{0,4},{2,6},{4,0},{6,2},{8,12},{10,14},{12,8},{14,10},{16,20},{18,... | collective-permute-start | bytes 196616 | tf_op jit(solution)/shard_map/ppermute | solution.py:1052
  667.3 22.8 %collective-permute-start.37 = (bf16[128,1792]{1,0:T(8,128)(2,1)S(1)}, bf16[128,1792]{1,0:T(8,128)(2,1)S(1)}, u32[]{:S(2)}, u32[]{:S(2)}) collective-permute-start(bf16[128,1792]{1,0:T(8,128)(2,1)S(1)} %join_parts.33), channel_id=1, source_target_pairs={{0,16},{2,18},{4,20},{6,22},{8,24},{10,26},{12,28},{14,30},{16,0},... | collective-permute-start | bytes 1376264 | tf_op jit(solution)/shard_map/ppermute | solution.py:1052
  670.0 20.1 %collective-permute-start.36 = (bf16[256,768]{1,0:T(8,128)(2,1)S(1)}, bf16[256,768]{1,0:T(8,128)(2,1)S(1)}, u32[]{:S(2)}, u32[]{:S(2)}) collective-permute-start(bf16[256,768]{1,0:T(8,128)(2,1)S(1)} %join_parts.32), channel_id=1, source_target_pairs={{0,8},{2,10},{4,12},{6,14},{8,0},{10,2},{12,4},{14,6},{16,24},{18,... | collective-permute-start | bytes 1179656 | tf_op jit(solution)/shard_map/ppermute | solution.py:1052
  670.0 20.1 %collective-permute-start.38 = (bf16[16,2048]{1,0:T(8,128)(2,1)S(1)}, bf16[16,2048]{1,0:T(8,128)(2,1)S(1)}, u32[]{:S(2)}, u32[]{:S(2)}) collective-permute-start(bf16[16,2048]{1,0:T(8,128)(2,1)S(1)} %add_rows.5.left_ref), channel_id=1, source_target_pairs={{0,8},{2,10},{4,12},{6,14},{8,0},{10,2},{12,4},{14,6},{16,24},{18,... | collective-permute-start | bytes 196616 | tf_op jit(solution)/shard_map/ppermute | solution.py:1052
  691.0 12.2 %collective-permute-start.39 = (bf16[128,768]{1,0:T(8,128)(2,1)}, bf16[128,768]{1,0:T(8,128)(2,1)}, u32[]{:S(2)}, u32[]{:S(2)}) collective-permute-start(bf16[128,768]{1,0:T(8,128)(2,1)} %join_parts.35), channel_id=1, source_target_pairs={{0,16},{2,18},{4,20},{6,22},{8,24},{10,26},{12,28},{14,30},{16,0},... | collective-permute-start | bytes 589832 | tf_op jit(solution)/shard_map/ppermute | solution.py:1052
  692.4 12.7 %collective-permute-start.40 = (bf16[16,2048]{1,0:T(8,128)(2,1)}, bf16[16,2048]{1,0:T(8,128)(2,1)}, u32[]{:S(2)}, u32[]{:S(2)}) collective-permute-start(bf16[16,2048]{1,0:T(8,128)(2,1)} %add_rows.6.left_ref), channel_id=1, source_target_pairs={{0,16},{2,18},{4,20},{6,22},{8,24},{10,26},{12,28},{14,30},{16,0},... | collective-permute-start | bytes 196616 | tf_op jit(solution)/shard_map/ppermute | solution.py:1052
  (124 other events, 491.6 us)
Sparse Core Ops, SparseCore 0:
  18.4 140.1 all-gather.2
  160.7 128.5 all-gather.4
